TPU v7x, 512 devices: a whole 4x4x16 slice. The times are simulated.
512 devices in a mesh: dp: 32 (over z, core), tensor: 16 (over y, x).
Axes of the slice: x: 4, y: 4, z: 16, core: 2. Of those that a mesh axis runs over, the one named last changes fastest.
Arguments:
- hidden: bfloat16 [8192, 4096], P(('dp', 'tensor')), may hold values from -3.6 to 3.6
- lengths: int32 [32, 32], P('dp'), may hold values from 1 to 80, 256 in all within a row
- positives: int32 [256], replicated, may hold values from 0 to 767, as said below
- negatives: int32 [256, 7], replicated, may hold values from 1 to 766, as said below
- in_gain: float32 [4096], replicated, may hold values from 0.25 to 1.75
- wq: bfloat16 [4096, 2048], P(None, 'tensor'), may hold values from -0.09375 to 0.09375
- wkv: bfloat16 [4096, 2048], P(None, 'tensor'), may hold values from -0.09375 to 0.09375
- q_gain: float32 [128], replicated, may hold values from 0.25 to 1.75
- k_gain: float32 [128], replicated, may hold values from 0.25 to 1.75
- wo: bfloat16 [2048, 4096], P('tensor'), may hold values from -0.125 to 0.125
- out_gain: float32 [4096], replicated, may hold values from 0.25 to 1.75
Outputs:
- d_hidden: bfloat16 [8192, 4096], P(('dp', 'tensor'))
- loss: float32 [], replicated
Inputs may be any that keep to these rules, and one draw needn't show every extreme that they name: Each group's 32 lengths sum to 256, and one of them is exactly 80. The 256 positives are distinct passages. The 7 hard negatives of a query are distinct, and none of them is any query's positive.
All inputs are finite; a program needn't handle non-finite values.
Results may differ from a plain program's by a relative error of at most 0.023.
Values may be sent and summed in bfloat16 or wider, within the bound.
No kernel may reach another device: no remote copies, remote signals or barrier semaphores. Data moves between devices by JAX's collectives and lax.ppermute only.
A program may use at most 64 MiB of HBM per device.

v0:
```python
import math

import jax
import jax.numpy as jnp
from jax import lax
from jax.sharding import PartitionSpec as P

QDEV = 8


EPSILON = 1e-06
SOFTMAX_TEMPER = 0.05
LOSS_MULTIPLIER = 8192.0
ROPE_BASE = 1000000.0


def swapped(value, axis, apart):
    mask = 2**apart
    pairs = [(source, source ^ mask) for source in range(lax.axis_size(axis))]
    return lax.ppermute(value, axis, pairs)


def rms_scale(tensor):
    return lax.rsqrt(jnp.mean(tensor * tensor, axis=-1, keepdims=True) + EPSILON)


def rope_tables(position, head_width):
    halfway = head_width // 2
    frequency = ROPE_BASE ** (-(jnp.arange(halfway, dtype=jnp.float32) * (2.0 / head_width)))
    angles = position[:, None] * frequency[None, :]
    angles = jnp.concatenate([angles, angles], axis=-1)
    return (jnp.cos(angles), jnp.sin(angles))


def rotate(tensor, cosine, sine):
    halfway = tensor.shape[-1] // 2
    turned = jnp.concatenate([-tensor[..., halfway:], tensor[..., :halfway]], axis=-1)
    return tensor * cosine + turned * sine


def segment_layout(lengths_row, total_tokens):
    seq_ends = jnp.cumsum(lengths_row)
    starts = seq_ends - lengths_row
    token_index = jnp.arange(total_tokens, dtype=jnp.int32)
    inside = (token_index[:, None] >= starts[None, :]) & (token_index[:, None] < seq_ends[None, :])
    offset = jnp.sum(jnp.where(inside, starts[None, :], 0), axis=1)
    position = (token_index - offset).astype(jnp.float32)
    return (inside, position, seq_ends - 1)


def head_forward(raw, gain, cosine, sine):
    inverse = rms_scale(raw)
    unit_form = raw * inverse
    return (unit_form, inverse, rotate(unit_form * gain, cosine, sine))


def norm_backward(grad, unit_form, inverse, gain):
    scaled = grad * gain
    return inverse * (scaled - unit_form * jnp.mean(unit_form * scaled, axis=-1, keepdims=True))


def head_backward(grad_rot, unit_form, inverse, gain, cosine, sine):
    return norm_backward(rotate(grad_rot, cosine, -sine), unit_form, inverse, gain)


def contrast(embeds16, positives, negatives):
    groups = embeds16.shape[0]
    feature_count = embeds16.shape[2]
    query_rows = embeds16[:, :QDEV].reshape(groups * QDEV, feature_count)
    passage_rows = embeds16[:, QDEV:].reshape(-1, feature_count)
    query_total_count = query_rows.shape[0]
    passage_ids = jnp.arange(passage_rows.shape[0], dtype=jnp.int32)
    similarity_logits = (
        jnp.dot(query_rows, passage_rows.T, preferred_element_type=jnp.float32) / SOFTMAX_TEMPER
    )
    positive_hot = positives[:, None] == passage_ids[None, :]
    hard_hot = jnp.any(negatives[:, :, None] == passage_ids[None, None, :], axis=1)
    permitted_mask = jnp.any(positive_hot, axis=0)[None, :] | hard_hot
    weight_params = jnp.where(
        permitted_mask, jnp.exp(similarity_logits - 1.0 / SOFTMAX_TEMPER), 0.0
    )
    running_totals = jnp.sum(weight_params, axis=1, keepdims=True)
    target_labels = jnp.sum(jnp.where(positive_hot, similarity_logits, 0.0), axis=1)
    loss = jnp.mean(jnp.log(running_totals[:, 0]) + 1.0 / SOFTMAX_TEMPER - target_labels)
    scaling_factor = LOSS_MULTIPLIER / (query_total_count * SOFTMAX_TEMPER)
    coef16 = (
        scaling_factor * (weight_params / running_totals - positive_hot.astype(jnp.float32))
    ).astype(jnp.bfloat16)
    d_queries = jnp.dot(coef16, passage_rows, preferred_element_type=jnp.float32)
    d_passages = jnp.dot(coef16.T, query_rows, preferred_element_type=jnp.float32)
    joined = jnp.concatenate(
        [
            d_queries.reshape(groups, QDEV, feature_count),
            d_passages.reshape(groups, -1, feature_count),
        ],
        axis=1,
    )
    return (loss, joined)


def on_device(
    hidden, lengths, positives, negatives, in_gain, wq, wkv, q_gain, k_gain, wo, out_gain
):
    tensor_count = lax.axis_size("tensor")
    own_rows = hidden.shape[0]
    tokens_count = own_rows * tensor_count
    head_width = wq.shape[1]
    root = math.sqrt(head_width)
    is_even = lax.axis_index("tensor") % 2 == 0
    own_index = lax.axis_index("tensor") * own_rows + jnp.arange(own_rows, dtype=jnp.int32)
    inside, position, last = segment_layout(lengths[0], tokens_count)
    hidden32 = hidden.astype(jnp.float32)
    inverse_in = rms_scale(hidden32)
    normed = (hidden32 * inverse_in * in_gain).astype(jnp.bfloat16)
    partner = swapped(wkv, "tensor", 0)
    both = jnp.concatenate(
        [jnp.where(is_even, wkv, partner), jnp.where(is_even, partner, wkv)], axis=1
    )
    piece = lax.all_gather(normed, "tensor", axis=0, tiled=True)
    kv_raw = jnp.dot(piece, both, preferred_element_type=jnp.float32)
    key_raw = kv_raw[:, :head_width]
    value_raw = kv_raw[:, head_width:]
    value16 = value_raw.astype(jnp.bfloat16)
    cos_key, sin_key = rope_tables(position, head_width)
    key_unit, key_inverse, key_rot = head_forward(key_raw, k_gain, cos_key, sin_key)
    key16 = key_rot.astype(jnp.bfloat16)
    last_rows = jnp.take(piece, last, axis=0)
    query_raw = jnp.dot(last_rows, wq, preferred_element_type=jnp.float32)
    cos_query, sin_query = rope_tables(jnp.take(position, last), head_width)
    query_unit, query_inverse, query_rot = head_forward(query_raw, q_gain, cos_query, sin_query)
    query16 = query_rot.astype(jnp.bfloat16)
    shift = root * jnp.max(q_gain) * jnp.max(k_gain)
    scores = jnp.dot(query16, key16.T, preferred_element_type=jnp.float32) / root
    weight_params = jnp.where(inside.T, jnp.exp(scores - shift), 0.0)
    probs = weight_params / jnp.sum(weight_params, axis=-1, keepdims=True)
    probs16 = probs.astype(jnp.bfloat16)
    attn16 = jnp.dot(probs16, value16, preferred_element_type=jnp.float32).astype(jnp.bfloat16)
    own_last = (last[:, None] == own_index[None, :]).astype(jnp.float32)
    partial_rows = jnp.dot(attn16, wo, preferred_element_type=jnp.float32)
    partial_rows = partial_rows + jnp.dot(own_last, hidden32, precision=lax.Precision.HIGHEST)
    resid = lax.psum(partial_rows, "tensor")
    resid_inverse = rms_scale(resid)
    resid_unit = resid * resid_inverse
    final = resid_unit * out_gain
    final_inverse = lax.rsqrt(jnp.sum(final * final, axis=-1, keepdims=True) + EPSILON)
    embed = final * final_inverse
    everyone = lax.all_gather(embed.astype(jnp.bfloat16), "dp", axis=0, tiled=True)
    groups = lax.axis_size("dp")
    loss, d_every = contrast(everyone.reshape(groups, -1, everyone.shape[1]), positives, negatives)
    d_embed = lax.dynamic_index_in_dim(d_every, lax.axis_index("dp"), 0, keepdims=False)
    d_final = final_inverse * (d_embed - embed * jnp.sum(embed * d_embed, axis=-1, keepdims=True))
    d_resid = norm_backward(d_final, resid_unit, resid_inverse, out_gain)
    d_attn16 = jnp.dot(
        d_resid.astype(jnp.bfloat16), wo.T, preferred_element_type=jnp.float32
    ).astype(jnp.bfloat16)
    d_probs = jnp.dot(d_attn16, value16.T, preferred_element_type=jnp.float32)
    d_scores16 = (
        probs * (d_probs - jnp.sum(probs * d_probs, axis=-1, keepdims=True)) / root
    ).astype(jnp.bfloat16)
    d_query_rot = jnp.dot(d_scores16, key16, preferred_element_type=jnp.float32)
    d_key_rot = jnp.dot(d_scores16.T, query16, preferred_element_type=jnp.float32)
    d_value = jnp.dot(probs16.T, d_attn16, preferred_element_type=jnp.float32)
    d_key_raw = head_backward(d_key_rot, key_unit, key_inverse, k_gain, cos_key, sin_key)
    d_query_raw = head_backward(
        d_query_rot, query_unit, query_inverse, q_gain, cos_query, sin_query
    )
    mine = jnp.where(is_even, d_key_raw, d_value)
    theirs = jnp.where(is_even, d_value, d_key_raw)
    column16 = (mine + swapped(theirs, "tensor", 0)).astype(jnp.bfloat16)
    query_term = jnp.dot(d_query_raw.astype(jnp.bfloat16), wq.T, preferred_element_type=jnp.float32)
    row_index = jnp.arange(own_rows * lax.axis_size("tensor"), dtype=jnp.int32)
    chosen = (row_index[:, None] == last[None, :]).astype(jnp.float32)
    product = jnp.dot(column16, wkv.T, preferred_element_type=jnp.float32)
    d_normed = lax.psum_scatter(
        (product + jnp.dot(chosen, query_term, precision=lax.Precision.HIGHEST)).astype(
            jnp.bfloat16
        ),
        "tensor",
        scatter_dimension=0,
        tiled=True,
    ).astype(jnp.float32)
    d_hidden = norm_backward(d_normed, hidden32 * inverse_in, inverse_in, in_gain)
    d_hidden = d_hidden + jnp.dot(own_last.T, d_resid, precision=lax.Precision.HIGHEST)
    return (d_hidden.astype(jnp.bfloat16), loss)


def solution(mesh):
    placed = (
        P(("dp", "tensor"), None),
        P("dp", None),
        P(),
        P(),
        P(),
        P(None, "tensor"),
        P(None, "tensor"),
        P(),
        P(),
        P("tensor", None),
        P(),
    )
    return jax.shard_map(
        on_device,
        mesh=mesh,
        in_specs=placed,
        out_specs=(P(("dp", "tensor"), None), P()),
        check_vma=False,
    )
```

profile of v0, /device:TPU:32, one launch (start us, length us, event | category | flops | bytes accessed | tf_op | source)
XLA Modules:
  0.0 409.4 jit_solution(15315074954518132723)
XLA Ops:
  7.2 1.1 fusion.41
  8.4 1.7 fusion.37
  10.1 0.0 all-reduce.2.cloned.1.call-start
  10.1 3.4 collective-permute-start
  13.5 0.7 copy.23
  14.3 0.1 reduce-window.4
  14.3 0.1 fusion.68
  14.4 0.7 fusion.86
  15.1 0.1 select_reduce_fusion.1
  15.2 1.3 reduce_max.19
  16.5 1.3 reduce_max.18
  19.0 0.7 gather_fusion.1
  19.8 0.1 broadcast_multiply_fusion.1
  19.8 0.1 broadcast_multiply_fusion
  19.9 1.2 fusion.66
  21.1 16.7 %collective-permute-done = bf16[4096,128]{1,0:T(8,128)(2,1)S(1)} collective-permute-done((bf16[4096,128]{1,0:T(8,128)(2,1)}, bf16[4096,128]{1,0:T(8,128)(2,1)S(1)}, u32[]{:S(2)}, u32[]{:S(2)}) %collective-permute-start) | collective-permute-done | bytes 1048608 | tf_op jit(solution)/shard_map/ppermute | solution.py:20
  37.8 2.7 broadcast_select_fusion.1
  40.5 35.5 %all-gather.3.cloned.1.call-done = bf16[256,4096]{1,0:T(8,128)(2,1)} async-done(((bf16[16,4096]{1,0:T(8,128)(2,1)}), bf16[256,4096]{1,0:T(8,128)(2,1)}) %all-gather.3.cloned.1.call-update) | async-done | bytes 2097168 | tf_op jit(solution)/shard_map/all_gather | solution.py:119
  76.0 2.8 gather_fusion
  78.9 0.4 multiply_reduce_fusion.7
  79.3 0.1 multiply_multiply_fusion.1
  79.4 0.1 slice_negate_fusion.3
  79.5 3.1 fusion.3
  82.7 0.1 fusion.59
  82.8 0.1 fusion.70
  82.9 0.5 fusion.53
  83.4 0.2 fusion.94
  83.7 1.3 convolution_add_fusion.1
  85.0 0.0 all-gather.5.cloned.1.call-start
  85.0 115.5 %all-reduce.2.cloned.1.call-done = f32[32,4096]{1,0:T(8,128)} async-done(((f32[32,4096]{1,0:T(8,128)}), f32[32,4096]{1,0:T(8,128)}) %all-reduce.2.cloned.1.call-update) | async-done | bytes 524304 | tf_op jit(solution)/shard_map/psum | solution.py:141
  200.5 1.2 multiply_reduce_fusion.2
  201.7 1.3 multiply_reduce_fusion.1
  203.0 1.9 fusion.33
  204.9 0.2 reduce-scatter.2.cloned.1.call-start
  205.2 0.2 fusion.21
  205.4 0.9 fusion
  206.3 77.7 %all-gather.5.cloned.1.call-done = bf16[1024,4096]{1,0:T(8,128)(2,1)} async-done(((bf16[32,4096]{1,0:T(8,128)(2,1)}), bf16[1024,4096]{1,0:T(8,128)(2,1)}) %all-gather.5.cloned.1.call-update) | async-done | bytes 8388624 | tf_op jit(solution)/shard_map/all_gather | solution.py:147
  284.0 3.2 slice.60
  287.2 3.7 select_reduce_fusion
  291.0 0.4 fusion.20
  291.3 4.1 %fusion.29 = f32[32,8,4096]{2,1,0:T(8,128)} fusion(bf16[768,4096,1]{1,0,2:T(8,128)(2,1)S(1)} %bitcast.69, s32[256]{0:T(256)S(1)} %copy-done.11, f32[256,768]{1,0:T(8,128)S(1)} %get-tuple-element.28, pred[256,768]{1,0:T(8,128)(4,1)S(1)} %fusion, f32[256]{0:T(256)S(1)} %get-tuple-element.3, pred[768]{0:T(1024)(128)(4,1)S(1)} %fusion.21), kind=kOutput, calls=%fused_computation.53 | convolution fusion | flops 1612382208 | bytes 11471616 | tf_op jit(solution)/shard_map/dot_general | solution.py:89
  295.4 0.2 copy.24
  295.6 3.5 fusion.7
  299.2 0.3 fusion.23
  299.5 0.3 multiply_reduce_fusion
  299.8 0.2 subtract_multiply_fusion
  300.1 0.4 convolution_convert_fusion
  300.6 0.2 multiply_reduce_fusion.5
  300.8 0.1 multiply_convert_fusion.1
  300.9 0.1 fusion.96
  301.0 0.2 fusion.95
  301.3 0.1 slice_negate_fusion.2
  301.3 0.2 multiply_reduce_fusion.6
  301.6 0.5 multiply_reduce_fusion.3
  302.1 0.2 broadcast_select_fusion.2
  302.4 3.6 collective-permute-start.1
  306.0 0.5 fusion.75
  306.5 1.8 fusion.58
  308.3 1.6 collective-permute-done.1
  309.9 2.1 fusion.1
  312.1 0.6 subtract_reduce_fusion
  313.3 85.2 %reduce-scatter.2.cloned.1.call-done = bf16[16,4096]{1,0:T(8,128)(2,1)} async-done(((bf16[256,4096]{1,0:T(8,128)(2,1)}), bf16[16,4096]{1,0:T(8,128)(2,1)}) %reduce-scatter.2.cloned.1.call-update) | async-done | bytes 131088 | tf_op jit(solution)/shard_map/reduce_scatter | solution.py:174
  398.6 1.1 fusion.38
  399.7 2.0 fusion.2
  (47 shorter events, 0.3 us)
Async XLA Ops:
  7.2 71.7 %copy-start = (bf16[4096,128]{1,0:T(8,128)(2,1)S(1)}, bf16[4096,128]{1,0:T(8,128)(2,1)}, u32[]{:S(2)}) copy-start(bf16[4096,128]{1,0:T(8,128)(2,1)} %param.16) | copy-start | bytes 3145732
  7.2 68.8 %all-gather.3.cloned.1.call-start = ((), (), s32[]{:S(2)}) async-start(), calls=%async_computation.1 | async-start | bytes 2228224 | tf_op jit(solution)/shard_map/all_gather | solution.py:119
  10.1 190.5 %all-reduce.2.cloned.1.call-start = ((), (), s32[]{:S(2)}) async-start(), calls=%async_computation.2 | async-start | bytes 1048576 | tf_op jit(solution)/shard_map/psum | solution.py:141
  10.1 27.7 %collective-permute-start = (bf16[4096,128]{1,0:T(8,128)(2,1)}, bf16[4096,128]{1,0:T(8,128)(2,1)S(1)}, u32[]{:S(2)}, u32[]{:S(2)}) collective-permute-start(bf16[4096,128]{1,0:T(8,128)(2,1)} %param.17), channel_id=1, source_target_pairs={{0,1},{1,0},{2,3},{3,2},{4,5},{5,4},{6,7},{7,6},{8,9},{9,8},{10,11... | collective-permute-start | bytes 3145736 | tf_op jit(solution)/shard_map/ppermute | solution.py:20
  19.9 59.4 %copy-start.9 = (f32[128]{0:T(128)S(1)}, f32[128]{0:T(128)}, u32[]{:S(2)}) copy-start(f32[128]{0:T(128)} %param.18) | copy-start | bytes 1540
  78.8 3.8 copy-start.10
  78.9 4.8 %copy-start.3 = (bf16[128,4096]{1,0:T(8,128)(2,1)S(1)}, bf16[128,4096]{1,0:T(8,128)(2,1)}, u32[]{:S(2)}) copy-start(bf16[128,4096]{1,0:T(8,128)(2,1)} %param.20) | copy-start | bytes 3145732
  79.5 122.2 %copy-start.6 = (f32[4096]{0:T(1024)S(1)}, f32[4096]{0:T(1024)}, u32[]{:S(2)}) copy-start(f32[4096]{0:T(1024)} %param.21) | copy-start | bytes 49156
  82.6 122.6 %copy-start.11 = (s32[256]{0:T(256)S(1)}, s32[256]{0:T(256)}, u32[]{:S(2)}) copy-start(s32[256]{0:T(256)} %param.13) | copy-start | bytes 3076
  82.6 122.7 %copy-start.8 = (s32[256,7]{0,1:T(8,128)S(1)}, s32[256,7]{0,1:T(8,128)}, u32[]{:S(2)}) copy-start(s32[256,7]{0,1:T(8,128)} %param.14) | copy-start | bytes 21508
  85.0 199.0 %all-gather.5.cloned.1.call-start = ((), (), s32[]{:S(2)}) async-start(), calls=%async_computation.3 | async-start | bytes 8650752 | tf_op jit(solution)/shard_map/all_gather | solution.py:147
  204.9 193.6 %reduce-scatter.2.cloned.1.call-start = ((), (), s32[]{:S(2)}) async-start(), calls=%async_computation.4 | async-start | bytes 2228224 | tf_op jit(solution)/shard_map/reduce_scatter | solution.py:174
  295.6 3.6 copy-start.1
  295.6 3.6 copy-start.4
  300.5 9.4 %copy-start.2 = (bf16[4096,128]{1,0:T(8,128)(2,1)S(1)}, bf16[4096,128]{1,0:T(8,128)(2,1)}, u32[]{:S(2)}) copy-start(bf16[4096,128]{1,0:T(8,128)(2,1)} %param.17) | copy-start | bytes 3145732
  302.4 7.5 %collective-permute-start.1 = (f32[256,128]{0,1:T(8,128)S(1)}, f32[256,128]{0,1:T(8,128)S(1)}, u32[]{:S(2)}, u32[]{:S(2)}) collective-permute-start(f32[256,128]{0,1:T(8,128)S(1)} %get-tuple-element.31), channel_id=1, source_target_pairs={{0,1},{1,0},{2,3},{3,2},{4,5},{5,4},{6,7},{7,6},{8,9},{9,8},{10,11... | collective-permute-start | bytes 393224 | tf_op jit(solution)/shard_map/ppermute | solution.py:20
  309.9 88.7 %copy-start.5 = (bf16[16,4096]{1,0:T(8,128)(2,1)S(1)}, bf16[16,4096]{1,0:T(8,128)(2,1)}, u32[]{:S(2)}) copy-start(bf16[16,4096]{1,0:T(8,128)(2,1)} %param.11) | copy-start | bytes 393220
  309.9 88.7 %copy-start.7 = (f32[4096]{0:T(1024)S(1)}, f32[4096]{0:T(1024)}, u32[]{:S(2)}) copy-start(f32[4096]{0:T(1024)} %param.15) | copy-start | bytes 49156
Sparse Core Ops, SparseCore 0:
  11.6 64.3 all-gather.2
  85.1 115.3 all-reduce.1
  205.1 78.8 all-gather.4
  312.2 86.3 reduce-scatter.1
where the time goes:
time: 410 us; the launch traced here: 409 us
  waiting for transfers between devices  332 us (81%)
  matrix products  25.3 us (6%)
  other arithmetic  19.4 us (5%)
  between operations  17.2 us (4%)
  local copies, waits for them, and re-layouts  7.71 us (2%)
  starting transfers between devices  7.35 us (2%)
    psum x1, waiting for transfers between devices, on_device(): resid = lax.psum(partial_rows, 'tensor')  115 us
    reduce_scatter x1, waiting for transfers between devices, on_device(): lax.psum_scatter((product + jnp.dot(chosen, query_term, precision=lax.Pre...  85.2 us
    all_gather x1, waiting for transfers between devices, on_device(): lax.all_gather(embed.astype(jnp.bfloat16), 'dp', axis=0, tiled=True)  77.7 us
    all_gather x1, waiting for transfers between devices, on_device(): piece = lax.all_gather(normed, 'tensor', axis=0, tiled=True)  35.5 us
    ppermute x2, waiting for transfers between devices, swapped(): return lax.ppermute(value, axis, pairs)  18.3 us
  transfers between devices with their start and end apart: 6, of which 6 were waited for; matrix products, arithmetic and copies ran while one was open for 3% of the time, Pallas kernels for 0%

commit v1 on v0

v1 whole, which is shorter than its diff:
```python
import math

import jax
import jax.numpy as jnp
from jax import lax
from jax.sharding import PartitionSpec as P

QDEV = 8


EPSILON = 1e-06
SOFTMAX_TEMPER = 0.05
LOSS_MULTIPLIER = 8192.0
ROPE_BASE = 1000000.0


def swapped(value, axis, apart):
    mask = 2**apart
    pairs = [(source, source ^ mask) for source in range(lax.axis_size(axis))]
    return lax.ppermute(value, axis, pairs)


def rms_scale(tensor):
    return lax.rsqrt(jnp.mean(tensor * tensor, axis=-1, keepdims=True) + EPSILON)


def rope_tables(position, head_width):
    halfway = head_width // 2
    frequency = ROPE_BASE ** (-(jnp.arange(halfway, dtype=jnp.float32) * (2.0 / head_width)))
    angles = position[:, None] * frequency[None, :]
    angles = jnp.concatenate([angles, angles], axis=-1)
    return (jnp.cos(angles), jnp.sin(angles))


def rotate(tensor, cosine, sine):
    halfway = tensor.shape[-1] // 2
    turned = jnp.concatenate([-tensor[..., halfway:], tensor[..., :halfway]], axis=-1)
    return tensor * cosine + turned * sine


def segment_layout(lengths_row, total_tokens):
    seq_ends = jnp.cumsum(lengths_row)
    starts = seq_ends - lengths_row
    token_index = jnp.arange(total_tokens, dtype=jnp.int32)
    inside = (token_index[:, None] >= starts[None, :]) & (token_index[:, None] < seq_ends[None, :])
    offset = jnp.sum(jnp.where(inside, starts[None, :], 0), axis=1)
    position = (token_index - offset).astype(jnp.float32)
    return (inside, position, seq_ends - 1)


def head_forward(raw, gain, cosine, sine):
    inverse = rms_scale(raw)
    unit_form = raw * inverse
    return (unit_form, inverse, rotate(unit_form * gain, cosine, sine))


def norm_backward(grad, unit_form, inverse, gain):
    scaled = grad * gain
    return inverse * (scaled - unit_form * jnp.mean(unit_form * scaled, axis=-1, keepdims=True))


def head_backward(grad_rot, unit_form, inverse, gain, cosine, sine):
    return norm_backward(rotate(grad_rot, cosine, -sine), unit_form, inverse, gain)


def exchange(blocks, axis):
    return lax.all_to_all(blocks, axis, 0, 0, tiled=True)


def gather_rows(rows, axis):
    count = lax.axis_size(axis)
    copies = jnp.broadcast_to(rows[None], (count,) + rows.shape)
    return exchange(copies, axis)


def to_lanes(block, lanes):
    rows, width = block.shape
    return block.reshape(rows, width // lanes, lanes).reshape(-1, lanes)


def split16(value):
    parts = []
    rest = value
    for _ in range(3):
        part = rest.astype(jnp.bfloat16)
        parts.append(part)
        rest = rest - part.astype(jnp.float32)
    return parts


def contrast(scaled16, out_gain, positives, negatives):
    groups, sequences, width = scaled16.shape
    tensor_count = lax.axis_size("tensor")
    query_rows = scaled16[:, :QDEV].reshape(groups * QDEV, width)
    passage_rows = scaled16[:, QDEV:].reshape(-1, width)
    query_count, passage_count = query_rows.shape[0], passage_rows.shape[0]
    own_queries = query_count // tensor_count
    features = width * tensor_count

    raw = jnp.dot(query_rows, passage_rows.T, preferred_element_type=jnp.float32)
    rows32 = jnp.concatenate([query_rows, passage_rows]).astype(jnp.float32)
    plain = rows32 / out_gain
    squares = jnp.sum(rows32 * rows32 + plain * plain * (EPSILON / features), axis=1)
    lanes = 128
    logit_rows = own_queries * passage_count // lanes
    packed = jnp.concatenate(
        [
            raw.reshape(tensor_count, own_queries, passage_count // lanes, lanes).reshape(
                tensor_count, logit_rows, lanes
            ),
            jnp.broadcast_to(
                squares.reshape(1, -1, lanes), (tensor_count, squares.shape[0] // lanes, lanes)
            ),
        ],
        axis=1,
    )
    summed = jnp.sum(exchange(packed, "tensor"), axis=0)
    inverse = lax.rsqrt(summed[logit_rows:].reshape(-1) + EPSILON * EPSILON)
    own = lax.axis_index("tensor") * own_queries
    inverse_query = lax.dynamic_slice_in_dim(inverse[:query_count], own, own_queries)
    inverse_passage = inverse[query_count:]
    logits = (
        summed[:logit_rows].reshape(own_queries, passage_count)
        * inverse_query[:, None]
        * inverse_passage[None, :]
        / SOFTMAX_TEMPER
    )

    passage_ids = jnp.arange(passage_count, dtype=jnp.int32)
    any_positive = jnp.any(positives[:, None] == passage_ids[None, :], axis=0)
    own_positives = lax.dynamic_slice_in_dim(positives, own, own_queries)
    own_negatives = lax.dynamic_slice_in_dim(negatives, own, own_queries)
    positive_hot = own_positives[:, None] == passage_ids[None, :]
    hard_hot = jnp.any(own_negatives[:, :, None] == passage_ids[None, None, :], axis=1)
    permitted_mask = any_positive[None, :] | hard_hot
    weight_params = jnp.where(permitted_mask, jnp.exp(logits - 1.0 / SOFTMAX_TEMPER), 0.0)
    totals = jnp.sum(weight_params, axis=1, keepdims=True)
    target_labels = jnp.sum(jnp.where(positive_hot, logits, 0.0), axis=1)
    loss_part = jnp.sum(jnp.log(totals[:, 0]) + 1.0 / SOFTMAX_TEMPER - target_labels)
    scaling_factor = LOSS_MULTIPLIER / (query_count * SOFTMAX_TEMPER)
    coef16 = (
        scaling_factor * (weight_params / totals - positive_hot.astype(jnp.float32))
    ).astype(jnp.bfloat16)
    weighted = coef16.astype(jnp.float32) * logits * SOFTMAX_TEMPER
    along_query = jnp.sum(weighted, axis=1)
    along_passage = jnp.sum(weighted, axis=0)

    small = jnp.concatenate(
        [
            along_passage,
            jnp.pad(jnp.concatenate([along_query, loss_part[None]]), (0, lanes - own_queries - 1)),
        ]
    ).reshape(-1, lanes)
    small_rows = small.shape[0]
    sent = jnp.concatenate([coef16.reshape(-1, lanes)] + split16(small))
    pad = -sent.shape[0] % 16
    sent = jnp.pad(sent, ((0, pad), (0, 0)))
    arrived = gather_rows(sent, "tensor").reshape(tensor_count, -1, lanes)
    coef_all = arrived[:, :logit_rows].reshape(query_count, passage_count)
    parts = arrived[:, logit_rows : logit_rows + 3 * small_rows].astype(jnp.float32)
    small_all = jnp.sum(parts.reshape(tensor_count, 3, small_rows, lanes), axis=1)
    along_passage = jnp.sum(small_all[:, : small_rows - 1], axis=0).reshape(-1)
    along_query = small_all[:, small_rows - 1, :own_queries].reshape(-1)
    loss = jnp.sum(small_all[:, small_rows - 1, own_queries]) / query_count

    embeds16 = (rows32 * inverse[:, None]).astype(jnp.bfloat16)
    d_queries = jnp.dot(
        coef_all, embeds16[query_count:], preferred_element_type=jnp.float32
    )
    d_passages = jnp.dot(
        coef_all.T, embeds16[:query_count], preferred_element_type=jnp.float32
    )
    own_group = lax.axis_index("dp")
    others = sequences - QDEV

    def own_part(of_queries, of_passages):
        return jnp.concatenate(
            [
                lax.dynamic_slice_in_dim(of_queries, own_group * QDEV, QDEV),
                lax.dynamic_slice_in_dim(of_passages, own_group * others, others),
            ]
        )

    return (
        loss,
        own_part(d_queries, d_passages),
        own_part(along_query, along_passage),
        own_part(inverse[:query_count], inverse_passage),
    )


def on_device(
    hidden, lengths, positives, negatives, in_gain, wq, wkv, q_gain, k_gain, wo, out_gain
):
    tensor_count = lax.axis_size("tensor")
    tensor_index = lax.axis_index("tensor")
    own_rows, features = hidden.shape
    tokens_count = own_rows * tensor_count
    head_width = wq.shape[1]
    sequences = lengths.shape[1]
    chunk = features // tensor_count
    root = math.sqrt(head_width)
    is_even = tensor_index % 2 == 0
    hidden32 = hidden.astype(jnp.float32)
    inverse_in = rms_scale(hidden32)
    normed = (hidden32 * inverse_in * in_gain).astype(jnp.bfloat16)
    piece = gather_rows(normed, "tensor").reshape(tokens_count, features)
    own_index = tensor_index * own_rows + jnp.arange(own_rows, dtype=jnp.int32)
    inside, position, last = segment_layout(lengths[0], tokens_count)
    own_last = (last[:, None] == own_index[None, :]).astype(jnp.bfloat16)
    token_index = jnp.arange(tokens_count, dtype=jnp.int32)
    chosen = (last[:, None] == token_index[None, :]).astype(jnp.bfloat16)
    kv_own = jnp.dot(piece, wkv, preferred_element_type=jnp.float32)
    kv_other = swapped(kv_own, "tensor", 0)
    last_rows = jnp.dot(chosen, piece, preferred_element_type=jnp.float32).astype(jnp.bfloat16)
    query_raw = jnp.dot(last_rows, wq, preferred_element_type=jnp.float32)
    key_raw = jnp.where(is_even, kv_own, kv_other)
    value16 = jnp.where(is_even, kv_other, kv_own).astype(jnp.bfloat16)
    cos_key, sin_key = rope_tables(position, head_width)
    key_unit, key_inverse, key_rot = head_forward(key_raw, k_gain, cos_key, sin_key)
    key16 = key_rot.astype(jnp.bfloat16)
    cos_query, sin_query = rope_tables((lengths[0] - 1).astype(jnp.float32), head_width)
    query_unit, query_inverse, query_rot = head_forward(query_raw, q_gain, cos_query, sin_query)
    query16 = query_rot.astype(jnp.bfloat16)
    shift = root * jnp.max(q_gain) * jnp.max(k_gain)
    scores = jnp.dot(query16, key16.T, preferred_element_type=jnp.float32) / root
    weight_params = jnp.where(inside.T, jnp.exp(scores - shift), 0.0)
    probs = weight_params / jnp.sum(weight_params, axis=-1, keepdims=True)
    probs16 = probs.astype(jnp.bfloat16)
    attn16 = jnp.dot(probs16, value16, preferred_element_type=jnp.float32).astype(jnp.bfloat16)
    partial_rows = jnp.dot(attn16, wo, preferred_element_type=jnp.float32) + jnp.dot(
        own_last, hidden, preferred_element_type=jnp.float32
    )
    blocks = partial_rows.astype(jnp.bfloat16).reshape(sequences, tensor_count, chunk)
    arrived = exchange(blocks.transpose(1, 0, 2), "tensor")
    resid = jnp.sum(arrived.astype(jnp.float32), axis=0)
    own_gain = lax.dynamic_slice_in_dim(out_gain, tensor_index * chunk, chunk)
    scaled = resid * own_gain
    everyone = lax.all_gather(scaled.astype(jnp.bfloat16), "dp", axis=0, tiled=True)
    groups = lax.axis_size("dp")
    loss, d_embed, along, inverse = contrast(
        everyone.reshape(groups, sequences, chunk), own_gain, positives, negatives
    )
    inverse, along = inverse[:, None], along[:, None]
    d_resid = inverse * own_gain * (d_embed - scaled * inverse * along) - resid * (
        along * inverse * inverse * (EPSILON / features)
    )
    d_resid16 = gather_rows(d_resid.astype(jnp.bfloat16), "tensor")
    d_resid16 = d_resid16.reshape(tensor_count, sequences, chunk)
    d_resid16 = d_resid16.transpose(1, 0, 2).reshape(sequences, features)
    d_attn16 = jnp.dot(d_resid16, wo.T, preferred_element_type=jnp.float32).astype(jnp.bfloat16)
    d_probs = jnp.dot(d_attn16, value16.T, preferred_element_type=jnp.float32)
    d_scores16 = (
        probs * (d_probs - jnp.sum(probs * d_probs, axis=-1, keepdims=True)) / root
    ).astype(jnp.bfloat16)
    d_query_rot = jnp.dot(d_scores16, key16, preferred_element_type=jnp.float32)
    d_key_rot = jnp.dot(d_scores16.T, query16, preferred_element_type=jnp.float32)
    d_value = jnp.dot(probs16.T, d_attn16, preferred_element_type=jnp.float32)
    d_key_raw = head_backward(d_key_rot, key_unit, key_inverse, k_gain, cos_key, sin_key)
    d_query_raw = head_backward(
        d_query_rot, query_unit, query_inverse, q_gain, cos_query, sin_query
    )
    mine = jnp.where(is_even, d_key_raw, d_value)
    theirs = jnp.where(is_even, d_value, d_key_raw)
    column16 = (mine + swapped(theirs, "tensor", 0)).astype(jnp.bfloat16)
    spread16 = jnp.dot(
        chosen.T, d_query_raw.astype(jnp.bfloat16), preferred_element_type=jnp.float32
    ).astype(jnp.bfloat16)
    product = jnp.dot(column16, wkv.T, preferred_element_type=jnp.float32) + jnp.dot(
        spread16, wq.T, preferred_element_type=jnp.float32
    )
    terms = exchange(product.astype(jnp.bfloat16), "tensor")
    d_normed = jnp.sum(
        terms.reshape(tensor_count, own_rows, features).astype(jnp.float32), axis=0
    )
    d_hidden = norm_backward(d_normed, hidden32 * inverse_in, inverse_in, in_gain)
    d_hidden = d_hidden + jnp.dot(own_last.T, d_resid16, preferred_element_type=jnp.float32)
    return (d_hidden.astype(jnp.bfloat16), loss)


def solution(mesh):
    placed = (
        P(("dp", "tensor"), None),
        P("dp", None),
        P(),
        P(),
        P(),
        P(None, "tensor"),
        P(None, "tensor"),
        P(),
        P(),
        P("tensor", None),
        P(),
    )
    return jax.shard_map(
        on_device,
        mesh=mesh,
        in_specs=placed,
        out_specs=(P(("dp", "tensor"), None), P()),
        check_vma=False,
    )
```

time: 410 us -> 218 us (0.53)
  the two profiles are of different devices: /device:TPU:32 before, /device:TPU:2 now
where the time goes in v1:
time: 218 us; the launch traced here: 217 us
  waiting for transfers between devices  74.1 us (34%)
  blocking collectives  51.1 us (23%)
  starting transfers between devices  37.9 us (17%)
  matrix products  16.9 us (8%)
  local copies, waits for them, and re-layouts  16.2 us (7%)
  other arithmetic  15.9 us (7%)
  between operations  4.59 us (2%)
    all_to_all x5, waiting for transfers between devices, exchange(): return lax.all_to_all(blocks, axis, 0, 0, tiled=True)  71.5 us
    all_gather x1, blocking collectives, on_device(): lax.all_gather(scaled.astype(jnp.bfloat16), 'dp', axis=0, tiled=True)  39.5 us
    all_to_all x5, starting transfers between devices, exchange(): return lax.all_to_all(blocks, axis, 0, 0, tiled=True)  29.7 us
    all_to_all x1, blocking collectives, exchange(): return lax.all_to_all(blocks, axis, 0, 0, tiled=True)  11.6 us
    ppermute x2, starting transfers between devices, swapped(): return lax.ppermute(value, axis, pairs)  8.13 us
  transfers between devices with their start and end apart: 7, of which 6 were waited for; matrix products, arithmetic and copies ran while one was open for 6% of the time, Pallas kernels for 0%

profile of v1, /device:TPU:2, one launch (start us, length us, event | category | flops | bytes accessed | tf_op | source)
XLA Modules:
  0.0 216.7 jit_solution(15755054820013921453)
XLA Ops:
  0.6 1.1 fusion.24
  1.8 0.5 copy-done.37
  2.3 1.0 fusion.20
  3.3 1.6 broadcast_in_dim.31
  4.9 9.6 %all-to-all-start = ((bf16[16,16,4096]{2,1,0:T(8,128)(2,1)}), bf16[16,16,4096]{2,1,0:T(8,128)(2,1)S(1)}, u32[]{:S(2)}, u32[]{:S(2)}) async-start(bf16[16,16,4096]{2,1,0:T(8,128)(2,1)} %broadcast_in_dim.31), calls=%async_computation | async-start | bytes 4194304 | tf_op jit(solution)/shard_map/all_to_all | solution.py:67
  14.5 0.6 reduce_max.19
  15.1 0.6 reduce_max.18
  17.5 1.1 fusion.53
  18.6 21.2 %all-to-all-done = bf16[16,16,4096]{2,1,0:T(8,128)(2,1)S(1)} async-done(((bf16[16,16,4096]{2,1,0:T(8,128)(2,1)}), bf16[16,16,4096]{2,1,0:T(8,128)(2,1)S(1)}, u32[]{:S(2)}, u32[]{:S(2)}) %all-to-all-start) | async-done | bytes 2097184 | tf_op jit(solution)/shard_map/all_to_all | solution.py:67
  39.8 2.0 multiply_reduce_fusion.6
  41.8 0.8 fusion.88
  42.7 4.8 %collective-permute-start = (f32[256,128]{0,1:T(8,128)S(1)}, f32[256,128]{0,1:T(8,128)S(1)}, u32[]{:S(2)}, u32[]{:S(2)}) collective-permute-start(f32[256,128]{0,1:T(8,128)S(1)} %fusion.88), channel_id=1, source_target_pairs={{0,1},{1,0},{2,3},{3,2},{4,5},{5,4},{6,7},{7,6},{8,9},{9,8},{10,11... | collective-permute-start | bytes 393224 | tf_op jit(solution)/shard_map/ppermute | solution.py:20
  47.8 2.6 %collective-permute-done = f32[256,128]{0,1:T(8,128)S(1)} collective-permute-done((f32[256,128]{0,1:T(8,128)S(1)}, f32[256,128]{0,1:T(8,128)S(1)}, u32[]{:S(2)}, u32[]{:S(2)}) %collective-permute-start) | collective-permute-done | bytes 131104 | tf_op jit(solution)/shard_map/ppermute | solution.py:20
  50.6 0.5 fusion.34
  51.1 0.6 copy-done.16
  52.1 0.5 fusion.1
  52.5 0.7 copy.44
  53.3 5.3 %all-to-all-start.1 = ((bf16[16,32,256]{2,1,0:T(8,128)(2,1)}), bf16[16,32,256]{2,1,0:T(8,128)(2,1)S(1)}, u32[]{:S(2)}, u32[]{:S(2)}) async-start(bf16[16,32,256]{2,1,0:T(8,128)(2,1)} %bitcast.79), calls=%async_computation.1 | async-start | bytes 524288 | tf_op jit(solution)/shard_map/all_to_all | solution.py:67
  58.6 0.8 dynamic_slice.30
  59.4 6.7 %all-to-all-done.1 = bf16[16,32,256]{2,1,0:T(8,128)(2,1)S(1)} async-done(((bf16[16,32,256]{2,1,0:T(8,128)(2,1)}), bf16[16,32,256]{2,1,0:T(8,128)(2,1)S(1)}, u32[]{:S(2)}, u32[]{:S(2)}) %all-to-all-start.1) | async-done | bytes 262176 | tf_op jit(solution)/shard_map/all_to_all | solution.py:67
  66.1 39.5 %all_gather.3 = bf16[1024,256]{1,0:T(8,128)(2,1)S(1)} all-gather(bf16[32,256]{1,0:T(8,128)(2,1)S(1)} %multiply_convert_fusion.3), channel_id=1, replica_groups=mesh['dp'=32,'tensor'=16] {'dp'}, dimensions={0}, use_global_device_ids=true | all-gather | bytes 540672 | tf_op jit(solution)/shard_map/all_gather | solution.py:239
  105.6 0.3 fusion.84
  105.9 0.3 copy-done.5
  106.2 0.3 fusion.9
  106.5 0.9 reshape_reshape.3
  107.5 2.1 pad_maximum_fusion
  109.6 4.9 %all-to-all-start.2 = ((f32[16,104,128]{2,1,0:T(8,128)}), f32[16,104,128]{2,1,0:T(8,128)S(1)}, u32[]{:S(2)}, u32[]{:S(2)}) async-start(f32[16,104,128]{2,1,0:T(8,128)} %pad_maximum_fusion), calls=%async_computation.2 | async-start | bytes 1703936 | tf_op jit(solution)/shard_map/all_to_all | solution.py:67
  114.6 0.6 eq.105
  115.5 0.6 reduce_or.22
  116.3 0.6 or.21
  116.9 0.6 eq.111
  117.6 11.6 %all-to-all-done.2 = f32[16,104,128]{2,1,0:T(8,128)S(1)} async-done(((f32[16,104,128]{2,1,0:T(8,128)}), f32[16,104,128]{2,1,0:T(8,128)S(1)}, u32[]{:S(2)}, u32[]{:S(2)}) %all-to-all-start.2) | async-done | bytes 852000 | tf_op jit(solution)/shard_map/all_to_all | solution.py:67
  129.5 0.9 fusion.51
  130.9 1.0 multiply_reduce_fusion.2
  132.3 0.6 subtract_reduce_fusion
  133.0 0.7 fusion.81
  133.7 0.8 multiply_reduce_fusion.3
  134.5 0.9 broadcast_in_dim.40
  135.5 5.6 %all-to-all-start.3 = ((bf16[16,128,128]{2,1,0:T(8,128)(2,1)}), bf16[16,128,128]{2,1,0:T(8,128)(2,1)}, u32[]{:S(2)}, u32[]{:S(2)}) async-start(bf16[16,128,128]{2,1,0:T(8,128)(2,1)} %broadcast_in_dim.40), calls=%async_computation.3 | async-start | bytes 1048576 | tf_op jit(solution)/shard_map/all_to_all | solution.py:67
  141.1 0.7 dynamic_slice.31
  141.7 0.6 dynamic_slice.32
  142.5 8.9 %all-to-all-done.3 = bf16[16,128,128]{2,1,0:T(8,128)(2,1)} async-done(((bf16[16,128,128]{2,1,0:T(8,128)(2,1)}), bf16[16,128,128]{2,1,0:T(8,128)(2,1)}, u32[]{:S(2)}, u32[]{:S(2)}) %all-to-all-start.3) | async-done | bytes 524320 | tf_op jit(solution)/shard_map/all_to_all | solution.py:67
  151.4 0.9 slice.105
  152.4 0.6 slice_reduce_fusion
  153.0 0.6 slice.106
  153.6 1.0 slice.102
  154.6 0.4 reshape.336
  155.1 0.3 fusion.14
  155.3 1.2 fusion.25
  156.8 0.7 dynamic_slice.39
  157.5 0.7 constant_dynamic-slice_fusion
  158.5 11.6 %all_to_all.34 = bf16[16,32,256]{2,1,0:T(8,128)(2,1)S(1)} all-to-all(bf16[16,32,256]{2,1,0:T(8,128)(2,1)S(1)} %broadcast_in_dim.41), channel_id=1, replica_groups=mesh['dp'=32,'tensor'=16] {'tensor'}, dimensions={0} | all-to-all | bytes 524288 | tf_op jit(solution)/shard_map/all_to_all | solution.py:67
  170.1 0.4 convolution_convert_fusion.2
  171.4 0.2 multiply_reduce_fusion.5
  171.7 0.5 multiply_reduce_fusion
  172.5 3.4 %collective-permute-start.1 = (f32[256,128]{0,1:T(8,128)S(1)}, f32[256,128]{0,1:T(8,128)S(1)}, u32[]{:S(2)}, u32[]{:S(2)}) collective-permute-start(f32[256,128]{0,1:T(8,128)S(1)} %get-tuple-element.39), channel_id=1, source_target_pairs={{0,1},{1,0},{2,3},{3,2},{4,5},{5,4},{6,7},{7,6},{8,9},{9,8},{10,11... | collective-permute-start | bytes 393224 | tf_op jit(solution)/shard_map/ppermute | solution.py:20
  175.9 4.1 %fusion.4 = f32[256,4096]{1,0:T(8,128)} fusion(bf16[4096,128]{1,0:T(8,128)(2,1)} %param.16, s32[32]{0:T(128)S(1)} %copy-done.31, f32[32,128]{1,0:T(8,128)S(1)} %get-tuple-element.7, f32[32,128]{1,0:T(8,128)S(1)} %get-tuple-element.34, f32[32]{0:T(128)S(1)} %broadcast_multiply_fusion.3, f32[32]{0:T(128)S(1)} %copy-done.34), kind=kOutput, calls=%fused_computation.13 | convolution fusion | flops 270594048 | bytes 5276032 | tf_op jit(solution)/shard_map/dot_general | solution.py:269
  180.0 4.3 %fusion = bf16[256,4096]{1,0:T(8,128)(2,1)} fusion(f32[256,4096]{1,0:T(8,128)} %fusion.4, bf16[4096,128]{1,0:T(8,128)(2,1)S(1)} %copy-done, f32[256,128]{0,1:T(8,128)S(1)} %collective-permute-done.1, f32[256,128]{0,1:T(8,128)S(1)} %get-tuple-element.40, pred[]{:T(512)S(6)} %eq.91, f32[256,128]{0,1:T(8,128)S(1)} %get-tuple-element.5, ...), kind=kOutput, calls=%fused_computation.1 | convolution fusion | flops 270761984 | bytes 7866369 | tf_op jit(solution)/shard_map/dot_general | solution.py:269
  184.2 4.4 %all-to-all-start.5 = ((bf16[16,16,4096]{2,1,0:T(8,128)(2,1)}), bf16[16,16,4096]{2,1,0:T(8,128)(2,1)S(1)}, u32[]{:S(2)}, u32[]{:S(2)}) async-start(bf16[16,16,4096]{2,1,0:T(8,128)(2,1)} %bitcast.18), calls=%async_computation.5 | async-start | bytes 4194304 | tf_op jit(solution)/shard_map/all_to_all | solution.py:67
  188.6 1.4 slice_reduce_fusion.1
  190.7 23.1 %all-to-all-done.5 = bf16[16,16,4096]{2,1,0:T(8,128)(2,1)S(1)} async-done(((bf16[16,16,4096]{2,1,0:T(8,128)(2,1)}), bf16[16,16,4096]{2,1,0:T(8,128)(2,1)S(1)}, u32[]{:S(2)}, u32[]{:S(2)}) %all-to-all-start.5) | async-done | bytes 2097184 | tf_op jit(solution)/shard_map/all_to_all | solution.py:67
  213.7 0.3 convert_reduce_fusion
  214.1 0.3 copy-done.38
  214.6 1.0 fusion.2
  (175 shorter events, 5.0 us)
Async XLA Ops:
  0.6 41.2 %copy-start = (bf16[4096,128]{1,0:T(8,128)(2,1)S(1)}, bf16[4096,128]{1,0:T(8,128)(2,1)}, u32[]{:S(2)}) copy-start(bf16[4096,128]{1,0:T(8,128)(2,1)} %param.17) | copy-start | bytes 3145732
  1.8 0.5 copy-start.37
  4.9 9.6 %copy-start.41 = (f32[128]{0:T(128)S(1)}, f32[128]{0:T(128)}, u32[]{:S(2)}) copy-start(f32[128]{0:T(128)} %param.19) | copy-start | bytes 1540
  4.9 10.2 %copy-start.35 = (f32[128]{0:T(128)S(1)}, f32[128]{0:T(128)}, u32[]{:S(2)}) copy-start(f32[128]{0:T(128)} %param.18) | copy-start | bytes 1540
  4.9 10.8 %copy-start.47 = (s32[1,32]{1,0:T(1,128)S(1)}, s32[1,32]{1,0:T(1,128)}, u32[]{:S(2)}) copy-start(s32[1,32]{1,0:T(1,128)} %param.12) | copy-start | bytes 388
  4.9 12.6 %copy-start.2 = (bf16[16,4096]{1,0:T(8,128)(2,1)S(1)}, bf16[16,4096]{1,0:T(8,128)(2,1)}, u32[]{:S(2)}) copy-start(bf16[16,4096]{1,0:T(8,128)(2,1)} %param.11) | copy-start | bytes 393220
  4.9 34.9 %all-to-all-start = ((bf16[16,16,4096]{2,1,0:T(8,128)(2,1)}), bf16[16,16,4096]{2,1,0:T(8,128)(2,1)S(1)}, u32[]{:S(2)}, u32[]{:S(2)}) async-start(bf16[16,16,4096]{2,1,0:T(8,128)(2,1)} %broadcast_in_dim.31), calls=%async_computation | async-start | bytes 4194304 | tf_op jit(solution)/shard_map/all_to_all | solution.py:67
  17.3 25.4 %copy-start.43 = (s32[16]{0:T(128)}, s32[16]{0:T(128)S(1)}, u32[]{:S(2)}) copy-start(s32[16]{0:T(128)S(1)} %iota_add_fusion) | copy-start | bytes 196
  17.4 25.3 %copy-start.30 = (s32[32]{0:T(128)}, s32[32]{0:T(128)S(1)}, u32[]{:S(2)}) copy-start(s32[32]{0:T(128)S(1)} %broadcast_add_fusion) | copy-start | bytes 388
  17.5 33.1 %copy-start.7 = (f32[256,64]{0,1:T(8,128)}, f32[256,64]{0,1:T(8,128)S(1)}, u32[]{:S(2)}) copy-start(f32[256,64]{0,1:T(8,128)S(1)} %broadcast_multiply_fusion) | copy-start | bytes 196612
  42.7 9.4 %copy-start.1 = (bf16[128,4096]{1,0:T(8,128)(2,1)S(1)}, bf16[128,4096]{1,0:T(8,128)(2,1)}, u32[]{:S(2)}) copy-start(bf16[128,4096]{1,0:T(8,128)(2,1)} %param.20) | copy-start | bytes 3145732
  42.7 9.4 %copy-start.4 = (f32[32,4096]{1,0:T(8,128)S(1)}, f32[32,4096]{1,0:T(8,128)}, u32[]{:S(2)}) copy-start(f32[32,4096]{1,0:T(8,128)} %fusion.53) | copy-start | bytes 1572868
  42.7 7.8 %copy-start.33 = (f32[32]{0:T(128)}, f32[32]{0:T(128)S(1)}, u32[]{:S(2)}) copy-start(f32[32]{0:T(128)S(1)} %add_rsqrt_fusion.1) | copy-start | bytes 388
  42.7 7.7 %collective-permute-start = (f32[256,128]{0,1:T(8,128)S(1)}, f32[256,128]{0,1:T(8,128)S(1)}, u32[]{:S(2)}, u32[]{:S(2)}) collective-permute-start(f32[256,128]{0,1:T(8,128)S(1)} %fusion.88), channel_id=1, source_target_pairs={{0,1},{1,0},{2,3},{3,2},{4,5},{5,4},{6,7},{7,6},{8,9},{9,8},{10,11... | collective-permute-start | bytes 393224 | tf_op jit(solution)/shard_map/ppermute | solution.py:20
  47.6 2.9 %copy-start.19 = (f32[32,64]{1,0:T(8,128)}, f32[32,64]{1,0:T(8,128)S(1)}, u32[]{:S(2)}) copy-start(f32[32,64]{1,0:T(8,128)S(1)} %get-tuple-element.41) | copy-start | bytes 24580
  47.8 5.5 %copy-start.24 = (bf16[32,128]{1,0:T(8,128)(2,1)}, bf16[32,128]{1,0:T(8,128)(2,1)S(1)}, u32[]{:S(2)}) copy-start(bf16[32,128]{1,0:T(8,128)(2,1)S(1)} %fusion.56) | copy-start | bytes 24580
  50.5 2.8 %copy-start.22 = (f32[256]{0:T(256)}, f32[256]{0:T(256)S(1)}, u32[]{:S(2)}) copy-start(f32[256]{0:T(256)S(1)} %add_rsqrt_fusion) | copy-start | bytes 3076
  51.1 0.6 copy-start.16
  52.0 53.6 %copy-start.9 = (f32[32,256]{1,0:T(8,128)}, f32[32,256]{1,0:T(8,128)S(1)}, u32[]{:S(2)}) copy-start(f32[32,256]{1,0:T(8,128)S(1)} %get-tuple-element.36) | copy-start | bytes 98308
  52.0 53.6 %copy-start.39 = (f32[32]{0:T(128)}, f32[32]{0:T(128)S(1)}, u32[]{:S(2)}) copy-start(f32[32]{0:T(128)S(1)} %get-tuple-element.35) | copy-start | bytes 388
  52.0 7.3 %copy-start.14 = (bf16[256,128]{0,1:T(8,128)(2,1)}, bf16[256,128]{0,1:T(8,128)(2,1)S(1)}, u32[]{:S(2)}) copy-start(bf16[256,128]{0,1:T(8,128)(2,1)S(1)} %select_convert_fusion) | copy-start | bytes 196612
  53.3 12.7 %all-to-all-start.1 = ((bf16[16,32,256]{2,1,0:T(8,128)(2,1)}), bf16[16,32,256]{2,1,0:T(8,128)(2,1)S(1)}, u32[]{:S(2)}, u32[]{:S(2)}) async-start(bf16[16,32,256]{2,1,0:T(8,128)(2,1)} %bitcast.79), calls=%async_computation.1 | async-start | bytes 524288 | tf_op jit(solution)/shard_map/all_to_all | solution.py:67
  59.3 48.1 %copy-start.27 = (f32[256]{0:T(256)}, f32[256]{0:T(256)S(1)}, u32[]{:S(2)}) copy-start(f32[256]{0:T(256)S(1)} %dynamic_slice.30) | copy-start | bytes 3076
  66.0 39.5 %copy-start.11 = (f32[32,256]{1,0:T(8,128)}, f32[32,256]{1,0:T(8,128)S(1)}, u32[]{:S(2)}) copy-start(f32[32,256]{1,0:T(8,128)S(1)} %convert_reduce_fusion.1) | copy-start | bytes 98308
  105.6 0.7 copy-start.5
  107.5 7.0 %copy-start.48 = (s32[256]{0:T(256)S(1)}, s32[256]{0:T(256)}, u32[]{:S(2)}) copy-start(s32[256]{0:T(256)} %param.13) | copy-start | bytes 3076
  107.5 7.8 %copy-start.46 = (s32[256,7]{0,1:T(8,128)S(1)}, s32[256,7]{0,1:T(8,128)}, u32[]{:S(2)}) copy-start(s32[256,7]{0,1:T(8,128)} %param.14) | copy-start | bytes 21508
  109.6 19.6 %all-to-all-start.2 = ((f32[16,104,128]{2,1,0:T(8,128)}), f32[16,104,128]{2,1,0:T(8,128)S(1)}, u32[]{:S(2)}, u32[]{:S(2)}) async-start(f32[16,104,128]{2,1,0:T(8,128)} %pad_maximum_fusion), calls=%async_computation.2 | async-start | bytes 1703936 | tf_op jit(solution)/shard_map/all_to_all | solution.py:67
  114.6 0.7 copy-start.45
  115.4 1.5 copy-start.21
  116.3 0.6 copy-start.29
  129.2 13.1 %copy-start.6 = (bf16[256,256]{1,0:T(8,128)(2,1)S(1)}, bf16[256,256]{1,0:T(8,128)(2,1)}, u32[]{:S(2)}) copy-start(bf16[256,256]{1,0:T(8,128)(2,1)} %copy-done.5) | copy-start | bytes 393220
  135.5 16.0 %all-to-all-start.3 = ((bf16[16,128,128]{2,1,0:T(8,128)(2,1)}), bf16[16,128,128]{2,1,0:T(8,128)(2,1)}, u32[]{:S(2)}, u32[]{:S(2)}) async-start(bf16[16,128,128]{2,1,0:T(8,128)(2,1)} %broadcast_in_dim.40), calls=%async_computation.3 | async-start | bytes 1048576 | tf_op jit(solution)/shard_map/all_to_all | solution.py:67
  152.4 0.6 copy-start.13
  155.0 1.5 copy-start.26
  155.0 3.2 %copy-start.49 = (f32[8]{0:T(128)S(1)}, f32[8]{0:T(128)}, u32[]{:S(2)}) copy-start(f32[8]{0:T(128)} %dynamic_slice.31) | copy-start | bytes 100
  155.0 3.2 %copy-start.50 = (f32[24]{0:T(128)S(1)}, f32[24]{0:T(128)}, u32[]{:S(2)}) copy-start(f32[24]{0:T(128)} %dynamic_slice.32) | copy-start | bytes 292
  155.0 3.3 %copy-start.12 = (f32[32,256]{1,0:T(8,128)S(1)}, f32[32,256]{1,0:T(8,128)}, u32[]{:S(2)}) copy-start(f32[32,256]{1,0:T(8,128)} %copy-done.11) | copy-start | bytes 98308
  155.0 3.3 %copy-start.28 = (f32[256]{0:T(256)S(1)}, f32[256]{0:T(256)}, u32[]{:S(2)}) copy-start(f32[256]{0:T(256)} %copy-done.27) | copy-start | bytes 3076
  155.3 15.2 %copy-start.10 = (f32[32,256]{1,0:T(8,128)S(1)}, f32[32,256]{1,0:T(8,128)}, u32[]{:S(2)}) copy-start(f32[32,256]{1,0:T(8,128)} %copy-done.9) | copy-start | bytes 98308
  156.5 14.1 %copy-start.15 = (bf16[256,128]{0,1:T(8,128)(2,1)S(1)}, bf16[256,128]{0,1:T(8,128)(2,1)}, u32[]{:S(2)}) copy-start(bf16[256,128]{0,1:T(8,128)(2,1)} %copy-done.14) | copy-start | bytes 196612
  156.5 14.1 %copy-start.40 = (f32[32]{0:T(128)S(1)}, f32[32]{0:T(128)}, u32[]{:S(2)}) copy-start(f32[32]{0:T(128)} %copy-done.39) | copy-start | bytes 388
  156.5 14.4 %copy-start.17 = (bf16[256,128]{0,1:T(8,128)(2,1)S(1)}, bf16[256,128]{0,1:T(8,128)(2,1)}, u32[]{:S(2)}) copy-start(bf16[256,128]{0,1:T(8,128)(2,1)} %copy-done.16) | copy-start | bytes 196612
  156.5 14.5 %copy-start.25 = (bf16[32,128]{1,0:T(8,128)(2,1)S(1)}, bf16[32,128]{1,0:T(8,128)(2,1)}, u32[]{:S(2)}) copy-start(bf16[32,128]{1,0:T(8,128)(2,1)} %copy-done.24) | copy-start | bytes 24580
  156.6 14.9 %copy-start.20 = (f32[32,64]{1,0:T(8,128)S(1)}, f32[32,64]{1,0:T(8,128)}, u32[]{:S(2)}) copy-start(f32[32,64]{1,0:T(8,128)} %copy-done.19) | copy-start | bytes 24580
  156.6 14.8 %copy-start.34 = (f32[32]{0:T(128)S(1)}, f32[32]{0:T(128)}, u32[]{:S(2)}) copy-start(f32[32]{0:T(128)} %copy-done.33) | copy-start | bytes 388
  156.6 14.8 %copy-start.36 = (f32[128]{0:T(128)S(1)}, f32[128]{0:T(128)}, u32[]{:S(2)}) copy-start(f32[128]{0:T(128)} %param.18) | copy-start | bytes 1540
  156.6 15.1 %copy-start.8 = (f32[256,64]{0,1:T(8,128)S(1)}, f32[256,64]{0,1:T(8,128)}, u32[]{:S(2)}) copy-start(f32[256,64]{0,1:T(8,128)} %copy-done.7) | copy-start | bytes 196612
  156.6 15.1 %copy-start.23 = (f32[256]{0:T(256)S(1)}, f32[256]{0:T(256)}, u32[]{:S(2)}) copy-start(f32[256]{0:T(256)} %copy-done.22) | copy-start | bytes 3076
  156.6 15.1 %copy-start.42 = (f32[128]{0:T(128)S(1)}, f32[128]{0:T(128)}, u32[]{:S(2)}) copy-start(f32[128]{0:T(128)} %param.19) | copy-start | bytes 1540
  170.1 5.8 %copy-start.31 = (s32[32]{0:T(128)S(1)}, s32[32]{0:T(128)}, u32[]{:S(2)}) copy-start(s32[32]{0:T(128)} %copy-done.30) | copy-start | bytes 388
  172.5 7.5 %collective-permute-start.1 = (f32[256,128]{0,1:T(8,128)S(1)}, f32[256,128]{0,1:T(8,128)S(1)}, u32[]{:S(2)}, u32[]{:S(2)}) collective-permute-start(f32[256,128]{0,1:T(8,128)S(1)} %get-tuple-element.39), channel_id=1, source_target_pairs={{0,1},{1,0},{2,3},{3,2},{4,5},{5,4},{6,7},{7,6},{8,9},{9,8},{10,11... | collective-permute-start | bytes 393224 | tf_op jit(solution)/shard_map/ppermute | solution.py:20
  184.2 29.5 %all-to-all-start.5 = ((bf16[16,16,4096]{2,1,0:T(8,128)(2,1)}), bf16[16,16,4096]{2,1,0:T(8,128)(2,1)S(1)}, u32[]{:S(2)}, u32[]{:S(2)}) async-start(bf16[16,16,4096]{2,1,0:T(8,128)(2,1)} %bitcast.18), calls=%async_computation.5 | async-start | bytes 4194304 | tf_op jit(solution)/shard_map/all_to_all | solution.py:67
  188.6 25.4 %copy-start.3 = (bf16[16,4096]{1,0:T(8,128)(2,1)S(1)}, bf16[16,4096]{1,0:T(8,128)(2,1)}, u32[]{:S(2)}) copy-start(bf16[16,4096]{1,0:T(8,128)(2,1)} %param.11) | copy-start | bytes 393220
  188.6 25.5 %copy-start.18 = (f32[4096]{0:T(1024)S(1)}, f32[4096]{0:T(1024)}, u32[]{:S(2)}) copy-start(f32[4096]{0:T(1024)} %param.15) | copy-start | bytes 49156
  213.7 0.6 copy-start.38
  213.7 0.8 copy-start.32
  213.7 0.8 copy-start.44

commit v2 on v1

--- a/solution.py
+++ b/solution.py
@@ -69,35 +69,39 @@
 
 def gather_rows(rows, axis):
     count = lax.axis_size(axis)
-    copies = jnp.broadcast_to(rows[None], (count,) + rows.shape)
-    return exchange(copies, axis)
-
-
-def to_lanes(block, lanes):
+    return exchange(jnp.broadcast_to(rows[None], (count,) + rows.shape), axis)
+
+
+def to_tiles(block):
     rows, width = block.shape
-    return block.reshape(rows, width // lanes, lanes).reshape(-1, lanes)
+    tiles = block.reshape(rows // 8, 8, width // 128, 128).transpose(0, 2, 1, 3)
+    return tiles.reshape(rows // 8, width // 16, 128)
+
+
+def from_tiles(tiles):
+    count, height = tiles.shape[:2]
+    block = tiles.reshape(count, height // 8, 8, 128).transpose(0, 2, 1, 3)
+    return block.reshape(count * 8, height * 16)
 
 
 def split16(value):
-    parts = []
-    rest = value
-    for _ in range(3):
-        part = rest.astype(jnp.bfloat16)
-        parts.append(part)
-        rest = rest - part.astype(jnp.float32)
-    return parts
+    high = value.astype(jnp.bfloat16)
+    return [high, (value - high.astype(jnp.float32)).astype(jnp.bfloat16)]
 
 
 def contrast(scaled16, out_gain, positives, negatives):
     groups, sequences, width = scaled16.shape
-    tensor_count = lax.axis_size("tensor")
+    tensor_count, core_count = lax.axis_size("tensor"), lax.axis_size("core")
     query_rows = scaled16[:, :QDEV].reshape(groups * QDEV, width)
     passage_rows = scaled16[:, QDEV:].reshape(-1, width)
     query_count, passage_count = query_rows.shape[0], passage_rows.shape[0]
-    own_queries = query_count // tensor_count
+    core_queries = query_count // core_count
+    own_queries = core_queries // tensor_count
     features = width * tensor_count
 
-    raw = jnp.dot(query_rows, passage_rows.T, preferred_element_type=jnp.float32)
+    core_start = lax.axis_index("core") * core_queries
+    core_rows = lax.dynamic_slice_in_dim(query_rows, core_start, core_queries)
+    raw = jnp.dot(core_rows, passage_rows.T, preferred_element_type=jnp.float32)
     rows32 = jnp.concatenate([query_rows, passage_rows]).astype(jnp.float32)
     plain = rows32 / out_gain
     squares = jnp.sum(rows32 * rows32 + plain * plain * (EPSILON / features), axis=1)
@@ -105,9 +109,7 @@
     logit_rows = own_queries * passage_count // lanes
     packed = jnp.concatenate(
         [
-            raw.reshape(tensor_count, own_queries, passage_count // lanes, lanes).reshape(
-                tensor_count, logit_rows, lanes
-            ),
+            to_tiles(raw),
             jnp.broadcast_to(
                 squares.reshape(1, -1, lanes), (tensor_count, squares.shape[0] // lanes, lanes)
             ),
@@ -116,11 +118,11 @@
     )
     summed = jnp.sum(exchange(packed, "tensor"), axis=0)
     inverse = lax.rsqrt(summed[logit_rows:].reshape(-1) + EPSILON * EPSILON)
-    own = lax.axis_index("tensor") * own_queries
+    own = core_start + lax.axis_index("tensor") * own_queries
     inverse_query = lax.dynamic_slice_in_dim(inverse[:query_count], own, own_queries)
     inverse_passage = inverse[query_count:]
     logits = (
-        summed[:logit_rows].reshape(own_queries, passage_count)
+        from_tiles(summed[None, :logit_rows])
         * inverse_query[:, None]
         * inverse_passage[None, :]
         / SOFTMAX_TEMPER
@@ -152,13 +154,13 @@
         ]
     ).reshape(-1, lanes)
     small_rows = small.shape[0]
-    sent = jnp.concatenate([coef16.reshape(-1, lanes)] + split16(small))
-    pad = -sent.shape[0] % 16
-    sent = jnp.pad(sent, ((0, pad), (0, 0)))
-    arrived = gather_rows(sent, "tensor").reshape(tensor_count, -1, lanes)
-    coef_all = arrived[:, :logit_rows].reshape(query_count, passage_count)
-    parts = arrived[:, logit_rows : logit_rows + 3 * small_rows].astype(jnp.float32)
-    small_all = jnp.sum(parts.reshape(tensor_count, 3, small_rows, lanes), axis=1)
+    sent = jnp.concatenate([to_tiles(coef16)[0]] + split16(small))
+    sent = jnp.pad(sent, ((0, -sent.shape[0] % 16), (0, 0)))
+    arrived = lax.all_gather(gather_rows(sent, "tensor"), "core", axis=0, tiled=True)
+    arrived = arrived.reshape(core_count * tensor_count, -1, lanes)
+    coef_all = from_tiles(arrived[:, :logit_rows])
+    parts = arrived[:, logit_rows : logit_rows + 2 * small_rows].astype(jnp.float32)
+    small_all = parts[:, :small_rows] + parts[:, small_rows:]
     along_passage = jnp.sum(small_all[:, : small_rows - 1], axis=0).reshape(-1)
     along_query = small_all[:, small_rows - 1, :own_queries].reshape(-1)
     loss = jnp.sum(small_all[:, small_rows - 1, own_queries]) / query_count
@@ -170,7 +172,7 @@
     d_passages = jnp.dot(
         coef_all.T, embeds16[:query_count], preferred_element_type=jnp.float32
     )
-    own_group = lax.axis_index("dp")
+    own_group = lax.axis_index("z") * core_count + lax.axis_index("core")
     others = sequences - QDEV
 
     def own_part(of_queries, of_passages):
@@ -210,10 +212,13 @@
     own_last = (last[:, None] == own_index[None, :]).astype(jnp.bfloat16)
     token_index = jnp.arange(tokens_count, dtype=jnp.int32)
     chosen = (last[:, None] == token_index[None, :]).astype(jnp.bfloat16)
-    kv_own = jnp.dot(piece, wkv, preferred_element_type=jnp.float32)
+    weights = jnp.concatenate([wkv, wq], axis=1)
+    projected = jnp.dot(piece, weights, preferred_element_type=jnp.float32)
+    kv_own = projected[:, :head_width]
     kv_other = swapped(kv_own, "tensor", 0)
-    last_rows = jnp.dot(chosen, piece, preferred_element_type=jnp.float32).astype(jnp.bfloat16)
-    query_raw = jnp.dot(last_rows, wq, preferred_element_type=jnp.float32)
+    query_raw = jnp.dot(
+        chosen.astype(jnp.float32), projected[:, head_width:], precision=lax.Precision.HIGHEST
+    )
     key_raw = jnp.where(is_even, kv_own, kv_other)
     value16 = jnp.where(is_even, kv_other, kv_own).astype(jnp.bfloat16)
     cos_key, sin_key = rope_tables(position, head_width)
@@ -236,11 +241,10 @@
     resid = jnp.sum(arrived.astype(jnp.float32), axis=0)
     own_gain = lax.dynamic_slice_in_dim(out_gain, tensor_index * chunk, chunk)
     scaled = resid * own_gain
-    everyone = lax.all_gather(scaled.astype(jnp.bfloat16), "dp", axis=0, tiled=True)
-    groups = lax.axis_size("dp")
-    loss, d_embed, along, inverse = contrast(
-        everyone.reshape(groups, sequences, chunk), own_gain, positives, negatives
-    )
+    same_core = gather_rows(scaled.astype(jnp.bfloat16), "z")
+    everyone = lax.all_gather(same_core, "core", axis=1)
+    everyone = everyone.reshape(-1, sequences, chunk)
+    loss, d_embed, along, inverse = contrast(everyone, own_gain, positives, negatives)
     inverse, along = inverse[:, None], along[:, None]
     d_resid = inverse * own_gain * (d_embed - scaled * inverse * along) - resid * (
         along * inverse * inverse * (EPSILON / features)
@@ -266,8 +270,10 @@
     spread16 = jnp.dot(
         chosen.T, d_query_raw.astype(jnp.bfloat16), preferred_element_type=jnp.float32
     ).astype(jnp.bfloat16)
-    product = jnp.dot(column16, wkv.T, preferred_element_type=jnp.float32) + jnp.dot(
-        spread16, wq.T, preferred_element_type=jnp.float32
+    product = jnp.dot(
+        jnp.concatenate([column16, spread16], axis=1),
+        weights.T,
+        preferred_element_type=jnp.float32,
     )
     terms = exchange(product.astype(jnp.bfloat16), "tensor")
     d_normed = jnp.sum(
@@ -279,9 +285,13 @@
 
 
 def solution(mesh):
+    z_count = mesh.shape["dp"] // 2
+    chips = mesh.devices.reshape(z_count, 2, mesh.shape["tensor"])
+    mesh = jax.sharding.Mesh(chips, ("z", "core", "tensor"))
+    everywhere = P(("z", "core", "tensor"), None)
     placed = (
-        P(("dp", "tensor"), None),
-        P("dp", None),
+        everywhere,
+        P(("z", "core"), None),
         P(),
         P(),
         P(),
@@ -293,9 +303,5 @@
         P(),
     )
     return jax.shard_map(
-        on_device,
-        mesh=mesh,
-        in_specs=placed,
-        out_specs=(P(("dp", "tensor"), None), P()),
-        check_vma=False,
-    )
+        on_device, mesh=mesh, in_specs=placed, out_specs=(everywhere, P()), check_vma=False
+    )

time: 218 us -> 216 us (level)
  the two profiles are of different devices: /device:TPU:2 before, /device:TPU:32 now
where the time goes in v2:
time: 216 us; the launch traced here: 215 us
  waiting for transfers between devices  96.1 us (44%)
  starting transfers between devices  42.5 us (20%)
  other arithmetic  21.7 us (10%)
  matrix products  17.1 us (8%)
  local copies, waits for them, and re-layouts  16.4 us (8%)
  blocking collectives  16.4 us (8%)
  between operations  4.43 us (2%)
    all_to_all x6, waiting for transfers between devices, exchange(): return lax.all_to_all(blocks, axis, 0, 0, tiled=True)  88.2 us
    all_to_all x6, starting transfers between devices, exchange(): return lax.all_to_all(blocks, axis, 0, 0, tiled=True)  38.1 us
    all_to_all x1, blocking collectives, exchange(): return lax.all_to_all(blocks, axis, 0, 0, tiled=True)  11.9 us
    ppermute x2, waiting for transfers between devices, swapped(): return lax.ppermute(value, axis, pairs)  7.89 us
    unnamed x85, local copies, waits for them, and re-layouts  4.64 us
    ppermute x2, starting transfers between devices, swapped(): return lax.ppermute(value, axis, pairs)  4.39 us
  transfers between devices with their start and end apart: 8, of which 8 were waited for; matrix products, arithmetic and copies ran while one was open for 8% of the time, Pallas kernels for 0%

profile of v2, /device:TPU:32, one launch (start us, length us, event | category | flops | bytes accessed | tf_op | source)
XLA Modules:
  0.0 214.6 jit_solution(15539383536607513403)
XLA Ops:
  0.6 1.1 fusion.21
  1.8 1.0 fusion.17
  2.8 1.5 broadcast_in_dim.31
  4.4 7.2 %all-to-all-start = ((bf16[16,16,4096]{2,1,0:T(8,128)(2,1)}), bf16[16,16,4096]{2,1,0:T(8,128)(2,1)}, u32[]{:S(2)}, u32[]{:S(2)}) async-start(bf16[16,16,4096]{2,1,0:T(8,128)(2,1)} %broadcast_in_dim.31), calls=%async_computation | async-start | bytes 4194304 | tf_op jit(solution)/shard_map/all_to_all | solution.py:67
  12.0 0.6 reduce_max.18
  12.6 0.6 reduce_max.19
  14.7 1.1 fusion.59
  15.7 1.4 constant_dynamic-update-slice_fusion.1
  17.1 1.5 constant_dynamic-update-slice_fusion
  18.6 24.7 %all-to-all-done = bf16[16,16,4096]{2,1,0:T(8,128)(2,1)} async-done(((bf16[16,16,4096]{2,1,0:T(8,128)(2,1)}), bf16[16,16,4096]{2,1,0:T(8,128)(2,1)}, u32[]{:S(2)}, u32[]{:S(2)}) %all-to-all-start) | async-done | bytes 2097184 | tf_op jit(solution)/shard_map/all_to_all | solution.py:67
  43.3 2.5 %fusion.97 = f32[256,256]{0,1:T(8,128)S(1)} fusion(bf16[256,4096]{1,0:T(8,128)(2,1)} %bitcast, bf16[4096,256]{1,0:T(8,128)(2,1)S(1)} %constant_dynamic-update-slice_fusion), kind=kOutput, calls=%fused_computation.189 | convolution fusion | flops 536870912 | bytes 4456448 | tf_op jit(solution)/shard_map/dot_general | solution.py:216
  46.2 1.9 collective-permute-start
  48.9 4.2 %collective-permute-done = f32[256,128]{0,1:T(8,128)S(1)} collective-permute-done((f32[256,128]{0,1:T(8,128)S(1)}, f32[256,128]{0,1:T(8,128)S(1)}, u32[]{:S(2)}, u32[]{:S(2)}) %collective-permute-start) | collective-permute-done | bytes 131104 | tf_op jit(solution)/shard_map/ppermute | solution.py:20
  54.2 0.6 copy-done.14
  55.2 1.5 fusion
  56.7 0.7 copy.35
  57.4 3.6 %all-to-all-start.1 = ((bf16[16,32,256]{2,1,0:T(8,128)(2,1)}), bf16[16,32,256]{2,1,0:T(8,128)(2,1)S(1)}, u32[]{:S(2)}, u32[]{:S(2)}) async-start(bf16[16,32,256]{2,1,0:T(8,128)(2,1)} %bitcast.139), calls=%async_computation.1 | async-start | bytes 524288 | tf_op jit(solution)/shard_map/all_to_all | solution.py:67
  61.0 0.8 dynamic_slice.33
  61.8 7.9 %all-to-all-done.1 = bf16[16,32,256]{2,1,0:T(8,128)(2,1)S(1)} async-done(((bf16[16,32,256]{2,1,0:T(8,128)(2,1)}), bf16[16,32,256]{2,1,0:T(8,128)(2,1)S(1)}, u32[]{:S(2)}, u32[]{:S(2)}) %all-to-all-start.1) | async-done | bytes 262176 | tf_op jit(solution)/shard_map/all_to_all | solution.py:67
  69.7 0.6 copy-done.11
  70.3 0.7 broadcast_in_dim.35
  71.1 15.2 %all-to-all-start.2 = ((bf16[16,32,256]{2,1,0:T(8,128)(2,1)}), bf16[16,32,256]{2,1,0:T(8,128)(2,1)S(1)}, u32[]{:S(2)}, u32[]{:S(2)}) async-start(bf16[16,32,256]{2,1,0:T(8,128)(2,1)} %broadcast_in_dim.35), calls=%async_computation.2 | async-start | bytes 524288 | tf_op jit(solution)/shard_map/all_to_all | solution.py:67
  86.3 0.6 dynamic_slice.39
  86.9 16.0 %all-to-all-done.2 = bf16[16,32,256]{2,1,0:T(8,128)(2,1)S(1)} async-done(((bf16[16,32,256]{2,1,0:T(8,128)(2,1)}), bf16[16,32,256]{2,1,0:T(8,128)(2,1)S(1)}, u32[]{:S(2)}, u32[]{:S(2)}) %all-to-all-start.2) | async-done | bytes 262176 | tf_op jit(solution)/shard_map/all_to_all | solution.py:67
  102.9 2.2 %all-gather = bf16[16,64,256]{2,1,0:T(8,128)(2,1)S(1)} all-gather(bf16[16,32,256]{2,1,0:T(8,128)(2,1)S(1)} %all-to-all-done.2), channel_id=2, replica_groups=mesh['z'=16,'core'=2,'tensor'=16] {'core'}, dimensions={1}, use_global_device_ids=true | all-gather | bytes 786432 | tf_op jit(solution)/shard_map/all_gather | solution.py:245
  105.1 1.0 fusion.6
  106.4 0.8 pad_maximum_fusion.1
  107.2 4.2 %all-to-all-start.3 = ((f32[16,56,128]{2,1,0:T(8,128)}), f32[16,56,128]{2,1,0:T(8,128)}, u32[]{:S(2)}, u32[]{:S(2)}) async-start(f32[16,56,128]{2,1,0:T(8,128)} %pad_maximum_fusion.1), calls=%async_computation.3 | async-start | bytes 917504 | tf_op jit(solution)/shard_map/all_to_all | solution.py:67
  111.5 0.6 multiply_add_fusion
  112.1 0.8 constant_dynamic-slice_fusion.2
  112.8 0.7 fusion.22
  113.5 1.4 fusion.10
  114.9 8.0 %all-to-all-done.3 = f32[16,56,128]{2,1,0:T(8,128)} async-done(((f32[16,56,128]{2,1,0:T(8,128)}), f32[16,56,128]{2,1,0:T(8,128)}, u32[]{:S(2)}, u32[]{:S(2)}) %all-to-all-start.3) | async-done | bytes 458784 | tf_op jit(solution)/shard_map/all_to_all | solution.py:67
  122.9 1.7 reduce_sum.189
  124.6 1.3 fusion.91
  125.8 0.6 slice_bitcast_fusion.6
  126.4 0.6 fusion.95
  127.0 1.0 fusion.69
  128.0 1.0 fusion.71
  129.0 0.7 subtract_reduce_fusion
  129.7 0.8 fusion.88
  130.5 0.8 broadcast_in_dim.40
  131.2 4.2 %all-to-all-start.4 = ((bf16[16,64,128]{2,1,0:T(8,128)(2,1)}), bf16[16,64,128]{2,1,0:T(8,128)(2,1)}, u32[]{:S(2)}, u32[]{:S(2)}) async-start(bf16[16,64,128]{2,1,0:T(8,128)(2,1)} %broadcast_in_dim.40), calls=%async_computation.4 | async-start | bytes 524288 | tf_op jit(solution)/shard_map/all_to_all | solution.py:67
  135.4 1.3 dynamic_slice.36
  136.7 1.9 fusion.9
  138.6 5.5 %all-to-all-done.4 = bf16[16,64,128]{2,1,0:T(8,128)(2,1)} async-done(((bf16[16,64,128]{2,1,0:T(8,128)(2,1)}), bf16[16,64,128]{2,1,0:T(8,128)(2,1)}, u32[]{:S(2)}, u32[]{:S(2)}) %all-to-all-start.4) | async-done | bytes 262176 | tf_op jit(solution)/shard_map/all_to_all | solution.py:67
  144.1 2.4 %all_gather.11 = bf16[32,64,128]{2,1,0:T(8,128)(2,1)S(1)} all-gather(bf16[16,64,128]{2,1,0:T(8,128)(2,1)} %all-to-all-done.4), channel_id=1, replica_groups=mesh['z'=16,'core'=2,'tensor'=16] {'core'}, dimensions={0}, use_global_device_ids=true | all-gather | bytes 786432 | tf_op jit(solution)/shard_map/all_gather | solution.py:159
  146.6 0.6 copy-done.6
  147.2 2.0 fusion.11
  149.2 2.1 fusion.13
  151.6 0.7 constant_dynamic-slice_fusion.1
  152.3 0.7 constant_dynamic-slice_fusion
  153.3 11.9 %all_to_all.39 = bf16[16,32,256]{2,1,0:T(8,128)(2,1)S(1)} all-to-all(bf16[16,32,256]{2,1,0:T(8,128)(2,1)S(1)} %broadcast_in_dim.41), channel_id=1, replica_groups=mesh['z'=16,'core'=2,'tensor'=16] {'tensor'}, dimensions={0} | all-to-all | bytes 524288 | tf_op jit(solution)/shard_map/all_to_all | solution.py:67
  165.6 1.1 multiply_reduce_fusion.2
  166.8 0.8 multiply_convert_fusion
  167.6 0.9 fusion.98
  168.5 1.0 fusion.99
  170.4 2.5 %collective-permute-start.1 = (f32[256,128]{0,1:T(8,128)S(1)}, f32[256,128]{0,1:T(8,128)S(1)}, u32[]{:S(2)}, u32[]{:S(2)}) collective-permute-start(f32[256,128]{0,1:T(8,128)S(1)} %get-tuple-element.37), channel_id=1, source_target_pairs={{0,1},{1,0},{2,3},{3,2},{4,5},{5,4},{6,7},{7,6},{8,9},{9,8},{10,11... | collective-permute-start | bytes 393224 | tf_op jit(solution)/shard_map/ppermute | solution.py:20
  173.5 3.7 %collective-permute-done.1 = f32[256,128]{0,1:T(8,128)S(1)} collective-permute-done((f32[256,128]{0,1:T(8,128)S(1)}, f32[256,128]{0,1:T(8,128)S(1)}, u32[]{:S(2)}, u32[]{:S(2)}) %collective-permute-start.1) | collective-permute-done | bytes 131104 | tf_op jit(solution)/shard_map/ppermute | solution.py:20
  177.3 2.1 convolution_convert_fusion
  179.4 3.7 %all-to-all-start.6 = ((bf16[16,16,4096]{2,1,0:T(8,128)(2,1)}), bf16[16,16,4096]{2,1,0:T(8,128)(2,1)S(1)}, u32[]{:S(2)}, u32[]{:S(2)}) async-start(bf16[16,16,4096]{2,1,0:T(8,128)(2,1)} %bitcast.131), calls=%async_computation.6 | async-start | bytes 4194304 | tf_op jit(solution)/shard_map/all_to_all | solution.py:67
  183.1 1.6 slice_reduce_fusion.1
  185.4 26.2 %all-to-all-done.6 = bf16[16,16,4096]{2,1,0:T(8,128)(2,1)S(1)} async-done(((bf16[16,16,4096]{2,1,0:T(8,128)(2,1)}), bf16[16,16,4096]{2,1,0:T(8,128)(2,1)S(1)}, u32[]{:S(2)}, u32[]{:S(2)}) %all-to-all-start.6) | async-done | bytes 2097184 | tf_op jit(solution)/shard_map/all_to_all | solution.py:67
  212.5 1.0 fusion.1
  (139 shorter events, 6.8 us)
Async XLA Ops:
  0.6 54.5 %copy-start = (bf16[128,4096]{1,0:T(8,128)(2,1)S(1)}, bf16[128,4096]{1,0:T(8,128)(2,1)}, u32[]{:S(2)}) copy-start(bf16[128,4096]{1,0:T(8,128)(2,1)} %param.20) | copy-start | bytes 3145732
  1.8 2.6 %copy-start.25 = (f32[16]{0:T(128)}, f32[16]{0:T(128)S(1)}, u32[]{:S(2)}) copy-start(f32[16]{0:T(128)S(1)} %add_rsqrt_fusion.2) | copy-start | bytes 196
  4.3 7.3 %copy-start.38 = (s32[1,32]{1,0:T(1,128)S(1)}, s32[1,32]{1,0:T(1,128)}, u32[]{:S(2)}) copy-start(s32[1,32]{1,0:T(1,128)} %param.12) | copy-start | bytes 388
  4.3 7.7 %copy-start.23 = (f32[128]{0:T(128)S(1)}, f32[128]{0:T(128)}, u32[]{:S(2)}) copy-start(f32[128]{0:T(128)} %param.18) | copy-start | bytes 1540
  4.3 8.3 %copy-start.34 = (f32[128]{0:T(128)S(1)}, f32[128]{0:T(128)}, u32[]{:S(2)}) copy-start(f32[128]{0:T(128)} %param.19) | copy-start | bytes 1540
  4.3 10.3 %copy-start.3 = (bf16[16,4096]{1,0:T(8,128)(2,1)S(1)}, bf16[16,4096]{1,0:T(8,128)(2,1)}, u32[]{:S(2)}) copy-start(bf16[16,4096]{1,0:T(8,128)(2,1)} %param.11) | copy-start | bytes 393220
  4.4 38.9 %all-to-all-start = ((bf16[16,16,4096]{2,1,0:T(8,128)(2,1)}), bf16[16,16,4096]{2,1,0:T(8,128)(2,1)}, u32[]{:S(2)}, u32[]{:S(2)}) async-start(bf16[16,16,4096]{2,1,0:T(8,128)(2,1)} %broadcast_in_dim.31), calls=%async_computation | async-start | bytes 4194304 | tf_op jit(solution)/shard_map/all_to_all | solution.py:67
  14.5 4.1 %copy-start.36 = (s32[16]{0:T(128)}, s32[16]{0:T(128)S(1)}, u32[]{:S(2)}) copy-start(s32[16]{0:T(128)S(1)} %iota_add_fusion) | copy-start | bytes 196
  14.6 31.3 %copy-start.27 = (s32[32]{0:T(128)}, s32[32]{0:T(128)S(1)}, u32[]{:S(2)}) copy-start(s32[32]{0:T(128)S(1)} %broadcast_add_fusion) | copy-start | bytes 388
  14.7 38.6 %copy-start.7 = (f32[256,64]{0,1:T(8,128)}, f32[256,64]{0,1:T(8,128)S(1)}, u32[]{:S(2)}) copy-start(f32[256,64]{0,1:T(8,128)S(1)} %broadcast_multiply_fusion) | copy-start | bytes 196612
  46.2 6.9 %collective-permute-start = (f32[256,128]{0,1:T(8,128)S(1)}, f32[256,128]{0,1:T(8,128)S(1)}, u32[]{:S(2)}, u32[]{:S(2)}) collective-permute-start(f32[256,128]{0,1:T(8,128)S(1)} %slice.110), channel_id=1, source_target_pairs={{0,1},{1,0},{2,3},{3,2},{4,5},{5,4},{6,7},{7,6},{8,9},{9,8},{10,11... | collective-permute-start | bytes 393224 | tf_op jit(solution)/shard_map/ppermute | solution.py:20
  48.1 9.3 %copy-start.30 = (f32[32]{0:T(128)}, f32[32]{0:T(128)S(1)}, u32[]{:S(2)}) copy-start(f32[32]{0:T(128)S(1)} %add_rsqrt_fusion.1) | copy-start | bytes 388
  48.3 0.6 copy-start.16
  48.9 8.5 %copy-start.20 = (bf16[32,128]{1,0:T(8,128)(2,1)}, bf16[32,128]{1,0:T(8,128)(2,1)S(1)}, u32[]{:S(2)}) copy-start(bf16[32,128]{1,0:T(8,128)(2,1)S(1)} %fusion.64) | copy-start | bytes 24580
  53.1 0.6 copy-start.1
  53.1 4.3 %copy-start.18 = (f32[256]{0:T(256)}, f32[256]{0:T(256)S(1)}, u32[]{:S(2)}) copy-start(f32[256]{0:T(256)S(1)} %add_rsqrt_fusion) | copy-start | bytes 3076
  54.2 0.6 copy-start.14
  55.1 14.6 %copy-start.32 = (f32[32]{0:T(128)}, f32[32]{0:T(128)S(1)}, u32[]{:S(2)}) copy-start(f32[32]{0:T(128)S(1)} %get-tuple-element.33) | copy-start | bytes 388
  55.1 16.0 %copy-start.9 = (f32[32,256]{1,0:T(8,128)}, f32[32,256]{1,0:T(8,128)S(1)}, u32[]{:S(2)}) copy-start(f32[32,256]{1,0:T(8,128)S(1)} %get-tuple-element.34) | copy-start | bytes 98308
  55.1 49.9 %copy-start.13 = (bf16[256,128]{0,1:T(8,128)(2,1)}, bf16[256,128]{0,1:T(8,128)(2,1)S(1)}, u32[]{:S(2)}) copy-start(bf16[256,128]{0,1:T(8,128)(2,1)S(1)} %select_convert_fusion) | copy-start | bytes 196612
  55.2 31.1 %copy-start.40 = (s32[256]{0:T(256)S(1)}, s32[256]{0:T(256)}, u32[]{:S(2)}) copy-start(s32[256]{0:T(256)} %param.13) | copy-start | bytes 3076
  57.4 12.3 %all-to-all-start.1 = ((bf16[16,32,256]{2,1,0:T(8,128)(2,1)}), bf16[16,32,256]{2,1,0:T(8,128)(2,1)S(1)}, u32[]{:S(2)}, u32[]{:S(2)}) async-start(bf16[16,32,256]{2,1,0:T(8,128)(2,1)} %bitcast.139), calls=%async_computation.1 | async-start | bytes 524288 | tf_op jit(solution)/shard_map/all_to_all | solution.py:67
  61.8 43.3 %copy-start.21 = (f32[256]{0:T(256)}, f32[256]{0:T(256)S(1)}, u32[]{:S(2)}) copy-start(f32[256]{0:T(256)S(1)} %dynamic_slice.33) | copy-start | bytes 3076
  69.7 0.6 copy-start.11
  71.1 31.8 %all-to-all-start.2 = ((bf16[16,32,256]{2,1,0:T(8,128)(2,1)}), bf16[16,32,256]{2,1,0:T(8,128)(2,1)S(1)}, u32[]{:S(2)}, u32[]{:S(2)}) async-start(bf16[16,32,256]{2,1,0:T(8,128)(2,1)} %broadcast_in_dim.35), calls=%async_computation.2 | async-start | bytes 524288 | tf_op jit(solution)/shard_map/all_to_all | solution.py:67
  105.1 1.0 copy-start.5
  107.2 15.7 %all-to-all-start.3 = ((f32[16,56,128]{2,1,0:T(8,128)}), f32[16,56,128]{2,1,0:T(8,128)}, u32[]{:S(2)}, u32[]{:S(2)}) async-start(f32[16,56,128]{2,1,0:T(8,128)} %pad_maximum_fusion.1), calls=%async_computation.3 | async-start | bytes 917504 | tf_op jit(solution)/shard_map/all_to_all | solution.py:67
  131.2 12.9 %all-to-all-start.4 = ((bf16[16,64,128]{2,1,0:T(8,128)(2,1)}), bf16[16,64,128]{2,1,0:T(8,128)(2,1)}, u32[]{:S(2)}, u32[]{:S(2)}) async-start(bf16[16,64,128]{2,1,0:T(8,128)(2,1)} %broadcast_in_dim.40), calls=%async_computation.4 | async-start | bytes 524288 | tf_op jit(solution)/shard_map/all_to_all | solution.py:67
  138.6 14.4 %copy-start.39 = (f32[8]{0:T(128)S(1)}, f32[8]{0:T(128)}, u32[]{:S(2)}) copy-start(f32[8]{0:T(128)} %get-tuple-element.27) | copy-start | bytes 100
  138.6 14.4 %copy-start.41 = (f32[24]{0:T(128)S(1)}, f32[24]{0:T(128)}, u32[]{:S(2)}) copy-start(f32[24]{0:T(128)} %dynamic_slice.36) | copy-start | bytes 292
  138.6 14.5 %copy-start.12 = (f32[32,256]{1,0:T(8,128)S(1)}, f32[32,256]{1,0:T(8,128)}, u32[]{:S(2)}) copy-start(f32[32,256]{1,0:T(8,128)} %copy-done.11) | copy-start | bytes 98308
  138.6 14.5 %copy-start.22 = (f32[256]{0:T(256)S(1)}, f32[256]{0:T(256)}, u32[]{:S(2)}) copy-start(f32[256]{0:T(256)} %copy-done.21) | copy-start | bytes 3076
  146.5 0.7 copy-start.6
  151.3 18.2 %copy-start.2 = (f32[256,128]{0,1:T(8,128)S(1)}, f32[256,128]{0,1:T(8,128)}, u32[]{:S(2)}) copy-start(f32[256,128]{0,1:T(8,128)} %copy-done.1) | copy-start | bytes 393220
  151.4 18.1 %copy-start.8 = (f32[256,64]{0,1:T(8,128)S(1)}, f32[256,64]{0,1:T(8,128)}, u32[]{:S(2)}) copy-start(f32[256,64]{0,1:T(8,128)} %copy-done.7) | copy-start | bytes 196612
  151.4 18.1 %copy-start.19 = (f32[256]{0:T(256)S(1)}, f32[256]{0:T(256)}, u32[]{:S(2)}) copy-start(f32[256]{0:T(256)} %copy-done.18) | copy-start | bytes 3076
  151.4 18.1 %copy-start.35 = (f32[128]{0:T(128)S(1)}, f32[128]{0:T(128)}, u32[]{:S(2)}) copy-start(f32[128]{0:T(128)} %param.19) | copy-start | bytes 1540
  151.6 18.5 %copy-start.10 = (f32[32,256]{1,0:T(8,128)S(1)}, f32[32,256]{1,0:T(8,128)}, u32[]{:S(2)}) copy-start(f32[32,256]{1,0:T(8,128)} %copy-done.9) | copy-start | bytes 98308
  151.6 18.5 %copy-start.33 = (f32[32]{0:T(128)S(1)}, f32[32]{0:T(128)}, u32[]{:S(2)}) copy-start(f32[32]{0:T(128)} %copy-done.32) | copy-start | bytes 388
  153.2 19.7 %copy-start.17 = (f32[32,64]{1,0:T(8,128)S(1)}, f32[32,64]{1,0:T(8,128)}, u32[]{:S(2)}) copy-start(f32[32,64]{1,0:T(8,128)} %copy-done.16) | copy-start | bytes 24580
  153.3 19.7 %copy-start.24 = (f32[128]{0:T(128)S(1)}, f32[128]{0:T(128)}, u32[]{:S(2)}) copy-start(f32[128]{0:T(128)} %param.18) | copy-start | bytes 1540
  153.3 19.7 %copy-start.31 = (f32[32]{0:T(128)S(1)}, f32[32]{0:T(128)}, u32[]{:S(2)}) copy-start(f32[32]{0:T(128)} %copy-done.30) | copy-start | bytes 388
  165.2 8.0 %copy-start.28 = (s32[32]{0:T(128)S(1)}, s32[32]{0:T(128)}, u32[]{:S(2)}) copy-start(s32[32]{0:T(128)} %copy-done.27) | copy-start | bytes 388
  170.4 6.9 %collective-permute-start.1 = (f32[256,128]{0,1:T(8,128)S(1)}, f32[256,128]{0,1:T(8,128)S(1)}, u32[]{:S(2)}, u32[]{:S(2)}) collective-permute-start(f32[256,128]{0,1:T(8,128)S(1)} %get-tuple-element.37), channel_id=1, source_target_pairs={{0,1},{1,0},{2,3},{3,2},{4,5},{5,4},{6,7},{7,6},{8,9},{9,8},{10,11... | collective-permute-start | bytes 393224 | tf_op jit(solution)/shard_map/ppermute | solution.py:20
  179.4 32.2 %all-to-all-start.6 = ((bf16[16,16,4096]{2,1,0:T(8,128)(2,1)}), bf16[16,16,4096]{2,1,0:T(8,128)(2,1)S(1)}, u32[]{:S(2)}, u32[]{:S(2)}) async-start(bf16[16,16,4096]{2,1,0:T(8,128)(2,1)} %bitcast.131), calls=%async_computation.6 | async-start | bytes 4194304 | tf_op jit(solution)/shard_map/all_to_all | solution.py:67
  183.1 28.8 %copy-start.4 = (bf16[16,4096]{1,0:T(8,128)(2,1)S(1)}, bf16[16,4096]{1,0:T(8,128)(2,1)}, u32[]{:S(2)}) copy-start(bf16[16,4096]{1,0:T(8,128)(2,1)} %param.11) | copy-start | bytes 393220
  183.1 28.8 %copy-start.15 = (f32[4096]{0:T(1024)S(1)}, f32[4096]{0:T(1024)}, u32[]{:S(2)}) copy-start(f32[4096]{0:T(1024)} %param.15) | copy-start | bytes 49156
  211.6 0.7 copy-start.26
  211.6 0.9 copy-start.29
  211.6 0.9 copy-start.37

commit v3 on v2

--- a/solution.py
+++ b/solution.py
@@ -3,9 +3,12 @@
 import jax
 import jax.numpy as jnp
 from jax import lax
+from jax.experimental import pallas as pl
+from jax.experimental.pallas import tpu as pltpu
 from jax.sharding import PartitionSpec as P
 
 QDEV = 8
+LANES = 128
 
 
 EPSILON = 1e-06
@@ -72,123 +75,277 @@
     return exchange(jnp.broadcast_to(rows[None], (count,) + rows.shape), axis)
 
 
-def to_tiles(block):
-    rows, width = block.shape
-    tiles = block.reshape(rows // 8, 8, width // 128, 128).transpose(0, 2, 1, 3)
-    return tiles.reshape(rows // 8, width // 16, 128)
-
-
-def from_tiles(tiles):
-    count, height = tiles.shape[:2]
-    block = tiles.reshape(count, height // 8, 8, 128).transpose(0, 2, 1, 3)
-    return block.reshape(count * 8, height * 16)
-
-
-def split16(value):
-    high = value.astype(jnp.bfloat16)
-    return [high, (value - high.astype(jnp.float32)).astype(jnp.bfloat16)]
-
-
-def contrast(scaled16, out_gain, positives, negatives):
-    groups, sequences, width = scaled16.shape
+def halves(value):
+    high = value.astype(jnp.bfloat16).astype(jnp.float32)
+    return jnp.concatenate([high, value - high], axis=0)
+
+
+def iota(shape, axis):
+    return lax.broadcasted_iota(jnp.int32, shape, axis)
+
+
+def columns_to_lanes(column, out_ref):
+    diagonal = iota((LANES, LANES), 0) == iota((LANES, LANES), 1)
+    for k in range(column.shape[0] // LANES):
+        block = jnp.where(diagonal, column[LANES * k : LANES * (k + 1)], 0.0)
+        out_ref[k : k + 1, :] = jnp.sum(block, axis=0, keepdims=True)
+
+
+def partial_logits_kernel(rows_ref, query_hot_ref, positive_hot_ref, listed_ref, gain_ref, out_ref, held_ref):
+    rows = rows_ref[...]
+    queries = jnp.dot(query_hot_ref[...], rows, preferred_element_type=jnp.float32)
+    positives = jnp.dot(positive_hot_ref[...], rows, preferred_element_type=jnp.float32)
+    queries = queries.astype(jnp.bfloat16)
+    features = gain_ref.shape[1] * out_ref.shape[0]
+    rows32 = rows.astype(jnp.float32)
+    plain = rows32 / gain_ref[...]
+    squares = jnp.sum(rows32 * rows32, axis=1, keepdims=True) + jnp.sum(
+        plain * plain, axis=1, keepdims=True
+    ) * (EPSILON / features)
+    against = (((1,), (1,)), ((), ()))
+    with_positives = lax.dot_general(
+        positives.astype(jnp.bfloat16), queries, against, preferred_element_type=jnp.float32
+    )
+    with_all = lax.dot_general(rows, queries, against, preferred_element_type=jnp.float32)
+    row_index = iota(with_all.shape, 0)
+    for j in range(8):
+        listed = row_index == listed_ref[j : j + 1, :]
+        held_ref[j : j + 1, :] = jnp.sum(jnp.where(listed, with_all, 0.0), axis=0, keepdims=True)
+        held_ref[8 + j : 9 + j, :] = jnp.sum(
+            jnp.where(listed, squares, 0.0), axis=0, keepdims=True
+        )
+    columns_to_lanes(squares, held_ref.at[16:24])
+    count = with_positives.shape[0]
+    sent = [with_positives.astype(jnp.bfloat16)]
+    for start in (0, 8, 16):
+        sent.append(halves(held_ref[start : start + 8, :]).astype(jnp.bfloat16))
+    for t in range(out_ref.shape[0]):
+        out_ref[t, :count, :] = sent[0]
+        for k in range(3):
+            out_ref[t, count + 16 * k : count + 16 * (k + 1), :] = sent[k + 1]
+
+
+def softmax_kernel(core_start_ref, arrived_ref, positive_hot_ref, out_ref, inverse_ref):
+    count = positive_hot_ref.shape[0]
+    summed = arrived_ref[0].astype(jnp.float32)
+    for t in range(1, arrived_ref.shape[0]):
+        summed = summed + arrived_ref[t].astype(jnp.float32)
+
+    def small(k):
+        block = summed[count + 16 * k : count + 16 * (k + 1)]
+        return block[:8] + block[8:]
+
+    inverse_listed = lax.rsqrt(small(1) + EPSILON * EPSILON)
+    inverse = lax.rsqrt(small(2) + EPSILON * EPSILON)
+    inverse_ref[...] = inverse
+    inverse_query = inverse_listed[7:8, :]
+    picked = jnp.zeros((count, LANES), jnp.float32)
+    for k in range(8):
+        hot = positive_hot_ref[:, LANES * k : LANES * (k + 1)].astype(jnp.float32)
+        picked = picked + hot * inverse[k : k + 1, :]
+    inverse_positive = jnp.sum(picked, axis=1, keepdims=True)
+    logits = summed[:count] * inverse_positive * inverse_query / SOFTMAX_TEMPER
+    hard = small(0) * inverse_listed * inverse_query / SOFTMAX_TEMPER
+    is_hard = iota(hard.shape, 0) < 7
+    is_own = iota(logits.shape, 0) == iota(logits.shape, 1) + core_start_ref[0]
+    weights = jnp.exp(logits - 1.0 / SOFTMAX_TEMPER)
+    hard_weights = jnp.where(is_hard, jnp.exp(hard - 1.0 / SOFTMAX_TEMPER), 0.0)
+    totals = jnp.sum(weights, axis=0, keepdims=True) + jnp.sum(hard_weights, axis=0, keepdims=True)
+    target = jnp.sum(jnp.where(is_own, logits, 0.0), axis=0, keepdims=True)
+    losses = jnp.log(totals) + 1.0 / SOFTMAX_TEMPER - target
+    scaling_factor = LOSS_MULTIPLIER / (count * SOFTMAX_TEMPER)
+
+    def rounded(value):
+        return value.astype(jnp.bfloat16).astype(jnp.float32)
+
+    coef = rounded(scaling_factor * (weights / totals - is_own.astype(jnp.float32)))
+    hard_coef = rounded(scaling_factor * (hard_weights / totals))
+    weighted = coef * logits * SOFTMAX_TEMPER
+    hard_weighted = jnp.where(is_hard, hard_coef * hard * SOFTMAX_TEMPER, 0.0)
+    along_query = jnp.sum(weighted, axis=0, keepdims=True) + jnp.sum(
+        hard_weighted, axis=0, keepdims=True
+    )
+    out_ref[:count, :] = coef
+    out_ref[count : count + 8, :] = jnp.where(is_hard, hard_coef, along_query)
+    out_ref[count + 8 : count + 16, :] = jnp.where(is_hard, hard_weighted, losses)
+    out_ref[count + 16 :, :] = jnp.zeros_like(out_ref[count + 16 :, :])
+    columns_to_lanes(jnp.sum(weighted, axis=1, keepdims=True), out_ref.at[count + 16 :])
+
+
+def resid_grad_kernel(
+    group_ref,
+    both_ref,
+    inverse_ref,
+    rows_ref,
+    positive_hot_ref,
+    query_hot_ref,
+    positive_row_ref,
+    listed_ref,
+    own_listed_ref,
+    resid_ref,
+    gain_ref,
+    out_ref,
+    loss_ref,
+):
+    sequences = resid_ref.shape[0]
+    count, total_rows = positive_hot_ref.shape
+    first_row = group_ref[0] * sequences
+    first_query = group_ref[0] * QDEV
+    across = (((1,), (1,)), ((), ()))
+
+    def joined(start, stop):
+        return jnp.concatenate([both_ref[0, start:stop, :], both_ref[1, start:stop, :]], axis=1)
+
+    coef = joined(0, count)
+    coef16 = coef.astype(jnp.bfloat16)
+    hard = joined(count, count + 8)
+    hard_weighted = joined(count + 8, count + 16)
+    along_passage = both_ref[0, count + 16 : count + 24, :] + both_ref[1, count + 16 : count + 24, :]
+    along_passage = jnp.concatenate([along_passage[0:1], along_passage[1:2]], axis=1)
+    inverse = jnp.concatenate([inverse_ref[k : k + 1, :] for k in range(8)], axis=1)
+
+    own_row = first_row + iota((sequences, count), 0)
+    own_query = (iota((sequences, count), 0) < QDEV) & (
+        iota((sequences, count), 1) == first_query + iota((sequences, count), 0)
+    )
+    own_positive = positive_row_ref[...] == own_row
+    to_positives = lax.dot_general(
+        own_query.astype(jnp.bfloat16), coef16, across, preferred_element_type=jnp.float32
+    )
+    to_queries = jnp.dot(
+        own_positive.astype(jnp.bfloat16), coef16, preferred_element_type=jnp.float32
+    )
+    along = jnp.sum(
+        jnp.where(own_query, hard[7:8, :], 0.0) + jnp.where(own_positive, along_passage, 0.0),
+        axis=1,
+        keepdims=True,
+    )
+    for j in range(7):
+        listed = listed_ref[j : j + 1, :] == own_row
+        to_queries = to_queries + jnp.where(listed, hard[j : j + 1, :], 0.0)
+        along = along + jnp.sum(
+            jnp.where(listed, hard_weighted[j : j + 1, :], 0.0), axis=1, keepdims=True
+        )
+    matrix = jnp.dot(
+        to_positives.astype(jnp.bfloat16), positive_hot_ref[...], preferred_element_type=jnp.float32
+    ) + jnp.dot(
+        to_queries.astype(jnp.bfloat16), query_hot_ref[...], preferred_element_type=jnp.float32
+    )
+    row_index = iota((sequences, total_rows), 1)
+    for j in range(7):
+        own_hard = jnp.sum(jnp.where(own_query, hard[j : j + 1, :], 0.0), axis=1, keepdims=True)
+        listed = row_index == own_listed_ref[:, j : j + 1]
+        matrix = matrix + jnp.where(listed, own_hard, 0.0)
+    matrix = matrix * inverse
+    high = matrix.astype(jnp.bfloat16)
+    low = (matrix - high.astype(jnp.float32)).astype(jnp.bfloat16)
+    rows = rows_ref[...]
+    d_embed = jnp.dot(high, rows, preferred_element_type=jnp.float32) + jnp.dot(
+        low, rows, preferred_element_type=jnp.float32
+    )
+
+    is_own_row = row_index == first_row + iota((sequences, total_rows), 0)
+    own_inverse = jnp.sum(jnp.where(is_own_row, inverse, 0.0), axis=1, keepdims=True)
+    resid = resid_ref[...]
+    gain = gain_ref[...]
+    features = gain.shape[1] * out_ref.shape[0]
+    d_resid = own_inverse * gain * (
+        d_embed - resid * gain * own_inverse * along
+    ) - resid * (along * own_inverse * own_inverse * (EPSILON / features))
+    d_resid16 = d_resid.astype(jnp.bfloat16)
+    for t in range(out_ref.shape[0]):
+        out_ref[t] = d_resid16
+    losses = jnp.sum(hard_weighted[7:8, :], axis=1, keepdims=True)
+    loss_ref[...] = jnp.broadcast_to(losses / count, loss_ref.shape)
+
+
+def kernel_call(body, outs, arrays, scalars=0, scratch=()):
+    specs = [pl.BlockSpec(memory_space=pltpu.SMEM)] * scalars
+    specs += [pl.BlockSpec(memory_space=pltpu.VMEM)] * (len(arrays) - scalars)
+    return pl.pallas_call(
+        body,
+        out_shape=[jax.ShapeDtypeStruct(shape, dtype) for shape, dtype in outs],
+        in_specs=specs,
+        out_specs=[pl.BlockSpec(memory_space=pltpu.VMEM)] * len(outs),
+        scratch_shapes=list(scratch),
+        compiler_params=pltpu.CompilerParams(vmem_limit_bytes=40 * 2**20),
+    )(*arrays)
+
+
+def candidate_tables(positives, negatives, core, group, sequences, core_count):
+    others = sequences - QDEV
+    query_count = positives.shape[0]
+    total_rows = query_count // QDEV * sequences
+    core_queries = query_count // core_count
+
+    def row_of(passage):
+        return passage // others * sequences + QDEV + passage % others
+
+    queries = jnp.arange(query_count, dtype=jnp.int32)
+    query_row = queries // QDEV * sequences + queries % QDEV
+    positive_row = row_of(positives)
+    rows = jnp.arange(total_rows, dtype=jnp.int32)
+    query_hot = (query_row[:, None] == rows[None, :]).astype(jnp.bfloat16)
+    positive_hot = (positive_row[:, None] == rows[None, :]).astype(jnp.bfloat16)
+    listed = jnp.concatenate([row_of(negatives), query_row[:, None]], axis=1)
+    own_listed = lax.dynamic_slice_in_dim(listed, group * QDEV, QDEV)
+    own_listed = jnp.pad(
+        own_listed, ((0, sequences - QDEV), (0, LANES - listed.shape[1])), constant_values=-1
+    )
+    core_start = core * core_queries
+    return (
+        positive_row[None, :],
+        query_hot,
+        lax.dynamic_slice_in_dim(query_hot, core_start, core_queries),
+        positive_hot,
+        listed.T,
+        lax.dynamic_slice_in_dim(listed, core_start, core_queries).T,
+        own_listed,
+    )
+
+
+def contrast(everyone, resid, out_gain, tables, group):
     tensor_count, core_count = lax.axis_size("tensor"), lax.axis_size("core")
-    query_rows = scaled16[:, :QDEV].reshape(groups * QDEV, width)
-    passage_rows = scaled16[:, QDEV:].reshape(-1, width)
-    query_count, passage_count = query_rows.shape[0], passage_rows.shape[0]
-    core_queries = query_count // core_count
-    own_queries = core_queries // tensor_count
-    features = width * tensor_count
-
-    core_start = lax.axis_index("core") * core_queries
-    core_rows = lax.dynamic_slice_in_dim(query_rows, core_start, core_queries)
-    raw = jnp.dot(core_rows, passage_rows.T, preferred_element_type=jnp.float32)
-    rows32 = jnp.concatenate([query_rows, passage_rows]).astype(jnp.float32)
-    plain = rows32 / out_gain
-    squares = jnp.sum(rows32 * rows32 + plain * plain * (EPSILON / features), axis=1)
-    lanes = 128
-    logit_rows = own_queries * passage_count // lanes
-    packed = jnp.concatenate(
+    sequences, width = resid.shape
+    positive_row, query_hot, core_hot, positive_hot, listed, core_listed, own_listed = tables
+    count, total_rows = positive_hot.shape
+    rows = everyone.reshape(total_rows, width)
+    gain = out_gain[None, :]
+    core_queries = core_hot.shape[0]
+    core_start = (lax.axis_index("core") * core_queries)[None]
+    (sent,) = kernel_call(
+        partial_logits_kernel,
+        [((tensor_count, count + 48, core_queries), jnp.bfloat16)],
+        [rows, core_hot, positive_hot, core_listed, gain],
+        scratch=[pltpu.VMEM((24, core_queries), jnp.float32)],
+    )
+    arrived = exchange(sent, "tensor")
+    coefs, inverse = kernel_call(
+        softmax_kernel,
+        [((count + 24, core_queries), jnp.float32), ((8, LANES), jnp.float32)],
+        [core_start, arrived, positive_hot],
+        scalars=1,
+    )
+    both = lax.all_gather(coefs, "core", axis=0)
+    d_resid16, loss = kernel_call(
+        resid_grad_kernel,
+        [((tensor_count, sequences, width), jnp.bfloat16), ((8, LANES), jnp.float32)],
         [
-            to_tiles(raw),
-            jnp.broadcast_to(
-                squares.reshape(1, -1, lanes), (tensor_count, squares.shape[0] // lanes, lanes)
-            ),
+            group[None],
+            both,
+            inverse,
+            rows,
+            positive_hot,
+            query_hot,
+            positive_row,
+            listed,
+            own_listed,
+            resid,
+            gain,
         ],
-        axis=1,
-    )
-    summed = jnp.sum(exchange(packed, "tensor"), axis=0)
-    inverse = lax.rsqrt(summed[logit_rows:].reshape(-1) + EPSILON * EPSILON)
-    own = core_start + lax.axis_index("tensor") * own_queries
-    inverse_query = lax.dynamic_slice_in_dim(inverse[:query_count], own, own_queries)
-    inverse_passage = inverse[query_count:]
-    logits = (
-        from_tiles(summed[None, :logit_rows])
-        * inverse_query[:, None]
-        * inverse_passage[None, :]
-        / SOFTMAX_TEMPER
-    )
-
-    passage_ids = jnp.arange(passage_count, dtype=jnp.int32)
-    any_positive = jnp.any(positives[:, None] == passage_ids[None, :], axis=0)
-    own_positives = lax.dynamic_slice_in_dim(positives, own, own_queries)
-    own_negatives = lax.dynamic_slice_in_dim(negatives, own, own_queries)
-    positive_hot = own_positives[:, None] == passage_ids[None, :]
-    hard_hot = jnp.any(own_negatives[:, :, None] == passage_ids[None, None, :], axis=1)
-    permitted_mask = any_positive[None, :] | hard_hot
-    weight_params = jnp.where(permitted_mask, jnp.exp(logits - 1.0 / SOFTMAX_TEMPER), 0.0)
-    totals = jnp.sum(weight_params, axis=1, keepdims=True)
-    target_labels = jnp.sum(jnp.where(positive_hot, logits, 0.0), axis=1)
-    loss_part = jnp.sum(jnp.log(totals[:, 0]) + 1.0 / SOFTMAX_TEMPER - target_labels)
-    scaling_factor = LOSS_MULTIPLIER / (query_count * SOFTMAX_TEMPER)
-    coef16 = (
-        scaling_factor * (weight_params / totals - positive_hot.astype(jnp.float32))
-    ).astype(jnp.bfloat16)
-    weighted = coef16.astype(jnp.float32) * logits * SOFTMAX_TEMPER
-    along_query = jnp.sum(weighted, axis=1)
-    along_passage = jnp.sum(weighted, axis=0)
-
-    small = jnp.concatenate(
-        [
-            along_passage,
-            jnp.pad(jnp.concatenate([along_query, loss_part[None]]), (0, lanes - own_queries - 1)),
-        ]
-    ).reshape(-1, lanes)
-    small_rows = small.shape[0]
-    sent = jnp.concatenate([to_tiles(coef16)[0]] + split16(small))
-    sent = jnp.pad(sent, ((0, -sent.shape[0] % 16), (0, 0)))
-    arrived = lax.all_gather(gather_rows(sent, "tensor"), "core", axis=0, tiled=True)
-    arrived = arrived.reshape(core_count * tensor_count, -1, lanes)
-    coef_all = from_tiles(arrived[:, :logit_rows])
-    parts = arrived[:, logit_rows : logit_rows + 2 * small_rows].astype(jnp.float32)
-    small_all = parts[:, :small_rows] + parts[:, small_rows:]
-    along_passage = jnp.sum(small_all[:, : small_rows - 1], axis=0).reshape(-1)
-    along_query = small_all[:, small_rows - 1, :own_queries].reshape(-1)
-    loss = jnp.sum(small_all[:, small_rows - 1, own_queries]) / query_count
-
-    embeds16 = (rows32 * inverse[:, None]).astype(jnp.bfloat16)
-    d_queries = jnp.dot(
-        coef_all, embeds16[query_count:], preferred_element_type=jnp.float32
-    )
-    d_passages = jnp.dot(
-        coef_all.T, embeds16[:query_count], preferred_element_type=jnp.float32
-    )
-    own_group = lax.axis_index("z") * core_count + lax.axis_index("core")
-    others = sequences - QDEV
-
-    def own_part(of_queries, of_passages):
-        return jnp.concatenate(
-            [
-                lax.dynamic_slice_in_dim(of_queries, own_group * QDEV, QDEV),
-                lax.dynamic_slice_in_dim(of_passages, own_group * others, others),
-            ]
-        )
-
-    return (
-        loss,
-        own_part(d_queries, d_passages),
-        own_part(along_query, along_passage),
-        own_part(inverse[:query_count], inverse_passage),
-    )
+        scalars=1,
+    )
+    return loss[0, 0], exchange(d_resid16, "tensor")
 
 
 def on_device(
@@ -206,6 +363,10 @@
     hidden32 = hidden.astype(jnp.float32)
     inverse_in = rms_scale(hidden32)
     normed = (hidden32 * inverse_in * in_gain).astype(jnp.bfloat16)
+    core_count = lax.axis_size("core")
+    core = lax.axis_index("core")
+    group = lax.axis_index("z") * core_count + core
+    tables = candidate_tables(positives, negatives, core, group, sequences, core_count)
     piece = gather_rows(normed, "tensor").reshape(tokens_count, features)
     own_index = tensor_index * own_rows + jnp.arange(own_rows, dtype=jnp.int32)
     inside, position, last = segment_layout(lengths[0], tokens_count)
@@ -243,14 +404,7 @@
     scaled = resid * own_gain
     same_core = gather_rows(scaled.astype(jnp.bfloat16), "z")
     everyone = lax.all_gather(same_core, "core", axis=1)
-    everyone = everyone.reshape(-1, sequences, chunk)
-    loss, d_embed, along, inverse = contrast(everyone, own_gain, positives, negatives)
-    inverse, along = inverse[:, None], along[:, None]
-    d_resid = inverse * own_gain * (d_embed - scaled * inverse * along) - resid * (
-        along * inverse * inverse * (EPSILON / features)
-    )
-    d_resid16 = gather_rows(d_resid.astype(jnp.bfloat16), "tensor")
-    d_resid16 = d_resid16.reshape(tensor_count, sequences, chunk)
+    loss, d_resid16 = contrast(everyone, resid, own_gain, tables, group)
     d_resid16 = d_resid16.transpose(1, 0, 2).reshape(sequences, features)
     d_attn16 = jnp.dot(d_resid16, wo.T, preferred_element_type=jnp.float32).astype(jnp.bfloat16)
     d_probs = jnp.dot(d_attn16, value16.T, preferred_element_type=jnp.float32)

time: 216 us -> 195 us (0.903)
  other arithmetic: 21.7 us -> 9.69 us
  waiting for transfers between devices: 96.1 us -> 104 us
  matrix products: 17.1 us -> 9.26 us
  local copies, waits for them, and re-layouts: 16.4 us -> 9.55 us
  starting transfers between devices: 42.5 us -> 38.5 us
  Pallas kernels: 0 us -> 3.92 us
    all_to_all x6 -> x5, waiting for transfers between devices: 88.2 us -> 95.9 us  [exchange(): return lax.all_to_all(blocks, axis, 0, 0, tiled=True)]
    reduce_sum x7 -> x0, other arithmetic: 6.97 us -> none  [the longest x1 1.65 us: contrast(): summed = jnp.sum(exchange(packed, 'tensor'), axis=0)]
    dynamic_slice x8 -> x1, local copies, waits for them, and re-layouts: 4.85 us -> 0.03 us  [candidate_tables(): lax.dynamic_slice_in_dim(query_hot, core_start, core_queries)]
    dot_general x3 -> x0, matrix products: 4.37 us -> none  [the longest x1 2.09 us: contrast(): jnp.dot(coef_all.T, embeds16[:query_count], preferred_element_type=jnp.fl...]
    all_to_all x6 -> x5, starting transfers between devices: 38.1 us -> 34.1 us  [exchange(): return lax.all_to_all(blocks, axis, 0, 0, tiled=True)]
    pallas_call x0 -> x3, Pallas kernels: none -> 3.92 us  [kernel_call(): pl.pallas_call(body, out_shape=[jax.ShapeDtypeStruct(shape, dtype) for sh...]
    unnamed x85 -> x94, local copies, waits for them, and re-layouts: 4.64 us -> 3.59 us
  transfers between devices with their start and end apart: 8 -> 7, of which waited for: 8 -> 7; matrix products, arithmetic and copies ran while one was open for 8% -> 5% of each run, Pallas kernels for 0% -> 0%
where the time goes in v3:
time: 195 us; the launch traced here: 194 us
  waiting for transfers between devices  104 us (53%)
  starting transfers between devices  38.5 us (20%)
  blocking collectives  16 us (8%)
  other arithmetic  9.69 us (5%)
  local copies, waits for them, and re-layouts  9.55 us (5%)
  matrix products  9.26 us (5%)
  Pallas kernels  3.92 us (2%)
  between operations  2.71 us (1%)
    all_to_all x5, waiting for transfers between devices, exchange(): return lax.all_to_all(blocks, axis, 0, 0, tiled=True)  95.9 us
    all_to_all x5, starting transfers between devices, exchange(): return lax.all_to_all(blocks, axis, 0, 0, tiled=True)  34.1 us
    all_to_all x1, blocking collectives, exchange(): return lax.all_to_all(blocks, axis, 0, 0, tiled=True)  11.9 us
    ppermute x2, waiting for transfers between devices, swapped(): return lax.ppermute(value, axis, pairs)  8.04 us
    ppermute x2, starting transfers between devices, swapped(): return lax.ppermute(value, axis, pairs)  4.4 us
    pallas_call x3, Pallas kernels, kernel_call(): pl.pallas_call(body, out_shape=[jax.ShapeDtypeStruct(shape, dtype) for sh...  3.92 us
  transfers between devices with their start and end apart: 7, of which 7 were waited for; matrix products, arithmetic and copies ran while one was open for 5% of the time, Pallas kernels for 0%

profile of v3, /device:TPU:32, one launch (start us, length us, event | category | flops | bytes accessed | tf_op | source)
XLA Modules:
  0.0 193.7 jit_solution(9823845092452698327)
XLA Ops:
  0.6 1.1 fusion.14
  1.8 0.6 copy-done.27
  2.4 1.0 fusion.10
  3.4 1.6 broadcast_in_dim.25
  5.0 7.2 %all-to-all-start = ((bf16[16,16,4096]{2,1,0:T(8,128)(2,1)}), bf16[16,16,4096]{2,1,0:T(8,128)(2,1)}, u32[]{:S(2)}, u32[]{:S(2)}) async-start(bf16[16,16,4096]{2,1,0:T(8,128)(2,1)} %broadcast_in_dim.25), calls=%async_computation | async-start | bytes 4194304 | tf_op jit(solution)/shard_map/all_to_all | solution.py:70
  12.3 0.1 copy.36
  12.4 0.1 reduce
  12.6 0.1 select_reduce_fusion
  12.7 0.6 reduce_max.18
  13.3 0.6 reduce_max.19
  15.2 0.7 broadcast_multiply_fusion
  15.9 1.1 fusion.34
  17.0 1.4 constant_dynamic-update-slice_fusion.1
  18.4 1.5 constant_dynamic-update-slice_fusion
  19.9 24.0 %all-to-all-done = bf16[16,16,4096]{2,1,0:T(8,128)(2,1)} async-done(((bf16[16,16,4096]{2,1,0:T(8,128)(2,1)}), bf16[16,16,4096]{2,1,0:T(8,128)(2,1)}, u32[]{:S(2)}, u32[]{:S(2)}) %all-to-all-start) | async-done | bytes 2097184 | tf_op jit(solution)/shard_map/all_to_all | solution.py:70
  43.9 2.6 %fusion.74 = f32[256,256]{0,1:T(8,128)S(1)} fusion(bf16[256,4096]{1,0:T(8,128)(2,1)} %bitcast, bf16[4096,256]{1,0:T(8,128)(2,1)S(1)} %constant_dynamic-update-slice_fusion), kind=kOutput, calls=%fused_computation.153 | convolution fusion | flops 536870912 | bytes 4456448 | tf_op jit(solution)/shard_map/dot_general | solution.py:377
  46.6 0.3 multiply_reduce_fusion.4
  46.9 1.9 collective-permute-start
  49.0 0.1 fusion.37
  49.2 0.3 copy-done.31
  49.4 4.3 %collective-permute-done = f32[256,128]{0,1:T(8,128)S(1)} collective-permute-done((f32[256,128]{0,1:T(8,128)S(1)}, f32[256,128]{0,1:T(8,128)S(1)}, u32[]{:S(2)}, u32[]{:S(2)}) %collective-permute-start) | collective-permute-done | bytes 131104 | tf_op jit(solution)/shard_map/ppermute | solution.py:23
  53.8 0.1 multiply_multiply_fusion
  54.0 0.5 fusion.24
  54.5 0.2 fusion.73
  54.8 0.3 copy-done.16
  55.1 0.5 fusion
  55.6 0.7 copy.44
  56.3 3.6 %all-to-all-start.1 = ((bf16[16,32,256]{2,1,0:T(8,128)(2,1)}), bf16[16,32,256]{2,1,0:T(8,128)(2,1)S(1)}, u32[]{:S(2)}, u32[]{:S(2)}) async-start(bf16[16,32,256]{2,1,0:T(8,128)(2,1)} %bitcast.49), calls=%async_computation.1 | async-start | bytes 524288 | tf_op jit(solution)/shard_map/all_to_all | solution.py:70
  59.9 0.8 dynamic_slice.12
  60.7 7.9 %all-to-all-done.1 = bf16[16,32,256]{2,1,0:T(8,128)(2,1)S(1)} async-done(((bf16[16,32,256]{2,1,0:T(8,128)(2,1)}), bf16[16,32,256]{2,1,0:T(8,128)(2,1)S(1)}, u32[]{:S(2)}, u32[]{:S(2)}) %all-to-all-start.1) | async-done | bytes 262176 | tf_op jit(solution)/shard_map/all_to_all | solution.py:70
  68.6 0.7 broadcast_in_dim.30
  69.4 15.2 %all-to-all-start.2 = ((bf16[16,32,256]{2,1,0:T(8,128)(2,1)}), bf16[16,32,256]{2,1,0:T(8,128)(2,1)S(1)}, u32[]{:S(2)}, u32[]{:S(2)}) async-start(bf16[16,32,256]{2,1,0:T(8,128)(2,1)} %broadcast_in_dim.30), calls=%async_computation.2 | async-start | bytes 524288 | tf_op jit(solution)/shard_map/all_to_all | solution.py:70
  84.6 0.1 fusion.60.listed_ref
  84.7 0.2 fusion.5.query_hot_ref
  84.9 0.7 copy-done.1
  85.6 0.1 fusion.6.positive_hot_ref
  85.8 15.3 %all-to-all-done.2 = bf16[16,32,256]{2,1,0:T(8,128)(2,1)S(1)} async-done(((bf16[16,32,256]{2,1,0:T(8,128)(2,1)}), bf16[16,32,256]{2,1,0:T(8,128)(2,1)S(1)}, u32[]{:S(2)}, u32[]{:S(2)}) %all-to-all-start.2) | async-done | bytes 262176 | tf_op jit(solution)/shard_map/all_to_all | solution.py:70
  101.2 2.2 %all-gather = bf16[16,64,256]{2,1,0:T(8,128)(2,1)S(1)} all-gather(bf16[16,32,256]{2,1,0:T(8,128)(2,1)S(1)} %all-to-all-done.2), channel_id=2, replica_groups=mesh['z'=16,'core'=2,'tensor'=16] {'core'}, dimensions={1}, use_global_device_ids=true | all-gather | bytes 786432 | tf_op jit(solution)/shard_map/all_gather | solution.py:406
  103.3 2.5 %shard_map.122 = bf16[16,304,128]{2,1,0:T(8,128)(2,1)} custom-call(bf16[1024,256]{1,0:T(8,128)(2,1)S(1)} %bitcast.50, bf16[128,1024]{1,0:T(8,128)(2,1)S(1)} %constant_dynamic-slice_fusion.query_hot_ref, bf16[256,1024]{1,0:T(8,128)(2,1)S(1)} %fusion.6.positive_hot_ref, s32[8,128]{1,0:T(8,128)S(1)} %fusion.60.listed_ref, f32[1,256]{1,0:T(1,128)S(1)} %bitcast.53), custom_call_target="tpu_custom_call" | custom-call | tf_op jit(solution)/shard_map/pallas_call | solution.py:265
  105.9 3.7 %all-to-all-start.3 = ((bf16[16,304,128]{2,1,0:T(8,128)(2,1)}), bf16[16,304,128]{2,1,0:T(8,128)(2,1)S(1)}, u32[]{:S(2)}, u32[]{:S(2)}) async-start(bf16[16,304,128]{2,1,0:T(8,128)(2,1)} %shard_map.122), calls=%async_computation.3 | async-start | bytes 2490368 | tf_op jit(solution)/shard_map/all_to_all | solution.py:70
  109.7 0.7 fusion.47.listed_ref
  110.4 20.4 %all-to-all-done.3.arrived_ref = bf16[16,304,128]{2,1,0:T(8,128)(2,1)S(1)} async-done(((bf16[16,304,128]{2,1,0:T(8,128)(2,1)}), bf16[16,304,128]{2,1,0:T(8,128)(2,1)S(1)}, u32[]{:S(2)}, u32[]{:S(2)}) %all-to-all-start.3) | async-done | bytes 1245216 | tf_op jit(solution)/shard_map/all_to_all | solution.py:70
  130.8 0.5 shard_map.123
  131.3 2.0 %all-gather.1 = f32[560,128]{1,0:T(8,128)S(1)} all-gather(f32[280,128]{1,0:T(8,128)S(1)} %get-tuple-element.6), channel_id=3, replica_groups=mesh['z'=16,'core'=2,'tensor'=16] {'core'}, dimensions={0}, use_global_device_ids=true | all-gather | bytes 430080 | tf_op jit(solution)/shard_map/all_gather | solution.py:329
  133.4 0.9 shard_map.124
  134.3 11.9 %all_to_all.34 = bf16[16,32,256]{2,1,0:T(8,128)(2,1)S(1)} all-to-all(bf16[16,32,256]{2,1,0:T(8,128)(2,1)S(1)} %get-tuple-element.8), channel_id=1, replica_groups=mesh['z'=16,'core'=2,'tensor'=16] {'tensor'}, dimensions={0} | all-to-all | bytes 524288 | tf_op jit(solution)/shard_map/all_to_all | solution.py:70
  146.3 0.4 convolution_convert_fusion.2
  146.7 0.2 multiply_reduce_fusion.2
  147.0 0.1 multiply_convert_fusion
  147.1 0.2 fusion.75
  147.3 0.1 fusion.76
  147.5 0.5 multiply_reduce_fusion
  148.0 0.2 broadcast_select_fusion
  148.3 2.5 %collective-permute-start.1 = (f32[256,128]{0,1:T(8,128)S(1)}, f32[256,128]{0,1:T(8,128)S(1)}, u32[]{:S(2)}, u32[]{:S(2)}) collective-permute-start(f32[256,128]{0,1:T(8,128)S(1)} %get-tuple-element.32), channel_id=1, source_target_pairs={{0,1},{1,0},{2,3},{3,2},{4,5},{5,4},{6,7},{7,6},{8,9},{9,8},{10,11... | collective-permute-start | bytes 393224 | tf_op jit(solution)/shard_map/ppermute | solution.py:23
  150.9 0.2 multiply_reduce_fusion.3
  151.1 0.3 convolution_convert_fusion.1
  151.4 3.7 %collective-permute-done.1 = f32[256,128]{0,1:T(8,128)S(1)} collective-permute-done((f32[256,128]{0,1:T(8,128)S(1)}, f32[256,128]{0,1:T(8,128)S(1)}, u32[]{:S(2)}, u32[]{:S(2)}) %collective-permute-start.1) | collective-permute-done | bytes 131104 | tf_op jit(solution)/shard_map/ppermute | solution.py:23
  155.2 2.1 %convolution_convert_fusion = bf16[256,4096]{1,0:T(8,128)(2,1)} fusion(bf16[4096,256]{1,0:T(8,128)(2,1)S(1)} %copy-done.4, bf16[256,128]{0,1:T(8,128)(2,1)S(1)} %convolution_convert_fusion.1, bf16[256,128]{0,1:T(8,128)(2,1)S(1)} %add_convert_fusion), kind=kOutput, calls=%fused_computation | convolution fusion | flops 538181632 | bytes 4325376 | tf_op jit(solution)/shard_map/dot_general | solution.py:427
  157.3 4.5 %all-to-all-start.5 = ((bf16[16,16,4096]{2,1,0:T(8,128)(2,1)}), bf16[16,16,4096]{2,1,0:T(8,128)(2,1)}, u32[]{:S(2)}, u32[]{:S(2)}) async-start(bf16[16,16,4096]{2,1,0:T(8,128)(2,1)} %bitcast.14), calls=%async_computation.5 | async-start | bytes 4194304 | tf_op jit(solution)/shard_map/all_to_all | solution.py:70
  161.8 0.5 slice.43
  162.3 28.2 %all-to-all-done.5 = bf16[16,16,4096]{2,1,0:T(8,128)(2,1)} async-done(((bf16[16,16,4096]{2,1,0:T(8,128)(2,1)}), bf16[16,16,4096]{2,1,0:T(8,128)(2,1)}, u32[]{:S(2)}, u32[]{:S(2)}) %all-to-all-start.5) | async-done | bytes 2097184 | tf_op jit(solution)/shard_map/all_to_all | solution.py:70
  190.5 1.9 convert_reduce_fusion
  192.5 0.2 fusion.11
  192.7 1.0 fusion.1
  (119 shorter events, 1.0 us)
Async XLA Ops:
  0.6 54.5 %copy-start = (bf16[128,4096]{1,0:T(8,128)(2,1)S(1)}, bf16[128,4096]{1,0:T(8,128)(2,1)}, u32[]{:S(2)}) copy-start(bf16[128,4096]{1,0:T(8,128)(2,1)} %param.20) | copy-start | bytes 3145732
  1.8 0.6 copy-start.27
  5.0 7.3 %copy-start.42 = (s32[1,32]{1,0:T(1,128)S(1)}, s32[1,32]{1,0:T(1,128)}, u32[]{:S(2)}) copy-start(s32[1,32]{1,0:T(1,128)} %param.12) | copy-start | bytes 388
  5.0 7.7 %copy-start.25 = (f32[128]{0:T(128)S(1)}, f32[128]{0:T(128)}, u32[]{:S(2)}) copy-start(f32[128]{0:T(128)} %param.18) | copy-start | bytes 1540
  5.0 8.3 %copy-start.37 = (f32[128]{0:T(128)S(1)}, f32[128]{0:T(128)}, u32[]{:S(2)}) copy-start(f32[128]{0:T(128)} %param.19) | copy-start | bytes 1540
  5.0 11.0 %copy-start.5 = (bf16[16,4096]{1,0:T(8,128)(2,1)S(1)}, bf16[16,4096]{1,0:T(8,128)(2,1)}, u32[]{:S(2)}) copy-start(bf16[16,4096]{1,0:T(8,128)(2,1)} %param.11) | copy-start | bytes 393220
  5.0 38.9 %all-to-all-start = ((bf16[16,16,4096]{2,1,0:T(8,128)(2,1)}), bf16[16,16,4096]{2,1,0:T(8,128)(2,1)}, u32[]{:S(2)}, u32[]{:S(2)}) async-start(bf16[16,16,4096]{2,1,0:T(8,128)(2,1)} %broadcast_in_dim.25), calls=%async_computation | async-start | bytes 4194304 | tf_op jit(solution)/shard_map/all_to_all | solution.py:70
  12.5 3.4 %copy-start.33 = (s32[32]{0:T(128)}, s32[32]{0:T(128)S(1)}, u32[]{:S(2)}) copy-start(s32[32]{0:T(128)S(1)} %reduce) | copy-start | bytes 388
  12.6 2.6 %copy-start.43 = (s32[32]{0:T(128)}, s32[32]{0:T(128)S(1)}, u32[]{:S(2)}) copy-start(s32[32]{0:T(128)S(1)} %get-tuple-element.24) | copy-start | bytes 388
  15.2 0.8 copy-start.40
  15.2 31.3 %copy-start.29 = (s32[32]{0:T(128)}, s32[32]{0:T(128)S(1)}, u32[]{:S(2)}) copy-start(s32[32]{0:T(128)S(1)} %broadcast_add_fusion) | copy-start | bytes 388
  19.9 26.6 %copy-start.3 = (bf16[4096,256]{1,0:T(8,128)(2,1)}, bf16[4096,256]{1,0:T(8,128)(2,1)S(1)}, u32[]{:S(2)}) copy-start(bf16[4096,256]{1,0:T(8,128)(2,1)S(1)} %constant_dynamic-update-slice_fusion) | copy-start | bytes 6291460
  43.9 9.9 %copy-start.38 = (f32[128]{0:T(128)S(1)}, f32[128]{0:T(128)}, u32[]{:S(2)}) copy-start(f32[128]{0:T(128)} %param.19) | copy-start | bytes 1540
  43.9 10.0 %copy-start.8 = (f32[256,64]{0,1:T(8,128)S(1)}, f32[256,64]{0,1:T(8,128)}, u32[]{:S(2)}) copy-start(f32[256,64]{0,1:T(8,128)} %broadcast_multiply_fusion) | copy-start | bytes 196612
  43.9 10.5 %copy-start.34 = (s32[32]{0:T(128)S(1)}, s32[32]{0:T(128)}, u32[]{:S(2)}) copy-start(s32[32]{0:T(128)} %copy-done.33) | copy-start | bytes 388
  43.9 10.5 %copy-start.44 = (s32[32]{0:T(128)S(1)}, s32[32]{0:T(128)}, u32[]{:S(2)}) copy-start(s32[32]{0:T(128)} %copy-done.43) | copy-start | bytes 388
  46.5 8.6 %copy-start.7 = (f32[32,4096]{1,0:T(8,128)S(1)}, f32[32,4096]{1,0:T(8,128)}, u32[]{:S(2)}) copy-start(f32[32,4096]{1,0:T(8,128)} %fusion.34) | copy-start | bytes 1572868
  46.9 6.9 %copy-start.12 = (f32[32,128]{1,0:T(8,128)}, f32[32,128]{1,0:T(8,128)S(1)}, u32[]{:S(2)}) copy-start(f32[32,128]{1,0:T(8,128)S(1)} %get-tuple-element.27) | copy-start | bytes 49156
  46.9 6.9 %collective-permute-start = (f32[256,128]{0,1:T(8,128)S(1)}, f32[256,128]{0,1:T(8,128)S(1)}, u32[]{:S(2)}, u32[]{:S(2)}) collective-permute-start(f32[256,128]{0,1:T(8,128)S(1)} %slice.44), channel_id=1, source_target_pairs={{0,1},{1,0},{2,3},{3,2},{4,5},{5,4},{6,7},{7,6},{8,9},{9,8},{10,11... | collective-permute-start | bytes 393224 | tf_op jit(solution)/shard_map/ppermute | solution.py:23
  48.8 0.6 copy-start.31
  49.0 4.8 %copy-start.19 = (f32[32,64]{1,0:T(8,128)}, f32[32,64]{1,0:T(8,128)S(1)}, u32[]{:S(2)}) copy-start(f32[32,64]{1,0:T(8,128)S(1)} %get-tuple-element.36) | copy-start | bytes 24580
  49.4 6.9 %copy-start.21 = (bf16[32,128]{1,0:T(8,128)(2,1)}, bf16[32,128]{1,0:T(8,128)(2,1)S(1)}, u32[]{:S(2)}) copy-start(bf16[32,128]{1,0:T(8,128)(2,1)S(1)} %fusion.37) | copy-start | bytes 24580
  53.9 6.7 %copy-start.24 = (s32[256,7]{0,1:T(8,128)S(1)}, s32[256,7]{0,1:T(8,128)}, u32[]{:S(2)}) copy-start(s32[256,7]{0,1:T(8,128)} %param.14) | copy-start | bytes 21508
  54.5 0.6 copy-start.16
  54.7 14.6 %copy-start.10 = (f32[32,256]{1,0:T(8,128)}, f32[32,256]{1,0:T(8,128)S(1)}, u32[]{:S(2)}) copy-start(f32[32,256]{1,0:T(8,128)S(1)} %get-tuple-element.29) | copy-start | bytes 98308
  54.8 14.6 %copy-start.35 = (f32[32]{0:T(128)}, f32[32]{0:T(128)S(1)}, u32[]{:S(2)}) copy-start(f32[32]{0:T(128)S(1)} %get-tuple-element.28) | copy-start | bytes 388
  54.8 29.9 %copy-start.14 = (bf16[256,128]{0,1:T(8,128)(2,1)}, bf16[256,128]{0,1:T(8,128)(2,1)S(1)}, u32[]{:S(2)}) copy-start(bf16[256,128]{0,1:T(8,128)(2,1)S(1)} %select_convert_fusion) | copy-start | bytes 196612
  55.1 29.6 %copy-start.45 = (s32[256]{0:T(256)S(1)}, s32[256]{0:T(256)}, u32[]{:S(2)}) copy-start(s32[256]{0:T(256)} %param.13) | copy-start | bytes 3076
  56.3 12.2 %all-to-all-start.1 = ((bf16[16,32,256]{2,1,0:T(8,128)(2,1)}), bf16[16,32,256]{2,1,0:T(8,128)(2,1)S(1)}, u32[]{:S(2)}, u32[]{:S(2)}) async-start(bf16[16,32,256]{2,1,0:T(8,128)(2,1)} %bitcast.49), calls=%async_computation.1 | async-start | bytes 524288 | tf_op jit(solution)/shard_map/all_to_all | solution.py:70
  69.4 31.8 %all-to-all-start.2 = ((bf16[16,32,256]{2,1,0:T(8,128)(2,1)}), bf16[16,32,256]{2,1,0:T(8,128)(2,1)S(1)}, u32[]{:S(2)}, u32[]{:S(2)}) async-start(bf16[16,32,256]{2,1,0:T(8,128)(2,1)} %broadcast_in_dim.30), calls=%async_computation.2 | async-start | bytes 524288 | tf_op jit(solution)/shard_map/all_to_all | solution.py:70
  84.6 25.1 %copy-start.23 = (s32[256,1]{0,1:T(1,128)}, s32[256,1]{0,1:T(1,128)S(1)}, u32[]{:S(2)}) copy-start(s32[256,1]{0,1:T(1,128)S(1)} %fusion.64) | copy-start | bytes 3076
  84.9 0.8 copy-start.1
  105.9 25.0 %all-to-all-start.3 = ((bf16[16,304,128]{2,1,0:T(8,128)(2,1)}), bf16[16,304,128]{2,1,0:T(8,128)(2,1)S(1)}, u32[]{:S(2)}, u32[]{:S(2)}) async-start(bf16[16,304,128]{2,1,0:T(8,128)(2,1)} %shard_map.122), calls=%async_computation.3 | async-start | bytes 2490368 | tf_op jit(solution)/shard_map/all_to_all | solution.py:70
  130.8 2.5 %copy-start.2 = (bf16[256,1024]{1,0:T(8,128)(2,1)S(1)}, bf16[256,1024]{1,0:T(8,128)(2,1)}, u32[]{:S(2)}) copy-start(bf16[256,1024]{1,0:T(8,128)(2,1)} %copy-done.1) | copy-start | bytes 1572868
  133.3 13.4 %copy-start.11 = (f32[32,256]{1,0:T(8,128)S(1)}, f32[32,256]{1,0:T(8,128)}, u32[]{:S(2)}) copy-start(f32[32,256]{1,0:T(8,128)} %copy-done.10) | copy-start | bytes 98308
  133.3 13.4 %copy-start.15 = (bf16[256,128]{0,1:T(8,128)(2,1)S(1)}, bf16[256,128]{0,1:T(8,128)(2,1)}, u32[]{:S(2)}) copy-start(bf16[256,128]{0,1:T(8,128)(2,1)} %copy-done.14) | copy-start | bytes 196612
  133.3 13.4 %copy-start.36 = (f32[32]{0:T(128)S(1)}, f32[32]{0:T(128)}, u32[]{:S(2)}) copy-start(f32[32]{0:T(128)} %copy-done.35) | copy-start | bytes 388
  133.3 13.7 %copy-start.22 = (bf16[32,128]{1,0:T(8,128)(2,1)S(1)}, bf16[32,128]{1,0:T(8,128)(2,1)}, u32[]{:S(2)}) copy-start(bf16[32,128]{1,0:T(8,128)(2,1)} %copy-done.21) | copy-start | bytes 24580
  133.3 14.0 %copy-start.17 = (bf16[256,128]{0,1:T(8,128)(2,1)S(1)}, bf16[256,128]{0,1:T(8,128)(2,1)}, u32[]{:S(2)}) copy-start(bf16[256,128]{0,1:T(8,128)(2,1)} %copy-done.16) | copy-start | bytes 196612
  133.4 14.1 %copy-start.9 = (f32[256,64]{0,1:T(8,128)S(1)}, f32[256,64]{0,1:T(8,128)}, u32[]{:S(2)}) copy-start(f32[256,64]{0,1:T(8,128)} %broadcast_multiply_fusion) | copy-start | bytes 196612
  133.4 14.1 %copy-start.39 = (f32[128]{0:T(128)S(1)}, f32[128]{0:T(128)}, u32[]{:S(2)}) copy-start(f32[128]{0:T(128)} %param.19) | copy-start | bytes 1540
  134.3 16.5 %copy-start.13 = (f32[32,128]{1,0:T(8,128)S(1)}, f32[32,128]{1,0:T(8,128)}, u32[]{:S(2)}) copy-start(f32[32,128]{1,0:T(8,128)} %copy-done.12) | copy-start | bytes 49156
  134.3 16.5 %copy-start.20 = (f32[32,64]{1,0:T(8,128)S(1)}, f32[32,64]{1,0:T(8,128)}, u32[]{:S(2)}) copy-start(f32[32,64]{1,0:T(8,128)} %copy-done.19) | copy-start | bytes 24580
  134.3 16.5 %copy-start.26 = (f32[128]{0:T(128)S(1)}, f32[128]{0:T(128)}, u32[]{:S(2)}) copy-start(f32[128]{0:T(128)} %param.18) | copy-start | bytes 1540
  134.3 16.5 %copy-start.32 = (f32[32]{0:T(128)S(1)}, f32[32]{0:T(128)}, u32[]{:S(2)}) copy-start(f32[32]{0:T(128)} %copy-done.31) | copy-start | bytes 388
  146.2 4.9 %copy-start.30 = (s32[32]{0:T(128)S(1)}, s32[32]{0:T(128)}, u32[]{:S(2)}) copy-start(s32[32]{0:T(128)} %copy-done.29) | copy-start | bytes 388
  146.2 8.9 %copy-start.4 = (bf16[4096,256]{1,0:T(8,128)(2,1)S(1)}, bf16[4096,256]{1,0:T(8,128)(2,1)}, u32[]{:S(2)}) copy-start(bf16[4096,256]{1,0:T(8,128)(2,1)} %copy-done.3) | copy-start | bytes 6291460
  148.3 6.9 %collective-permute-start.1 = (f32[256,128]{0,1:T(8,128)S(1)}, f32[256,128]{0,1:T(8,128)S(1)}, u32[]{:S(2)}, u32[]{:S(2)}) collective-permute-start(f32[256,128]{0,1:T(8,128)S(1)} %get-tuple-element.32), channel_id=1, source_target_pairs={{0,1},{1,0},{2,3},{3,2},{4,5},{5,4},{6,7},{7,6},{8,9},{9,8},{10,11... | collective-permute-start | bytes 393224 | tf_op jit(solution)/shard_map/ppermute | solution.py:23
  157.3 33.2 %all-to-all-start.5 = ((bf16[16,16,4096]{2,1,0:T(8,128)(2,1)}), bf16[16,16,4096]{2,1,0:T(8,128)(2,1)}, u32[]{:S(2)}, u32[]{:S(2)}) async-start(bf16[16,16,4096]{2,1,0:T(8,128)(2,1)} %bitcast.14), calls=%async_computation.5 | async-start | bytes 4194304 | tf_op jit(solution)/shard_map/all_to_all | solution.py:70
  161.7 30.7 %copy-start.6 = (bf16[16,4096]{1,0:T(8,128)(2,1)S(1)}, bf16[16,4096]{1,0:T(8,128)(2,1)}, u32[]{:S(2)}) copy-start(bf16[16,4096]{1,0:T(8,128)(2,1)} %param.11) | copy-start | bytes 393220
  161.8 30.7 %copy-start.18 = (f32[4096]{0:T(1024)S(1)}, f32[4096]{0:T(1024)}, u32[]{:S(2)}) copy-start(f32[4096]{0:T(1024)} %param.15) | copy-start | bytes 49156
  161.8 30.7 %copy-start.28 = (f32[16]{0:T(128)S(1)}, f32[16]{0:T(128)}, u32[]{:S(2)}) copy-start(f32[16]{0:T(128)} %copy-done.27) | copy-start | bytes 196
  161.8 30.9 %copy-start.41 = (s32[16]{0:T(128)S(1)}, s32[16]{0:T(128)}, u32[]{:S(2)}) copy-start(s32[16]{0:T(128)} %copy-done.40) | copy-start | bytes 196

commit v4 on v3

--- a/solution.py
+++ b/solution.py
@@ -33,12 +33,6 @@
     angles = position[:, None] * frequency[None, :]
     angles = jnp.concatenate([angles, angles], axis=-1)
     return (jnp.cos(angles), jnp.sin(angles))
-
-
-def rotate(tensor, cosine, sine):
-    halfway = tensor.shape[-1] // 2
-    turned = jnp.concatenate([-tensor[..., halfway:], tensor[..., :halfway]], axis=-1)
-    return tensor * cosine + turned * sine
 
 
 def segment_layout(lengths_row, total_tokens):
@@ -51,28 +45,13 @@
     return (inside, position, seq_ends - 1)
 
 
-def head_forward(raw, gain, cosine, sine):
-    inverse = rms_scale(raw)
-    unit_form = raw * inverse
-    return (unit_form, inverse, rotate(unit_form * gain, cosine, sine))
-
-
 def norm_backward(grad, unit_form, inverse, gain):
     scaled = grad * gain
     return inverse * (scaled - unit_form * jnp.mean(unit_form * scaled, axis=-1, keepdims=True))
 
 
-def head_backward(grad_rot, unit_form, inverse, gain, cosine, sine):
-    return norm_backward(rotate(grad_rot, cosine, -sine), unit_form, inverse, gain)
-
-
 def exchange(blocks, axis):
     return lax.all_to_all(blocks, axis, 0, 0, tiled=True)
-
-
-def gather_rows(rows, axis):
-    count = lax.axis_size(axis)
-    return exchange(jnp.broadcast_to(rows[None], (count,) + rows.shape), axis)
 
 
 def halves(value):
@@ -268,7 +247,7 @@
         in_specs=specs,
         out_specs=[pl.BlockSpec(memory_space=pltpu.VMEM)] * len(outs),
         scratch_shapes=list(scratch),
-        compiler_params=pltpu.CompilerParams(vmem_limit_bytes=40 * 2**20),
+        compiler_params=pltpu.CompilerParams(vmem_limit_bytes=24 * 2**20),
     )(*arrays)
 
 
@@ -348,94 +327,300 @@
     return loss[0, 0], exchange(d_resid16, "tensor")
 
 
+def copied_norm_kernel(hidden_ref, gain_ref, out_ref):
+    hidden32 = hidden_ref[...].astype(jnp.float32)
+    normed = (hidden32 * rms_scale(hidden32) * gain_ref[...]).astype(jnp.bfloat16)
+    for t in range(out_ref.shape[0]):
+        out_ref[t] = normed
+
+
+def projection_kernel(rows_ref, weights_ref, chosen_ref, kv_ref, query_ref):
+    width = kv_ref.shape[1]
+    projected = jnp.dot(rows_ref[...], weights_ref[...], preferred_element_type=jnp.float32)
+    kv_ref[...] = projected[:, :width]
+    query_ref[...] = jnp.dot(
+        chosen_ref[...].astype(jnp.float32),
+        projected[:, width:],
+        precision=lax.Precision.HIGHEST,
+        preferred_element_type=jnp.float32,
+    )
+
+
+def half_turned(tensor, cosine, signed_sine):
+    halfway = tensor.shape[1] // 2
+    return tensor * cosine + pltpu.roll(tensor, halfway, 1) * signed_sine
+
+
+def attention_kernel(
+    even_ref,
+    own_ref,
+    other_ref,
+    query_raw_ref,
+    key_turn_ref,
+    query_turn_ref,
+    gains_ref,
+    inside_ref,
+    own_last_ref,
+    hidden_ref,
+    wo_ref,
+    out_ref,
+    key_raw_ref,
+    key_ref,
+    value_ref,
+    query_ref,
+    probs_ref,
+):
+    root = math.sqrt(own_ref.shape[1])
+    is_even = even_ref[0] == 1
+    own, other = own_ref[...], other_ref[...]
+    key_raw = jnp.where(is_even, own, other)
+    value16 = jnp.where(is_even, other, own).astype(jnp.bfloat16)
+    query_raw = query_raw_ref[...]
+    q_gain, k_gain = gains_ref[0:1, :], gains_ref[1:2, :]
+    key16 = half_turned(
+        key_raw * rms_scale(key_raw) * k_gain, key_turn_ref[0], key_turn_ref[1]
+    ).astype(jnp.bfloat16)
+    query16 = half_turned(
+        query_raw * rms_scale(query_raw) * q_gain, query_turn_ref[0], query_turn_ref[1]
+    ).astype(jnp.bfloat16)
+    shift = (
+        root
+        * jnp.max(q_gain, axis=1, keepdims=True)
+        * jnp.max(k_gain, axis=1, keepdims=True)
+    )
+    scores = (
+        lax.dot_general(
+            query16, key16, (((1,), (1,)), ((), ())), preferred_element_type=jnp.float32
+        )
+        / root
+    )
+    weights = jnp.where(inside_ref[...] > 0.0, jnp.exp(scores - shift), 0.0)
+    probs = weights / jnp.sum(weights, axis=1, keepdims=True)
+    attn16 = jnp.dot(
+        probs.astype(jnp.bfloat16), value16, preferred_element_type=jnp.float32
+    ).astype(jnp.bfloat16)
+    chunk = out_ref.shape[2]
+    for t in range(out_ref.shape[0]):
+        columns = slice(t * chunk, (t + 1) * chunk)
+        block = jnp.dot(attn16, wo_ref[:, columns], preferred_element_type=jnp.float32)
+        block = block + jnp.dot(
+            own_last_ref[...], hidden_ref[:, columns], preferred_element_type=jnp.float32
+        )
+        out_ref[t] = block.astype(jnp.bfloat16)
+    key_raw_ref[...] = key_raw
+    key_ref[...] = key16
+    value_ref[...] = value16
+    query_ref[...] = query16
+    probs_ref[...] = probs
+
+
+def resid_kernel(arrived_ref, gain_ref, weights_ref, resid_ref, out_ref, weights_out_ref):
+    resid = arrived_ref[0].astype(jnp.float32)
+    for t in range(1, arrived_ref.shape[0]):
+        resid = resid + arrived_ref[t].astype(jnp.float32)
+    resid_ref[...] = resid
+    scaled16 = (resid * gain_ref[...]).astype(jnp.bfloat16)
+    for t in range(out_ref.shape[0]):
+        out_ref[t] = scaled16
+    weights_out_ref[...] = weights_ref[...]
+
+
+def gradient_kernel(
+    even_ref,
+    d_resid_ref,
+    wo_t_ref,
+    key_raw_ref,
+    query_raw_ref,
+    key_ref,
+    value_ref,
+    query_ref,
+    probs_ref,
+    key_turn_ref,
+    query_turn_ref,
+    gains_ref,
+    chosen_ref,
+    own_weights_ref,
+    other_weights_ref,
+    query_weights_ref,
+    out_ref,
+):
+    root = math.sqrt(key_ref.shape[1])
+    is_even = even_ref[0] == 1
+    q_gain, k_gain = gains_ref[0:1, :], gains_ref[1:2, :]
+    chunk = d_resid_ref.shape[2]
+    d_attn = jnp.dot(d_resid_ref[0], wo_t_ref[:chunk, :], preferred_element_type=jnp.float32)
+    for t in range(1, d_resid_ref.shape[0]):
+        d_attn = d_attn + jnp.dot(
+            d_resid_ref[t],
+            wo_t_ref[t * chunk : (t + 1) * chunk, :],
+            preferred_element_type=jnp.float32,
+        )
+    d_attn16 = d_attn.astype(jnp.bfloat16)
+    probs = probs_ref[...]
+    key16, query16 = key_ref[...], query_ref[...]
+    d_probs = lax.dot_general(
+        d_attn16, value_ref[...], (((1,), (1,)), ((), ())), preferred_element_type=jnp.float32
+    )
+    d_scores16 = (
+        probs * (d_probs - jnp.sum(probs * d_probs, axis=1, keepdims=True)) / root
+    ).astype(jnp.bfloat16)
+    down = (((0,), (0,)), ((), ()))
+    d_query_rot = jnp.dot(d_scores16, key16, preferred_element_type=jnp.float32)
+    d_key_rot = lax.dot_general(d_scores16, query16, down, preferred_element_type=jnp.float32)
+    d_value = lax.dot_general(
+        probs.astype(jnp.bfloat16), d_attn16, down, preferred_element_type=jnp.float32
+    )
+
+    def head_gradient(grad_rot, raw, gain, turn_ref):
+        inverse = rms_scale(raw)
+        turned_back = half_turned(grad_rot, turn_ref[0], -turn_ref[1])
+        return norm_backward(turned_back, raw * inverse, inverse, gain)
+
+    d_key = head_gradient(d_key_rot, key_raw_ref[...], k_gain, key_turn_ref)
+    d_query = head_gradient(d_query_rot, query_raw_ref[...], q_gain, query_turn_ref)
+    own16 = jnp.where(is_even, d_key, d_value).astype(jnp.bfloat16)
+    other16 = jnp.where(is_even, d_value, d_key).astype(jnp.bfloat16)
+    spread16 = lax.dot_general(
+        chosen_ref[...], d_query.astype(jnp.bfloat16), down, preferred_element_type=jnp.float32
+    ).astype(jnp.bfloat16)
+    for t in range(out_ref.shape[1] // chunk):
+        columns = slice(t * chunk, (t + 1) * chunk)
+        term = jnp.dot(own16, own_weights_ref[:, columns], preferred_element_type=jnp.float32)
+        term = term + jnp.dot(
+            other16, other_weights_ref[:, columns], preferred_element_type=jnp.float32
+        )
+        term = term + jnp.dot(
+            spread16, query_weights_ref[:, columns], preferred_element_type=jnp.float32
+        )
+        out_ref[:, columns] = term.astype(jnp.bfloat16)
+
+
+def d_hidden_kernel(terms_ref, hidden_ref, gain_ref, last_ref, d_resid_ref, out_ref):
+    d_normed = terms_ref[0].astype(jnp.float32)
+    for t in range(1, terms_ref.shape[0]):
+        d_normed = d_normed + terms_ref[t].astype(jnp.float32)
+    hidden32 = hidden_ref[...].astype(jnp.float32)
+    inverse = rms_scale(hidden32)
+    d_hidden = norm_backward(d_normed, hidden32 * inverse, inverse, gain_ref[...])
+    last = last_ref[...]
+    chunk = d_resid_ref.shape[2]
+    for t in range(d_resid_ref.shape[0]):
+        columns = slice(t * chunk, (t + 1) * chunk)
+        added = jnp.dot(last, d_resid_ref[t], preferred_element_type=jnp.float32)
+        out_ref[:, columns] = (d_hidden[:, columns] + added).astype(jnp.bfloat16)
+
+
+def turn_tables(position, head_width):
+    cosine, sine = rope_tables(position, head_width)
+    sign = jnp.where(jnp.arange(head_width) < head_width // 2, -1.0, 1.0)
+    return jnp.stack([cosine, sine * sign])
+
+
 def on_device(
     hidden, lengths, positives, negatives, in_gain, wq, wkv, q_gain, k_gain, wo, out_gain
 ):
-    tensor_count = lax.axis_size("tensor")
-    tensor_index = lax.axis_index("tensor")
+    tensor_count, core_count = lax.axis_size("tensor"), lax.axis_size("core")
+    tensor_index, core = lax.axis_index("tensor"), lax.axis_index("core")
+    z_count = lax.axis_size("z")
+    group = lax.axis_index("z") * core_count + core
     own_rows, features = hidden.shape
     tokens_count = own_rows * tensor_count
     head_width = wq.shape[1]
     sequences = lengths.shape[1]
     chunk = features // tensor_count
-    root = math.sqrt(head_width)
-    is_even = tensor_index % 2 == 0
-    hidden32 = hidden.astype(jnp.float32)
-    inverse_in = rms_scale(hidden32)
-    normed = (hidden32 * inverse_in * in_gain).astype(jnp.bfloat16)
-    core_count = lax.axis_size("core")
-    core = lax.axis_index("core")
-    group = lax.axis_index("z") * core_count + core
-    tables = candidate_tables(positives, negatives, core, group, sequences, core_count)
-    piece = gather_rows(normed, "tensor").reshape(tokens_count, features)
+    f32, bf16 = jnp.float32, jnp.bfloat16
+    is_even = (1 - tensor_index % 2).astype(jnp.int32)[None]
+    input_gain = in_gain[None, :]
+
+    (copies,) = kernel_call(
+        copied_norm_kernel, [((tensor_count, own_rows, features), bf16)], [hidden, input_gain]
+    )
+    piece = exchange(copies, "tensor").reshape(tokens_count, features)
+
     own_index = tensor_index * own_rows + jnp.arange(own_rows, dtype=jnp.int32)
     inside, position, last = segment_layout(lengths[0], tokens_count)
-    own_last = (last[:, None] == own_index[None, :]).astype(jnp.bfloat16)
+    own_last = (last[:, None] == own_index[None, :]).astype(bf16)
     token_index = jnp.arange(tokens_count, dtype=jnp.int32)
-    chosen = (last[:, None] == token_index[None, :]).astype(jnp.bfloat16)
-    weights = jnp.concatenate([wkv, wq], axis=1)
-    projected = jnp.dot(piece, weights, preferred_element_type=jnp.float32)
-    kv_own = projected[:, :head_width]
+    chosen = (last[:, None] == token_index[None, :]).astype(bf16)
+    key_turn = turn_tables(position, head_width)
+    query_turn = turn_tables((lengths[0] - 1).astype(f32), head_width)
+    gains = jnp.stack([q_gain, k_gain])
+    tables = candidate_tables(positives, negatives, core, group, sequences, core_count)
+    own_gain = lax.dynamic_slice_in_dim(out_gain, tensor_index * chunk, chunk)
+
+    kv_own, query_raw = kernel_call(
+        projection_kernel,
+        [((tokens_count, head_width), f32), ((sequences, head_width), f32)],
+        [piece, jnp.concatenate([wkv, wq], axis=1), chosen],
+    )
     kv_other = swapped(kv_own, "tensor", 0)
-    query_raw = jnp.dot(
-        chosen.astype(jnp.float32), projected[:, head_width:], precision=lax.Precision.HIGHEST
-    )
-    key_raw = jnp.where(is_even, kv_own, kv_other)
-    value16 = jnp.where(is_even, kv_other, kv_own).astype(jnp.bfloat16)
-    cos_key, sin_key = rope_tables(position, head_width)
-    key_unit, key_inverse, key_rot = head_forward(key_raw, k_gain, cos_key, sin_key)
-    key16 = key_rot.astype(jnp.bfloat16)
-    cos_query, sin_query = rope_tables((lengths[0] - 1).astype(jnp.float32), head_width)
-    query_unit, query_inverse, query_rot = head_forward(query_raw, q_gain, cos_query, sin_query)
-    query16 = query_rot.astype(jnp.bfloat16)
-    shift = root * jnp.max(q_gain) * jnp.max(k_gain)
-    scores = jnp.dot(query16, key16.T, preferred_element_type=jnp.float32) / root
-    weight_params = jnp.where(inside.T, jnp.exp(scores - shift), 0.0)
-    probs = weight_params / jnp.sum(weight_params, axis=-1, keepdims=True)
-    probs16 = probs.astype(jnp.bfloat16)
-    attn16 = jnp.dot(probs16, value16, preferred_element_type=jnp.float32).astype(jnp.bfloat16)
-    partial_rows = jnp.dot(attn16, wo, preferred_element_type=jnp.float32) + jnp.dot(
-        own_last, hidden, preferred_element_type=jnp.float32
-    )
-    blocks = partial_rows.astype(jnp.bfloat16).reshape(sequences, tensor_count, chunk)
-    arrived = exchange(blocks.transpose(1, 0, 2), "tensor")
-    resid = jnp.sum(arrived.astype(jnp.float32), axis=0)
-    own_gain = lax.dynamic_slice_in_dim(out_gain, tensor_index * chunk, chunk)
-    scaled = resid * own_gain
-    same_core = gather_rows(scaled.astype(jnp.bfloat16), "z")
-    everyone = lax.all_gather(same_core, "core", axis=1)
+    blocks, key_raw, key16, value16, query16, probs = kernel_call(
+        attention_kernel,
+        [
+            ((tensor_count, sequences, chunk), bf16),
+            ((tokens_count, head_width), f32),
+            ((tokens_count, head_width), bf16),
+            ((tokens_count, head_width), bf16),
+            ((sequences, head_width), bf16),
+            ((sequences, tokens_count), f32),
+        ],
+        [
+            is_even,
+            kv_own,
+            kv_other,
+            query_raw,
+            key_turn,
+            query_turn,
+            gains,
+            inside.T.astype(f32),
+            own_last,
+            hidden,
+            wo,
+        ],
+        scalars=1,
+    )
+    resid, scaled, own_weights = kernel_call(
+        resid_kernel,
+        [
+            ((sequences, chunk), f32),
+            ((z_count, sequences, chunk), bf16),
+            ((head_width, features), bf16),
+        ],
+        [exchange(blocks, "tensor"), own_gain[None, :], wkv.T],
+    )
+    other_weights = swapped(own_weights, "tensor", 0)
+    everyone = lax.all_gather(exchange(scaled, "z"), "core", axis=1)
     loss, d_resid16 = contrast(everyone, resid, own_gain, tables, group)
-    d_resid16 = d_resid16.transpose(1, 0, 2).reshape(sequences, features)
-    d_attn16 = jnp.dot(d_resid16, wo.T, preferred_element_type=jnp.float32).astype(jnp.bfloat16)
-    d_probs = jnp.dot(d_attn16, value16.T, preferred_element_type=jnp.float32)
-    d_scores16 = (
-        probs * (d_probs - jnp.sum(probs * d_probs, axis=-1, keepdims=True)) / root
-    ).astype(jnp.bfloat16)
-    d_query_rot = jnp.dot(d_scores16, key16, preferred_element_type=jnp.float32)
-    d_key_rot = jnp.dot(d_scores16.T, query16, preferred_element_type=jnp.float32)
-    d_value = jnp.dot(probs16.T, d_attn16, preferred_element_type=jnp.float32)
-    d_key_raw = head_backward(d_key_rot, key_unit, key_inverse, k_gain, cos_key, sin_key)
-    d_query_raw = head_backward(
-        d_query_rot, query_unit, query_inverse, q_gain, cos_query, sin_query
-    )
-    mine = jnp.where(is_even, d_key_raw, d_value)
-    theirs = jnp.where(is_even, d_value, d_key_raw)
-    column16 = (mine + swapped(theirs, "tensor", 0)).astype(jnp.bfloat16)
-    spread16 = jnp.dot(
-        chosen.T, d_query_raw.astype(jnp.bfloat16), preferred_element_type=jnp.float32
-    ).astype(jnp.bfloat16)
-    product = jnp.dot(
-        jnp.concatenate([column16, spread16], axis=1),
-        weights.T,
-        preferred_element_type=jnp.float32,
-    )
-    terms = exchange(product.astype(jnp.bfloat16), "tensor")
-    d_normed = jnp.sum(
-        terms.reshape(tensor_count, own_rows, features).astype(jnp.float32), axis=0
-    )
-    d_hidden = norm_backward(d_normed, hidden32 * inverse_in, inverse_in, in_gain)
-    d_hidden = d_hidden + jnp.dot(own_last.T, d_resid16, preferred_element_type=jnp.float32)
-    return (d_hidden.astype(jnp.bfloat16), loss)
+    (product,) = kernel_call(
+        gradient_kernel,
+        [((tokens_count, features), bf16)],
+        [
+            is_even,
+            d_resid16,
+            wo.T,
+            key_raw,
+            query_raw,
+            key16,
+            value16,
+            query16,
+            probs,
+            key_turn,
+            query_turn,
+            gains,
+            chosen,
+            own_weights,
+            other_weights,
+            wq.T,
+        ],
+        scalars=1,
+    )
+    terms = exchange(product, "tensor").reshape(tensor_count, own_rows, features)
+    (d_hidden,) = kernel_call(
+        d_hidden_kernel,
+        [((own_rows, features), bf16)],
+        [terms, hidden, input_gain, own_last.T, d_resid16],
+    )
+    return (d_hidden, loss)
 
 
 def solution(mesh):

time: 195 us -> 210 us (1.077)
  local copies, waits for them, and re-layouts: 9.55 us -> 24.1 us
  blocking collectives: 16 us -> 4.18 us
  Pallas kernels: 3.92 us -> 15.7 us
  matrix products: 9.26 us -> 0 us
  waiting for transfers between devices: 104 us -> 112 us
  starting transfers between devices: 38.5 us -> 43.4 us
    unnamed x94 -> x100, local copies, waits for them, and re-layouts: 3.59 us -> 22.1 us
    all_to_all x1 -> x0, blocking collectives: 11.9 us -> none  [exchange(): return lax.all_to_all(blocks, axis, 0, 0, tiled=True)]
    pallas_call x3 -> x9, Pallas kernels: 3.92 us -> 15.7 us  [kernel_call(): pl.pallas_call(body, out_shape=[jax.ShapeDtypeStruct(shape, dtype) for sh...]
    dot_general x13 -> x0, matrix products: 9.26 us -> none  [the longest x1 2.55 us: on_device(): projected = jnp.dot(piece, weights, preferred_element_type=jnp.float32)]
    all_to_all x5 -> x6, waiting for transfers between devices: 95.9 us -> 101 us  [exchange(): return lax.all_to_all(blocks, axis, 0, 0, tiled=True)]
    reduce_sum x7 -> x0, other arithmetic: 4.13 us -> none  [the longest x1 1.92 us: on_device(): jnp.sum(terms.reshape(tensor_count, own_rows, features).astype(jnp.float3...]
    all_to_all x5 -> x6, starting transfers between devices: 34.1 us -> 37.8 us  [exchange(): return lax.all_to_all(blocks, axis, 0, 0, tiled=True)]
    concatenate x0 -> x3, other arithmetic: none -> 3 us  [the longest x1 2.83 us: on_device(): jnp.concatenate([wkv, wq], axis=1)]
  transfers between devices with their start and end apart: 7 -> 8, of which waited for: 7 -> 8; matrix products, arithmetic and copies ran while one was open for 5% -> 7% of each run, Pallas kernels for 0% -> 1%
where the time goes in v4:
time: 210 us; the launch traced here: 208 us
  waiting for transfers between devices  112 us (53%)
  starting transfers between devices  43.4 us (21%)
  local copies, waits for them, and re-layouts  24.1 us (11%)
  Pallas kernels  15.7 us (7%)
  other arithmetic  7.8 us (4%)
  blocking collectives  4.18 us (2%)
    all_to_all x6, waiting for transfers between devices, exchange(): return lax.all_to_all(blocks, axis, 0, 0, tiled=True)  101 us
    all_to_all x6, starting transfers between devices, exchange(): return lax.all_to_all(blocks, axis, 0, 0, tiled=True)  37.8 us
    unnamed x100, local copies, waits for them, and re-layouts  22.1 us
    pallas_call x9, Pallas kernels, kernel_call(): pl.pallas_call(body, out_shape=[jax.ShapeDtypeStruct(shape, dtype) for sh...  15.7 us
    ppermute x2, waiting for transfers between devices, swapped(): return lax.ppermute(value, axis, pairs)  10.4 us
    ppermute x2, starting transfers between devices, swapped(): return lax.ppermute(value, axis, pairs)  5.62 us
  transfers between devices with their start and end apart: 8, of which 8 were waited for; matrix products, arithmetic and copies ran while one was open for 7% of the time, Pallas kernels for 1%

profile of v4, /device:TPU:32, one launch (start us, length us, event | category | flops | bytes accessed | tf_op | source)
XLA Modules:
  0.0 208.0 jit_solution(5479932598691392652)
XLA Ops:
  0.6 0.9 copy-done.7
  1.5 0.7 copy-done.19
  2.3 0.3 shard_map.122
  2.5 1.3 copy-done
  3.9 7.2 %all-to-all-start = ((bf16[16,16,4096]{2,1,0:T(8,128)(2,1)}), bf16[16,16,4096]{2,1,0:T(8,128)(2,1)S(1)}, u32[]{:S(2)}, u32[]{:S(2)}) async-start(bf16[16,16,4096]{2,1,0:T(8,128)(2,1)} %copy-done), calls=%async_computation | async-start | bytes 4194304 | tf_op jit(solution)/shard_map/all_to_all | solution.py:54
  11.3 0.1 reduce
  11.6 0.1 fusion.7
  11.8 0.7 compare_convert_fusion.own_last_ref
  12.7 1.3 fusion.2
  14.0 2.8 %pad_maximum_fusion.weights_ref = bf16[4096,256]{1,0:T(8,128)(2,1)} fusion(bf16[4096,128]{1,0:T(8,128)(2,1)} %param.16, bf16[4096,128]{1,0:T(8,128)(2,1)S(1)} %copy-done.36), kind=kLoop, calls=%fused_computation | loop fusion | flops 4194304 | bytes 4194304 | tf_op jit(solution)/shard_map/concatenate | solution.py:554
  16.8 25.9 %all-to-all-done = bf16[16,16,4096]{2,1,0:T(8,128)(2,1)S(1)} async-done(((bf16[16,16,4096]{2,1,0:T(8,128)(2,1)}), bf16[16,16,4096]{2,1,0:T(8,128)(2,1)S(1)}, u32[]{:S(2)}, u32[]{:S(2)}) %all-to-all-start) | async-done | bytes 2097184 | tf_op jit(solution)/shard_map/all_to_all | solution.py:54
  42.7 1.6 copy-done.1
  44.3 1.0 shard_map.123
  45.3 1.9 collective-permute-start
  47.3 1.0 pad_maximum_fusion.1.key_turn_ref
  48.3 3.9 %collective-permute-done.other_ref = f32[256,128]{1,0:T(8,128)S(1)} collective-permute-done((f32[256,128]{1,0:T(8,128)S(1)}, f32[256,128]{1,0:T(8,128)S(1)}, u32[]{:S(2)}, u32[]{:S(2)}) %collective-permute-start) | collective-permute-done | bytes 131104 | tf_op jit(solution)/shard_map/ppermute | solution.py:23
  52.2 0.7 copy-done.22
  52.9 0.7 copy-done.28
  53.6 1.6 shard_map.124
  55.2 0.7 copy-done.5
  55.9 0.7 copy-done.13
  56.5 0.6 copy-done.15
  57.2 0.6 copy-done.24
  57.8 0.6 copy-done.33
  58.4 3.6 %all-to-all-start.1 = ((bf16[16,32,256]{2,1,0:T(8,128)(2,1)}), bf16[16,32,256]{2,1,0:T(8,128)(2,1)S(1)}, u32[]{:S(2)}, u32[]{:S(2)}) async-start(bf16[16,32,256]{2,1,0:T(8,128)(2,1)} %get-tuple-element.19), calls=%async_computation.1 | async-start | bytes 524288 | tf_op jit(solution)/shard_map/all_to_all | solution.py:54
  61.9 1.5 copy.43
  63.4 0.8 dynamic_slice.12
  64.2 6.4 %all-to-all-done.1.arrived_ref = bf16[16,32,256]{2,1,0:T(8,128)(2,1)S(1)} async-done(((bf16[16,32,256]{2,1,0:T(8,128)(2,1)}), bf16[16,32,256]{2,1,0:T(8,128)(2,1)S(1)}, u32[]{:S(2)}, u32[]{:S(2)}) %all-to-all-start.1) | async-done | bytes 262176 | tf_op jit(solution)/shard_map/all_to_all | solution.py:54
  70.6 0.8 shard_map.125
  71.4 1.0 copy-done.9
  72.4 0.6 copy-done.26
  73.0 15.2 %all-to-all-start.2 = ((bf16[16,32,256]{2,1,0:T(8,128)(2,1)}), bf16[16,32,256]{2,1,0:T(8,128)(2,1)S(1)}, u32[]{:S(2)}, u32[]{:S(2)}) async-start(bf16[16,32,256]{2,1,0:T(8,128)(2,1)} %get-tuple-element.20), calls=%async_computation.2 | async-start | bytes 524288 | tf_op jit(solution)/shard_map/all_to_all | solution.py:54
  88.4 0.2 fusion.query_hot_ref
  88.6 0.8 copy-done.3
  89.3 0.1 fusion.1.positive_hot_ref
  89.5 15.4 %all-to-all-done.2 = bf16[16,32,256]{2,1,0:T(8,128)(2,1)S(1)} async-done(((bf16[16,32,256]{2,1,0:T(8,128)(2,1)}), bf16[16,32,256]{2,1,0:T(8,128)(2,1)S(1)}, u32[]{:S(2)}, u32[]{:S(2)}) %all-to-all-start.2) | async-done | bytes 262176 | tf_op jit(solution)/shard_map/all_to_all | solution.py:54
  104.9 2.2 %all-gather = bf16[16,64,256]{2,1,0:T(8,128)(2,1)S(1)} all-gather(bf16[16,32,256]{2,1,0:T(8,128)(2,1)S(1)} %all-to-all-done.2), channel_id=2, replica_groups=mesh['z'=16,'core'=2,'tensor'=16] {'core'}, dimensions={1}, use_global_device_ids=true | all-gather | bytes 786432 | tf_op jit(solution)/shard_map/all_gather | solution.py:592
  107.0 2.6 %shard_map.126 = bf16[16,304,128]{2,1,0:T(8,128)(2,1)} custom-call(bf16[1024,256]{1,0:T(8,128)(2,1)S(1)} %bitcast.34, bf16[128,1024]{1,0:T(8,128)(2,1)S(1)} %constant_dynamic-slice_fusion.query_hot_ref, bf16[256,1024]{1,0:T(8,128)(2,1)S(1)} %fusion.1.positive_hot_ref, s32[8,128]{1,0:T(8,128)S(1)} %fusion.14.listed_ref, f32[1,256]{1,0:T(1,128)S(1)} %bitcast.43), custom_call_target="tpu_custom_call" | custom-call | tf_op jit(solution)/shard_map/pallas_call | solution.py:244
  109.6 3.8 %all-to-all-start.3 = ((bf16[16,304,128]{2,1,0:T(8,128)(2,1)}), bf16[16,304,128]{2,1,0:T(8,128)(2,1)S(1)}, u32[]{:S(2)}, u32[]{:S(2)}) async-start(bf16[16,304,128]{2,1,0:T(8,128)(2,1)} %shard_map.126), calls=%async_computation.3 | async-start | bytes 2490368 | tf_op jit(solution)/shard_map/all_to_all | solution.py:54
  113.4 3.7 %collective-permute-start.1 = (bf16[128,4096]{1,0:T(8,128)(2,1)}, bf16[128,4096]{1,0:T(8,128)(2,1)}, u32[]{:S(2)}, u32[]{:S(2)}) collective-permute-start(bf16[128,4096]{1,0:T(8,128)(2,1)} %copy-done.9), channel_id=1, source_target_pairs={{0,1},{1,0},{2,3},{3,2},{4,5},{5,4},{6,7},{7,6},{8,9},{9,8},{10,11... | collective-permute-start | bytes 3145736 | tf_op jit(solution)/shard_map/ppermute | solution.py:23
  117.3 0.7 fusion.11.listed_ref
  118.1 17.5 %all-to-all-done.3.arrived_ref = bf16[16,304,128]{2,1,0:T(8,128)(2,1)S(1)} async-done(((bf16[16,304,128]{2,1,0:T(8,128)(2,1)}), bf16[16,304,128]{2,1,0:T(8,128)(2,1)S(1)}, u32[]{:S(2)}, u32[]{:S(2)}) %all-to-all-start.3) | async-done | bytes 1245216 | tf_op jit(solution)/shard_map/all_to_all | solution.py:54
  135.6 0.5 shard_map.127
  136.0 2.0 all-gather.1
  138.0 1.6 shard_map.128
  139.7 0.6 copy-done.35
  140.3 4.2 %all-to-all-start.4 = ((bf16[16,32,256]{2,1,0:T(8,128)(2,1)}), bf16[16,32,256]{2,1,0:T(8,128)(2,1)}, u32[]{:S(2)}, u32[]{:S(2)}) async-start(bf16[16,32,256]{2,1,0:T(8,128)(2,1)} %get-tuple-element.24), calls=%async_computation.4 | async-start | bytes 524288 | tf_op jit(solution)/shard_map/all_to_all | solution.py:54
  144.5 0.7 copy.45
  145.2 1.5 copy.46
  146.7 6.5 %collective-permute-done.1.other_weights_ref = bf16[128,4096]{1,0:T(8,128)(2,1)} collective-permute-done((bf16[128,4096]{1,0:T(8,128)(2,1)}, bf16[128,4096]{1,0:T(8,128)(2,1)}, u32[]{:S(2)}, u32[]{:S(2)}) %collective-permute-start.1) | collective-permute-done | bytes 1048608 | tf_op jit(solution)/shard_map/ppermute | solution.py:23
  153.2 6.9 %all-to-all-done.4.d_resid_ref = bf16[16,32,256]{2,1,0:T(8,128)(2,1)} async-done(((bf16[16,32,256]{2,1,0:T(8,128)(2,1)}), bf16[16,32,256]{2,1,0:T(8,128)(2,1)}, u32[]{:S(2)}, u32[]{:S(2)}) %all-to-all-start.4) | async-done | bytes 262176 | tf_op jit(solution)/shard_map/all_to_all | solution.py:54
  160.1 0.8 copy-done.12
  160.9 0.9 copy-done.14
  161.8 0.8 copy-done.16
  162.6 0.8 copy-done.18
  163.5 0.7 copy-done.23
  164.2 0.8 copy-done.25
  165.0 0.6 copy-done.32
  165.6 0.7 copy-done.34
  166.3 5.3 %shard_map.129 = bf16[256,4096]{1,0:T(8,128)(2,1)} custom-call(s32[1]{0:T(128)} %bitcast.even_ref, bf16[16,32,256]{2,1,0:T(8,128)(2,1)} %all-to-all-done.4.d_resid_ref, bf16[4096,128]{1,0:T(8,128)(2,1)S(1)} %bitcast.36, f32[256,128]{1,0:T(8,128)S(1)} %copy-done.14, f32[32,128]{1,0:T(8,128)S(1)} %copy-done.23, bf16[256,128]{1,0:T(8,128)(2,1)S(1)} %copy-done.16, ...), custom_call_target="tpu_custom_call" | custom-call | tf_op jit(solution)/shard_map/pallas_call | solution.py:244
  171.6 3.8 %all-to-all-start.5 = ((bf16[16,16,4096]{2,1,0:T(8,128)(2,1)}), bf16[16,16,4096]{2,1,0:T(8,128)(2,1)S(1)}, u32[]{:S(2)}, u32[]{:S(2)}) async-start(bf16[16,16,4096]{2,1,0:T(8,128)(2,1)} %bitcast.21), calls=%async_computation.5 | async-start | bytes 4194304 | tf_op jit(solution)/shard_map/all_to_all | solution.py:54
  175.5 1.2 slice.3
  176.7 29.1 %all-to-all-done.5.terms_ref = bf16[16,16,4096]{2,1,0:T(8,128)(2,1)S(1)} async-done(((bf16[16,16,4096]{2,1,0:T(8,128)(2,1)}), bf16[16,16,4096]{2,1,0:T(8,128)(2,1)S(1)}, u32[]{:S(2)}, u32[]{:S(2)}) %all-to-all-start.5) | async-done | bytes 2097184 | tf_op jit(solution)/shard_map/all_to_all | solution.py:54
  205.8 2.1 %shard_map.130 = bf16[16,4096]{1,0:T(8,128)(2,1)} custom-call(bf16[16,16,4096]{2,1,0:T(8,128)(2,1)S(1)} %all-to-all-done.5.terms_ref, bf16[16,4096]{1,0:T(8,128)(2,1)S(1)} %copy-done.8, f32[1,4096]{1,0:T(1,128)S(1)} %bitcast.41, bf16[16,32]{1,0:T(8,128)(2,1)S(1)} %compare_convert_fusion.1.last_ref, bf16[16,32,256]{2,1,0:T(8,128)(2,1)} %all-to-all-done.4.d_resid_ref), custom_call_target="tpu_custom_call" | custom-call | tf_op jit(solution)/shard_map/pallas_call | solution.py:244
  (97 shorter events, 1.1 us)
Async XLA Ops:
  0.6 0.9 copy-start.7
  1.5 0.7 copy-start.19
  2.5 1.4 copy-start
  3.9 7.2 %copy-start.44 = (s32[1,32]{1,0:T(1,128)S(1)}, s32[1,32]{1,0:T(1,128)}, u32[]{:S(2)}) copy-start(s32[1,32]{1,0:T(1,128)} %param.12) | copy-start | bytes 388
  3.9 10.1 %copy-start.36 = (bf16[4096,128]{1,0:T(8,128)(2,1)S(1)}, bf16[4096,128]{1,0:T(8,128)(2,1)}, u32[]{:S(2)}) copy-start(bf16[4096,128]{1,0:T(8,128)(2,1)} %param.17) | copy-start | bytes 3145732
  3.9 38.8 %all-to-all-start = ((bf16[16,16,4096]{2,1,0:T(8,128)(2,1)}), bf16[16,16,4096]{2,1,0:T(8,128)(2,1)S(1)}, u32[]{:S(2)}, u32[]{:S(2)}) async-start(bf16[16,16,4096]{2,1,0:T(8,128)(2,1)} %copy-done), calls=%async_computation | async-start | bytes 4194304 | tf_op jit(solution)/shard_map/all_to_all | solution.py:54
  11.4 1.1 copy-start.40
  11.7 40.4 %copy-start.11 = (f32[2,32,128]{2,1,0:T(8,128)}, f32[2,32,128]{2,1,0:T(8,128)S(1)}, u32[]{:S(2)}) copy-start(f32[2,32,128]{2,1,0:T(8,128)S(1)} %pad_maximum_fusion.3.query_turn_ref) | copy-start | bytes 98308
  11.8 0.7 copy-start.42
  42.7 1.6 copy-start.1
  44.3 2.9 %copy-start.46 = (f32[128]{0:T(128)S(1)}, f32[128]{0:T(128)}, u32[]{:S(2)}) copy-start(f32[128]{0:T(128)} %param.19) | copy-start | bytes 1540
  44.3 2.9 %copy-start.47 = (f32[128]{0:T(128)S(1)}, f32[128]{0:T(128)}, u32[]{:S(2)}) copy-start(f32[128]{0:T(128)} %param.18) | copy-start | bytes 1540
  44.3 7.9 %copy-start.2 = (bf16[128,4096]{1,0:T(8,128)(2,1)S(1)}, bf16[128,4096]{1,0:T(8,128)(2,1)}, u32[]{:S(2)}) copy-start(bf16[128,4096]{1,0:T(8,128)(2,1)} %wo_ref.1) | copy-start | bytes 3145732
  44.3 7.9 %copy-start.8 = (bf16[16,4096]{1,0:T(8,128)(2,1)S(1)}, bf16[16,4096]{1,0:T(8,128)(2,1)}, u32[]{:S(2)}) copy-start(bf16[16,4096]{1,0:T(8,128)(2,1)} %hidden_ref.5) | copy-start | bytes 393220
  45.3 6.9 %copy-start.21 = (f32[32,128]{1,0:T(8,128)}, f32[32,128]{1,0:T(8,128)S(1)}, u32[]{:S(2)}) copy-start(f32[32,128]{1,0:T(8,128)S(1)} %get-tuple-element.18.query_raw_ref) | copy-start | bytes 49156
  45.3 6.9 %collective-permute-start = (f32[256,128]{1,0:T(8,128)S(1)}, f32[256,128]{1,0:T(8,128)S(1)}, u32[]{:S(2)}, u32[]{:S(2)}) collective-permute-start(f32[256,128]{1,0:T(8,128)S(1)} %get-tuple-element.17.own_ref), channel_id=1, source_target_pairs={{0,1},{1,0},{2,3},{3,2},{4,5},{5,4},{6,7},{7,6},{8,9},{9,8},{10,11... | collective-permute-start | bytes 393224 | tf_op jit(solution)/shard_map/ppermute | solution.py:23
  47.3 11.1 %copy-start.31 = (f32[2,128]{1,0:T(2,128)}, f32[2,128]{1,0:T(2,128)S(1)}, u32[]{:S(2)}) copy-start(f32[2,128]{1,0:T(2,128)S(1)} %pad_maximum_fusion.5.gains_ref) | copy-start | bytes 3076
  52.2 0.7 copy-start.22
  52.9 0.7 copy-start.28
  53.6 10.6 %copy-start.39 = (s32[256,7]{0,1:T(8,128)S(1)}, s32[256,7]{0,1:T(8,128)}, u32[]{:S(2)}) copy-start(s32[256,7]{0,1:T(8,128)} %param.14) | copy-start | bytes 21508
  55.2 0.7 copy-start.5
  55.9 0.7 copy-start.13
  56.5 0.6 copy-start.15
  57.2 0.6 copy-start.24
  57.8 0.6 copy-start.33
  58.4 14.7 %copy-start.17 = (bf16[256,128]{1,0:T(8,128)(2,1)}, bf16[256,128]{1,0:T(8,128)(2,1)S(1)}, u32[]{:S(2)}) copy-start(bf16[256,128]{1,0:T(8,128)(2,1)S(1)} %get-tuple-element.27.value_ref) | copy-start | bytes 196612
  58.4 12.2 %all-to-all-start.1 = ((bf16[16,32,256]{2,1,0:T(8,128)(2,1)}), bf16[16,32,256]{2,1,0:T(8,128)(2,1)S(1)}, u32[]{:S(2)}, u32[]{:S(2)}) async-start(bf16[16,32,256]{2,1,0:T(8,128)(2,1)} %get-tuple-element.19), calls=%async_computation.1 | async-start | bytes 524288 | tf_op jit(solution)/shard_map/all_to_all | solution.py:54
  61.9 26.4 %copy-start.45 = (s32[256]{0:T(256)S(1)}, s32[256]{0:T(256)}, u32[]{:S(2)}) copy-start(s32[256]{0:T(256)} %param.13) | copy-start | bytes 3076
  64.2 42.8 %copy-start.29 = (f32[256]{0:T(256)}, f32[256]{0:T(256)S(1)}, u32[]{:S(2)}) copy-start(f32[256]{0:T(256)S(1)} %dynamic_slice.12) | copy-start | bytes 3076
  64.2 52.9 %copy-start.37 = (s32[256,7]{0,1:T(8,128)}, s32[256,7]{0,1:T(8,128)S(1)}, u32[]{:S(2)}) copy-start(s32[256,7]{0,1:T(8,128)S(1)} %fusion.10) | copy-start | bytes 21508
  71.4 1.0 copy-start.9
  72.4 0.6 copy-start.26
  73.0 31.8 %all-to-all-start.2 = ((bf16[16,32,256]{2,1,0:T(8,128)(2,1)}), bf16[16,32,256]{2,1,0:T(8,128)(2,1)S(1)}, u32[]{:S(2)}, u32[]{:S(2)}) async-start(bf16[16,32,256]{2,1,0:T(8,128)(2,1)} %get-tuple-element.20), calls=%async_computation.2 | async-start | bytes 524288 | tf_op jit(solution)/shard_map/all_to_all | solution.py:54
  88.3 28.9 %copy-start.38 = (s32[256,1]{0,1:T(1,128)}, s32[256,1]{0,1:T(1,128)S(1)}, u32[]{:S(2)}) copy-start(s32[256,1]{0,1:T(1,128)S(1)} %fusion.18) | copy-start | bytes 3076
  88.5 0.8 copy-start.3
  109.6 28.4 %copy-start.27 = (f32[32,256]{1,0:T(8,128)S(1)}, f32[32,256]{1,0:T(8,128)}, u32[]{:S(2)}) copy-start(f32[32,256]{1,0:T(8,128)} %copy-done.26) | copy-start | bytes 98308
  109.6 28.4 %copy-start.30 = (f32[256]{0:T(256)S(1)}, f32[256]{0:T(256)}, u32[]{:S(2)}) copy-start(f32[256]{0:T(256)} %copy-done.29) | copy-start | bytes 3076
  109.6 25.9 %all-to-all-start.3 = ((bf16[16,304,128]{2,1,0:T(8,128)(2,1)}), bf16[16,304,128]{2,1,0:T(8,128)(2,1)S(1)}, u32[]{:S(2)}, u32[]{:S(2)}) async-start(bf16[16,304,128]{2,1,0:T(8,128)(2,1)} %shard_map.126), calls=%async_computation.3 | async-start | bytes 2490368 | tf_op jit(solution)/shard_map/all_to_all | solution.py:54
  113.4 39.8 %collective-permute-start.1 = (bf16[128,4096]{1,0:T(8,128)(2,1)}, bf16[128,4096]{1,0:T(8,128)(2,1)}, u32[]{:S(2)}, u32[]{:S(2)}) collective-permute-start(bf16[128,4096]{1,0:T(8,128)(2,1)} %copy-done.9), channel_id=1, source_target_pairs={{0,1},{1,0},{2,3},{3,2},{4,5},{5,4},{6,7},{7,6},{8,9},{9,8},{10,11... | collective-permute-start | bytes 3145736 | tf_op jit(solution)/shard_map/ppermute | solution.py:23
  135.5 2.5 %copy-start.4 = (bf16[256,1024]{1,0:T(8,128)(2,1)S(1)}, bf16[256,1024]{1,0:T(8,128)(2,1)}, u32[]{:S(2)}) copy-start(bf16[256,1024]{1,0:T(8,128)(2,1)} %copy-done.3) | copy-start | bytes 1572868
  139.7 0.6 copy-start.35
  140.3 19.9 %all-to-all-start.4 = ((bf16[16,32,256]{2,1,0:T(8,128)(2,1)}), bf16[16,32,256]{2,1,0:T(8,128)(2,1)}, u32[]{:S(2)}, u32[]{:S(2)}) async-start(bf16[16,32,256]{2,1,0:T(8,128)(2,1)} %get-tuple-element.24), calls=%async_computation.4 | async-start | bytes 524288 | tf_op jit(solution)/shard_map/all_to_all | solution.py:54
  144.5 15.7 %copy-start.10 = (bf16[128,4096]{1,0:T(8,128)(2,1)S(1)}, bf16[128,4096]{1,0:T(8,128)(2,1)}, u32[]{:S(2)}) copy-start(bf16[128,4096]{1,0:T(8,128)(2,1)} %copy-done.9) | copy-start | bytes 3145732
  145.1 15.0 %copy-start.6 = (f32[2,256,128]{2,1,0:T(8,128)S(1)}, f32[2,256,128]{2,1,0:T(8,128)}, u32[]{:S(2)}) copy-start(f32[2,256,128]{2,1,0:T(8,128)} %copy-done.5) | copy-start | bytes 786436
  160.1 0.8 copy-start.12
  160.9 0.9 copy-start.14
  161.8 0.8 copy-start.16
  162.6 0.8 copy-start.18
  163.5 0.7 copy-start.23
  164.2 0.8 copy-start.25
  165.0 0.6 copy-start.32
  165.6 0.7 copy-start.34
  171.6 3.9 %copy-start.41 = (s32[32]{0:T(128)S(1)}, s32[32]{0:T(128)}, u32[]{:S(2)}) copy-start(s32[32]{0:T(128)} %copy-done.40) | copy-start | bytes 388
  171.6 3.9 %copy-start.43 = (s32[16]{0:T(128)S(1)}, s32[16]{0:T(128)}, u32[]{:S(2)}) copy-start(s32[16]{0:T(128)} %copy-done.42) | copy-start | bytes 196
  171.6 34.3 %copy-start.20 = (f32[4096]{0:T(1024)S(1)}, f32[4096]{0:T(1024)}, u32[]{:S(2)}) copy-start(f32[4096]{0:T(1024)} %param.15) | copy-start | bytes 49156
  171.6 34.3 %all-to-all-start.5 = ((bf16[16,16,4096]{2,1,0:T(8,128)(2,1)}), bf16[16,16,4096]{2,1,0:T(8,128)(2,1)S(1)}, u32[]{:S(2)}, u32[]{:S(2)}) async-start(bf16[16,16,4096]{2,1,0:T(8,128)(2,1)} %bitcast.21), calls=%async_computation.5 | async-start | bytes 4194304 | tf_op jit(solution)/shard_map/all_to_all | solution.py:54

commit v5 on v4

v5 whole, which is shorter than its diff:
```python
import functools
import math

import jax
import jax.numpy as jnp
from jax import lax
from jax.experimental import pallas as pl
from jax.experimental.pallas import tpu as pltpu
from jax.sharding import PartitionSpec as P

QDEV = 8
LANES = 128
VMEM_BYTES = 32 * 2**20


EPSILON = 1e-06
SOFTMAX_TEMPER = 0.05
LOSS_MULTIPLIER = 8192.0
ROPE_BASE = 1000000.0


def swapped(value, axis, apart):
    mask = 2**apart
    pairs = [(source, source ^ mask) for source in range(lax.axis_size(axis))]
    return lax.ppermute(value, axis, pairs)


def rms_scale(tensor):
    return lax.rsqrt(jnp.mean(tensor * tensor, axis=-1, keepdims=True) + EPSILON)


def norm_backward(grad, unit_form, inverse, gain):
    scaled = grad * gain
    return inverse * (scaled - unit_form * jnp.mean(unit_form * scaled, axis=-1, keepdims=True))


def exchange(blocks, axis):
    return lax.all_to_all(blocks, axis, 0, 0, tiled=True)


def halves(value):
    high = value.astype(jnp.bfloat16).astype(jnp.float32)
    return jnp.concatenate([high, value - high], axis=0)


def iota(shape, axis):
    return lax.broadcasted_iota(jnp.int32, shape, axis)


def columns_to_lanes(column, out_ref):
    diagonal = iota((LANES, LANES), 0) == iota((LANES, LANES), 1)
    for k in range(column.shape[0] // LANES):
        block = jnp.where(diagonal, column[LANES * k : LANES * (k + 1)], 0.0)
        out_ref[k : k + 1, :] = jnp.sum(block, axis=0, keepdims=True)


def own_core_lanes():
    return pl.ds(pl.multiple_of(lax.axis_index("core") * LANES, LANES), LANES)


def partial_logits_kernel(
    rows_ref, query_hot_ref, positive_hot_ref, listed_all_ref, gain_ref, out_ref, rows_out_ref, held_ref
):
    rows = rows_ref[...]
    rows_out_ref[...] = rows
    listed_ref = listed_all_ref[:8, own_core_lanes()]
    core_hot = query_hot_ref[own_core_lanes(), :]
    queries = jnp.dot(core_hot, rows, preferred_element_type=jnp.float32)
    positives = jnp.dot(positive_hot_ref[...], rows, preferred_element_type=jnp.float32)
    queries = queries.astype(jnp.bfloat16)
    features = gain_ref.shape[1] * out_ref.shape[0]
    rows32 = rows.astype(jnp.float32)
    plain = rows32 / gain_ref[...]
    squares = jnp.sum(rows32 * rows32, axis=1, keepdims=True) + jnp.sum(
        plain * plain, axis=1, keepdims=True
    ) * (EPSILON / features)
    against = (((1,), (1,)), ((), ()))
    with_positives = lax.dot_general(
        positives.astype(jnp.bfloat16), queries, against, preferred_element_type=jnp.float32
    )
    with_all = lax.dot_general(rows, queries, against, preferred_element_type=jnp.float32)
    row_index = iota(with_all.shape, 0)
    for j in range(8):
        listed = row_index == listed_ref[j : j + 1, :]
        held_ref[j : j + 1, :] = jnp.sum(jnp.where(listed, with_all, 0.0), axis=0, keepdims=True)
        held_ref[8 + j : 9 + j, :] = jnp.sum(
            jnp.where(listed, squares, 0.0), axis=0, keepdims=True
        )
    columns_to_lanes(squares, held_ref.at[16:24])
    count = with_positives.shape[0]
    sent = [with_positives.astype(jnp.bfloat16)]
    for start in (0, 8, 16):
        sent.append(halves(held_ref[start : start + 8, :]).astype(jnp.bfloat16))
    for t in range(out_ref.shape[0]):
        out_ref[t, :count, :] = sent[0]
        for k in range(3):
            out_ref[t, count + 16 * k : count + 16 * (k + 1), :] = sent[k + 1]


def softmax_kernel(arrived_ref, positive_hot_ref, out_ref, inverse_ref):
    count = positive_hot_ref.shape[0]
    summed = arrived_ref[0].astype(jnp.float32)
    for t in range(1, arrived_ref.shape[0]):
        summed = summed + arrived_ref[t].astype(jnp.float32)

    def small(k):
        block = summed[count + 16 * k : count + 16 * (k + 1)]
        return block[:8] + block[8:]

    inverse_listed = lax.rsqrt(small(1) + EPSILON * EPSILON)
    inverse = lax.rsqrt(small(2) + EPSILON * EPSILON)
    inverse_ref[...] = inverse
    inverse_query = inverse_listed[7:8, :]
    picked = jnp.zeros((count, LANES), jnp.float32)
    for k in range(8):
        hot = positive_hot_ref[:, LANES * k : LANES * (k + 1)].astype(jnp.float32)
        picked = picked + hot * inverse[k : k + 1, :]
    inverse_positive = jnp.sum(picked, axis=1, keepdims=True)
    logits = summed[:count] * inverse_positive * inverse_query / SOFTMAX_TEMPER
    hard = small(0) * inverse_listed * inverse_query / SOFTMAX_TEMPER
    is_hard = iota(hard.shape, 0) < 7
    is_own = iota(logits.shape, 0) == iota(logits.shape, 1) + lax.axis_index("core") * LANES
    weights = jnp.exp(logits - 1.0 / SOFTMAX_TEMPER)
    hard_weights = jnp.where(is_hard, jnp.exp(hard - 1.0 / SOFTMAX_TEMPER), 0.0)
    totals = jnp.sum(weights, axis=0, keepdims=True) + jnp.sum(hard_weights, axis=0, keepdims=True)
    target = jnp.sum(jnp.where(is_own, logits, 0.0), axis=0, keepdims=True)
    losses = jnp.log(totals) + 1.0 / SOFTMAX_TEMPER - target
    scaling_factor = LOSS_MULTIPLIER / (count * SOFTMAX_TEMPER)

    def rounded(value):
        return value.astype(jnp.bfloat16).astype(jnp.float32)

    coef = rounded(scaling_factor * (weights / totals - is_own.astype(jnp.float32)))
    hard_coef = rounded(scaling_factor * (hard_weights / totals))
    weighted = coef * logits * SOFTMAX_TEMPER
    hard_weighted = jnp.where(is_hard, hard_coef * hard * SOFTMAX_TEMPER, 0.0)
    along_query = jnp.sum(weighted, axis=0, keepdims=True) + jnp.sum(
        hard_weighted, axis=0, keepdims=True
    )
    out_ref[:count, :] = coef
    out_ref[count : count + 8, :] = jnp.where(is_hard, hard_coef, along_query)
    out_ref[count + 8 : count + 16, :] = jnp.where(is_hard, hard_weighted, losses)
    out_ref[count + 16 :, :] = jnp.zeros_like(out_ref[count + 16 :, :])
    columns_to_lanes(jnp.sum(weighted, axis=1, keepdims=True), out_ref.at[count + 16 :])


def resid_grad_kernel(
    both_ref,
    inverse_ref,
    rows_ref,
    positive_hot_ref,
    query_hot_ref,
    listed_ref,
    resid_ref,
    gain_ref,
    out_ref,
    loss_ref,
):
    sequences = resid_ref.shape[0]
    count, total_rows = positive_hot_ref.shape
    group = lax.axis_index("z") * lax.axis_size("core") + lax.axis_index("core")
    first_row = group * sequences
    first_query = group * QDEV
    across = (((1,), (1,)), ((), ()))

    def joined(start, stop):
        return jnp.concatenate([both_ref[0, start:stop, :], both_ref[1, start:stop, :]], axis=1)

    coef = joined(0, count)
    coef16 = coef.astype(jnp.bfloat16)
    hard = joined(count, count + 8)
    hard_weighted = joined(count + 8, count + 16)
    along_passage = both_ref[0, count + 16 : count + 24, :] + both_ref[1, count + 16 : count + 24, :]
    along_passage = jnp.concatenate([along_passage[0:1], along_passage[1:2]], axis=1)
    inverse = jnp.concatenate([inverse_ref[k : k + 1, :] for k in range(8)], axis=1)

    own_row = first_row + iota((sequences, count), 0)
    own_query = (iota((sequences, count), 0) < QDEV) & (
        iota((sequences, count), 1) == first_query + iota((sequences, count), 0)
    )
    own_positive = listed_ref[8:9, :] == own_row
    to_positives = lax.dot_general(
        own_query.astype(jnp.bfloat16), coef16, across, preferred_element_type=jnp.float32
    )
    to_queries = jnp.dot(
        own_positive.astype(jnp.bfloat16), coef16, preferred_element_type=jnp.float32
    )
    along = jnp.sum(
        jnp.where(own_query, hard[7:8, :], 0.0) + jnp.where(own_positive, along_passage, 0.0),
        axis=1,
        keepdims=True,
    )
    for j in range(7):
        listed = listed_ref[j : j + 1, :] == own_row
        to_queries = to_queries + jnp.where(listed, hard[j : j + 1, :], 0.0)
        along = along + jnp.sum(
            jnp.where(listed, hard_weighted[j : j + 1, :], 0.0), axis=1, keepdims=True
        )
    matrix = jnp.dot(
        to_positives.astype(jnp.bfloat16), positive_hot_ref[...], preferred_element_type=jnp.float32
    ) + jnp.dot(
        to_queries.astype(jnp.bfloat16), query_hot_ref[...], preferred_element_type=jnp.float32
    )
    row_index = iota((sequences, total_rows), 1)
    for j in range(7):
        own_hard = jnp.sum(jnp.where(own_query, hard[j : j + 1, :], 0.0), axis=1, keepdims=True)
        own_listed = jnp.where(own_query, listed_ref[j : j + 1, :].astype(jnp.float32), 0.0)
        own_listed = jnp.sum(own_listed, axis=1, keepdims=True).astype(jnp.int32)
        listed = row_index == own_listed
        matrix = matrix + jnp.where(listed, own_hard, 0.0)
    matrix = matrix * inverse
    high = matrix.astype(jnp.bfloat16)
    low = (matrix - high.astype(jnp.float32)).astype(jnp.bfloat16)
    rows = rows_ref[...]
    d_embed = jnp.dot(high, rows, preferred_element_type=jnp.float32) + jnp.dot(
        low, rows, preferred_element_type=jnp.float32
    )

    is_own_row = row_index == first_row + iota((sequences, total_rows), 0)
    own_inverse = jnp.sum(jnp.where(is_own_row, inverse, 0.0), axis=1, keepdims=True)
    resid = resid_ref[...]
    gain = gain_ref[...]
    features = gain.shape[1] * out_ref.shape[0]
    d_resid = own_inverse * gain * (
        d_embed - resid * gain * own_inverse * along
    ) - resid * (along * own_inverse * own_inverse * (EPSILON / features))
    d_resid16 = d_resid.astype(jnp.bfloat16)
    for t in range(out_ref.shape[0]):
        out_ref[t] = d_resid16
    loss_ref[0] = jnp.sum(hard_weighted[7:8, :]) / count


def kernel_call(body, outs, arrays, near=(), near_outs=(), late=(), after=(), scratch=()):
    count = len(arrays)
    far = [i for i in range(count) if i not in near]
    scalar_outs = [i for i in range(len(outs)) if outs[i][0] == (1,)]
    far_outs = [i for i in range(len(outs)) if i not in near_outs and i not in scalar_outs]

    def spec(is_far):
        return pl.BlockSpec(memory_space=pltpu.HBM if is_far else pltpu.VMEM)

    def kernel(*refs):
        given = list(refs[:count])
        start = count + len(after)
        results = list(refs[start : start + len(outs)])
        start += len(outs)
        held_in = refs[start : start + len(far)]
        start += len(far)
        held_out = refs[start : start + len(far_outs)]
        start += len(far_outs)
        semaphores = refs[start]
        copies = {}
        for k, i in enumerate(far):
            copies[i] = pltpu.make_async_copy(given[i], held_in[k], semaphores.at[k])
            copies[i].start()
            given[i] = held_in[k]
        for i in far:
            if i not in late:
                copies[i].wait()

        def ready():
            for i in late:
                copies[i].wait()

        targets = [results[i] for i in far_outs]
        for k, i in enumerate(far_outs):
            results[i] = held_out[k]
        extra = (ready,) if late else ()
        body(*extra, *given, *results, *refs[start + 1 :])
        copies_out = [
            pltpu.make_async_copy(held_out[k], targets[k], semaphores.at[len(far) + k])
            for k in range(len(far_outs))
        ]
        for copy in copies_out:
            copy.start()
        for copy in copies_out:
            copy.wait()

    held = [pltpu.VMEM(arrays[i].shape, arrays[i].dtype) for i in far]
    held += [pltpu.VMEM(*outs[i]) for i in far_outs]
    held.append(pltpu.SemaphoreType.DMA((max(1, len(far) + len(far_outs)),)))
    return pl.pallas_call(
        kernel,
        out_shape=[jax.ShapeDtypeStruct(shape, dtype) for shape, dtype in outs],
        in_specs=[spec(i in far) for i in range(count)] + [pl.BlockSpec(memory_space=pl.ANY)] * len(after),
        out_specs=[
            pl.BlockSpec(memory_space=pltpu.SMEM) if i in scalar_outs else spec(i in far_outs)
            for i in range(len(outs))
        ],
        scratch_shapes=held + list(scratch),
        compiler_params=pltpu.CompilerParams(vmem_limit_bytes=VMEM_BYTES),
    )(*arrays, *after)


def candidate_kernel(positives_ref, negatives_ref, listed_ref, query_hot_ref, positive_hot_ref):
    query_count, total_rows = query_hot_ref.shape
    groups = query_count // QDEV
    sequences = total_rows // groups
    others = sequences - QDEV

    def row_of(passage):
        at = ((passage.astype(jnp.float32) + 0.5) * (1.0 / others)).astype(jnp.int32)
        return passage + at * QDEV + QDEV

    def query_row(query):
        return query + query // QDEV * others

    positive_row = row_of(positives_ref[...])
    count = negatives_ref.shape[0]
    listed_ref[:count, :] = row_of(negatives_ref[...])
    listed_ref[count : count + 1, :] = query_row(iota((1, query_count), 1))
    listed_ref[count + 1 :, :] = jnp.broadcast_to(
        positive_row, (listed_ref.shape[0] - count - 1, query_count)
    )
    shape = (LANES, total_rows)
    diagonal = iota((LANES, LANES), 0) == iota((LANES, LANES), 1)
    for k in range(query_count // LANES):
        rows = slice(LANES * k, LANES * (k + 1))
        query = query_row(iota(shape, 0) + LANES * k)
        query_hot_ref[rows, :] = (query == iota(shape, 1)).astype(jnp.float32).astype(jnp.bfloat16)
        lanes = positive_row[:, rows].astype(jnp.float32)
        column = jnp.sum(jnp.where(diagonal, lanes, 0.0), axis=1, keepdims=True)
        positive_hot_ref[rows, :] = (
            (column.astype(jnp.int32) == iota(shape, 1)).astype(jnp.float32).astype(jnp.bfloat16)
        )


def transpose_kernel(*refs):
    half = len(refs) // 2
    for given_ref, out_ref in zip(refs[:half], refs[half:]):
        given = given_ref[...]
        out_ref[...] = given.T
    if len(refs) > 2 * half:
        refs[-1][0] = jnp.float32(0.0)


def token_kernel(out_ref):
    out_ref[0] = jnp.float32(0.0)


def contrast(everyone, resid, gain, tables, after):
    tensor_count = lax.axis_size("tensor")
    sequences, width = resid.shape
    listed, query_hot, positive_hot = tables
    count, total_rows = positive_hot.shape
    sent, rows = kernel_call(
        partial_logits_kernel,
        [((tensor_count, count + 48, LANES), jnp.bfloat16), ((total_rows, width), jnp.bfloat16)],
        [everyone.reshape(total_rows, width), query_hot, positive_hot, listed, gain],
        near=(0,),
        near_outs=(0,),
        after=after,
        scratch=[pltpu.VMEM((24, LANES), jnp.float32)],
    )
    arrived = exchange(sent, "tensor")
    coefs, inverse = kernel_call(
        softmax_kernel,
        [((count + 24, LANES), jnp.float32), ((8, LANES), jnp.float32)],
        [arrived, positive_hot],
        near=(0,),
        near_outs=(0,),
    )
    both = lax.all_gather(coefs, "core", axis=0)
    d_resid16, loss = kernel_call(
        resid_grad_kernel,
        [((tensor_count, sequences, width), jnp.bfloat16), ((1,), jnp.float32)],
        [both, inverse, rows, positive_hot, query_hot, listed, resid, gain],
        near=(0,),
        near_outs=(0,),
    )
    return loss, exchange(d_resid16, "tensor")


def copied_norm_kernel(hidden_ref, gain_ref, out_ref):
    hidden32 = hidden_ref[...].astype(jnp.float32)
    normed = (hidden32 * rms_scale(hidden32) * gain_ref[...]).astype(jnp.bfloat16)
    height = normed.shape[0]
    for c in range(normed.shape[1] // LANES):
        block = normed[:, LANES * c : LANES * (c + 1)]
        for t in range(out_ref.shape[0]):
            out_ref[t, height * c : height * (c + 1), :] = block


def projection_kernel(rows_ref, kv_weights_ref, query_weights_ref, kv_ref, query_ref):
    tensor_count, tall, _ = rows_ref.shape
    blocks = kv_weights_ref.shape[0] // LANES
    height = tall // blocks

    def block(c):
        part = rows_ref[:, height * c : height * (c + 1), :]
        return part.reshape(tensor_count * height, LANES)

    kv = jnp.zeros(kv_ref.shape, jnp.float32)
    query = jnp.zeros(query_ref.shape, jnp.float32)
    for c in range(0, blocks, 2):
        rows = jnp.concatenate([block(c), block(c + 1)], axis=1)
        columns = slice(LANES * c, LANES * (c + 2))
        kv = kv + jnp.dot(rows, kv_weights_ref[columns, :], preferred_element_type=jnp.float32)
        query = query + jnp.dot(
            rows, query_weights_ref[columns, :], preferred_element_type=jnp.float32
        )
    kv_ref[...] = kv
    query_ref[...] = query


def half_turned(tensor, cosine, signed_sine):
    halfway = tensor.shape[1] // 2
    return tensor * cosine + pltpu.roll(tensor, halfway, 1) * signed_sine


def is_even_tensor():
    return lax.axis_index("tensor") % 2 == 0


def attention_kernel(
    own_ref,
    other_ref,
    query_all_ref,
    layout_ref,
    q_gain_ref,
    k_gain_ref,
    hidden_ref,
    wo_ref,
    out_ref,
    saved_ref,
):
    root = math.sqrt(own_ref.shape[1])
    tokens_count, sequences, own_rows = own_ref.shape[0], out_ref.shape[1], hidden_ref.shape[0]
    at, _ = layout_rows(tokens_count, sequences, own_rows)
    to, _ = saved_rows(tokens_count, sequences)
    is_even = is_even_tensor()
    own, other = own_ref[...], other_ref[...]
    key_raw = jnp.where(is_even, own, other)
    value16 = jnp.where(is_even, other, own).astype(jnp.bfloat16)
    query_raw = jnp.dot(
        unfolded(layout_ref[at["chosen"], :], sequences),
        query_all_ref[...],
        precision=lax.Precision.HIGHEST,
        preferred_element_type=jnp.float32,
    )
    q_gain, k_gain = q_gain_ref[...], k_gain_ref[...]
    key16 = half_turned(
        key_raw * rms_scale(key_raw) * k_gain,
        layout_ref[at["key_cosine"], :],
        layout_ref[at["key_sine"], :],
    ).astype(jnp.bfloat16)
    query16 = half_turned(
        query_raw * rms_scale(query_raw) * q_gain,
        layout_ref[at["query_cosine"], :],
        layout_ref[at["query_sine"], :],
    ).astype(jnp.bfloat16)
    shift = (
        root
        * jnp.max(q_gain, axis=1, keepdims=True)
        * jnp.max(k_gain, axis=1, keepdims=True)
    )
    scores = (
        lax.dot_general(
            query16, key16, (((1,), (1,)), ((), ())), preferred_element_type=jnp.float32
        )
        / root
    )
    inside = unfolded(layout_ref[at["inside"], :], sequences)
    weights = jnp.where(inside > 0.0, jnp.exp(scores - shift), 0.0)
    probs = weights / jnp.sum(weights, axis=1, keepdims=True)
    attn16 = jnp.dot(
        probs.astype(jnp.bfloat16), value16, preferred_element_type=jnp.float32
    ).astype(jnp.bfloat16)
    own_last = layout_ref[at["own_last"], :][:, :own_rows].astype(jnp.bfloat16)
    chunk = out_ref.shape[2]
    for t in range(out_ref.shape[0]):
        columns = slice(t * chunk, (t + 1) * chunk)
        block = jnp.dot(attn16, wo_ref[:, columns], preferred_element_type=jnp.float32)
        block = block + jnp.dot(
            own_last, hidden_ref[:, columns], preferred_element_type=jnp.float32
        )
        out_ref[t] = block.astype(jnp.bfloat16)
    saved_ref[to["key_raw"], :] = key_raw
    saved_ref[to["key"], :] = key16.astype(jnp.float32)
    saved_ref[to["value"], :] = value16.astype(jnp.float32)
    saved_ref[to["query_raw"], :] = query_raw
    saved_ref[to["query"], :] = query16.astype(jnp.float32)
    saved_ref[to["probs"], :] = folded(probs)


def resid_kernel(arrived_ref, gains_ref, resid_ref, out_ref, gain_ref):
    chunk = resid_ref.shape[1]
    start = pl.multiple_of(lax.axis_index("tensor") * chunk, chunk)
    gain = gains_ref[:, pl.ds(start, chunk)]
    gain_ref[...] = gain
    resid = arrived_ref[0].astype(jnp.float32)
    for t in range(1, arrived_ref.shape[0]):
        resid = resid + arrived_ref[t].astype(jnp.float32)
    resid_ref[...] = resid
    scaled16 = (resid * gain).astype(jnp.bfloat16)
    for t in range(out_ref.shape[0]):
        out_ref[t] = scaled16


def gradient_kernel(
    d_resid_ref,
    wo_t_ref,
    saved_ref,
    layout_ref,
    q_gain_ref,
    k_gain_ref,
    own_weights_ref,
    other_weights_ref,
    query_weights_ref,
    out_ref,
    added_ref,
):
    head_width = saved_ref.shape[1]
    root = math.sqrt(head_width)
    sequences = d_resid_ref.shape[1]
    own_rows = added_ref.shape[0]
    tokens_count = own_rows * out_ref.shape[0]
    at, _ = layout_rows(tokens_count, sequences, own_rows)
    to, _ = saved_rows(tokens_count, sequences)
    is_even = is_even_tensor()
    chunk = d_resid_ref.shape[2]
    d_attn = jnp.dot(d_resid_ref[0], wo_t_ref[:chunk, :], preferred_element_type=jnp.float32)
    for t in range(1, d_resid_ref.shape[0]):
        d_attn = d_attn + jnp.dot(
            d_resid_ref[t],
            wo_t_ref[t * chunk : (t + 1) * chunk, :],
            preferred_element_type=jnp.float32,
        )
    d_attn16 = d_attn.astype(jnp.bfloat16)
    probs = unfolded(saved_ref[to["probs"], :], sequences)
    key16 = saved_ref[to["key"], :].astype(jnp.bfloat16)
    query16 = saved_ref[to["query"], :].astype(jnp.bfloat16)
    value16 = saved_ref[to["value"], :].astype(jnp.bfloat16)
    d_probs = lax.dot_general(
        d_attn16, value16, (((1,), (1,)), ((), ())), preferred_element_type=jnp.float32
    )
    d_scores16 = (
        probs * (d_probs - jnp.sum(probs * d_probs, axis=1, keepdims=True)) / root
    ).astype(jnp.bfloat16)
    down = (((0,), (0,)), ((), ()))
    d_query_rot = jnp.dot(d_scores16, key16, preferred_element_type=jnp.float32)
    d_key_rot = lax.dot_general(d_scores16, query16, down, preferred_element_type=jnp.float32)
    d_value = lax.dot_general(
        probs.astype(jnp.bfloat16), d_attn16, down, preferred_element_type=jnp.float32
    )

    def head_gradient(grad_rot, name, gain):
        raw = saved_ref[to[name + "_raw"], :]
        inverse = rms_scale(raw)
        turned_back = half_turned(
            grad_rot, layout_ref[at[name + "_cosine"], :], -layout_ref[at[name + "_sine"], :]
        )
        return norm_backward(turned_back, raw * inverse, inverse, gain)

    d_key = head_gradient(d_key_rot, "key", k_gain_ref[...])
    d_query = head_gradient(d_query_rot, "query", q_gain_ref[...])
    own16 = jnp.where(is_even, d_key, d_value).astype(jnp.bfloat16)
    other16 = jnp.where(is_even, d_value, d_key).astype(jnp.bfloat16)
    spread16 = lax.dot_general(
        unfolded(layout_ref[at["chosen"], :], sequences).astype(jnp.bfloat16),
        d_query.astype(jnp.bfloat16),
        down,
        preferred_element_type=jnp.float32,
    ).astype(jnp.bfloat16)
    last = layout_ref[at["own_last_t"], :][:, :sequences].astype(jnp.bfloat16)
    height = out_ref.shape[1] * LANES // added_ref.shape[1]
    for t in range(added_ref.shape[1] // chunk):
        columns = slice(t * chunk, (t + 1) * chunk)
        added_ref[:, columns] = jnp.dot(last, d_resid_ref[t], preferred_element_type=jnp.float32)
        term = jnp.dot(own16, own_weights_ref[:, columns], preferred_element_type=jnp.float32)
        term = term + jnp.dot(
            other16, other_weights_ref[:, columns], preferred_element_type=jnp.float32
        )
        term = term + jnp.dot(
            spread16, query_weights_ref[:, columns], preferred_element_type=jnp.float32
        )
        term16 = term.astype(jnp.bfloat16)
        for k in range(chunk // LANES):
            c = t * (chunk // LANES) + k
            block = term16[:, LANES * k : LANES * (k + 1)]
            out_ref[:, height * c : height * (c + 1), :] = block.reshape(-1, height, LANES)


def d_hidden_kernel(terms_ref, hidden_ref, gain_ref, added_ref, out_ref):
    d_normed = terms_ref[0].astype(jnp.float32)
    for t in range(1, terms_ref.shape[0]):
        d_normed = d_normed + terms_ref[t].astype(jnp.float32)
    hidden32 = hidden_ref[...].astype(jnp.float32)
    height = hidden32.shape[0]
    d_normed = jnp.concatenate(
        [d_normed[height * c : height * (c + 1)] for c in range(hidden32.shape[1] // LANES)],
        axis=1,
    )
    inverse = rms_scale(hidden32)
    d_hidden = norm_backward(d_normed, hidden32 * inverse, inverse, gain_ref[...])
    out_ref[...] = (d_hidden + added_ref[...]).astype(jnp.bfloat16)


def packed_rows(sizes):
    starts, total = {}, 0
    for name, rows in sizes:
        starts[name] = slice(total, total + rows)
        total += rows
    return starts, total


def layout_rows(tokens_count, sequences, own_rows):
    wide = sequences * tokens_count // LANES
    return packed_rows(
        [
            ("key_cosine", tokens_count),
            ("key_sine", tokens_count),
            ("query_cosine", sequences),
            ("query_sine", sequences),
            ("inside", wide),
            ("chosen", wide),
            ("own_last", sequences),
            ("own_last_t", own_rows),
        ]
    )


def saved_rows(tokens_count, sequences):
    return packed_rows(
        [
            ("key_raw", tokens_count),
            ("key", tokens_count),
            ("value", tokens_count),
            ("query_raw", sequences),
            ("query", sequences),
            ("probs", sequences * tokens_count // LANES),
        ]
    )


def folded(block):
    parts = [block[:, LANES * k : LANES * (k + 1)] for k in range(block.shape[1] // LANES)]
    return jnp.concatenate(parts, axis=0)


def unfolded(block, rows):
    parts = [block[rows * k : rows * (k + 1)] for k in range(block.shape[0] // rows)]
    return jnp.concatenate(parts, axis=1)


def sequence_kernel(lengths_ref, out_ref, *, tokens_count, own_rows):
    sequences = lengths_ref.shape[1]
    at, _ = layout_rows(tokens_count, sequences, own_rows)
    lengths = lengths_ref[...].astype(jnp.float32)
    square = (sequences, sequences)
    ends = jnp.sum(
        jnp.where(iota(square, 1) <= iota(square, 0), lengths, 0.0), axis=1, keepdims=True
    )
    own_length = jnp.sum(
        jnp.where(iota(square, 1) == iota(square, 0), lengths, 0.0), axis=1, keepdims=True
    )
    starts = ends - own_length
    ends_row = jnp.sum(
        jnp.where(iota(square, 0) <= iota(square, 1), own_length, 0.0), axis=0, keepdims=True
    )
    starts_row = ends_row - lengths
    token = iota((sequences, tokens_count), 1).astype(jnp.float32)
    out_ref[at["inside"], :] = folded(((token >= starts) & (token < ends)).astype(jnp.float32))
    out_ref[at["chosen"], :] = folded((token == ends - 1.0).astype(jnp.float32))
    first = (lax.axis_index("tensor") * own_rows).astype(jnp.float32)
    own_token = iota((sequences, LANES), 1).astype(jnp.float32) + first
    own_token = jnp.where(iota((sequences, LANES), 1) < own_rows, own_token, -1.0)
    out_ref[at["own_last"], :] = (own_token == ends - 1.0).astype(jnp.float32)
    own_token = iota((own_rows, sequences), 0).astype(jnp.float32) + first
    own_last_t = (own_token == ends_row - 1.0).astype(jnp.float32)
    out_ref[at["own_last_t"], :] = jnp.concatenate(
        [own_last_t, jnp.zeros((own_rows, LANES - sequences), jnp.float32)], axis=1
    )
    token = iota((tokens_count, sequences), 0).astype(jnp.float32)
    held = (token >= starts_row) & (token < ends_row)
    position = jnp.sum(jnp.where(held, token - starts_row, 0.0), axis=1, keepdims=True)
    lane = iota((1, LANES), 1)
    halfway = LANES // 2
    pair = jnp.where(lane < halfway, lane, lane - halfway).astype(jnp.float32)
    frequency = jnp.exp(pair * (-2.0 / LANES * math.log(ROPE_BASE)))
    sign = jnp.where(lane < halfway, -1.0, 1.0)
    for name, place in (("key", position), ("query", own_length - 1.0)):
        angles = place * frequency
        out_ref[at[name + "_cosine"], :] = jnp.cos(angles)
        out_ref[at[name + "_sine"], :] = jnp.sin(angles) * sign


def on_device(
    hidden, lengths, positives, negatives, in_gain, wq, wkv, q_gain, k_gain, wo, out_gain
):
    tensor_count, z_count = lax.axis_size("tensor"), lax.axis_size("z")
    own_rows, features = hidden.shape
    tokens_count = own_rows * tensor_count
    head_width = wq.shape[1]
    sequences = lengths.shape[1]
    query_count = positives.shape[0]
    total_rows = query_count // QDEV * sequences
    chunk = features // tensor_count
    f32, bf16 = jnp.float32, jnp.bfloat16
    head = (tokens_count, head_width)
    weights_shape = (head_width, features)
    flat = (tensor_count, own_rows * features // LANES, LANES)
    gain_rows = [q_gain[None, :], k_gain[None, :]]

    (copies,) = kernel_call(
        copied_norm_kernel, [(flat, bf16)], [hidden, in_gain[None, :]], near_outs=(0,)
    )
    piece = exchange(copies, "tensor")
    kv_own, query_all = kernel_call(
        projection_kernel,
        [(head, f32), (head, f32)],
        [piece, wkv, wq],
        near=(0,),
        near_outs=(0,),
    )
    kv_other = swapped(kv_own, "tensor", 0)
    (layout,) = kernel_call(
        functools.partial(sequence_kernel, tokens_count=tokens_count, own_rows=own_rows),
        [((layout_rows(tokens_count, sequences, own_rows)[1], LANES), f32)],
        [lengths],
        after=[query_all],
    )
    blocks, saved = kernel_call(
        attention_kernel,
        [
            ((tensor_count, sequences, chunk), bf16),
            ((saved_rows(tokens_count, sequences)[1], LANES), f32),
        ],
        [kv_own, kv_other, query_all, layout, *gain_rows, hidden, wo],
        near=(0, 1),
        near_outs=(0,),
    )
    (own_weights,) = kernel_call(
        transpose_kernel, [(weights_shape, bf16)], [wkv], after=[saved]
    )
    other_weights = swapped(own_weights, "tensor", 0)
    resid, scaled, own_gain = kernel_call(
        resid_kernel,
        [((sequences, chunk), f32), ((z_count, sequences, chunk), bf16), ((1, chunk), f32)],
        [exchange(blocks, "tensor"), out_gain[None, :]],
        near=(0,),
        near_outs=(1,),
    )
    query_weights, wo_t, transposed = kernel_call(
        transpose_kernel,
        [(weights_shape, bf16), ((features, head_width), bf16), ((1,), f32)],
        [wq, wo],
        after=[resid],
    )
    (fetched,) = kernel_call(token_kernel, [((1,), f32)], [], after=[other_weights])
    tables = kernel_call(
        candidate_kernel,
        [
            ((16, query_count), jnp.int32),
            ((query_count, total_rows), bf16),
            ((query_count, total_rows), bf16),
        ],
        [positives[None, :], negatives.T],
        after=[resid],
    )
    everyone = lax.all_gather(exchange(scaled, "z"), "core", axis=1)
    loss, d_resid16 = contrast(
        everyone, resid, own_gain, tables, [transposed, fetched]
    )
    product, added = kernel_call(
        gradient_kernel,
        [(flat, bf16), ((own_rows, features), f32)],
        [
            d_resid16,
            wo_t,
            saved,
            layout,
            *gain_rows,
            own_weights,
            other_weights,
            query_weights,
        ],
        near=(0,),
        near_outs=(0,),
    )
    terms = exchange(product, "tensor")
    (d_hidden,) = kernel_call(
        d_hidden_kernel,
        [((own_rows, features), bf16)],
        [terms, hidden, in_gain[None, :], added],
        near=(0,),
    )
    return (d_hidden, loss[0])


def solution(mesh):
    z_count = mesh.shape["dp"] // 2
    chips = mesh.devices.reshape(z_count, 2, mesh.shape["tensor"])
    mesh = jax.sharding.Mesh(chips, ("z", "core", "tensor"))
    everywhere = P(("z", "core", "tensor"), None)
    placed = (
        everywhere,
        P(("z", "core"), None),
        P(),
        P(),
        P(),
        P(None, "tensor"),
        P(None, "tensor"),
        P(),
        P(),
        P("tensor", None),
        P(),
    )
    return jax.shard_map(
        on_device, mesh=mesh, in_specs=placed, out_specs=(everywhere, P()), check_vma=False
    )
```

time: 210 us -> 180 us (0.86)
  blocking collectives: 4.18 us -> 106 us
  waiting for transfers between devices: 112 us -> 16.1 us
  starting transfers between devices: 43.4 us -> 25.7 us
  local copies, waits for them, and re-layouts: 24.1 us -> 8.82 us
  other arithmetic: 7.8 us -> 0 us
  Pallas kernels: 15.7 us -> 20.7 us
    all_to_all x0 -> x4, blocking collectives: none -> 102 us  [exchange(): return lax.all_to_all(blocks, axis, 0, 0, tiled=True)]
    all_to_all x6 -> x2, waiting for transfers between devices: 101 us -> 12.6 us  [exchange(): return lax.all_to_all(blocks, axis, 0, 0, tiled=True)]
    all_to_all x6 -> x2, starting transfers between devices: 37.8 us -> 19.5 us  [exchange(): return lax.all_to_all(blocks, axis, 0, 0, tiled=True)]
    unnamed x100 -> x60, local copies, waits for them, and re-layouts: 22.1 us -> 8.82 us
    ppermute x2, waiting for transfers between devices: 10.4 us -> 3.48 us  [swapped(): return lax.ppermute(value, axis, pairs)]
    pallas_call x9 -> x14, Pallas kernels: 15.7 us -> 20.7 us  [kernel_call(): pl.pallas_call(kernel, out_shape=[jax.ShapeDtypeStruct(shape, dtype) for...]
    concatenate x4 -> x0, other arithmetic: 3.07 us -> none  [the longest x1 2.83 us: on_device(): jnp.concatenate([wkv, wq], axis=1)]
  transfers between devices with their start and end apart: 8 -> 4, of which waited for: 8 -> 3; matrix products, arithmetic and copies ran while one was open for 7% -> 0% of each run, Pallas kernels for 1% -> 3%
where the time goes in v5:
time: 180 us; the launch traced here: 179 us
  blocking collectives  106 us (59%)
  starting transfers between devices  25.7 us (14%)
  Pallas kernels  20.7 us (12%)
  waiting for transfers between devices  16.1 us (9%)
  local copies, waits for them, and re-layouts  8.82 us (5%)
    all_to_all x4, blocking collectives, exchange(): return lax.all_to_all(blocks, axis, 0, 0, tiled=True)  102 us
    pallas_call x14, Pallas kernels, kernel_call(): pl.pallas_call(kernel, out_shape=[jax.ShapeDtypeStruct(shape, dtype) for...  20.7 us
    all_to_all x2, starting transfers between devices, exchange(): return lax.all_to_all(blocks, axis, 0, 0, tiled=True)  19.5 us
    all_to_all x2, waiting for transfers between devices, exchange(): return lax.all_to_all(blocks, axis, 0, 0, tiled=True)  12.6 us
    unnamed x60, local copies, waits for them, and re-layouts  8.82 us
    ppermute x2, starting transfers between devices, swapped(): return lax.ppermute(value, axis, pairs)  6.13 us
  transfers between devices with their start and end apart: 4, of which 3 were waited for; matrix products, arithmetic and copies ran while one was open for 0% of the time, Pallas kernels for 3%

profile of v5, /device:TPU:32, one launch (start us, length us, event | category | flops | bytes accessed | tf_op | source)
XLA Modules:
  0.0 178.8 jit_solution(9754790210262660537)
XLA Ops:
  0.6 0.0 copy-start.6
  0.6 0.9 copy-done.6
  1.5 0.7 copy-done.18
  2.3 0.5 shard_map.122
  2.8 0.0 copy-start.1
  2.8 0.0 copy-start.2
  2.8 35.4 %all_to_all.30.refs_0_ = bf16[16,512,128]{2,1,0:T(8,128)(2,1)S(1)} all-to-all(bf16[16,512,128]{2,1,0:T(8,128)(2,1)S(1)} %shard_map.122), channel_id=1, replica_groups=mesh['z'=16,'core'=2,'tensor'=16] {'tensor'}, dimensions={0} | all-to-all | bytes 4194304 | tf_op jit(solution)/shard_map/all_to_all | solution.py:38
  38.2 0.0 copy-done.1
  38.2 0.0 copy-done.2
  38.2 0.0 copy-start.7
  38.2 0.0 copy-start.24
  38.2 0.0 copy-start.26
  38.2 1.6 shard_map.123
  39.8 2.5 %collective-permute-start = (f32[256,128]{1,0:T(8,128)S(1)}, f32[256,128]{1,0:T(8,128)S(1)}, u32[]{:S(2)}, u32[]{:S(2)}) collective-permute-start(f32[256,128]{1,0:T(8,128)S(1)} %get-tuple-element.23.refs_0_), channel_id=1, source_target_pairs={{0,1},{1,0},{2,3},{3,2},{4,5},{5,4},{6,7},{7,6},{8,9},{9,8},{10,11... | collective-permute-start | bytes 393224 | tf_op jit(solution)/shard_map/ppermute | solution.py:25
  42.3 0.0 copy-done.29
  42.3 0.9 shard_map.124.refs_3_
  43.2 3.5 %collective-permute-done.refs_1_ = f32[256,128]{1,0:T(8,128)S(1)} collective-permute-done((f32[256,128]{1,0:T(8,128)S(1)}, f32[256,128]{1,0:T(8,128)S(1)}, u32[]{:S(2)}, u32[]{:S(2)}) %collective-permute-start) | collective-permute-done | bytes 131104 | tf_op jit(solution)/shard_map/ppermute | solution.py:25
  46.7 0.0 copy-done
  46.7 0.0 copy-done.24
  46.7 0.0 copy-start.20
  46.7 2.0 %shard_map.125 = (bf16[16,32,256]{2,1,0:T(8,128)(2,1)S(1)}, f32[896,128]{1,0:T(8,128)S(1)}) custom-call(f32[256,128]{1,0:T(8,128)S(1)} %get-tuple-element.23.refs_0_, f32[256,128]{1,0:T(8,128)S(1)} %collective-permute-done.refs_1_, f32[256,128]{1,0:T(8,128)S(1)} %get-tuple-element.24.refs_1_.refs_2_, f32[752,128]{1,0:T(8,128)S(1)} %shard_map.124.refs_3_, ...), custom_call_target="tpu_custom_call" | custom-call | tf_op jit(solution)/shard_map/pallas_call | solution.py:282
  48.7 0.0 copy-start.3
  48.7 0.8 copy-done.3
  49.4 0.7 copy-done.17
  50.2 4.2 %all-to-all-start.1 = ((bf16[16,32,256]{2,1,0:T(8,128)(2,1)}), bf16[16,32,256]{2,1,0:T(8,128)(2,1)}, u32[]{:S(2)}, u32[]{:S(2)}) async-start(bf16[16,32,256]{2,1,0:T(8,128)(2,1)} %copy-done.17), calls=%async_computation.1 | async-start | bytes 524288 | tf_op jit(solution)/shard_map/all_to_all | solution.py:38
  54.4 0.0 copy-start.4
  54.4 1.0 copy-done.4
  55.4 1.4 shard_map.129.refs_6_
  56.8 0.0 copy-start.21
  56.8 3.7 %collective-permute-start.1 = (bf16[128,4096]{1,0:T(8,128)(2,1)}, bf16[128,4096]{1,0:T(8,128)(2,1)S(1)}, u32[]{:S(2)}, u32[]{:S(2)}) collective-permute-start(bf16[128,4096]{1,0:T(8,128)(2,1)} %shard_map.129.refs_6_), channel_id=1, source_target_pairs={{0,1},{1,0},{2,3},{3,2},{4,5},{5,4},{6,7},{7,6},{8,9},{9,8},{10,11... | collective-permute-start | bytes 3145736 | tf_op jit(solution)/shard_map/ppermute | solution.py:25
  60.5 2.6 %all-to-all-done.1.refs_0_ = bf16[16,32,256]{2,1,0:T(8,128)(2,1)} async-done(((bf16[16,32,256]{2,1,0:T(8,128)(2,1)}), bf16[16,32,256]{2,1,0:T(8,128)(2,1)}, u32[]{:S(2)}, u32[]{:S(2)}) %all-to-all-start.1) | async-done | bytes 262176 | tf_op jit(solution)/shard_map/all_to_all | solution.py:38
  63.1 0.0 copy-done.20
  63.1 1.1 shard_map.126
  64.1 0.0 copy-start.13
  64.2 0.6 copy-done.13
  64.8 0.7 copy-done.16
  65.5 0.6 copy-done.22
  66.0 15.3 %all-to-all-start.2 = ((bf16[16,32,256]{2,1,0:T(8,128)(2,1)}), bf16[16,32,256]{2,1,0:T(8,128)(2,1)}, u32[]{:S(2)}, u32[]{:S(2)}) async-start(bf16[16,32,256]{2,1,0:T(8,128)(2,1)} %copy-done.16), calls=%async_computation.2 | async-start | bytes 524288 | tf_op jit(solution)/shard_map/all_to_all | solution.py:38
  81.4 0.0 copy-start.14
  81.4 0.7 copy-done.14
  82.2 1.4 shard_map.128
  83.6 1.0 copy-done.9
  84.6 1.0 copy-done.11
  85.6 0.0 copy-done.28
  85.6 0.4 shard_map.127
  86.0 0.0 collective-permute-done.1.refs_0_.refs_7_
  86.0 0.5 shard_map.130.refs_6_
  86.5 10.0 %all-to-all-done.2 = bf16[16,32,256]{2,1,0:T(8,128)(2,1)} async-done(((bf16[16,32,256]{2,1,0:T(8,128)(2,1)}), bf16[16,32,256]{2,1,0:T(8,128)(2,1)}, u32[]{:S(2)}, u32[]{:S(2)}) %all-to-all-start.2) | async-done | bytes 262176 | tf_op jit(solution)/shard_map/all_to_all | solution.py:38
  96.5 2.4 %all-gather = bf16[16,64,256]{2,1,0:T(8,128)(2,1)S(1)} all-gather(bf16[16,32,256]{2,1,0:T(8,128)(2,1)} %all-to-all-done.2), channel_id=2, replica_groups=mesh['z'=16,'core'=2,'tensor'=16] {'core'}, dimensions={1}, use_global_device_ids=true | all-gather | bytes 786432 | tf_op jit(solution)/shard_map/all_gather | solution.py:761
  98.9 0.0 copy-done.23
  98.9 2.8 %shard_map.131 = (bf16[16,304,128]{2,1,0:T(8,128)(2,1)S(1)}, bf16[1024,256]{1,0:T(8,128)(2,1)S(1)}) custom-call(bf16[1024,256]{1,0:T(8,128)(2,1)S(1)} %bitcast.9, bf16[256,1024]{1,0:T(8,128)(2,1)S(1)} %get-tuple-element.28.refs_1_.refs_4_, bf16[256,1024]{1,0:T(8,128)(2,1)S(1)} %get-tuple-element.29.refs_2_.refs_1_.refs_3_, ...), custom_call_target="tpu_custom_call" | custom-call | tf_op jit(solution)/shard_map/pallas_call | solution.py:282
  101.8 0.0 copy-start.15
  101.8 23.8 %all_to_all.31.refs_0_ = bf16[16,304,128]{2,1,0:T(8,128)(2,1)S(1)} all-to-all(bf16[16,304,128]{2,1,0:T(8,128)(2,1)S(1)} %get-tuple-element.34), channel_id=1, replica_groups=mesh['z'=16,'core'=2,'tensor'=16] {'tensor'}, dimensions={0} | all-to-all | bytes 2490368 | tf_op jit(solution)/shard_map/all_to_all | solution.py:38
  125.6 0.0 copy-start.27
  125.6 0.5 shard_map.132
  126.1 2.1 %all-gather.1 = f32[560,128]{1,0:T(8,128)S(1)} all-gather(f32[280,128]{1,0:T(8,128)S(1)} %get-tuple-element.35), channel_id=3, replica_groups=mesh['z'=16,'core'=2,'tensor'=16] {'core'}, dimensions={0}, use_global_device_ids=true | all-gather | bytes 430080 | tf_op jit(solution)/shard_map/all_gather | solution.py:363
  128.3 1.5 shard_map.133
  129.8 12.0 %all_to_all.32.refs_0_ = bf16[16,32,256]{2,1,0:T(8,128)(2,1)S(1)} all-to-all(bf16[16,32,256]{2,1,0:T(8,128)(2,1)S(1)} %get-tuple-element.38), channel_id=1, replica_groups=mesh['z'=16,'core'=2,'tensor'=16] {'tensor'}, dimensions={0} | all-to-all | bytes 524288 | tf_op jit(solution)/shard_map/all_to_all | solution.py:38
  141.8 0.0 copy-done.10
  141.8 4.7 %shard_map.134 = (bf16[16,512,128]{2,1,0:T(8,128)(2,1)S(1)}, f32[16,4096]{1,0:T(8,128)S(1)}) custom-call(bf16[16,32,256]{2,1,0:T(8,128)(2,1)S(1)} %all_to_all.32.refs_0_, bf16[4096,128]{1,0:T(8,128)(2,1)S(1)} %copy-done.12, f32[896,128]{1,0:T(8,128)S(1)} %copy-done.5, f32[752,128]{1,0:T(8,128)S(1)} %shard_map.124.refs_3_, f32[1,128]{1,0:T(1,128)S(1)} %bitcast.16, ...), custom_call_target="tpu_custom_call" | custom-call | tf_op jit(solution)/shard_map/pallas_call | solution.py:282
  146.6 0.0 copy-start.8
  146.6 0.0 copy-start.19
  146.6 30.8 %all_to_all.33.refs_0_ = bf16[16,512,128]{2,1,0:T(8,128)(2,1)S(1)} all-to-all(bf16[16,512,128]{2,1,0:T(8,128)(2,1)S(1)} %get-tuple-element.41), channel_id=1, replica_groups=mesh['z'=16,'core'=2,'tensor'=16] {'tensor'}, dimensions={0} | all-to-all | bytes 4194304 | tf_op jit(solution)/shard_map/all_to_all | solution.py:38
  177.4 1.4 shard_map.135
  (24 shorter events, 0.0 us)
Async XLA Ops:
  0.6 0.9 copy-start.6
  1.5 0.7 copy-start.18
  2.8 35.4 %copy-start.1 = (bf16[4096,128]{1,0:T(8,128)(2,1)S(1)}, bf16[4096,128]{1,0:T(8,128)(2,1)}, u32[]{:S(2)}) copy-start(bf16[4096,128]{1,0:T(8,128)(2,1)} %refs_0_.7) | copy-start | bytes 3145732
  2.8 35.4 %copy-start.2 = (bf16[4096,128]{1,0:T(8,128)(2,1)S(1)}, bf16[4096,128]{1,0:T(8,128)(2,1)}, u32[]{:S(2)}) copy-start(bf16[4096,128]{1,0:T(8,128)(2,1)} %refs_0_.6) | copy-start | bytes 3145732
  38.2 4.1 %copy-start.29 = (s32[1,32]{1,0:T(1,128)S(1)}, s32[1,32]{1,0:T(1,128)}, u32[]{:S(2)}) copy-start(s32[1,32]{1,0:T(1,128)} %refs_0_.5) | copy-start | bytes 388
  38.2 8.5 %copy-start = (bf16[128,4096]{1,0:T(8,128)(2,1)S(1)}, bf16[128,4096]{1,0:T(8,128)(2,1)}, u32[]{:S(2)}) copy-start(bf16[128,4096]{1,0:T(8,128)(2,1)} %refs_1_.4) | copy-start | bytes 3145732
  38.2 8.5 %copy-start.7 = (bf16[16,4096]{1,0:T(8,128)(2,1)S(1)}, bf16[16,4096]{1,0:T(8,128)(2,1)}, u32[]{:S(2)}) copy-start(bf16[16,4096]{1,0:T(8,128)(2,1)} %refs_1_.5) | copy-start | bytes 393220
  38.2 8.5 %copy-start.24 = (f32[128]{0:T(128)S(1)}, f32[128]{0:T(128)}, u32[]{:S(2)}) copy-start(f32[128]{0:T(128)} %param.18) | copy-start | bytes 1540
  38.2 8.5 %copy-start.26 = (f32[128]{0:T(128)S(1)}, f32[128]{0:T(128)}, u32[]{:S(2)}) copy-start(f32[128]{0:T(128)} %param.19) | copy-start | bytes 1540
  39.8 6.9 %collective-permute-start = (f32[256,128]{1,0:T(8,128)S(1)}, f32[256,128]{1,0:T(8,128)S(1)}, u32[]{:S(2)}, u32[]{:S(2)}) collective-permute-start(f32[256,128]{1,0:T(8,128)S(1)} %get-tuple-element.23.refs_0_), channel_id=1, source_target_pairs={{0,1},{1,0},{2,3},{3,2},{4,5},{5,4},{6,7},{7,6},{8,9},{9,8},{10,11... | collective-permute-start | bytes 393224 | tf_op jit(solution)/shard_map/ppermute | solution.py:25
  46.7 16.4 %copy-start.20 = (f32[4096]{0:T(1024)S(1)}, f32[4096]{0:T(1024)}, u32[]{:S(2)}) copy-start(f32[4096]{0:T(1024)} %param.21) | copy-start | bytes 49156
  48.7 0.8 copy-start.3
  49.4 0.7 copy-start.17
  50.2 12.9 %all-to-all-start.1 = ((bf16[16,32,256]{2,1,0:T(8,128)(2,1)}), bf16[16,32,256]{2,1,0:T(8,128)(2,1)}, u32[]{:S(2)}, u32[]{:S(2)}) async-start(bf16[16,32,256]{2,1,0:T(8,128)(2,1)} %copy-done.17), calls=%async_computation.1 | async-start | bytes 524288 | tf_op jit(solution)/shard_map/all_to_all | solution.py:38
  54.4 1.0 copy-start.4
  56.8 28.8 %copy-start.21 = (s32[256,7]{0,1:T(8,128)S(1)}, s32[256,7]{0,1:T(8,128)}, u32[]{:S(2)}) copy-start(s32[256,7]{0,1:T(8,128)} %param.14) | copy-start | bytes 21508
  56.8 29.2 %collective-permute-start.1 = (bf16[128,4096]{1,0:T(8,128)(2,1)}, bf16[128,4096]{1,0:T(8,128)(2,1)S(1)}, u32[]{:S(2)}, u32[]{:S(2)}) collective-permute-start(bf16[128,4096]{1,0:T(8,128)(2,1)} %shard_map.129.refs_6_), channel_id=1, source_target_pairs={{0,1},{1,0},{2,3},{3,2},{4,5},{5,4},{6,7},{7,6},{8,9},{9,8},{10,11... | collective-permute-start | bytes 3145736 | tf_op jit(solution)/shard_map/ppermute | solution.py:25
  64.1 0.6 copy-start.13
  64.8 0.7 copy-start.16
  65.5 0.6 copy-start.22
  66.0 19.5 %copy-start.28 = (s32[256]{0:T(256)S(1)}, s32[256]{0:T(256)}, u32[]{:S(2)}) copy-start(s32[256]{0:T(256)} %param.13) | copy-start | bytes 3076
  66.0 30.5 %all-to-all-start.2 = ((bf16[16,32,256]{2,1,0:T(8,128)(2,1)}), bf16[16,32,256]{2,1,0:T(8,128)(2,1)}, u32[]{:S(2)}, u32[]{:S(2)}) async-start(bf16[16,32,256]{2,1,0:T(8,128)(2,1)} %copy-done.16), calls=%async_computation.2 | async-start | bytes 524288 | tf_op jit(solution)/shard_map/all_to_all | solution.py:38
  81.4 17.5 %copy-start.23 = (f32[1,256]{1,0:T(1,128)S(1)}, f32[1,256]{1,0:T(1,128)}, u32[]{:S(2)}) copy-start(f32[1,256]{1,0:T(1,128)} %copy-done.22) | copy-start | bytes 3076
  81.4 0.8 copy-start.14
  83.6 1.0 copy-start.9
  84.6 1.0 copy-start.11
  101.8 26.5 %copy-start.15 = (f32[32,256]{1,0:T(8,128)S(1)}, f32[32,256]{1,0:T(8,128)}, u32[]{:S(2)}) copy-start(f32[32,256]{1,0:T(8,128)} %copy-done.13) | copy-start | bytes 98308
  125.6 16.2 %copy-start.5 = (f32[896,128]{1,0:T(8,128)S(1)}, f32[896,128]{1,0:T(8,128)}, u32[]{:S(2)}) copy-start(f32[896,128]{1,0:T(8,128)} %copy-done.3) | copy-start | bytes 1376260
  125.6 16.2 %copy-start.10 = (bf16[128,4096]{1,0:T(8,128)(2,1)S(1)}, bf16[128,4096]{1,0:T(8,128)(2,1)}, u32[]{:S(2)}) copy-start(bf16[128,4096]{1,0:T(8,128)(2,1)} %copy-done.9) | copy-start | bytes 3145732
  125.6 16.2 %copy-start.12 = (bf16[4096,128]{1,0:T(8,128)(2,1)S(1)}, bf16[4096,128]{1,0:T(8,128)(2,1)}, u32[]{:S(2)}) copy-start(bf16[4096,128]{1,0:T(8,128)(2,1)} %copy-done.11) | copy-start | bytes 3145732
  125.6 16.2 %copy-start.25 = (f32[128]{0:T(128)S(1)}, f32[128]{0:T(128)}, u32[]{:S(2)}) copy-start(f32[128]{0:T(128)} %param.18) | copy-start | bytes 1540
  125.6 16.2 %copy-start.27 = (f32[128]{0:T(128)S(1)}, f32[128]{0:T(128)}, u32[]{:S(2)}) copy-start(f32[128]{0:T(128)} %param.19) | copy-start | bytes 1540
  146.6 30.8 %copy-start.8 = (bf16[16,4096]{1,0:T(8,128)(2,1)S(1)}, bf16[16,4096]{1,0:T(8,128)(2,1)}, u32[]{:S(2)}) copy-start(bf16[16,4096]{1,0:T(8,128)(2,1)} %refs_1_.5) | copy-start | bytes 393220
  146.6 30.8 %copy-start.19 = (f32[4096]{0:T(1024)S(1)}, f32[4096]{0:T(1024)}, u32[]{:S(2)}) copy-start(f32[4096]{0:T(1024)} %param.15) | copy-start | bytes 49156

commit v6 on v5

--- a/solution.py
+++ b/solution.py
@@ -40,7 +40,7 @@
 
 def halves(value):
     high = value.astype(jnp.bfloat16).astype(jnp.float32)
-    return jnp.concatenate([high, value - high], axis=0)
+    return high, value - high
 
 
 def iota(shape, axis):
@@ -54,23 +54,51 @@
         out_ref[k : k + 1, :] = jnp.sum(block, axis=0, keepdims=True)
 
 
-def own_core_lanes():
-    return pl.ds(pl.multiple_of(lax.axis_index("core") * LANES, LANES), LANES)
+HALF = LANES // 2
+
+
+def query_block():
+    return lax.axis_index("z_pair"), lax.axis_index("core")
+
+
+def block_lanes(block):
+    return pl.ds(pl.multiple_of(block * LANES, LANES), LANES)
+
+
+def in_first_half(shape):
+    return iota(shape, len(shape) - 1) < HALF
+
+
+def fold_half(first, second, half):
+    is_first = in_first_half(first.shape)
+    low = jnp.where(is_first, first, pltpu.roll(second, HALF, 1))
+    high = jnp.where(is_first, pltpu.roll(first, HALF, 1), second)
+    return jnp.where(half == 0, low, high)
+
+
+def unfold_half(block):
+    return block, pltpu.roll(block, HALF, 1)
+
+
+def own_columns(gains_ref, width):
+    start = pl.multiple_of(lax.axis_index("tensor") * width, width)
+    return gains_ref[:, pl.ds(start, width)]
 
 
 def partial_logits_kernel(
-    rows_ref, query_hot_ref, positive_hot_ref, listed_all_ref, gain_ref, out_ref, rows_out_ref, held_ref
+    rows_ref, query_hot_ref, positive_hot_ref, listed_all_ref, gains_ref, out_ref, rows_out_ref, held_ref
 ):
     rows = rows_ref[...]
     rows_out_ref[...] = rows
-    listed_ref = listed_all_ref[:8, own_core_lanes()]
-    core_hot = query_hot_ref[own_core_lanes(), :]
-    queries = jnp.dot(core_hot, rows, preferred_element_type=jnp.float32)
+    query_at, half = query_block()
+    listed_ref = listed_all_ref[:8, block_lanes(query_at)]
+    block_hot = query_hot_ref[block_lanes(query_at), :]
+    queries = jnp.dot(block_hot, rows, preferred_element_type=jnp.float32)
     positives = jnp.dot(positive_hot_ref[...], rows, preferred_element_type=jnp.float32)
     queries = queries.astype(jnp.bfloat16)
-    features = gain_ref.shape[1] * out_ref.shape[0]
+    features = gains_ref.shape[1]
     rows32 = rows.astype(jnp.float32)
-    plain = rows32 / gain_ref[...]
+    plain = rows32 / own_columns(gains_ref, rows.shape[1])
     squares = jnp.sum(rows32 * rows32, axis=1, keepdims=True) + jnp.sum(
         plain * plain, axis=1, keepdims=True
     ) * (EPSILON / features)
@@ -87,14 +115,15 @@
             jnp.where(listed, squares, 0.0), axis=0, keepdims=True
         )
     columns_to_lanes(squares, held_ref.at[16:24])
-    count = with_positives.shape[0]
-    sent = [with_positives.astype(jnp.bfloat16)]
-    for start in (0, 8, 16):
-        sent.append(halves(held_ref[start : start + 8, :]).astype(jnp.bfloat16))
+    count = with_positives.shape[0] // 2
+    sent = fold_half(with_positives[:count], with_positives[count:], half).astype(jnp.bfloat16)
+    high, low = halves(held_ref[0:16, :])
+    listed16 = fold_half(high, low, half).astype(jnp.bfloat16)
+    squares16 = jnp.concatenate(halves(held_ref[16:24, :])).astype(jnp.bfloat16)
     for t in range(out_ref.shape[0]):
-        out_ref[t, :count, :] = sent[0]
-        for k in range(3):
-            out_ref[t, count + 16 * k : count + 16 * (k + 1), :] = sent[k + 1]
+        out_ref[t, :count, :] = sent
+        out_ref[t, count : count + 16, :] = listed16
+        out_ref[t, count + 16 : count + 32, :] = squares16
 
 
 def softmax_kernel(arrived_ref, positive_hot_ref, out_ref, inverse_ref):
@@ -102,13 +131,19 @@
     summed = arrived_ref[0].astype(jnp.float32)
     for t in range(1, arrived_ref.shape[0]):
         summed = summed + arrived_ref[t].astype(jnp.float32)
-
-    def small(k):
-        block = summed[count + 16 * k : count + 16 * (k + 1)]
-        return block[:8] + block[8:]
-
-    inverse_listed = lax.rsqrt(small(1) + EPSILON * EPSILON)
-    inverse = lax.rsqrt(small(2) + EPSILON * EPSILON)
+    query_at, half = query_block()
+    first_query = query_at * LANES + half * HALF
+    start = count // 2
+    with_positives = jnp.concatenate(unfold_half(summed[:start]), axis=0)
+    high, low = unfold_half(summed[start : start + 16])
+    hard, listed_squares = high[:8] + low[:8], high[8:] + low[8:]
+    squares = summed[start + 16 : start + 24] + summed[start + 24 : start + 32]
+
+    def valid(value, other):
+        return jnp.where(in_first_half(value.shape), value, other)
+
+    inverse_listed = lax.rsqrt(valid(listed_squares, 1.0) + EPSILON * EPSILON)
+    inverse = lax.rsqrt(squares + EPSILON * EPSILON)
     inverse_ref[...] = inverse
     inverse_query = inverse_listed[7:8, :]
     picked = jnp.zeros((count, LANES), jnp.float32)
@@ -116,11 +151,12 @@
         hot = positive_hot_ref[:, LANES * k : LANES * (k + 1)].astype(jnp.float32)
         picked = picked + hot * inverse[k : k + 1, :]
     inverse_positive = jnp.sum(picked, axis=1, keepdims=True)
-    logits = summed[:count] * inverse_positive * inverse_query / SOFTMAX_TEMPER
-    hard = small(0) * inverse_listed * inverse_query / SOFTMAX_TEMPER
+    logits = valid(with_positives, 0.0) * inverse_positive * inverse_query / SOFTMAX_TEMPER
+    hard = valid(hard, 0.0) * inverse_listed * inverse_query / SOFTMAX_TEMPER
     is_hard = iota(hard.shape, 0) < 7
-    is_own = iota(logits.shape, 0) == iota(logits.shape, 1) + lax.axis_index("core") * LANES
-    weights = jnp.exp(logits - 1.0 / SOFTMAX_TEMPER)
+    is_own = iota(logits.shape, 0) == iota(logits.shape, 1) + first_query
+    is_own = is_own & in_first_half(logits.shape)
+    weights = valid(jnp.exp(logits - 1.0 / SOFTMAX_TEMPER), 1.0)
     hard_weights = jnp.where(is_hard, jnp.exp(hard - 1.0 / SOFTMAX_TEMPER), 0.0)
     totals = jnp.sum(weights, axis=0, keepdims=True) + jnp.sum(hard_weights, axis=0, keepdims=True)
     target = jnp.sum(jnp.where(is_own, logits, 0.0), axis=0, keepdims=True)
@@ -132,16 +168,22 @@
 
     coef = rounded(scaling_factor * (weights / totals - is_own.astype(jnp.float32)))
     hard_coef = rounded(scaling_factor * (hard_weights / totals))
-    weighted = coef * logits * SOFTMAX_TEMPER
+    weighted = valid(coef * logits * SOFTMAX_TEMPER, 0.0)
     hard_weighted = jnp.where(is_hard, hard_coef * hard * SOFTMAX_TEMPER, 0.0)
     along_query = jnp.sum(weighted, axis=0, keepdims=True) + jnp.sum(
         hard_weighted, axis=0, keepdims=True
     )
-    out_ref[:count, :] = coef
-    out_ref[count : count + 8, :] = jnp.where(is_hard, hard_coef, along_query)
-    out_ref[count + 8 : count + 16, :] = jnp.where(is_hard, hard_weighted, losses)
-    out_ref[count + 16 :, :] = jnp.zeros_like(out_ref[count + 16 :, :])
-    columns_to_lanes(jnp.sum(weighted, axis=1, keepdims=True), out_ref.at[count + 16 :])
+    folded_coef = fold_half(coef[:start], coef[start:], 0)
+    folded_hard = fold_half(
+        jnp.where(is_hard, hard_coef, along_query), jnp.where(is_hard, hard_weighted, losses), 0
+    )
+    for k in range(out_ref.shape[0]):
+        out_ref[k, :start, :] = folded_coef
+        out_ref[k, start : start + 8, :] = folded_hard
+        out_ref[k, start + 8 :, :] = jnp.zeros_like(out_ref[k, start + 8 :, :])
+        columns_to_lanes(
+            jnp.sum(weighted, axis=1, keepdims=True), out_ref.at[k, start + 8 : start + 16]
+        )
 
 
 def resid_grad_kernel(
@@ -152,25 +194,32 @@
     query_hot_ref,
     listed_ref,
     resid_ref,
-    gain_ref,
+    gains_ref,
     out_ref,
     loss_ref,
 ):
     sequences = resid_ref.shape[0]
     count, total_rows = positive_hot_ref.shape
-    group = lax.axis_index("z") * lax.axis_size("core") + lax.axis_index("core")
+    z = lax.axis_index("z_far") * lax.axis_size("z_pair") + lax.axis_index("z_pair")
+    group = z * lax.axis_size("core") + lax.axis_index("core")
     first_row = group * sequences
     first_query = group * QDEV
     across = (((1,), (1,)), ((), ()))
 
     def joined(start, stop):
-        return jnp.concatenate([both_ref[0, start:stop, :], both_ref[1, start:stop, :]], axis=1)
-
-    coef = joined(0, count)
-    coef16 = coef.astype(jnp.bfloat16)
-    hard = joined(count, count + 8)
-    hard_weighted = joined(count + 8, count + 16)
-    along_passage = both_ref[0, count + 16 : count + 24, :] + both_ref[1, count + 16 : count + 24, :]
+        firsts, seconds = [], []
+        for k in (0, 2):
+            first, second = both_ref[k, start:stop, :], both_ref[k + 1, start:stop, :]
+            firsts.append(fold_half(first, second, 0))
+            seconds.append(fold_half(pltpu.roll(first, HALF, 1), pltpu.roll(second, HALF, 1), 0))
+        return jnp.concatenate(firsts, axis=1), jnp.concatenate(seconds, axis=1)
+
+    start = count // 2
+    coef16 = jnp.concatenate(joined(0, start), axis=0).astype(jnp.bfloat16)
+    hard, hard_weighted = joined(start, start + 8)
+    along_passage = both_ref[0, start + 8 : start + 16, :]
+    for k in range(1, both_ref.shape[0]):
+        along_passage = along_passage + both_ref[k, start + 8 : start + 16, :]
     along_passage = jnp.concatenate([along_passage[0:1], along_passage[1:2]], axis=1)
     inverse = jnp.concatenate([inverse_ref[k : k + 1, :] for k in range(8)], axis=1)
 
@@ -219,8 +268,8 @@
     is_own_row = row_index == first_row + iota((sequences, total_rows), 0)
     own_inverse = jnp.sum(jnp.where(is_own_row, inverse, 0.0), axis=1, keepdims=True)
     resid = resid_ref[...]
-    gain = gain_ref[...]
-    features = gain.shape[1] * out_ref.shape[0]
+    gain = own_columns(gains_ref, resid.shape[1])
+    features = gains_ref.shape[1]
     d_resid = own_inverse * gain * (
         d_embed - resid * gain * own_inverse * along
     ) - resid * (along * own_inverse * own_inverse * (EPSILON / features))
@@ -334,19 +383,25 @@
         refs[-1][0] = jnp.float32(0.0)
 
 
-def token_kernel(out_ref):
-    out_ref[0] = jnp.float32(0.0)
-
-
-def contrast(everyone, resid, gain, tables, after):
+def stack_kernel(first_ref, second_ref, out_ref, token_ref):
+    rows = first_ref.shape[0]
+    out_ref[:rows, :] = first_ref[...]
+    out_ref[rows:, :] = second_ref[...]
+    token_ref[0] = jnp.float32(0.0)
+
+
+def contrast(everyone, resid, gains, tables, after):
     tensor_count = lax.axis_size("tensor")
     sequences, width = resid.shape
     listed, query_hot, positive_hot = tables
     count, total_rows = positive_hot.shape
     sent, rows = kernel_call(
         partial_logits_kernel,
-        [((tensor_count, count + 48, LANES), jnp.bfloat16), ((total_rows, width), jnp.bfloat16)],
-        [everyone.reshape(total_rows, width), query_hot, positive_hot, listed, gain],
+        [
+            ((tensor_count, count // 2 + 32, LANES), jnp.bfloat16),
+            ((total_rows, width), jnp.bfloat16),
+        ],
+        [everyone.reshape(total_rows, width), query_hot, positive_hot, listed, gains],
         near=(0,),
         near_outs=(0,),
         after=after,
@@ -355,16 +410,16 @@
     arrived = exchange(sent, "tensor")
     coefs, inverse = kernel_call(
         softmax_kernel,
-        [((count + 24, LANES), jnp.float32), ((8, LANES), jnp.float32)],
+        [((4, count // 2 + 16, LANES), jnp.float32), ((8, LANES), jnp.float32)],
         [arrived, positive_hot],
         near=(0,),
         near_outs=(0,),
     )
-    both = lax.all_gather(coefs, "core", axis=0)
+    both = exchange(coefs, ("z_pair", "core"))
     d_resid16, loss = kernel_call(
         resid_grad_kernel,
         [((tensor_count, sequences, width), jnp.bfloat16), ((1,), jnp.float32)],
-        [both, inverse, rows, positive_hot, query_hot, listed, resid, gain],
+        [both, inverse, rows, positive_hot, query_hot, listed, resid, gains],
         near=(0,),
         near_outs=(0,),
     )
@@ -483,11 +538,8 @@
     saved_ref[to["probs"], :] = folded(probs)
 
 
-def resid_kernel(arrived_ref, gains_ref, resid_ref, out_ref, gain_ref):
-    chunk = resid_ref.shape[1]
-    start = pl.multiple_of(lax.axis_index("tensor") * chunk, chunk)
-    gain = gains_ref[:, pl.ds(start, chunk)]
-    gain_ref[...] = gain
+def resid_kernel(arrived_ref, gains_ref, resid_ref, out_ref):
+    gain = own_columns(gains_ref, resid_ref.shape[1])
     resid = arrived_ref[0].astype(jnp.float32)
     for t in range(1, arrived_ref.shape[0]):
         resid = resid + arrived_ref[t].astype(jnp.float32)
@@ -504,8 +556,7 @@
     layout_ref,
     q_gain_ref,
     k_gain_ref,
-    own_weights_ref,
-    other_weights_ref,
+    both_weights_ref,
     query_weights_ref,
     out_ref,
     added_ref,
@@ -554,8 +605,9 @@
 
     d_key = head_gradient(d_key_rot, "key", k_gain_ref[...])
     d_query = head_gradient(d_query_rot, "query", q_gain_ref[...])
-    own16 = jnp.where(is_even, d_key, d_value).astype(jnp.bfloat16)
-    other16 = jnp.where(is_even, d_value, d_key).astype(jnp.bfloat16)
+    own_other16 = jnp.concatenate(
+        [jnp.where(is_even, d_key, d_value), jnp.where(is_even, d_value, d_key)], axis=1
+    ).astype(jnp.bfloat16)
     spread16 = lax.dot_general(
         unfolded(layout_ref[at["chosen"], :], sequences).astype(jnp.bfloat16),
         d_query.astype(jnp.bfloat16),
@@ -567,9 +619,8 @@
     for t in range(added_ref.shape[1] // chunk):
         columns = slice(t * chunk, (t + 1) * chunk)
         added_ref[:, columns] = jnp.dot(last, d_resid_ref[t], preferred_element_type=jnp.float32)
-        term = jnp.dot(own16, own_weights_ref[:, columns], preferred_element_type=jnp.float32)
-        term = term + jnp.dot(
-            other16, other_weights_ref[:, columns], preferred_element_type=jnp.float32
+        term = jnp.dot(
+            own_other16, both_weights_ref[:, columns], preferred_element_type=jnp.float32
         )
         term = term + jnp.dot(
             spread16, query_weights_ref[:, columns], preferred_element_type=jnp.float32
@@ -643,7 +694,8 @@
     return jnp.concatenate(parts, axis=1)
 
 
-def sequence_kernel(lengths_ref, out_ref, *, tokens_count, own_rows):
+def sequence_kernel(lengths_ref, out_ref, token_ref, *, tokens_count, own_rows):
+    token_ref[0] = jnp.float32(0.0)
     sequences = lengths_ref.shape[1]
     at, _ = layout_rows(tokens_count, sequences, own_rows)
     lengths = lengths_ref[...].astype(jnp.float32)
@@ -688,7 +740,8 @@
 def on_device(
     hidden, lengths, positives, negatives, in_gain, wq, wkv, q_gain, k_gain, wo, out_gain
 ):
-    tensor_count, z_count = lax.axis_size("tensor"), lax.axis_size("z")
+    tensor_count = lax.axis_size("tensor")
+    z_count = lax.axis_size("z_far") * lax.axis_size("z_pair")
     own_rows, features = hidden.shape
     tokens_count = own_rows * tensor_count
     head_width = wq.shape[1]
@@ -714,12 +767,15 @@
         near_outs=(0,),
     )
     kv_other = swapped(kv_own, "tensor", 0)
-    (layout,) = kernel_call(
-        functools.partial(sequence_kernel, tokens_count=tokens_count, own_rows=own_rows),
-        [((layout_rows(tokens_count, sequences, own_rows)[1], LANES), f32)],
-        [lengths],
-        after=[query_all],
-    )
+    def sequence_layout(after):
+        return kernel_call(
+            functools.partial(sequence_kernel, tokens_count=tokens_count, own_rows=own_rows),
+            [((layout_rows(tokens_count, sequences, own_rows)[1], LANES), f32), ((1,), f32)],
+            [lengths],
+            after=[after],
+        )
+
+    layout, _ = sequence_layout(query_all)
     blocks, saved = kernel_call(
         attention_kernel,
         [
@@ -734,10 +790,11 @@
         transpose_kernel, [(weights_shape, bf16)], [wkv], after=[saved]
     )
     other_weights = swapped(own_weights, "tensor", 0)
-    resid, scaled, own_gain = kernel_call(
+    output_gain = out_gain[None, :]
+    resid, scaled = kernel_call(
         resid_kernel,
-        [((sequences, chunk), f32), ((z_count, sequences, chunk), bf16), ((1, chunk), f32)],
-        [exchange(blocks, "tensor"), out_gain[None, :]],
+        [((sequences, chunk), f32), ((z_count, sequences, chunk), bf16)],
+        [exchange(blocks, "tensor"), output_gain],
         near=(0,),
         near_outs=(1,),
     )
@@ -747,7 +804,12 @@
         [wq, wo],
         after=[resid],
     )
-    (fetched,) = kernel_call(token_kernel, [((1,), f32)], [], after=[other_weights])
+    both_weights, fetched = kernel_call(
+        stack_kernel,
+        [((2 * head_width, features), bf16), ((1,), f32)],
+        [own_weights, other_weights],
+    )
+    layout_again, placed = sequence_layout(resid)
     tables = kernel_call(
         candidate_kernel,
         [
@@ -758,9 +820,9 @@
         [positives[None, :], negatives.T],
         after=[resid],
     )
-    everyone = lax.all_gather(exchange(scaled, "z"), "core", axis=1)
+    everyone = lax.all_gather(exchange(scaled, ("z_far", "z_pair")), "core", axis=1)
     loss, d_resid16 = contrast(
-        everyone, resid, own_gain, tables, [transposed, fetched]
+        everyone, resid, output_gain, tables, [transposed, fetched, placed]
     )
     product, added = kernel_call(
         gradient_kernel,
@@ -769,10 +831,9 @@
             d_resid16,
             wo_t,
             saved,
-            layout,
+            layout_again,
             *gain_rows,
-            own_weights,
-            other_weights,
+            both_weights,
             query_weights,
         ],
         near=(0,),
@@ -790,12 +851,12 @@
 
 def solution(mesh):
     z_count = mesh.shape["dp"] // 2
-    chips = mesh.devices.reshape(z_count, 2, mesh.shape["tensor"])
-    mesh = jax.sharding.Mesh(chips, ("z", "core", "tensor"))
-    everywhere = P(("z", "core", "tensor"), None)
+    chips = mesh.devices.reshape(z_count // 2, 2, 2, mesh.shape["tensor"])
+    mesh = jax.sharding.Mesh(chips, ("z_far", "z_pair", "core", "tensor"))
+    everywhere = P(("z_far", "z_pair", "core", "tensor"), None)
     placed = (
         everywhere,
-        P(("z", "core"), None),
+        P(("z_far", "z_pair", "core"), None),
         P(),
         P(),
         P(),

time: 180 us -> 177 us (0.983)
  the two profiles are of different devices: /device:TPU:32 before, /device:TPU:2 now
where the time goes in v6:
time: 177 us; the launch traced here: 176 us
  blocking collectives  107 us (60%)
  starting transfers between devices  25.2 us (14%)
  Pallas kernels  20.2 us (11%)
  local copies, waits for them, and re-layouts  12.9 us (7%)
  waiting for transfers between devices  9.61 us (5%)
    all_to_all x5, blocking collectives, exchange(): return lax.all_to_all(blocks, axis, 0, 0, tiled=True)  104 us
    pallas_call x15, Pallas kernels, kernel_call(): pl.pallas_call(kernel, out_shape=[jax.ShapeDtypeStruct(shape, dtype) for...  20.2 us
    all_to_all x2, starting transfers between devices, exchange(): return lax.all_to_all(blocks, axis, 0, 0, tiled=True)  19.5 us
    unnamed x68, local copies, waits for them, and re-layouts  12.9 us
    all_to_all x2, waiting for transfers between devices, exchange(): return lax.all_to_all(blocks, axis, 0, 0, tiled=True)  7.77 us
    ppermute x2, starting transfers between devices, swapped(): return lax.ppermute(value, axis, pairs)  5.72 us
  transfers between devices with their start and end apart: 4, of which 3 were waited for; matrix products, arithmetic and copies ran while one was open for 0% of the time, Pallas kernels for 4%

profile of v6, /device:TPU:2, one launch (start us, length us, event | category | flops | bytes accessed | tf_op | source)
XLA Modules:
  0.0 175.6 jit_solution(4908222313380075545)
XLA Ops:
  0.6 0.0 copy-start.9
  0.6 0.9 copy-done.9
  1.5 0.7 copy-done.24
  2.3 0.5 shard_map.122
  2.8 0.0 copy-start.1
  2.8 0.0 copy-start.2
  2.8 35.0 %all_to_all.35.refs_0_ = bf16[16,512,128]{2,1,0:T(8,128)(2,1)S(1)} all-to-all(bf16[16,512,128]{2,1,0:T(8,128)(2,1)S(1)} %shard_map.122), channel_id=1, replica_groups=mesh['z_far'=8,'z_pair'=2,'core'=2,'tensor'=16] {'tensor'}, dimensions={0} | all-to-all | bytes 4194304 | tf_op jit(solution)/shard_map/all_to_all | solution.py:38
  37.8 0.0 copy-start.10
  37.8 0.0 copy-start.29
  37.8 0.0 copy-start.31
  37.8 1.6 shard_map.123
  39.4 3.6 %collective-permute-start = (f32[256,128]{1,0:T(8,128)S(1)}, f32[256,128]{1,0:T(8,128)S(1)}, u32[]{:S(2)}, u32[]{:S(2)}) collective-permute-start(f32[256,128]{1,0:T(8,128)S(1)} %get-tuple-element.27.refs_0_), channel_id=1, source_target_pairs={{0,1},{1,0},{2,3},{3,2},{4,5},{5,4},{6,7},{7,6},{8,9},{9,8},{10,11... | collective-permute-start | bytes 393224 | tf_op jit(solution)/shard_map/ppermute | solution.py:25
  43.0 0.0 copy-done.27
  43.0 1.4 shard_map.124
  44.4 1.8 %collective-permute-done.refs_1_ = f32[256,128]{1,0:T(8,128)S(1)} collective-permute-done((f32[256,128]{1,0:T(8,128)S(1)}, f32[256,128]{1,0:T(8,128)S(1)}, u32[]{:S(2)}, u32[]{:S(2)}) %collective-permute-start) | collective-permute-done | bytes 131104 | tf_op jit(solution)/shard_map/ppermute | solution.py:25
  46.3 0.0 copy-done.10
  46.3 0.0 copy-start.23
  46.3 2.0 %shard_map.125 = (bf16[16,32,256]{2,1,0:T(8,128)(2,1)S(1)}, f32[896,128]{1,0:T(8,128)S(1)}) custom-call(f32[256,128]{1,0:T(8,128)S(1)} %get-tuple-element.27.refs_0_, f32[256,128]{1,0:T(8,128)S(1)} %collective-permute-done.refs_1_, f32[256,128]{1,0:T(8,128)S(1)} %get-tuple-element.28.refs_1_.refs_2_, f32[752,128]{1,0:T(8,128)S(1)} %get-tuple-element.29.refs_3_, ...), custom_call_target="tpu_custom_call" | custom-call | tf_op jit(solution)/shard_map/pallas_call | solution.py:331
  48.3 0.8 copy-done.6
  49.1 0.7 copy-done.22
  49.8 5.0 %all-to-all-start.1 = ((bf16[16,32,256]{2,1,0:T(8,128)(2,1)}), bf16[16,32,256]{2,1,0:T(8,128)(2,1)S(1)}, u32[]{:S(2)}, u32[]{:S(2)}) async-start(bf16[16,32,256]{2,1,0:T(8,128)(2,1)} %copy-done.22), calls=%async_computation.1 | async-start | bytes 524288 | tf_op jit(solution)/shard_map/all_to_all | solution.py:38
  54.8 1.0 copy-done.7
  55.8 0.5 shard_map.129.refs_0_
  56.3 2.1 %collective-permute-start.1 = (bf16[128,4096]{1,0:T(8,128)(2,1)S(1)}, bf16[128,4096]{1,0:T(8,128)(2,1)S(1)}, u32[]{:S(2)}, u32[]{:S(2)}) collective-permute-start(bf16[128,4096]{1,0:T(8,128)(2,1)S(1)} %shard_map.129.refs_0_), channel_id=1, source_target_pairs={{0,1},{1,0},{2,3},{3,2},{4,5},{5,4},{6,7},{7,6},{8,9},{9,8},{10,11... | collective-permute-start | bytes 3145736 | tf_op jit(solution)/shard_map/ppermute | solution.py:25
  58.4 5.1 %all-to-all-done.1.refs_0_ = bf16[16,32,256]{2,1,0:T(8,128)(2,1)S(1)} async-done(((bf16[16,32,256]{2,1,0:T(8,128)(2,1)}), bf16[16,32,256]{2,1,0:T(8,128)(2,1)S(1)}, u32[]{:S(2)}, u32[]{:S(2)}) %all-to-all-start.1) | async-done | bytes 262176 | tf_op jit(solution)/shard_map/all_to_all | solution.py:38
  63.5 0.0 copy-done.23
  63.5 0.1 shard_map.126
  63.7 0.0 copy-start.15
  63.7 0.6 copy-done.15
  64.3 0.7 copy-done.21
  65.0 14.5 %all-to-all-start.2 = ((bf16[16,32,256]{2,1,0:T(8,128)(2,1)}), bf16[16,32,256]{2,1,0:T(8,128)(2,1)}, u32[]{:S(2)}, u32[]{:S(2)}) async-start(bf16[16,32,256]{2,1,0:T(8,128)(2,1)} %copy-done.21), calls=%async_computation.2 | async-start | bytes 524288 | tf_op jit(solution)/shard_map/all_to_all | solution.py:38
  79.4 0.0 copy-start.16
  79.5 0.7 copy-done.16
  80.2 0.7 copy-done.28
  80.9 1.4 shard_map.131
  82.3 0.0 copy-start.19
  82.3 0.7 copy-done.19
  83.0 1.2 copy-done.3
  84.3 0.8 copy-done.17
  85.0 1.4 shard_map.128
  86.5 0.9 copy-done.11
  87.4 1.0 copy-done.13
  88.4 0.0 copy-done.26
  88.4 0.4 shard_map.127
  88.8 0.0 collective-permute-done.1.refs_1_
  88.8 1.0 shard_map.130
  89.8 1.3 copy-done.4
  91.1 2.7 %all-to-all-done.2 = bf16[16,32,256]{2,1,0:T(8,128)(2,1)} async-done(((bf16[16,32,256]{2,1,0:T(8,128)(2,1)}), bf16[16,32,256]{2,1,0:T(8,128)(2,1)}, u32[]{:S(2)}, u32[]{:S(2)}) %all-to-all-start.2) | async-done | bytes 262176 | tf_op jit(solution)/shard_map/all_to_all | solution.py:38
  93.8 2.4 %all-gather = bf16[16,64,256]{2,1,0:T(8,128)(2,1)S(1)} all-gather(bf16[16,32,256]{2,1,0:T(8,128)(2,1)} %all-to-all-done.2), channel_id=2, replica_groups=mesh['z_far'=8,'z_pair'=2,'core'=2,'tensor'=16] {'core'}, dimensions={1}, use_global_device_ids=true | all-gather | bytes 786432 | tf_op jit(solution)/shard_map/all_gather | solution.py:823
  96.2 3.5 %shard_map.132 = (bf16[16,160,128]{2,1,0:T(8,128)(2,1)S(1)}, bf16[1024,256]{1,0:T(8,128)(2,1)S(1)}) custom-call(bf16[1024,256]{1,0:T(8,128)(2,1)S(1)} %bitcast.8, bf16[256,1024]{1,0:T(8,128)(2,1)S(1)} %get-tuple-element.33.refs_1_.refs_4_, bf16[256,1024]{1,0:T(8,128)(2,1)S(1)} %get-tuple-element.34.refs_2_.refs_1_.refs_3_, ...), custom_call_target="tpu_custom_call" | custom-call | tf_op jit(solution)/shard_map/pallas_call | solution.py:331
  99.7 0.0 copy-start.14
  99.7 18.2 %all_to_all.36.refs_0_ = bf16[16,160,128]{2,1,0:T(8,128)(2,1)S(1)} all-to-all(bf16[16,160,128]{2,1,0:T(8,128)(2,1)S(1)} %get-tuple-element.40), channel_id=1, replica_groups=mesh['z_far'=8,'z_pair'=2,'core'=2,'tensor'=16] {'tensor'}, dimensions={0} | all-to-all | bytes 1310720 | tf_op jit(solution)/shard_map/all_to_all | solution.py:38
  117.9 0.0 copy-start.30
  118.0 0.0 copy-start.32
  118.0 0.6 shard_map.133
  118.5 8.9 %all_to_all.37.refs_0_ = f32[4,144,128]{2,1,0:T(8,128)S(1)} all-to-all(f32[4,144,128]{2,1,0:T(8,128)S(1)} %get-tuple-element.41), channel_id=1, replica_groups=mesh['z_far'=8,'z_pair'=2,'core'=2,'tensor'=16] {'z_pair','core'}, dimensions={0} | all-to-all | bytes 589824 | tf_op jit(solution)/shard_map/all_to_all | solution.py:38
  127.4 0.0 copy-done.18
  127.4 1.3 shard_map.134
  128.7 11.9 %all_to_all.38.refs_0_ = bf16[16,32,256]{2,1,0:T(8,128)(2,1)S(1)} all-to-all(bf16[16,32,256]{2,1,0:T(8,128)(2,1)S(1)} %get-tuple-element.44), channel_id=1, replica_groups=mesh['z_far'=8,'z_pair'=2,'core'=2,'tensor'=16] {'tensor'}, dimensions={0} | all-to-all | bytes 524288 | tf_op jit(solution)/shard_map/all_to_all | solution.py:38
  140.6 0.0 copy-done.8
  140.6 3.2 %shard_map.135 = (bf16[16,512,128]{2,1,0:T(8,128)(2,1)S(1)}, f32[16,4096]{1,0:T(8,128)S(1)}) custom-call(bf16[16,32,256]{2,1,0:T(8,128)(2,1)S(1)} %all_to_all.38.refs_0_, bf16[4096,128]{1,0:T(8,128)(2,1)S(1)} %copy-done.14, f32[896,128]{1,0:T(8,128)S(1)} %copy-done.8, f32[752,128]{1,0:T(8,128)S(1)} %copy-done.20, f32[1,128]{1,0:T(1,128)S(1)} %bitcast.16, ...), custom_call_target="tpu_custom_call" | custom-call | tf_op jit(solution)/shard_map/pallas_call | solution.py:331
  143.8 0.0 copy-start.25
  143.9 30.4 %all_to_all.39.refs_0_ = bf16[16,512,128]{2,1,0:T(8,128)(2,1)S(1)} all-to-all(bf16[16,512,128]{2,1,0:T(8,128)(2,1)S(1)} %get-tuple-element.49), channel_id=1, replica_groups=mesh['z_far'=8,'z_pair'=2,'core'=2,'tensor'=16] {'tensor'}, dimensions={0} | all-to-all | bytes 4194304 | tf_op jit(solution)/shard_map/all_to_all | solution.py:38
  174.3 1.4 shard_map.136
  (33 shorter events, 0.1 us)
Async XLA Ops:
  0.6 0.9 copy-start.9
  1.5 0.7 copy-start.24
  2.8 35.0 %copy-start.1 = (bf16[4096,128]{1,0:T(8,128)(2,1)S(1)}, bf16[4096,128]{1,0:T(8,128)(2,1)}, u32[]{:S(2)}) copy-start(bf16[4096,128]{1,0:T(8,128)(2,1)} %refs_0_.8) | copy-start | bytes 3145732
  2.8 35.0 %copy-start.2 = (bf16[4096,128]{1,0:T(8,128)(2,1)S(1)}, bf16[4096,128]{1,0:T(8,128)(2,1)}, u32[]{:S(2)}) copy-start(bf16[4096,128]{1,0:T(8,128)(2,1)} %refs_0_.7) | copy-start | bytes 3145732
  37.8 5.2 %copy-start.27 = (s32[1,32]{1,0:T(1,128)S(1)}, s32[1,32]{1,0:T(1,128)}, u32[]{:S(2)}) copy-start(s32[1,32]{1,0:T(1,128)} %refs_0_.9) | copy-start | bytes 388
  37.8 8.5 %copy-start = (bf16[128,4096]{1,0:T(8,128)(2,1)S(1)}, bf16[128,4096]{1,0:T(8,128)(2,1)}, u32[]{:S(2)}) copy-start(bf16[128,4096]{1,0:T(8,128)(2,1)} %refs_1_.4) | copy-start | bytes 3145732
  37.8 8.5 %copy-start.10 = (bf16[16,4096]{1,0:T(8,128)(2,1)S(1)}, bf16[16,4096]{1,0:T(8,128)(2,1)}, u32[]{:S(2)}) copy-start(bf16[16,4096]{1,0:T(8,128)(2,1)} %refs_1_.5) | copy-start | bytes 393220
  37.8 8.5 %copy-start.29 = (f32[128]{0:T(128)S(1)}, f32[128]{0:T(128)}, u32[]{:S(2)}) copy-start(f32[128]{0:T(128)} %param.18) | copy-start | bytes 1540
  37.8 8.5 %copy-start.31 = (f32[128]{0:T(128)S(1)}, f32[128]{0:T(128)}, u32[]{:S(2)}) copy-start(f32[128]{0:T(128)} %param.19) | copy-start | bytes 1540
  39.4 6.9 %collective-permute-start = (f32[256,128]{1,0:T(8,128)S(1)}, f32[256,128]{1,0:T(8,128)S(1)}, u32[]{:S(2)}, u32[]{:S(2)}) collective-permute-start(f32[256,128]{1,0:T(8,128)S(1)} %get-tuple-element.27.refs_0_), channel_id=1, source_target_pairs={{0,1},{1,0},{2,3},{3,2},{4,5},{5,4},{6,7},{7,6},{8,9},{9,8},{10,11... | collective-permute-start | bytes 393224 | tf_op jit(solution)/shard_map/ppermute | solution.py:25
  46.3 17.2 %copy-start.23 = (f32[4096]{0:T(1024)S(1)}, f32[4096]{0:T(1024)}, u32[]{:S(2)}) copy-start(f32[4096]{0:T(1024)} %param.21) | copy-start | bytes 49156
  48.3 0.8 copy-start.6
  49.1 0.7 copy-start.22
  49.8 13.8 %all-to-all-start.1 = ((bf16[16,32,256]{2,1,0:T(8,128)(2,1)}), bf16[16,32,256]{2,1,0:T(8,128)(2,1)S(1)}, u32[]{:S(2)}, u32[]{:S(2)}) async-start(bf16[16,32,256]{2,1,0:T(8,128)(2,1)} %copy-done.22), calls=%async_computation.1 | async-start | bytes 524288 | tf_op jit(solution)/shard_map/all_to_all | solution.py:38
  54.8 1.0 copy-start.7
  56.3 32.5 %collective-permute-start.1 = (bf16[128,4096]{1,0:T(8,128)(2,1)S(1)}, bf16[128,4096]{1,0:T(8,128)(2,1)S(1)}, u32[]{:S(2)}, u32[]{:S(2)}) collective-permute-start(bf16[128,4096]{1,0:T(8,128)(2,1)S(1)} %shard_map.129.refs_0_), channel_id=1, source_target_pairs={{0,1},{1,0},{2,3},{3,2},{4,5},{5,4},{6,7},{7,6},{8,9},{9,8},{10,11... | collective-permute-start | bytes 3145736 | tf_op jit(solution)/shard_map/ppermute | solution.py:25
  63.7 0.6 copy-start.15
  64.3 0.7 copy-start.21
  65.0 23.4 %copy-start.26 = (s32[256,7]{0,1:T(8,128)S(1)}, s32[256,7]{0,1:T(8,128)}, u32[]{:S(2)}) copy-start(s32[256,7]{0,1:T(8,128)} %param.14) | copy-start | bytes 21508
  65.0 23.4 %copy-start.33 = (s32[256]{0:T(256)S(1)}, s32[256]{0:T(256)}, u32[]{:S(2)}) copy-start(s32[256]{0:T(256)} %param.13) | copy-start | bytes 3076
  65.0 28.8 %all-to-all-start.2 = ((bf16[16,32,256]{2,1,0:T(8,128)(2,1)}), bf16[16,32,256]{2,1,0:T(8,128)(2,1)}, u32[]{:S(2)}, u32[]{:S(2)}) async-start(bf16[16,32,256]{2,1,0:T(8,128)(2,1)} %copy-done.21), calls=%async_computation.2 | async-start | bytes 524288 | tf_op jit(solution)/shard_map/all_to_all | solution.py:38
  79.4 0.8 copy-start.16
  80.2 0.7 copy-start.28
  82.3 0.8 copy-start.19
  83.0 1.2 copy-start.3
  84.3 0.8 copy-start.17
  86.5 1.0 copy-start.11
  87.4 1.0 copy-start.13
  89.8 1.3 copy-start.4
  96.2 31.2 %copy-start.18 = (f32[32,256]{1,0:T(8,128)S(1)}, f32[32,256]{1,0:T(8,128)}, u32[]{:S(2)}) copy-start(f32[32,256]{1,0:T(8,128)} %copy-done.15) | copy-start | bytes 98308
  99.7 40.8 %copy-start.14 = (bf16[4096,128]{1,0:T(8,128)(2,1)S(1)}, bf16[4096,128]{1,0:T(8,128)(2,1)}, u32[]{:S(2)}) copy-start(bf16[4096,128]{1,0:T(8,128)(2,1)} %copy-done.13) | copy-start | bytes 3145732
  117.9 22.6 %copy-start.5 = (bf16[256,4096]{1,0:T(8,128)(2,1)S(1)}, bf16[256,4096]{1,0:T(8,128)(2,1)}, u32[]{:S(2)}) copy-start(bf16[256,4096]{1,0:T(8,128)(2,1)} %copy-done.4) | copy-start | bytes 6291460
  117.9 22.6 %copy-start.8 = (f32[896,128]{1,0:T(8,128)S(1)}, f32[896,128]{1,0:T(8,128)}, u32[]{:S(2)}) copy-start(f32[896,128]{1,0:T(8,128)} %copy-done.6) | copy-start | bytes 1376260
  117.9 22.6 %copy-start.12 = (bf16[128,4096]{1,0:T(8,128)(2,1)S(1)}, bf16[128,4096]{1,0:T(8,128)(2,1)}, u32[]{:S(2)}) copy-start(bf16[128,4096]{1,0:T(8,128)(2,1)} %copy-done.11) | copy-start | bytes 3145732
  117.9 22.6 %copy-start.20 = (f32[752,128]{1,0:T(8,128)S(1)}, f32[752,128]{1,0:T(8,128)}, u32[]{:S(2)}) copy-start(f32[752,128]{1,0:T(8,128)} %copy-done.19) | copy-start | bytes 1155076
  117.9 22.6 %copy-start.30 = (f32[128]{0:T(128)S(1)}, f32[128]{0:T(128)}, u32[]{:S(2)}) copy-start(f32[128]{0:T(128)} %param.18) | copy-start | bytes 1540
  118.0 22.6 %copy-start.32 = (f32[128]{0:T(128)S(1)}, f32[128]{0:T(128)}, u32[]{:S(2)}) copy-start(f32[128]{0:T(128)} %param.19) | copy-start | bytes 1540
  143.8 30.4 %copy-start.25 = (f32[4096]{0:T(1024)S(1)}, f32[4096]{0:T(1024)}, u32[]{:S(2)}) copy-start(f32[4096]{0:T(1024)} %param.15) | copy-start | bytes 49156

commit v7 on v6

--- a/solution.py
+++ b/solution.py
@@ -86,10 +86,9 @@
 
 
 def partial_logits_kernel(
-    rows_ref, query_hot_ref, positive_hot_ref, listed_all_ref, gains_ref, out_ref, rows_out_ref, held_ref
+    rows_ref, query_hot_ref, positive_hot_ref, listed_all_ref, gains_ref, out_ref, held_ref
 ):
     rows = rows_ref[...]
-    rows_out_ref[...] = rows
     query_at, half = query_block()
     listed_ref = listed_all_ref[:8, block_lanes(query_at)]
     block_hot = query_hot_ref[block_lanes(query_at), :]
@@ -98,7 +97,7 @@
     queries = queries.astype(jnp.bfloat16)
     features = gains_ref.shape[1]
     rows32 = rows.astype(jnp.float32)
-    plain = rows32 / own_columns(gains_ref, rows.shape[1])
+    plain = rows32 * (1.0 / own_columns(gains_ref, rows.shape[1]))
     squares = jnp.sum(rows32 * rows32, axis=1, keepdims=True) + jnp.sum(
         plain * plain, axis=1, keepdims=True
     ) * (EPSILON / features)
@@ -279,64 +278,22 @@
     loss_ref[0] = jnp.sum(hard_weighted[7:8, :]) / count
 
 
-def kernel_call(body, outs, arrays, near=(), near_outs=(), late=(), after=(), scratch=()):
+def kernel_call(body, outs, arrays, after=(), scratch=()):
     count = len(arrays)
-    far = [i for i in range(count) if i not in near]
-    scalar_outs = [i for i in range(len(outs)) if outs[i][0] == (1,)]
-    far_outs = [i for i in range(len(outs)) if i not in near_outs and i not in scalar_outs]
-
-    def spec(is_far):
-        return pl.BlockSpec(memory_space=pltpu.HBM if is_far else pltpu.VMEM)
 
     def kernel(*refs):
-        given = list(refs[:count])
-        start = count + len(after)
-        results = list(refs[start : start + len(outs)])
-        start += len(outs)
-        held_in = refs[start : start + len(far)]
-        start += len(far)
-        held_out = refs[start : start + len(far_outs)]
-        start += len(far_outs)
-        semaphores = refs[start]
-        copies = {}
-        for k, i in enumerate(far):
-            copies[i] = pltpu.make_async_copy(given[i], held_in[k], semaphores.at[k])
-            copies[i].start()
-            given[i] = held_in[k]
-        for i in far:
-            if i not in late:
-                copies[i].wait()
-
-        def ready():
-            for i in late:
-                copies[i].wait()
-
-        targets = [results[i] for i in far_outs]
-        for k, i in enumerate(far_outs):
-            results[i] = held_out[k]
-        extra = (ready,) if late else ()
-        body(*extra, *given, *results, *refs[start + 1 :])
-        copies_out = [
-            pltpu.make_async_copy(held_out[k], targets[k], semaphores.at[len(far) + k])
-            for k in range(len(far_outs))
-        ]
-        for copy in copies_out:
-            copy.start()
-        for copy in copies_out:
-            copy.wait()
-
-    held = [pltpu.VMEM(arrays[i].shape, arrays[i].dtype) for i in far]
-    held += [pltpu.VMEM(*outs[i]) for i in far_outs]
-    held.append(pltpu.SemaphoreType.DMA((max(1, len(far) + len(far_outs)),)))
+        body(*refs[:count], *refs[count + len(after) :])
+
+    def out_spec(shape):
+        return pl.BlockSpec(memory_space=pltpu.SMEM if shape == (1,) else pltpu.VMEM)
+
     return pl.pallas_call(
         kernel,
         out_shape=[jax.ShapeDtypeStruct(shape, dtype) for shape, dtype in outs],
-        in_specs=[spec(i in far) for i in range(count)] + [pl.BlockSpec(memory_space=pl.ANY)] * len(after),
-        out_specs=[
-            pl.BlockSpec(memory_space=pltpu.SMEM) if i in scalar_outs else spec(i in far_outs)
-            for i in range(len(outs))
-        ],
-        scratch_shapes=held + list(scratch),
+        in_specs=[pl.BlockSpec(memory_space=pltpu.VMEM)] * count
+        + [pl.BlockSpec(memory_space=pl.ANY)] * len(after),
+        out_specs=[out_spec(shape) for shape, _ in outs],
+        scratch_shapes=list(scratch),
         compiler_params=pltpu.CompilerParams(vmem_limit_bytes=VMEM_BYTES),
     )(*arrays, *after)
 
@@ -395,15 +352,11 @@
     sequences, width = resid.shape
     listed, query_hot, positive_hot = tables
     count, total_rows = positive_hot.shape
-    sent, rows = kernel_call(
+    rows = everyone.reshape(total_rows, width)
+    (sent,) = kernel_call(
         partial_logits_kernel,
-        [
-            ((tensor_count, count // 2 + 32, LANES), jnp.bfloat16),
-            ((total_rows, width), jnp.bfloat16),
-        ],
-        [everyone.reshape(total_rows, width), query_hot, positive_hot, listed, gains],
-        near=(0,),
-        near_outs=(0,),
+        [((tensor_count, count // 2 + 32, LANES), jnp.bfloat16)],
+        [rows, query_hot, positive_hot, listed, gains],
         after=after,
         scratch=[pltpu.VMEM((24, LANES), jnp.float32)],
     )
@@ -412,16 +365,12 @@
         softmax_kernel,
         [((4, count // 2 + 16, LANES), jnp.float32), ((8, LANES), jnp.float32)],
         [arrived, positive_hot],
-        near=(0,),
-        near_outs=(0,),
     )
     both = exchange(coefs, ("z_pair", "core"))
     d_resid16, loss = kernel_call(
         resid_grad_kernel,
         [((tensor_count, sequences, width), jnp.bfloat16), ((1,), jnp.float32)],
         [both, inverse, rows, positive_hot, query_hot, listed, resid, gains],
-        near=(0,),
-        near_outs=(0,),
     )
     return loss, exchange(d_resid16, "tensor")
 
@@ -436,7 +385,7 @@
             out_ref[t, height * c : height * (c + 1), :] = block
 
 
-def projection_kernel(rows_ref, kv_weights_ref, query_weights_ref, kv_ref, query_ref):
+def projection_kernel(rows_ref, kv_weights_ref, query_weights_ref, kv_ref, sent_ref, query_ref):
     tensor_count, tall, _ = rows_ref.shape
     blocks = kv_weights_ref.shape[0] // LANES
     height = tall // blocks
@@ -455,6 +404,7 @@
             rows, query_weights_ref[columns, :], preferred_element_type=jnp.float32
         )
     kv_ref[...] = kv
+    sent_ref[...] = kv.astype(jnp.bfloat16)
     query_ref[...] = query
 
 
@@ -484,7 +434,7 @@
     at, _ = layout_rows(tokens_count, sequences, own_rows)
     to, _ = saved_rows(tokens_count, sequences)
     is_even = is_even_tensor()
-    own, other = own_ref[...], other_ref[...]
+    own, other = own_ref[...], other_ref[...].astype(jnp.float32)
     key_raw = jnp.where(is_even, own, other)
     value16 = jnp.where(is_even, other, own).astype(jnp.bfloat16)
     query_raw = jnp.dot(
@@ -756,17 +706,13 @@
     gain_rows = [q_gain[None, :], k_gain[None, :]]
 
     (copies,) = kernel_call(
-        copied_norm_kernel, [(flat, bf16)], [hidden, in_gain[None, :]], near_outs=(0,)
+        copied_norm_kernel, [(flat, bf16)], [hidden, in_gain[None, :]]
     )
     piece = exchange(copies, "tensor")
-    kv_own, query_all = kernel_call(
-        projection_kernel,
-        [(head, f32), (head, f32)],
-        [piece, wkv, wq],
-        near=(0,),
-        near_outs=(0,),
-    )
-    kv_other = swapped(kv_own, "tensor", 0)
+    kv_own, kv_own16, query_all = kernel_call(
+        projection_kernel, [(head, f32), (head, bf16), (head, f32)], [piece, wkv, wq]
+    )
+    kv_other = swapped(kv_own16, "tensor", 0)
     def sequence_layout(after):
         return kernel_call(
             functools.partial(sequence_kernel, tokens_count=tokens_count, own_rows=own_rows),
@@ -783,11 +729,9 @@
             ((saved_rows(tokens_count, sequences)[1], LANES), f32),
         ],
         [kv_own, kv_other, query_all, layout, *gain_rows, hidden, wo],
-        near=(0, 1),
-        near_outs=(0,),
     )
     (own_weights,) = kernel_call(
-        transpose_kernel, [(weights_shape, bf16)], [wkv], after=[saved]
+        transpose_kernel, [(weights_shape, bf16)], [wkv], after=[query_all]
     )
     other_weights = swapped(own_weights, "tensor", 0)
     output_gain = out_gain[None, :]
@@ -795,8 +739,6 @@
         resid_kernel,
         [((sequences, chunk), f32), ((z_count, sequences, chunk), bf16)],
         [exchange(blocks, "tensor"), output_gain],
-        near=(0,),
-        near_outs=(1,),
     )
     query_weights, wo_t, transposed = kernel_call(
         transpose_kernel,
@@ -836,15 +778,12 @@
             both_weights,
             query_weights,
         ],
-        near=(0,),
-        near_outs=(0,),
     )
     terms = exchange(product, "tensor")
     (d_hidden,) = kernel_call(
         d_hidden_kernel,
         [((own_rows, features), bf16)],
         [terms, hidden, in_gain[None, :], added],
-        near=(0,),
     )
     return (d_hidden, loss[0])
 

time: 177 us -> 173 us (0.977)
  waiting for transfers between devices: 9.61 us -> 14.6 us
  Pallas kernels: 20.2 us -> 15.8 us
  local copies, waits for them, and re-layouts: 12.9 us -> 9.19 us
    all_to_all x2, waiting for transfers between devices: 7.77 us -> 12.7 us  [exchange(): return lax.all_to_all(blocks, axis, 0, 0, tiled=True)]
    pallas_call x15, Pallas kernels: 20.2 us -> 15.8 us  [kernel_call(): pl.pallas_call(kernel, out_shape=[jax.ShapeDtypeStruct(shape, dtype) for...]
    unnamed x68 -> x52, local copies, waits for them, and re-layouts: 12.9 us -> 9.19 us
  transfers between devices with their start and end apart: 4 -> 4, of which waited for: 3 -> 3; matrix products, arithmetic and copies ran while one was open for 0% -> 0% of each run, Pallas kernels for 4% -> 3%
where the time goes in v7:
time: 173 us; the launch traced here: 172 us
  blocking collectives  106 us (61%)
  starting transfers between devices  25.8 us (15%)
  Pallas kernels  15.8 us (9%)
  waiting for transfers between devices  14.6 us (8%)
  local copies, waits for them, and re-layouts  9.19 us (5%)
    all_to_all x5, blocking collectives, exchange(): return lax.all_to_all(blocks, axis, 0, 0, tiled=True)  103 us
    all_to_all x2, starting transfers between devices, exchange(): return lax.all_to_all(blocks, axis, 0, 0, tiled=True)  20 us
    pallas_call x15, Pallas kernels, kernel_call(): pl.pallas_call(kernel, out_shape=[jax.ShapeDtypeStruct(shape, dtype) for...  15.8 us
    all_to_all x2, waiting for transfers between devices, exchange(): return lax.all_to_all(blocks, axis, 0, 0, tiled=True)  12.7 us
    unnamed x52, local copies, waits for them, and re-layouts  9.19 us
    ppermute x2, starting transfers between devices, swapped(): return lax.ppermute(value, axis, pairs)  5.79 us
  transfers between devices with their start and end apart: 4, of which 3 were waited for; matrix products, arithmetic and copies ran while one was open for 0% of the time, Pallas kernels for 3%

profile of v7, /device:TPU:2, one launch (start us, length us, event | category | flops | bytes accessed | tf_op | source)
XLA Modules:
  0.0 172.2 jit_solution(13756796348092790281)
XLA Ops:
  0.6 0.0 copy-start.6
  0.6 0.9 copy-done.6
  1.5 0.7 copy-done.19
  2.3 0.3 shard_map.122
  2.6 0.0 copy-start.1
  2.6 0.0 copy-start.2
  2.6 35.0 %all_to_all.35.refs_0_ = bf16[16,512,128]{2,1,0:T(8,128)(2,1)S(1)} all-to-all(bf16[16,512,128]{2,1,0:T(8,128)(2,1)S(1)} %shard_map.122), channel_id=1, replica_groups=mesh['z_far'=8,'z_pair'=2,'core'=2,'tensor'=16] {'tensor'}, dimensions={0} | all-to-all | bytes 4194304 | tf_op jit(solution)/shard_map/all_to_all | solution.py:38
  37.6 0.0 copy-done.1
  37.6 0.0 copy-done.2
  37.6 0.0 copy-start.7
  37.6 0.0 copy-start.23
  37.6 0.0 copy-start.24
  37.7 1.2 shard_map.123
  38.9 3.6 %collective-permute-start = (bf16[256,128]{1,0:T(8,128)(2,1)S(1)}, bf16[256,128]{1,0:T(8,128)(2,1)S(1)}, u32[]{:S(2)}, u32[]{:S(2)}) collective-permute-start(bf16[256,128]{1,0:T(8,128)(2,1)S(1)} %get-tuple-element.27), channel_id=1, source_target_pairs={{0,1},{1,0},{2,3},{3,2},{4,5},{5,4},{6,7},{7,6},{8,9},{9,8},{10,11... | collective-permute-start | bytes 196616 | tf_op jit(solution)/shard_map/ppermute | solution.py:25
  42.5 0.0 copy-done.22
  42.5 0.7 shard_map.124
  43.2 1.8 %collective-permute-done.refs_1_ = bf16[256,128]{1,0:T(8,128)(2,1)S(1)} collective-permute-done((bf16[256,128]{1,0:T(8,128)(2,1)S(1)}, bf16[256,128]{1,0:T(8,128)(2,1)S(1)}, u32[]{:S(2)}, u32[]{:S(2)}) %collective-permute-start) | collective-permute-done | bytes 65568 | tf_op jit(solution)/shard_map/ppermute | solution.py:25
  45.1 0.0 copy-done
  45.1 0.0 copy-done.7
  45.1 0.0 copy-done.23
  45.1 0.0 copy-done.24
  45.1 0.0 copy-start.18
  45.1 1.0 shard_map.125
  46.1 0.0 copy-start.12
  46.2 0.8 copy-done.12
  46.9 0.7 copy-done.17
  47.6 5.6 %all-to-all-start.1 = ((bf16[16,32,256]{2,1,0:T(8,128)(2,1)}), bf16[16,32,256]{2,1,0:T(8,128)(2,1)}, u32[]{:S(2)}, u32[]{:S(2)}) async-start(bf16[16,32,256]{2,1,0:T(8,128)(2,1)} %copy-done.17), calls=%async_computation.1 | async-start | bytes 524288 | tf_op jit(solution)/shard_map/all_to_all | solution.py:38
  53.2 0.0 copy-start.25
  53.2 0.3 shard_map.129.refs_0_
  53.6 2.2 %collective-permute-start.1 = (bf16[128,4096]{1,0:T(8,128)(2,1)S(1)}, bf16[128,4096]{1,0:T(8,128)(2,1)S(1)}, u32[]{:S(2)}, u32[]{:S(2)}) collective-permute-start(bf16[128,4096]{1,0:T(8,128)(2,1)S(1)} %shard_map.129.refs_0_), channel_id=1, source_target_pairs={{0,1},{1,0},{2,3},{3,2},{4,5},{5,4},{6,7},{7,6},{8,9},{9,8},{10,11... | collective-permute-start | bytes 3145736 | tf_op jit(solution)/shard_map/ppermute | solution.py:25
  55.8 6.4 %all-to-all-done.1.refs_0_ = bf16[16,32,256]{2,1,0:T(8,128)(2,1)} async-done(((bf16[16,32,256]{2,1,0:T(8,128)(2,1)}), bf16[16,32,256]{2,1,0:T(8,128)(2,1)}, u32[]{:S(2)}, u32[]{:S(2)}) %all-to-all-start.1) | async-done | bytes 262176 | tf_op jit(solution)/shard_map/all_to_all | solution.py:38
  62.2 0.0 copy-done.18
  62.2 1.0 shard_map.126
  63.2 0.0 copy-start.16
  63.2 0.7 copy-done.16
  63.9 14.4 %all-to-all-start.2 = ((bf16[16,32,256]{2,1,0:T(8,128)(2,1)}), bf16[16,32,256]{2,1,0:T(8,128)(2,1)}, u32[]{:S(2)}, u32[]{:S(2)}) async-start(bf16[16,32,256]{2,1,0:T(8,128)(2,1)} %copy-done.16), calls=%async_computation.2 | async-start | bytes 524288 | tf_op jit(solution)/shard_map/all_to_all | solution.py:38
  78.3 0.7 shard_map.131
  79.0 0.0 copy-start.14
  79.1 0.7 copy-done.14
  79.8 1.2 copy-done.3
  81.0 0.8 shard_map.128
  81.9 0.0 copy-start.8
  81.9 1.0 copy-done.8
  82.9 1.0 copy-done.10
  83.9 0.0 copy-done.21
  83.9 0.0 copy-done.25
  83.9 0.2 shard_map.127
  84.1 0.0 collective-permute-done.1.refs_1_
  84.1 0.7 shard_map.130
  84.8 0.0 copy-start.4
  84.8 1.4 copy-done.4
  86.2 6.3 %all-to-all-done.2 = bf16[16,32,256]{2,1,0:T(8,128)(2,1)} async-done(((bf16[16,32,256]{2,1,0:T(8,128)(2,1)}), bf16[16,32,256]{2,1,0:T(8,128)(2,1)}, u32[]{:S(2)}, u32[]{:S(2)}) %all-to-all-start.2) | async-done | bytes 262176 | tf_op jit(solution)/shard_map/all_to_all | solution.py:38
  92.5 2.4 %all-gather = bf16[16,64,256]{2,1,0:T(8,128)(2,1)S(1)} all-gather(bf16[16,32,256]{2,1,0:T(8,128)(2,1)} %all-to-all-done.2), channel_id=2, replica_groups=mesh['z_far'=8,'z_pair'=2,'core'=2,'tensor'=16] {'core'}, dimensions={1}, use_global_device_ids=true | all-gather | bytes 786432 | tf_op jit(solution)/shard_map/all_gather | solution.py:765
  94.8 3.4 %shard_map.132 = bf16[16,160,128]{2,1,0:T(8,128)(2,1)S(1)} custom-call(bf16[1024,256]{1,0:T(8,128)(2,1)S(1)} %bitcast.8, bf16[256,1024]{1,0:T(8,128)(2,1)S(1)} %get-tuple-element.33.refs_1_.refs_4_, bf16[256,1024]{1,0:T(8,128)(2,1)S(1)} %get-tuple-element.34.refs_2_.refs_1_.refs_3_, s32[16,256]{1,0:T(8,128)S(1)} %get-tuple-element.35.refs_3_.refs_5_, ...), custom_call_target="tpu_custom_call" | custom-call | tf_op jit(solution)/shard_map/pallas_call | solution.py:290
  98.3 16.8 %all_to_all.36.refs_0_ = bf16[16,160,128]{2,1,0:T(8,128)(2,1)S(1)} all-to-all(bf16[16,160,128]{2,1,0:T(8,128)(2,1)S(1)} %shard_map.132), channel_id=1, replica_groups=mesh['z_far'=8,'z_pair'=2,'core'=2,'tensor'=16] {'tensor'}, dimensions={0} | all-to-all | bytes 1310720 | tf_op jit(solution)/shard_map/all_to_all | solution.py:38
  115.1 0.5 shard_map.133
  115.6 9.4 %all_to_all.37.refs_0_ = f32[4,144,128]{2,1,0:T(8,128)S(1)} all-to-all(f32[4,144,128]{2,1,0:T(8,128)S(1)} %get-tuple-element.39), channel_id=1, replica_groups=mesh['z_far'=8,'z_pair'=2,'core'=2,'tensor'=16] {'z_pair','core'}, dimensions={0} | all-to-all | bytes 589824 | tf_op jit(solution)/shard_map/all_to_all | solution.py:38
  125.0 1.3 shard_map.134
  126.3 11.9 %all_to_all.38.refs_0_ = bf16[16,32,256]{2,1,0:T(8,128)(2,1)S(1)} all-to-all(bf16[16,32,256]{2,1,0:T(8,128)(2,1)S(1)} %get-tuple-element.41), channel_id=1, replica_groups=mesh['z_far'=8,'z_pair'=2,'core'=2,'tensor'=16] {'tensor'}, dimensions={0} | all-to-all | bytes 524288 | tf_op jit(solution)/shard_map/all_to_all | solution.py:38
  138.2 0.0 copy-done.15
  138.2 2.4 %shard_map.135 = (bf16[16,512,128]{2,1,0:T(8,128)(2,1)S(1)}, f32[16,4096]{1,0:T(8,128)S(1)}) custom-call(bf16[16,32,256]{2,1,0:T(8,128)(2,1)S(1)} %all_to_all.38.refs_0_, bf16[4096,128]{1,0:T(8,128)(2,1)S(1)} %copy-done.11, f32[896,128]{1,0:T(8,128)S(1)} %copy-done.13, f32[752,128]{1,0:T(8,128)S(1)} %copy-done.15, f32[1,128]{1,0:T(1,128)S(1)} %bitcast.17, ...), custom_call_target="tpu_custom_call" | custom-call | tf_op jit(solution)/shard_map/pallas_call | solution.py:290
  140.6 0.0 copy-start.20
  140.6 30.4 %all_to_all.39.refs_0_ = bf16[16,512,128]{2,1,0:T(8,128)(2,1)S(1)} all-to-all(bf16[16,512,128]{2,1,0:T(8,128)(2,1)S(1)} %get-tuple-element.47), channel_id=1, replica_groups=mesh['z_far'=8,'z_pair'=2,'core'=2,'tensor'=16] {'tensor'}, dimensions={0} | all-to-all | bytes 4194304 | tf_op jit(solution)/shard_map/all_to_all | solution.py:38
  171.0 1.1 shard_map.136
  (17 shorter events, 0.0 us)
Async XLA Ops:
  0.6 0.9 copy-start.6
  1.5 0.7 copy-start.19
  2.6 35.0 %copy-start.1 = (bf16[4096,128]{1,0:T(8,128)(2,1)S(1)}, bf16[4096,128]{1,0:T(8,128)(2,1)}, u32[]{:S(2)}) copy-start(bf16[4096,128]{1,0:T(8,128)(2,1)} %refs_0_.8) | copy-start | bytes 3145732
  2.6 35.0 %copy-start.2 = (bf16[4096,128]{1,0:T(8,128)(2,1)S(1)}, bf16[4096,128]{1,0:T(8,128)(2,1)}, u32[]{:S(2)}) copy-start(bf16[4096,128]{1,0:T(8,128)(2,1)} %refs_0_.7) | copy-start | bytes 3145732
  37.6 4.9 %copy-start.22 = (s32[1,32]{1,0:T(1,128)S(1)}, s32[1,32]{1,0:T(1,128)}, u32[]{:S(2)}) copy-start(s32[1,32]{1,0:T(1,128)} %refs_0_.9) | copy-start | bytes 388
  37.6 7.5 %copy-start = (bf16[128,4096]{1,0:T(8,128)(2,1)S(1)}, bf16[128,4096]{1,0:T(8,128)(2,1)}, u32[]{:S(2)}) copy-start(bf16[128,4096]{1,0:T(8,128)(2,1)} %refs_1_.4) | copy-start | bytes 3145732
  37.6 7.5 %copy-start.7 = (bf16[16,4096]{1,0:T(8,128)(2,1)S(1)}, bf16[16,4096]{1,0:T(8,128)(2,1)}, u32[]{:S(2)}) copy-start(bf16[16,4096]{1,0:T(8,128)(2,1)} %refs_1_.5) | copy-start | bytes 393220
  37.6 7.4 %copy-start.23 = (f32[128]{0:T(128)S(1)}, f32[128]{0:T(128)}, u32[]{:S(2)}) copy-start(f32[128]{0:T(128)} %param.18) | copy-start | bytes 1540
  37.6 7.4 %copy-start.24 = (f32[128]{0:T(128)S(1)}, f32[128]{0:T(128)}, u32[]{:S(2)}) copy-start(f32[128]{0:T(128)} %param.19) | copy-start | bytes 1540
  38.9 6.2 %collective-permute-start = (bf16[256,128]{1,0:T(8,128)(2,1)S(1)}, bf16[256,128]{1,0:T(8,128)(2,1)S(1)}, u32[]{:S(2)}, u32[]{:S(2)}) collective-permute-start(bf16[256,128]{1,0:T(8,128)(2,1)S(1)} %get-tuple-element.27), channel_id=1, source_target_pairs={{0,1},{1,0},{2,3},{3,2},{4,5},{5,4},{6,7},{7,6},{8,9},{9,8},{10,11... | collective-permute-start | bytes 196616 | tf_op jit(solution)/shard_map/ppermute | solution.py:25
  45.1 17.1 %copy-start.18 = (f32[4096]{0:T(1024)S(1)}, f32[4096]{0:T(1024)}, u32[]{:S(2)}) copy-start(f32[4096]{0:T(1024)} %param.21) | copy-start | bytes 49156
  46.1 0.8 copy-start.12
  46.9 0.7 copy-start.17
  47.6 14.6 %all-to-all-start.1 = ((bf16[16,32,256]{2,1,0:T(8,128)(2,1)}), bf16[16,32,256]{2,1,0:T(8,128)(2,1)}, u32[]{:S(2)}, u32[]{:S(2)}) async-start(bf16[16,32,256]{2,1,0:T(8,128)(2,1)} %copy-done.17), calls=%async_computation.1 | async-start | bytes 524288 | tf_op jit(solution)/shard_map/all_to_all | solution.py:38
  53.2 30.7 %copy-start.21 = (s32[256,7]{0,1:T(8,128)S(1)}, s32[256,7]{0,1:T(8,128)}, u32[]{:S(2)}) copy-start(s32[256,7]{0,1:T(8,128)} %param.14) | copy-start | bytes 21508
  53.2 30.7 %copy-start.25 = (s32[256]{0:T(256)S(1)}, s32[256]{0:T(256)}, u32[]{:S(2)}) copy-start(s32[256]{0:T(256)} %param.13) | copy-start | bytes 3076
  53.6 30.6 %collective-permute-start.1 = (bf16[128,4096]{1,0:T(8,128)(2,1)S(1)}, bf16[128,4096]{1,0:T(8,128)(2,1)S(1)}, u32[]{:S(2)}, u32[]{:S(2)}) collective-permute-start(bf16[128,4096]{1,0:T(8,128)(2,1)S(1)} %shard_map.129.refs_0_), channel_id=1, source_target_pairs={{0,1},{1,0},{2,3},{3,2},{4,5},{5,4},{6,7},{7,6},{8,9},{9,8},{10,11... | collective-permute-start | bytes 3145736 | tf_op jit(solution)/shard_map/ppermute | solution.py:25
  63.2 0.7 copy-start.16
  63.9 28.5 %all-to-all-start.2 = ((bf16[16,32,256]{2,1,0:T(8,128)(2,1)}), bf16[16,32,256]{2,1,0:T(8,128)(2,1)}, u32[]{:S(2)}, u32[]{:S(2)}) async-start(bf16[16,32,256]{2,1,0:T(8,128)(2,1)} %copy-done.16), calls=%async_computation.2 | async-start | bytes 524288 | tf_op jit(solution)/shard_map/all_to_all | solution.py:38
  79.0 0.8 copy-start.14
  79.8 1.2 copy-start.3
  81.9 1.0 copy-start.8
  82.9 1.0 copy-start.10
  84.8 1.4 copy-start.4
  98.3 39.9 %copy-start.13 = (f32[896,128]{1,0:T(8,128)S(1)}, f32[896,128]{1,0:T(8,128)}, u32[]{:S(2)}) copy-start(f32[896,128]{1,0:T(8,128)} %copy-done.12) | copy-start | bytes 1376260
  98.3 39.9 %copy-start.15 = (f32[752,128]{1,0:T(8,128)S(1)}, f32[752,128]{1,0:T(8,128)}, u32[]{:S(2)}) copy-start(f32[752,128]{1,0:T(8,128)} %copy-done.14) | copy-start | bytes 1155076
  115.1 23.1 %copy-start.5 = (bf16[256,4096]{1,0:T(8,128)(2,1)S(1)}, bf16[256,4096]{1,0:T(8,128)(2,1)}, u32[]{:S(2)}) copy-start(bf16[256,4096]{1,0:T(8,128)(2,1)} %copy-done.4) | copy-start | bytes 6291460
  115.1 23.1 %copy-start.9 = (bf16[128,4096]{1,0:T(8,128)(2,1)S(1)}, bf16[128,4096]{1,0:T(8,128)(2,1)}, u32[]{:S(2)}) copy-start(bf16[128,4096]{1,0:T(8,128)(2,1)} %copy-done.8) | copy-start | bytes 3145732
  115.1 23.1 %copy-start.11 = (bf16[4096,128]{1,0:T(8,128)(2,1)S(1)}, bf16[4096,128]{1,0:T(8,128)(2,1)}, u32[]{:S(2)}) copy-start(bf16[4096,128]{1,0:T(8,128)(2,1)} %copy-done.10) | copy-start | bytes 3145732
  140.6 30.4 %copy-start.20 = (f32[4096]{0:T(1024)S(1)}, f32[4096]{0:T(1024)}, u32[]{:S(2)}) copy-start(f32[4096]{0:T(1024)} %param.15) | copy-start | bytes 49156

commit v8 on v7

--- a/solution.py
+++ b/solution.py
@@ -331,13 +331,18 @@
         )
 
 
-def transpose_kernel(*refs):
-    half = len(refs) // 2
-    for given_ref, out_ref in zip(refs[:half], refs[half:]):
-        given = given_ref[...]
-        out_ref[...] = given.T
-    if len(refs) > 2 * half:
-        refs[-1][0] = jnp.float32(0.0)
+def transpose_kernel(given_ref, out_ref, token_ref):
+    out_ref[...] = given_ref[...].T
+    token_ref[0] = jnp.float32(0.0)
+
+
+def half_weights_kernel(kv_ref, query_ref, kept_ref, sent_ref):
+    width, rows = kept_ref.shape[1], kv_ref.shape[1]
+    parity = lax.axis_index("tensor") % 2
+    for out_ref, half in ((kept_ref, parity), (sent_ref, 1 - parity)):
+        features = pl.ds(pl.multiple_of(half * width, width), width)
+        out_ref[:rows, :] = kv_ref[features, :].T
+        out_ref[rows:, :] = query_ref[features, :].T
 
 
 def stack_kernel(first_ref, second_ref, out_ref, token_ref):
@@ -500,25 +505,15 @@
 
 
 def gradient_kernel(
-    d_resid_ref,
-    wo_t_ref,
-    saved_ref,
-    layout_ref,
-    q_gain_ref,
-    k_gain_ref,
-    both_weights_ref,
-    query_weights_ref,
-    out_ref,
-    added_ref,
+    d_resid_ref, wo_t_ref, saved_ref, layout_ref, q_gain_ref, k_gain_ref, own_ref, sent_ref
 ):
     head_width = saved_ref.shape[1]
     root = math.sqrt(head_width)
     sequences = d_resid_ref.shape[1]
-    own_rows = added_ref.shape[0]
-    tokens_count = own_rows * out_ref.shape[0]
-    at, _ = layout_rows(tokens_count, sequences, own_rows)
+    tensor_count = d_resid_ref.shape[0]
+    tokens_count = (own_ref.shape[0] - sequences) // 2
+    at, _ = layout_rows(tokens_count, sequences, tokens_count // tensor_count)
     to, _ = saved_rows(tokens_count, sequences)
-    is_even = is_even_tensor()
     chunk = d_resid_ref.shape[2]
     d_attn = jnp.dot(d_resid_ref[0], wo_t_ref[:chunk, :], preferred_element_type=jnp.float32)
     for t in range(1, d_resid_ref.shape[0]):
@@ -555,43 +550,72 @@
 
     d_key = head_gradient(d_key_rot, "key", k_gain_ref[...])
     d_query = head_gradient(d_query_rot, "query", q_gain_ref[...])
-    own_other16 = jnp.concatenate(
-        [jnp.where(is_even, d_key, d_value), jnp.where(is_even, d_value, d_key)], axis=1
+    own = jnp.concatenate([d_key, d_value, d_query], axis=0)
+    own_ref[...] = own
+    sent_ref[...] = own.astype(jnp.bfloat16)
+
+
+def added_kernel(d_resid_ref, layout_ref, out_ref, token_ref):
+    own_rows = out_ref.shape[0]
+    tensor_count, sequences, chunk = d_resid_ref.shape
+    at, _ = layout_rows(own_rows * tensor_count, sequences, own_rows)
+    last = layout_ref[at["own_last_t"], :][:, :sequences].astype(jnp.bfloat16)
+    for t in range(tensor_count):
+        out_ref[:, t * chunk : (t + 1) * chunk] = jnp.dot(
+            last, d_resid_ref[t], preferred_element_type=jnp.float32
+        )
+    token_ref[0] = jnp.float32(0.0)
+
+
+def product_kernel(own_ref, other_ref, layout_ref, weights_ref, out_ref):
+    tensor_count, tall, _ = out_ref.shape
+    height = tall * LANES // weights_ref.shape[1]
+    tokens_count = height * tensor_count
+    sequences = own_ref.shape[0] - 2 * tokens_count
+    at, _ = layout_rows(tokens_count, sequences, height)
+    chosen = unfolded(layout_ref[at["chosen"], :], sequences).astype(jnp.bfloat16)
+
+    def spread(d_query):
+        return lax.dot_general(
+            chosen,
+            d_query.astype(jnp.bfloat16),
+            (((0,), (0,)), ((), ())),
+            preferred_element_type=jnp.float32,
+        )
+
+    own, other = own_ref[...], other_ref[...].astype(jnp.float32)
+    d_key = own[:tokens_count] + other[:tokens_count]
+    d_value = own[tokens_count : 2 * tokens_count] + other[tokens_count : 2 * tokens_count]
+    is_even = is_even_tensor()
+    gradients = jnp.concatenate(
+        [
+            jnp.where(is_even, d_key, d_value),
+            spread(own[2 * tokens_count :]),
+            jnp.where(is_even, d_value, d_key),
+            spread(other[2 * tokens_count :]),
+        ],
+        axis=1,
     ).astype(jnp.bfloat16)
-    spread16 = lax.dot_general(
-        unfolded(layout_ref[at["chosen"], :], sequences).astype(jnp.bfloat16),
-        d_query.astype(jnp.bfloat16),
-        down,
-        preferred_element_type=jnp.float32,
-    ).astype(jnp.bfloat16)
-    last = layout_ref[at["own_last_t"], :][:, :sequences].astype(jnp.bfloat16)
-    height = out_ref.shape[1] * LANES // added_ref.shape[1]
-    for t in range(added_ref.shape[1] // chunk):
-        columns = slice(t * chunk, (t + 1) * chunk)
-        added_ref[:, columns] = jnp.dot(last, d_resid_ref[t], preferred_element_type=jnp.float32)
+    wide = 2 * LANES
+    for k in range(weights_ref.shape[1] // wide):
         term = jnp.dot(
-            own_other16, both_weights_ref[:, columns], preferred_element_type=jnp.float32
-        )
-        term = term + jnp.dot(
-            spread16, query_weights_ref[:, columns], preferred_element_type=jnp.float32
-        )
-        term16 = term.astype(jnp.bfloat16)
-        for k in range(chunk // LANES):
-            c = t * (chunk // LANES) + k
-            block = term16[:, LANES * k : LANES * (k + 1)]
+            gradients, weights_ref[:, wide * k : wide * (k + 1)], preferred_element_type=jnp.float32
+        ).astype(jnp.bfloat16)
+        for c in (2 * k, 2 * k + 1):
+            block = term[:, LANES * (c - 2 * k) : LANES * (c - 2 * k + 1)]
             out_ref[:, height * c : height * (c + 1), :] = block.reshape(-1, height, LANES)
 
 
 def d_hidden_kernel(terms_ref, hidden_ref, gain_ref, added_ref, out_ref):
-    d_normed = terms_ref[0].astype(jnp.float32)
-    for t in range(1, terms_ref.shape[0]):
-        d_normed = d_normed + terms_ref[t].astype(jnp.float32)
     hidden32 = hidden_ref[...].astype(jnp.float32)
     height = hidden32.shape[0]
-    d_normed = jnp.concatenate(
-        [d_normed[height * c : height * (c + 1)] for c in range(hidden32.shape[1] // LANES)],
-        axis=1,
-    )
+    parts = []
+    for parity in range(2):
+        total = terms_ref[parity].astype(jnp.float32)
+        for t in range(parity + 2, terms_ref.shape[0], 2):
+            total = total + terms_ref[t].astype(jnp.float32)
+        parts += [total[height * c : height * (c + 1)] for c in range(total.shape[0] // height)]
+    d_normed = jnp.concatenate(parts, axis=1)
     inverse = rms_scale(hidden32)
     d_hidden = norm_backward(d_normed, hidden32 * inverse, inverse, gain_ref[...])
     out_ref[...] = (d_hidden + added_ref[...]).astype(jnp.bfloat16)
@@ -730,26 +754,24 @@
         ],
         [kv_own, kv_other, query_all, layout, *gain_rows, hidden, wo],
     )
-    (own_weights,) = kernel_call(
-        transpose_kernel, [(weights_shape, bf16)], [wkv], after=[query_all]
-    )
-    other_weights = swapped(own_weights, "tensor", 0)
+    half_shape = (2 * head_width, features // 2)
+    kept_weights, sent_weights = kernel_call(
+        half_weights_kernel, [(half_shape, bf16), (half_shape, bf16)], [wkv, wq], after=[query_all]
+    )
+    other_weights = swapped(sent_weights, "tensor", 0)
     output_gain = out_gain[None, :]
     resid, scaled = kernel_call(
         resid_kernel,
         [((sequences, chunk), f32), ((z_count, sequences, chunk), bf16)],
         [exchange(blocks, "tensor"), output_gain],
     )
-    query_weights, wo_t, transposed = kernel_call(
-        transpose_kernel,
-        [(weights_shape, bf16), ((features, head_width), bf16), ((1,), f32)],
-        [wq, wo],
-        after=[resid],
-    )
-    both_weights, fetched = kernel_call(
+    wo_t, transposed = kernel_call(
+        transpose_kernel, [((features, head_width), bf16), ((1,), f32)], [wo], after=[resid]
+    )
+    pair_weights, fetched = kernel_call(
         stack_kernel,
-        [((2 * head_width, features), bf16), ((1,), f32)],
-        [own_weights, other_weights],
+        [((4 * head_width, features // 2), bf16), ((1,), f32)],
+        [kept_weights, other_weights],
     )
     layout_again, placed = sequence_layout(resid)
     tables = kernel_call(
@@ -766,18 +788,22 @@
     loss, d_resid16 = contrast(
         everyone, resid, output_gain, tables, [transposed, fetched, placed]
     )
-    product, added = kernel_call(
+    gradient_shape = (2 * tokens_count + sequences, head_width)
+    own_gradients, sent_gradients = kernel_call(
         gradient_kernel,
-        [(flat, bf16), ((own_rows, features), f32)],
-        [
-            d_resid16,
-            wo_t,
-            saved,
-            layout_again,
-            *gain_rows,
-            both_weights,
-            query_weights,
-        ],
+        [(gradient_shape, f32), (gradient_shape, bf16)],
+        [d_resid16, wo_t, saved, layout_again, *gain_rows],
+        after=[loss],
+    )
+    other_gradients = swapped(sent_gradients, "tensor", 0)
+    added, summed = kernel_call(
+        added_kernel, [((own_rows, features), f32), ((1,), f32)], [d_resid16, layout_again]
+    )
+    (product,) = kernel_call(
+        product_kernel,
+        [((tensor_count, own_rows * features // LANES // 2, LANES), bf16)],
+        [own_gradients, other_gradients, layout_again, pair_weights],
+        after=[summed],
     )
     terms = exchange(product, "tensor")
     (d_hidden,) = kernel_call(

time: 173 us -> 168 us (0.971)
  blocking collectives: 106 us -> 92.9 us
  local copies, waits for them, and re-layouts: 9.19 us -> 11.9 us
  Pallas kernels: 15.8 us -> 17.7 us
  starting transfers between devices: 25.8 us -> 27.7 us
    all_to_all x5, blocking collectives: 103 us -> 90.5 us  [exchange(): return lax.all_to_all(blocks, axis, 0, 0, tiled=True)]
    ppermute x2 -> x3, starting transfers between devices: 5.79 us -> 9.09 us  [swapped(): return lax.ppermute(value, axis, pairs)]
    ppermute x2 -> x3, waiting for transfers between devices: 1.84 us -> 4.85 us  [swapped(): return lax.ppermute(value, axis, pairs)]
    unnamed x52 -> x60, local copies, waits for them, and re-layouts: 9.19 us -> 11.9 us
    all_to_all x2, waiting for transfers between devices: 12.7 us -> 10.8 us  [exchange(): return lax.all_to_all(blocks, axis, 0, 0, tiled=True)]
    pallas_call x15 -> x17, Pallas kernels: 15.8 us -> 17.7 us  [kernel_call(): pl.pallas_call(kernel, out_shape=[jax.ShapeDtypeStruct(shape, dtype) for...]
  transfers between devices with their start and end apart: 4 -> 5, of which waited for: 3 -> 4; matrix products, arithmetic and copies ran while one was open for 0% -> 0% of each run, Pallas kernels for 3% -> 3%
where the time goes in v8:
time: 168 us; the launch traced here: 167 us
  blocking collectives  92.9 us (55%)
  starting transfers between devices  27.7 us (16%)
  Pallas kernels  17.7 us (11%)
  waiting for transfers between devices  15.7 us (9%)
  local copies, waits for them, and re-layouts  11.9 us (7%)
    all_to_all x5, blocking collectives, exchange(): return lax.all_to_all(blocks, axis, 0, 0, tiled=True)  90.5 us
    all_to_all x2, starting transfers between devices, exchange(): return lax.all_to_all(blocks, axis, 0, 0, tiled=True)  18.6 us
    pallas_call x17, Pallas kernels, kernel_call(): pl.pallas_call(kernel, out_shape=[jax.ShapeDtypeStruct(shape, dtype) for...  17.7 us
    unnamed x60, local copies, waits for them, and re-layouts  11.9 us
    all_to_all x2, waiting for transfers between devices, exchange(): return lax.all_to_all(blocks, axis, 0, 0, tiled=True)  10.8 us
    ppermute x3, starting transfers between devices, swapped(): return lax.ppermute(value, axis, pairs)  9.09 us
    ppermute x3, waiting for transfers between devices, swapped(): return lax.ppermute(value, axis, pairs)  4.85 us
  transfers between devices with their start and end apart: 5, of which 4 were waited for; matrix products, arithmetic and copies ran while one was open for 0% of the time, Pallas kernels for 3%

profile of v8, /device:TPU:2, one launch (start us, length us, event | category | flops | bytes accessed | tf_op | source)
XLA Modules:
  0.0 166.7 jit_solution(9145776132205996550)
XLA Ops:
  0.6 0.0 copy-start.3
  0.6 0.9 copy-done.3
  1.5 0.7 copy-done.18
  2.3 0.3 shard_map.122
  2.6 0.0 copy-start.1
  2.6 0.0 copy-start.2
  2.6 35.0 %all_to_all.35.refs_0_ = bf16[16,512,128]{2,1,0:T(8,128)(2,1)S(1)} all-to-all(bf16[16,512,128]{2,1,0:T(8,128)(2,1)S(1)} %shard_map.122), channel_id=1, replica_groups=mesh['z_far'=8,'z_pair'=2,'core'=2,'tensor'=16] {'tensor'}, dimensions={0} | all-to-all | bytes 4194304 | tf_op jit(solution)/shard_map/all_to_all | solution.py:38
  37.6 0.0 copy-done.1
  37.6 0.0 copy-done.2
  37.6 0.0 copy-start.4
  37.6 0.0 copy-start.25
  37.6 0.0 copy-start.27
  37.7 1.2 shard_map.123
  38.9 3.6 %collective-permute-start = (bf16[256,128]{1,0:T(8,128)(2,1)S(1)}, bf16[256,128]{1,0:T(8,128)(2,1)S(1)}, u32[]{:S(2)}, u32[]{:S(2)}) collective-permute-start(bf16[256,128]{1,0:T(8,128)(2,1)S(1)} %get-tuple-element.30), channel_id=1, source_target_pairs={{0,1},{1,0},{2,3},{3,2},{4,5},{5,4},{6,7},{7,6},{8,9},{9,8},{10,11... | collective-permute-start | bytes 196616 | tf_op jit(solution)/shard_map/ppermute | solution.py:25
  42.5 0.0 copy-done.23
  42.5 0.7 shard_map.124
  43.2 1.8 %collective-permute-done.refs_1_ = bf16[256,128]{1,0:T(8,128)(2,1)S(1)} collective-permute-done((bf16[256,128]{1,0:T(8,128)(2,1)S(1)}, bf16[256,128]{1,0:T(8,128)(2,1)S(1)}, u32[]{:S(2)}, u32[]{:S(2)}) %collective-permute-start) | collective-permute-done | bytes 65568 | tf_op jit(solution)/shard_map/ppermute | solution.py:25
  45.1 0.0 copy-done
  45.1 0.0 copy-done.4
  45.1 0.0 copy-done.25
  45.1 0.0 copy-done.27
  45.1 0.0 copy-start.17
  45.1 1.0 shard_map.125
  46.1 0.8 copy-done.14
  46.9 0.7 copy-done.16
  47.6 5.0 %all-to-all-start.1 = ((bf16[16,32,256]{2,1,0:T(8,128)(2,1)}), bf16[16,32,256]{2,1,0:T(8,128)(2,1)S(1)}, u32[]{:S(2)}, u32[]{:S(2)}) async-start(bf16[16,32,256]{2,1,0:T(8,128)(2,1)} %copy-done.16), calls=%async_computation.1 | async-start | bytes 524288 | tf_op jit(solution)/shard_map/all_to_all | solution.py:38
  52.6 1.6 shard_map.129
  54.2 1.0 copy-done.8
  55.2 2.1 %collective-permute-start.1 = (bf16[256,2048]{1,0:T(8,128)(2,1)}, bf16[256,2048]{1,0:T(8,128)(2,1)S(1)}, u32[]{:S(2)}, u32[]{:S(2)}) collective-permute-start(bf16[256,2048]{1,0:T(8,128)(2,1)} %get-tuple-element.41), channel_id=1, source_target_pairs={{0,1},{1,0},{2,3},{3,2},{4,5},{5,4},{6,7},{7,6},{8,9},{9,8},{10,11... | collective-permute-start | bytes 3145736 | tf_op jit(solution)/shard_map/ppermute | solution.py:25
  57.3 3.6 %all-to-all-done.1.refs_0_ = bf16[16,32,256]{2,1,0:T(8,128)(2,1)S(1)} async-done(((bf16[16,32,256]{2,1,0:T(8,128)(2,1)}), bf16[16,32,256]{2,1,0:T(8,128)(2,1)S(1)}, u32[]{:S(2)}, u32[]{:S(2)}) %all-to-all-start.1) | async-done | bytes 262176 | tf_op jit(solution)/shard_map/all_to_all | solution.py:38
  60.9 0.8 shard_map.126
  61.7 13.6 %all-to-all-start.2 = ((bf16[16,32,256]{2,1,0:T(8,128)(2,1)}), bf16[16,32,256]{2,1,0:T(8,128)(2,1)}, u32[]{:S(2)}, u32[]{:S(2)}) async-start(bf16[16,32,256]{2,1,0:T(8,128)(2,1)} %get-tuple-element.34), calls=%async_computation.2 | async-start | bytes 524288 | tf_op jit(solution)/shard_map/all_to_all | solution.py:38
  75.3 0.5 shard_map.128
  75.8 1.0 copy-done.6
  76.8 0.7 copy-done.24
  77.5 0.7 shard_map.131
  78.2 0.0 copy-start.22
  78.2 0.7 copy-done.22
  78.9 0.7 copy-done.29
  79.5 0.2 shard_map.127
  79.8 0.6 copy-done.20
  80.4 0.0 collective-permute-done.1.refs_1_
  80.4 1.0 copy-done.10
  81.4 1.2 copy-done.9
  82.6 1.2 copy-done.11
  83.8 0.7 shard_map.130
  84.5 7.2 %all-to-all-done.2 = bf16[16,32,256]{2,1,0:T(8,128)(2,1)} async-done(((bf16[16,32,256]{2,1,0:T(8,128)(2,1)}), bf16[16,32,256]{2,1,0:T(8,128)(2,1)}, u32[]{:S(2)}, u32[]{:S(2)}) %all-to-all-start.2) | async-done | bytes 262176 | tf_op jit(solution)/shard_map/all_to_all | solution.py:38
  91.7 2.4 %all-gather = bf16[16,64,256]{2,1,0:T(8,128)(2,1)S(1)} all-gather(bf16[16,32,256]{2,1,0:T(8,128)(2,1)} %all-to-all-done.2), channel_id=2, replica_groups=mesh['z_far'=8,'z_pair'=2,'core'=2,'tensor'=16] {'core'}, dimensions={1}, use_global_device_ids=true | all-gather | bytes 786432 | tf_op jit(solution)/shard_map/all_gather | solution.py:787
  94.1 0.7 copy-done.21
  94.8 3.5 %shard_map.132 = bf16[16,160,128]{2,1,0:T(8,128)(2,1)S(1)} custom-call(bf16[1024,256]{1,0:T(8,128)(2,1)S(1)} %bitcast.8, bf16[256,1024]{1,0:T(8,128)(2,1)S(1)} %get-tuple-element.36.refs_1_.refs_4_, bf16[256,1024]{1,0:T(8,128)(2,1)S(1)} %get-tuple-element.37.refs_2_.refs_1_.refs_3_, s32[16,256]{1,0:T(8,128)S(1)} %copy-done.21, f32[1,4096]{1,0:T(1,128)S(1)} %bitcast.11, ...), custom_call_target="tpu_custom_call" | custom-call | tf_op jit(solution)/shard_map/pallas_call | solution.py:290
  98.3 16.9 %all_to_all.36.refs_0_ = bf16[16,160,128]{2,1,0:T(8,128)(2,1)S(1)} all-to-all(bf16[16,160,128]{2,1,0:T(8,128)(2,1)S(1)} %shard_map.132), channel_id=1, replica_groups=mesh['z_far'=8,'z_pair'=2,'core'=2,'tensor'=16] {'tensor'}, dimensions={0} | all-to-all | bytes 1310720 | tf_op jit(solution)/shard_map/all_to_all | solution.py:38
  115.2 0.5 shard_map.133
  115.7 8.9 %all_to_all.37.refs_0_ = f32[4,144,128]{2,1,0:T(8,128)S(1)} all-to-all(f32[4,144,128]{2,1,0:T(8,128)S(1)} %get-tuple-element.44), channel_id=1, replica_groups=mesh['z_far'=8,'z_pair'=2,'core'=2,'tensor'=16] {'z_pair','core'}, dimensions={0} | all-to-all | bytes 589824 | tf_op jit(solution)/shard_map/all_to_all | solution.py:38
  124.6 1.3 shard_map.134
  125.9 11.9 %all_to_all.38.refs_0_ = bf16[16,32,256]{2,1,0:T(8,128)(2,1)S(1)} all-to-all(bf16[16,32,256]{2,1,0:T(8,128)(2,1)S(1)} %get-tuple-element.46), channel_id=1, replica_groups=mesh['z_far'=8,'z_pair'=2,'core'=2,'tensor'=16] {'tensor'}, dimensions={0} | all-to-all | bytes 524288 | tf_op jit(solution)/shard_map/all_to_all | solution.py:38
  137.7 0.0 copy-done.15
  137.8 1.5 shard_map.135
  139.3 3.4 %collective-permute-start.2 = (bf16[544,128]{1,0:T(8,128)(2,1)S(1)}, bf16[544,128]{1,0:T(8,128)(2,1)S(1)}, u32[]{:S(2)}, u32[]{:S(2)}) collective-permute-start(bf16[544,128]{1,0:T(8,128)(2,1)S(1)} %get-tuple-element.52), channel_id=1, source_target_pairs={{0,1},{1,0},{2,3},{3,2},{4,5},{5,4},{6,7},{7,6},{8,9},{9,8},{10,11... | collective-permute-start | bytes 417800 | tf_op jit(solution)/shard_map/ppermute | solution.py:25
  142.7 0.6 shard_map.136
  143.2 3.0 %collective-permute-done.2.refs_1_ = bf16[544,128]{1,0:T(8,128)(2,1)S(1)} collective-permute-done((bf16[544,128]{1,0:T(8,128)(2,1)S(1)}, bf16[544,128]{1,0:T(8,128)(2,1)S(1)}, u32[]{:S(2)}, u32[]{:S(2)}) %collective-permute-start.2) | collective-permute-done | bytes 139296 | tf_op jit(solution)/shard_map/ppermute | solution.py:25
  146.2 1.6 shard_map.137
  147.8 17.9 %all_to_all.39.refs_0_ = bf16[16,256,128]{2,1,0:T(8,128)(2,1)S(1)} all-to-all(bf16[16,256,128]{2,1,0:T(8,128)(2,1)S(1)} %shard_map.137), channel_id=1, replica_groups=mesh['z_far'=8,'z_pair'=2,'core'=2,'tensor'=16] {'tensor'}, dimensions={0} | all-to-all | bytes 2097152 | tf_op jit(solution)/shard_map/all_to_all | solution.py:38
  165.7 0.0 copy-done.19
  165.7 1.0 shard_map.138
  (29 shorter events, 0.1 us)
Async XLA Ops:
  0.6 0.9 copy-start.3
  1.5 0.7 copy-start.18
  2.6 35.0 %copy-start.1 = (bf16[4096,128]{1,0:T(8,128)(2,1)S(1)}, bf16[4096,128]{1,0:T(8,128)(2,1)}, u32[]{:S(2)}) copy-start(bf16[4096,128]{1,0:T(8,128)(2,1)} %refs_0_.8) | copy-start | bytes 3145732
  2.6 35.0 %copy-start.2 = (bf16[4096,128]{1,0:T(8,128)(2,1)S(1)}, bf16[4096,128]{1,0:T(8,128)(2,1)}, u32[]{:S(2)}) copy-start(bf16[4096,128]{1,0:T(8,128)(2,1)} %refs_1_.4) | copy-start | bytes 3145732
  37.6 4.9 %copy-start.23 = (s32[1,32]{1,0:T(1,128)S(1)}, s32[1,32]{1,0:T(1,128)}, u32[]{:S(2)}) copy-start(s32[1,32]{1,0:T(1,128)} %refs_0_.9) | copy-start | bytes 388
  37.6 7.5 %copy-start = (bf16[128,4096]{1,0:T(8,128)(2,1)S(1)}, bf16[128,4096]{1,0:T(8,128)(2,1)}, u32[]{:S(2)}) copy-start(bf16[128,4096]{1,0:T(8,128)(2,1)} %refs_0_.7) | copy-start | bytes 3145732
  37.6 7.5 %copy-start.4 = (bf16[16,4096]{1,0:T(8,128)(2,1)S(1)}, bf16[16,4096]{1,0:T(8,128)(2,1)}, u32[]{:S(2)}) copy-start(bf16[16,4096]{1,0:T(8,128)(2,1)} %refs_1_.5) | copy-start | bytes 393220
  37.6 7.4 %copy-start.25 = (f32[128]{0:T(128)S(1)}, f32[128]{0:T(128)}, u32[]{:S(2)}) copy-start(f32[128]{0:T(128)} %param.18) | copy-start | bytes 1540
  37.6 7.4 %copy-start.27 = (f32[128]{0:T(128)S(1)}, f32[128]{0:T(128)}, u32[]{:S(2)}) copy-start(f32[128]{0:T(128)} %param.19) | copy-start | bytes 1540
  38.9 6.2 %collective-permute-start = (bf16[256,128]{1,0:T(8,128)(2,1)S(1)}, bf16[256,128]{1,0:T(8,128)(2,1)S(1)}, u32[]{:S(2)}, u32[]{:S(2)}) collective-permute-start(bf16[256,128]{1,0:T(8,128)(2,1)S(1)} %get-tuple-element.30), channel_id=1, source_target_pairs={{0,1},{1,0},{2,3},{3,2},{4,5},{5,4},{6,7},{7,6},{8,9},{9,8},{10,11... | collective-permute-start | bytes 196616 | tf_op jit(solution)/shard_map/ppermute | solution.py:25
  45.1 15.8 %copy-start.17 = (f32[4096]{0:T(1024)S(1)}, f32[4096]{0:T(1024)}, u32[]{:S(2)}) copy-start(f32[4096]{0:T(1024)} %param.21) | copy-start | bytes 49156
  46.1 0.8 copy-start.14
  46.9 0.7 copy-start.16
  47.6 13.3 %all-to-all-start.1 = ((bf16[16,32,256]{2,1,0:T(8,128)(2,1)}), bf16[16,32,256]{2,1,0:T(8,128)(2,1)S(1)}, u32[]{:S(2)}, u32[]{:S(2)}) async-start(bf16[16,32,256]{2,1,0:T(8,128)(2,1)} %copy-done.16), calls=%async_computation.1 | async-start | bytes 524288 | tf_op jit(solution)/shard_map/all_to_all | solution.py:38
  54.2 1.0 copy-start.8
  55.2 25.2 %collective-permute-start.1 = (bf16[256,2048]{1,0:T(8,128)(2,1)}, bf16[256,2048]{1,0:T(8,128)(2,1)S(1)}, u32[]{:S(2)}, u32[]{:S(2)}) collective-permute-start(bf16[256,2048]{1,0:T(8,128)(2,1)} %get-tuple-element.41), channel_id=1, source_target_pairs={{0,1},{1,0},{2,3},{3,2},{4,5},{5,4},{6,7},{7,6},{8,9},{9,8},{10,11... | collective-permute-start | bytes 3145736 | tf_op jit(solution)/shard_map/ppermute | solution.py:25
  61.7 18.7 %copy-start.12 = (f32[32,256]{1,0:T(8,128)}, f32[32,256]{1,0:T(8,128)S(1)}, u32[]{:S(2)}) copy-start(f32[32,256]{1,0:T(8,128)S(1)} %get-tuple-element.35.refs_2_.refs_1_.refs_6_) | copy-start | bytes 98308
  61.7 30.0 %all-to-all-start.2 = ((bf16[16,32,256]{2,1,0:T(8,128)(2,1)}), bf16[16,32,256]{2,1,0:T(8,128)(2,1)}, u32[]{:S(2)}, u32[]{:S(2)}) async-start(bf16[16,32,256]{2,1,0:T(8,128)(2,1)} %get-tuple-element.34), calls=%async_computation.2 | async-start | bytes 524288 | tf_op jit(solution)/shard_map/all_to_all | solution.py:38
  75.8 1.0 copy-start.6
  76.8 0.7 copy-start.24
  78.2 0.7 copy-start.22
  78.9 0.7 copy-start.29
  79.8 0.6 copy-start.20
  80.4 1.0 copy-start.10
  81.4 1.2 copy-start.9
  82.6 1.2 copy-start.11
  94.1 0.7 copy-start.21
  98.3 26.3 %copy-start.13 = (f32[32,256]{1,0:T(8,128)S(1)}, f32[32,256]{1,0:T(8,128)}, u32[]{:S(2)}) copy-start(f32[32,256]{1,0:T(8,128)} %copy-done.12) | copy-start | bytes 98308
  115.2 22.5 %copy-start.7 = (bf16[4096,128]{1,0:T(8,128)(2,1)S(1)}, bf16[4096,128]{1,0:T(8,128)(2,1)}, u32[]{:S(2)}) copy-start(bf16[4096,128]{1,0:T(8,128)(2,1)} %copy-done.6) | copy-start | bytes 3145732
  115.2 22.5 %copy-start.15 = (f32[896,128]{1,0:T(8,128)S(1)}, f32[896,128]{1,0:T(8,128)}, u32[]{:S(2)}) copy-start(f32[896,128]{1,0:T(8,128)} %copy-done.14) | copy-start | bytes 1376260
  115.2 22.5 %copy-start.26 = (f32[128]{0:T(128)S(1)}, f32[128]{0:T(128)}, u32[]{:S(2)}) copy-start(f32[128]{0:T(128)} %param.18) | copy-start | bytes 1540
  115.2 22.5 %copy-start.28 = (f32[128]{0:T(128)S(1)}, f32[128]{0:T(128)}, u32[]{:S(2)}) copy-start(f32[128]{0:T(128)} %param.19) | copy-start | bytes 1540
  139.3 6.9 %collective-permute-start.2 = (bf16[544,128]{1,0:T(8,128)(2,1)S(1)}, bf16[544,128]{1,0:T(8,128)(2,1)S(1)}, u32[]{:S(2)}, u32[]{:S(2)}) collective-permute-start(bf16[544,128]{1,0:T(8,128)(2,1)S(1)} %get-tuple-element.52), channel_id=1, source_target_pairs={{0,1},{1,0},{2,3},{3,2},{4,5},{5,4},{6,7},{7,6},{8,9},{9,8},{10,11... | collective-permute-start | bytes 417800 | tf_op jit(solution)/shard_map/ppermute | solution.py:25
  146.2 19.5 %copy-start.5 = (bf16[16,4096]{1,0:T(8,128)(2,1)S(1)}, bf16[16,4096]{1,0:T(8,128)(2,1)}, u32[]{:S(2)}) copy-start(bf16[16,4096]{1,0:T(8,128)(2,1)} %refs_1_.5) | copy-start | bytes 393220
  146.2 19.5 %copy-start.19 = (f32[4096]{0:T(1024)S(1)}, f32[4096]{0:T(1024)}, u32[]{:S(2)}) copy-start(f32[4096]{0:T(1024)} %param.15) | copy-start | bytes 49156

commit v9 on v8

--- a/solution.py
+++ b/solution.py
@@ -106,13 +106,18 @@
         positives.astype(jnp.bfloat16), queries, against, preferred_element_type=jnp.float32
     )
     with_all = lax.dot_general(rows, queries, against, preferred_element_type=jnp.float32)
-    row_index = iota(with_all.shape, 0)
+    squares_all = jnp.broadcast_to(squares, with_all.shape)
+    row_index = iota((LANES, LANES), 0)
     for j in range(8):
-        listed = row_index == listed_ref[j : j + 1, :]
-        held_ref[j : j + 1, :] = jnp.sum(jnp.where(listed, with_all, 0.0), axis=0, keepdims=True)
-        held_ref[8 + j : 9 + j, :] = jnp.sum(
-            jnp.where(listed, squares, 0.0), axis=0, keepdims=True
-        )
+        product = jnp.zeros((LANES, LANES), jnp.float32)
+        square = product
+        for k in range(with_all.shape[0] // LANES):
+            rows_at = slice(LANES * k, LANES * (k + 1))
+            hit = row_index == listed_ref[j : j + 1, :] - LANES * k
+            product = jnp.where(hit, with_all[rows_at], product)
+            square = jnp.where(hit, squares_all[rows_at], square)
+        held_ref[j : j + 1, :] = jnp.sum(product, axis=0, keepdims=True)
+        held_ref[8 + j : 9 + j, :] = jnp.sum(square, axis=0, keepdims=True)
     columns_to_lanes(squares, held_ref.at[16:24])
     count = with_positives.shape[0] // 2
     sent = fold_half(with_positives[:count], with_positives[count:], half).astype(jnp.bfloat16)
@@ -352,7 +357,7 @@
     token_ref[0] = jnp.float32(0.0)
 
 
-def contrast(everyone, resid, gains, tables, after):
+def contrast(everyone, resid, gains, tables, after, after_logits):
     tensor_count = lax.axis_size("tensor")
     sequences, width = resid.shape
     listed, query_hot, positive_hot = tables
@@ -370,6 +375,7 @@
         softmax_kernel,
         [((4, count // 2 + 16, LANES), jnp.float32), ((8, LANES), jnp.float32)],
         [arrived, positive_hot],
+        after=after_logits,
     )
     both = exchange(coefs, ("z_pair", "core"))
     d_resid16, loss = kernel_call(
@@ -786,7 +792,7 @@
     )
     everyone = lax.all_gather(exchange(scaled, ("z_far", "z_pair")), "core", axis=1)
     loss, d_resid16 = contrast(
-        everyone, resid, output_gain, tables, [transposed, fetched, placed]
+        everyone, resid, output_gain, tables, [transposed, placed], [fetched]
     )
     gradient_shape = (2 * tokens_count + sequences, head_width)
     own_gradients, sent_gradients = kernel_call(

time: 168 us -> 165 us (0.982)
  local copies, waits for them, and re-layouts: 11.9 us -> 6.89 us
  blocking collectives: 92.9 us -> 88 us
  waiting for transfers between devices: 15.7 us -> 19.5 us
  starting transfers between devices: 27.7 us -> 30 us
    unnamed x60 -> x44, local copies, waits for them, and re-layouts: 11.9 us -> 6.89 us
    all_to_all x5, blocking collectives: 90.5 us -> 85.7 us  [exchange(): return lax.all_to_all(blocks, axis, 0, 0, tiled=True)]
    all_to_all x2, waiting for transfers between devices: 10.8 us -> 14.6 us  [exchange(): return lax.all_to_all(blocks, axis, 0, 0, tiled=True)]
  transfers between devices with their start and end apart: 5 -> 5, of which waited for: 4 -> 4; matrix products, arithmetic and copies ran while one was open for 0% -> 0% of each run, Pallas kernels for 3% -> 6%
where the time goes in v9:
time: 165 us; the launch traced here: 164 us
  blocking collectives  88 us (53%)
  starting transfers between devices  30 us (18%)
  waiting for transfers between devices  19.5 us (12%)
  Pallas kernels  18.9 us (11%)
  local copies, waits for them, and re-layouts  6.89 us (4%)
    all_to_all x5, blocking collectives, exchange(): return lax.all_to_all(blocks, axis, 0, 0, tiled=True)  85.7 us
    all_to_all x2, starting transfers between devices, exchange(): return lax.all_to_all(blocks, axis, 0, 0, tiled=True)  19.7 us
    pallas_call x17, Pallas kernels, kernel_call(): pl.pallas_call(kernel, out_shape=[jax.ShapeDtypeStruct(shape, dtype) for...  18.9 us
    all_to_all x2, waiting for transfers between devices, exchange(): return lax.all_to_all(blocks, axis, 0, 0, tiled=True)  14.6 us
    ppermute x3, starting transfers between devices, swapped(): return lax.ppermute(value, axis, pairs)  10.3 us
    unnamed x44, local copies, waits for them, and re-layouts  6.89 us
    ppermute x3, waiting for transfers between devices, swapped(): return lax.ppermute(value, axis, pairs)  4.88 us
  transfers between devices with their start and end apart: 5, of which 4 were waited for; matrix products, arithmetic and copies ran while one was open for 0% of the time, Pallas kernels for 6%

profile of v9, /device:TPU:2, one launch (start us, length us, event | category | flops | bytes accessed | tf_op | source)
XLA Modules:
  0.0 164.2 jit_solution(5927814647957108542)
XLA Ops:
  0.6 0.0 copy-start.5
  0.6 0.9 copy-done.5
  1.5 0.7 copy-done.15
  2.3 0.3 shard_map.122
  2.6 0.0 copy-start.1
  2.6 0.0 copy-start.2
  2.6 35.0 %all_to_all.35.refs_0_ = bf16[16,512,128]{2,1,0:T(8,128)(2,1)S(1)} all-to-all(bf16[16,512,128]{2,1,0:T(8,128)(2,1)S(1)} %shard_map.122), channel_id=1, replica_groups=mesh['z_far'=8,'z_pair'=2,'core'=2,'tensor'=16] {'tensor'}, dimensions={0} | all-to-all | bytes 4194304 | tf_op jit(solution)/shard_map/all_to_all | solution.py:38
  37.6 0.0 copy-done.1
  37.6 0.0 copy-done.2
  37.6 0.0 copy-start.6
  37.6 0.0 copy-start.19
  37.6 0.0 copy-start.20
  37.7 1.2 shard_map.123
  38.9 0.0 copy-start.14
  38.9 3.6 %collective-permute-start = (bf16[256,128]{1,0:T(8,128)(2,1)S(1)}, bf16[256,128]{1,0:T(8,128)(2,1)S(1)}, u32[]{:S(2)}, u32[]{:S(2)}) collective-permute-start(bf16[256,128]{1,0:T(8,128)(2,1)S(1)} %get-tuple-element.30), channel_id=1, source_target_pairs={{0,1},{1,0},{2,3},{3,2},{4,5},{5,4},{6,7},{7,6},{8,9},{9,8},{10,11... | collective-permute-start | bytes 196616 | tf_op jit(solution)/shard_map/ppermute | solution.py:25
  42.5 0.0 copy-done.18
  42.5 0.7 shard_map.124
  43.2 1.8 %collective-permute-done.refs_1_ = bf16[256,128]{1,0:T(8,128)(2,1)S(1)} collective-permute-done((bf16[256,128]{1,0:T(8,128)(2,1)S(1)}, bf16[256,128]{1,0:T(8,128)(2,1)S(1)}, u32[]{:S(2)}, u32[]{:S(2)}) %collective-permute-start) | collective-permute-done | bytes 65568 | tf_op jit(solution)/shard_map/ppermute | solution.py:25
  45.1 0.0 copy-done
  45.1 0.0 copy-done.6
  45.1 0.0 copy-done.19
  45.1 0.0 copy-done.20
  45.1 1.0 shard_map.125
  46.1 0.0 copy-start.11
  46.1 11.5 %all_to_all.36.refs_0_ = bf16[16,32,256]{2,1,0:T(8,128)(2,1)S(1)} all-to-all(bf16[16,32,256]{2,1,0:T(8,128)(2,1)S(1)} %get-tuple-element.33), channel_id=1, replica_groups=mesh['z_far'=8,'z_pair'=2,'core'=2,'tensor'=16] {'tensor'}, dimensions={0} | all-to-all | bytes 524288 | tf_op jit(solution)/shard_map/all_to_all | solution.py:38
  57.7 0.0 copy-done.14
  57.7 0.0 copy-done.11
  57.7 0.0 copy-start.13
  57.7 0.7 copy-done.13
  58.4 14.8 %all-to-all-start.2 = ((bf16[16,32,256]{2,1,0:T(8,128)(2,1)}), bf16[16,32,256]{2,1,0:T(8,128)(2,1)}, u32[]{:S(2)}, u32[]{:S(2)}) async-start(bf16[16,32,256]{2,1,0:T(8,128)(2,1)} %copy-done.13), calls=%async_computation.2 | async-start | bytes 524288 | tf_op jit(solution)/shard_map/all_to_all | solution.py:38
  73.3 1.6 shard_map.131
  74.8 1.0 copy-done.9
  75.8 3.4 %collective-permute-start.1 = (bf16[256,2048]{1,0:T(8,128)(2,1)}, bf16[256,2048]{1,0:T(8,128)(2,1)}, u32[]{:S(2)}, u32[]{:S(2)}) collective-permute-start(bf16[256,2048]{1,0:T(8,128)(2,1)} %get-tuple-element.42), channel_id=1, source_target_pairs={{0,1},{1,0},{2,3},{3,2},{4,5},{5,4},{6,7},{7,6},{8,9},{9,8},{10,11... | collective-permute-start | bytes 3145736 | tf_op jit(solution)/shard_map/ppermute | solution.py:25
  79.2 0.7 shard_map.129
  79.9 0.5 shard_map.128
  80.4 0.0 copy-start.7
  80.4 1.0 copy-done.7
  81.4 0.0 copy-done.17
  81.4 0.0 copy-done.21
  81.4 0.2 shard_map.127
  81.7 6.7 %all-to-all-done.2 = bf16[16,32,256]{2,1,0:T(8,128)(2,1)} async-done(((bf16[16,32,256]{2,1,0:T(8,128)(2,1)}), bf16[16,32,256]{2,1,0:T(8,128)(2,1)}, u32[]{:S(2)}, u32[]{:S(2)}) %all-to-all-start.2) | async-done | bytes 262176 | tf_op jit(solution)/shard_map/all_to_all | solution.py:38
  88.4 2.4 %all-gather = bf16[16,64,256]{2,1,0:T(8,128)(2,1)S(1)} all-gather(bf16[16,32,256]{2,1,0:T(8,128)(2,1)} %all-to-all-done.2), channel_id=2, replica_groups=mesh['z_far'=8,'z_pair'=2,'core'=2,'tensor'=16] {'core'}, dimensions={1}, use_global_device_ids=true | all-gather | bytes 786432 | tf_op jit(solution)/shard_map/all_gather | solution.py:793
  90.8 3.6 %shard_map.130 = bf16[16,160,128]{2,1,0:T(8,128)(2,1)} custom-call(bf16[1024,256]{1,0:T(8,128)(2,1)S(1)} %bitcast.8, bf16[256,1024]{1,0:T(8,128)(2,1)S(1)} %get-tuple-element.36.refs_1_.refs_4_, bf16[256,1024]{1,0:T(8,128)(2,1)S(1)} %get-tuple-element.37.refs_2_.refs_1_.refs_3_, s32[16,256]{1,0:T(8,128)S(1)} %get-tuple-element.38.refs_3_.refs_5_, ...), custom_call_target="tpu_custom_call" | custom-call | tf_op jit(solution)/shard_map/pallas_call | solution.py:295
  94.3 4.8 %all-to-all-start.3 = ((bf16[16,160,128]{2,1,0:T(8,128)(2,1)}), bf16[16,160,128]{2,1,0:T(8,128)(2,1)S(1)}, u32[]{:S(2)}, u32[]{:S(2)}) async-start(bf16[16,160,128]{2,1,0:T(8,128)(2,1)} %shard_map.130), calls=%async_computation.3 | async-start | bytes 1310720 | tf_op jit(solution)/shard_map/all_to_all | solution.py:38
  99.2 0.0 collective-permute-done.1.refs_1_
  99.2 1.2 copy-done.10
  100.4 1.7 %shard_map.132 = (bf16[512,2048]{1,0:T(8,128)(2,1)S(1)}, f32[1]{0:T(128)}) custom-call(bf16[256,2048]{1,0:T(8,128)(2,1)S(1)} %copy-done.10, bf16[256,2048]{1,0:T(8,128)(2,1)} %collective-permute-done.1.refs_1_), custom_call_target="tpu_custom_call" | custom-call | tf_op jit(solution)/shard_map/pallas_call | solution.py:295
  102.2 0.0 copy-start.3
  102.2 1.3 copy-done.3
  103.5 7.9 %all-to-all-done.3.refs_0_ = bf16[16,160,128]{2,1,0:T(8,128)(2,1)S(1)} async-done(((bf16[16,160,128]{2,1,0:T(8,128)(2,1)}), bf16[16,160,128]{2,1,0:T(8,128)(2,1)S(1)}, u32[]{:S(2)}, u32[]{:S(2)}) %all-to-all-start.3) | async-done | bytes 655392 | tf_op jit(solution)/shard_map/all_to_all | solution.py:38
  111.4 1.3 shard_map.133
  112.7 9.4 %all_to_all.37.refs_0_ = f32[4,144,128]{2,1,0:T(8,128)S(1)} all-to-all(f32[4,144,128]{2,1,0:T(8,128)S(1)} %get-tuple-element.44), channel_id=1, replica_groups=mesh['z_far'=8,'z_pair'=2,'core'=2,'tensor'=16] {'z_pair','core'}, dimensions={0} | all-to-all | bytes 589824 | tf_op jit(solution)/shard_map/all_to_all | solution.py:38
  122.1 1.3 shard_map.134
  123.4 0.0 copy-start.4
  123.4 11.8 %all_to_all.38.refs_0_ = bf16[16,32,256]{2,1,0:T(8,128)(2,1)S(1)} all-to-all(bf16[16,32,256]{2,1,0:T(8,128)(2,1)S(1)} %get-tuple-element.46), channel_id=1, replica_groups=mesh['z_far'=8,'z_pair'=2,'core'=2,'tensor'=16] {'tensor'}, dimensions={0} | all-to-all | bytes 524288 | tf_op jit(solution)/shard_map/all_to_all | solution.py:38
  135.3 0.0 copy-done.8
  135.3 1.5 shard_map.135
  136.8 3.4 %collective-permute-start.2 = (bf16[544,128]{1,0:T(8,128)(2,1)S(1)}, bf16[544,128]{1,0:T(8,128)(2,1)S(1)}, u32[]{:S(2)}, u32[]{:S(2)}) collective-permute-start(bf16[544,128]{1,0:T(8,128)(2,1)S(1)} %get-tuple-element.52), channel_id=1, source_target_pairs={{0,1},{1,0},{2,3},{3,2},{4,5},{5,4},{6,7},{7,6},{8,9},{9,8},{10,11... | collective-permute-start | bytes 417800 | tf_op jit(solution)/shard_map/ppermute | solution.py:25
  140.2 0.6 shard_map.136
  140.7 3.0 %collective-permute-done.2.refs_1_ = bf16[544,128]{1,0:T(8,128)(2,1)S(1)} collective-permute-done((bf16[544,128]{1,0:T(8,128)(2,1)S(1)}, bf16[544,128]{1,0:T(8,128)(2,1)S(1)}, u32[]{:S(2)}, u32[]{:S(2)}) %collective-permute-start.2) | collective-permute-done | bytes 139296 | tf_op jit(solution)/shard_map/ppermute | solution.py:25
  143.7 1.5 shard_map.137
  145.3 17.9 %all_to_all.39.refs_0_ = bf16[16,256,128]{2,1,0:T(8,128)(2,1)S(1)} all-to-all(bf16[16,256,128]{2,1,0:T(8,128)(2,1)S(1)} %shard_map.137), channel_id=1, replica_groups=mesh['z_far'=8,'z_pair'=2,'core'=2,'tensor'=16] {'tensor'}, dimensions={0} | all-to-all | bytes 2097152 | tf_op jit(solution)/shard_map/all_to_all | solution.py:38
  163.2 0.0 copy-done.16
  163.2 1.0 shard_map.138
  (13 shorter events, 0.1 us)
Async XLA Ops:
  0.6 0.9 copy-start.5
  1.5 0.7 copy-start.15
  2.6 35.0 %copy-start.1 = (bf16[4096,128]{1,0:T(8,128)(2,1)S(1)}, bf16[4096,128]{1,0:T(8,128)(2,1)}, u32[]{:S(2)}) copy-start(bf16[4096,128]{1,0:T(8,128)(2,1)} %refs_0_.9) | copy-start | bytes 3145732
  2.6 35.0 %copy-start.2 = (bf16[4096,128]{1,0:T(8,128)(2,1)S(1)}, bf16[4096,128]{1,0:T(8,128)(2,1)}, u32[]{:S(2)}) copy-start(bf16[4096,128]{1,0:T(8,128)(2,1)} %refs_1_.4) | copy-start | bytes 3145732
  37.6 4.9 %copy-start.18 = (s32[1,32]{1,0:T(1,128)S(1)}, s32[1,32]{1,0:T(1,128)}, u32[]{:S(2)}) copy-start(s32[1,32]{1,0:T(1,128)} %refs_0_.8) | copy-start | bytes 388
  37.6 7.5 %copy-start = (bf16[128,4096]{1,0:T(8,128)(2,1)S(1)}, bf16[128,4096]{1,0:T(8,128)(2,1)}, u32[]{:S(2)}) copy-start(bf16[128,4096]{1,0:T(8,128)(2,1)} %refs_0_.7) | copy-start | bytes 3145732
  37.6 7.5 %copy-start.6 = (bf16[16,4096]{1,0:T(8,128)(2,1)S(1)}, bf16[16,4096]{1,0:T(8,128)(2,1)}, u32[]{:S(2)}) copy-start(bf16[16,4096]{1,0:T(8,128)(2,1)} %refs_1_.5) | copy-start | bytes 393220
  37.6 7.5 %copy-start.19 = (f32[128]{0:T(128)S(1)}, f32[128]{0:T(128)}, u32[]{:S(2)}) copy-start(f32[128]{0:T(128)} %param.18) | copy-start | bytes 1540
  37.6 7.4 %copy-start.20 = (f32[128]{0:T(128)S(1)}, f32[128]{0:T(128)}, u32[]{:S(2)}) copy-start(f32[128]{0:T(128)} %param.19) | copy-start | bytes 1540
  38.9 18.8 %copy-start.14 = (f32[4096]{0:T(1024)S(1)}, f32[4096]{0:T(1024)}, u32[]{:S(2)}) copy-start(f32[4096]{0:T(1024)} %param.21) | copy-start | bytes 49156
  38.9 6.2 %collective-permute-start = (bf16[256,128]{1,0:T(8,128)(2,1)S(1)}, bf16[256,128]{1,0:T(8,128)(2,1)S(1)}, u32[]{:S(2)}, u32[]{:S(2)}) collective-permute-start(bf16[256,128]{1,0:T(8,128)(2,1)S(1)} %get-tuple-element.30), channel_id=1, source_target_pairs={{0,1},{1,0},{2,3},{3,2},{4,5},{5,4},{6,7},{7,6},{8,9},{9,8},{10,11... | collective-permute-start | bytes 196616 | tf_op jit(solution)/shard_map/ppermute | solution.py:25
  46.1 11.6 %copy-start.11 = (f32[896,128]{1,0:T(8,128)}, f32[896,128]{1,0:T(8,128)S(1)}, u32[]{:S(2)}) copy-start(f32[896,128]{1,0:T(8,128)S(1)} %get-tuple-element.48.refs_2_) | copy-start | bytes 1376260
  57.7 23.8 %copy-start.17 = (s32[256,7]{0,1:T(8,128)S(1)}, s32[256,7]{0,1:T(8,128)}, u32[]{:S(2)}) copy-start(s32[256,7]{0,1:T(8,128)} %param.14) | copy-start | bytes 21508
  57.7 23.8 %copy-start.21 = (s32[256]{0:T(256)S(1)}, s32[256]{0:T(256)}, u32[]{:S(2)}) copy-start(s32[256]{0:T(256)} %param.13) | copy-start | bytes 3076
  57.7 0.7 copy-start.13
  58.4 29.9 %all-to-all-start.2 = ((bf16[16,32,256]{2,1,0:T(8,128)(2,1)}), bf16[16,32,256]{2,1,0:T(8,128)(2,1)}, u32[]{:S(2)}, u32[]{:S(2)}) async-start(bf16[16,32,256]{2,1,0:T(8,128)(2,1)} %copy-done.13), calls=%async_computation.2 | async-start | bytes 524288 | tf_op jit(solution)/shard_map/all_to_all | solution.py:38
  74.8 1.0 copy-start.9
  75.8 23.4 %collective-permute-start.1 = (bf16[256,2048]{1,0:T(8,128)(2,1)}, bf16[256,2048]{1,0:T(8,128)(2,1)}, u32[]{:S(2)}, u32[]{:S(2)}) collective-permute-start(bf16[256,2048]{1,0:T(8,128)(2,1)} %get-tuple-element.42), channel_id=1, source_target_pairs={{0,1},{1,0},{2,3},{3,2},{4,5},{5,4},{6,7},{7,6},{8,9},{9,8},{10,11... | collective-permute-start | bytes 3145736 | tf_op jit(solution)/shard_map/ppermute | solution.py:25
  80.4 1.0 copy-start.7
  94.3 17.1 %all-to-all-start.3 = ((bf16[16,160,128]{2,1,0:T(8,128)(2,1)}), bf16[16,160,128]{2,1,0:T(8,128)(2,1)S(1)}, u32[]{:S(2)}, u32[]{:S(2)}) async-start(bf16[16,160,128]{2,1,0:T(8,128)(2,1)} %shard_map.130), calls=%async_computation.3 | async-start | bytes 1310720 | tf_op jit(solution)/shard_map/all_to_all | solution.py:38
  99.2 1.2 copy-start.10
  102.2 1.4 copy-start.3
  111.4 23.8 %copy-start.8 = (bf16[4096,128]{1,0:T(8,128)(2,1)S(1)}, bf16[4096,128]{1,0:T(8,128)(2,1)}, u32[]{:S(2)}) copy-start(bf16[4096,128]{1,0:T(8,128)(2,1)} %copy-done.7) | copy-start | bytes 3145732
  111.4 23.8 %copy-start.12 = (f32[896,128]{1,0:T(8,128)S(1)}, f32[896,128]{1,0:T(8,128)}, u32[]{:S(2)}) copy-start(f32[896,128]{1,0:T(8,128)} %copy-done.11) | copy-start | bytes 1376260
  123.4 20.3 %copy-start.4 = (bf16[512,2048]{1,0:T(8,128)(2,1)S(1)}, bf16[512,2048]{1,0:T(8,128)(2,1)}, u32[]{:S(2)}) copy-start(bf16[512,2048]{1,0:T(8,128)(2,1)} %copy-done.3) | copy-start | bytes 6291460
  136.8 6.9 %collective-permute-start.2 = (bf16[544,128]{1,0:T(8,128)(2,1)S(1)}, bf16[544,128]{1,0:T(8,128)(2,1)S(1)}, u32[]{:S(2)}, u32[]{:S(2)}) collective-permute-start(bf16[544,128]{1,0:T(8,128)(2,1)S(1)} %get-tuple-element.52), channel_id=1, source_target_pairs={{0,1},{1,0},{2,3},{3,2},{4,5},{5,4},{6,7},{7,6},{8,9},{9,8},{10,11... | collective-permute-start | bytes 417800 | tf_op jit(solution)/shard_map/ppermute | solution.py:25
  143.7 19.5 %copy-start.16 = (f32[4096]{0:T(1024)S(1)}, f32[4096]{0:T(1024)}, u32[]{:S(2)}) copy-start(f32[4096]{0:T(1024)} %param.15) | copy-start | bytes 49156

commit v10 on v9

--- a/solution.py
+++ b/solution.py
@@ -34,8 +34,8 @@
     return inverse * (scaled - unit_form * jnp.mean(unit_form * scaled, axis=-1, keepdims=True))
 
 
-def exchange(blocks, axis):
-    return lax.all_to_all(blocks, axis, 0, 0, tiled=True)
+def exchange(blocks, axis, groups=None):
+    return lax.all_to_all(blocks, axis, 0, 0, axis_index_groups=groups, tiled=True)
 
 
 def halves(value):
@@ -54,30 +54,8 @@
         out_ref[k : k + 1, :] = jnp.sum(block, axis=0, keepdims=True)
 
 
-HALF = LANES // 2
-
-
-def query_block():
-    return lax.axis_index("z_pair"), lax.axis_index("core")
-
-
-def block_lanes(block):
-    return pl.ds(pl.multiple_of(block * LANES, LANES), LANES)
-
-
-def in_first_half(shape):
-    return iota(shape, len(shape) - 1) < HALF
-
-
-def fold_half(first, second, half):
-    is_first = in_first_half(first.shape)
-    low = jnp.where(is_first, first, pltpu.roll(second, HALF, 1))
-    high = jnp.where(is_first, pltpu.roll(first, HALF, 1), second)
-    return jnp.where(half == 0, low, high)
-
-
-def unfold_half(block):
-    return block, pltpu.roll(block, HALF, 1)
+def core_rows():
+    return pl.ds(pl.multiple_of(lax.axis_index("core") * LANES, LANES), LANES)
 
 
 def own_columns(gains_ref, width):
@@ -89,9 +67,8 @@
     rows_ref, query_hot_ref, positive_hot_ref, listed_all_ref, gains_ref, out_ref, held_ref
 ):
     rows = rows_ref[...]
-    query_at, half = query_block()
-    listed_ref = listed_all_ref[:8, block_lanes(query_at)]
-    block_hot = query_hot_ref[block_lanes(query_at), :]
+    listed_ref = listed_all_ref[:8, core_rows()]
+    block_hot = query_hot_ref[core_rows(), :]
     queries = jnp.dot(block_hot, rows, preferred_element_type=jnp.float32)
     positives = jnp.dot(positive_hot_ref[...], rows, preferred_element_type=jnp.float32)
     queries = queries.astype(jnp.bfloat16)
@@ -119,34 +96,38 @@
         held_ref[j : j + 1, :] = jnp.sum(product, axis=0, keepdims=True)
         held_ref[8 + j : 9 + j, :] = jnp.sum(square, axis=0, keepdims=True)
     columns_to_lanes(squares, held_ref.at[16:24])
-    count = with_positives.shape[0] // 2
-    sent = fold_half(with_positives[:count], with_positives[count:], half).astype(jnp.bfloat16)
-    high, low = halves(held_ref[0:16, :])
-    listed16 = fold_half(high, low, half).astype(jnp.bfloat16)
-    squares16 = jnp.concatenate(halves(held_ref[16:24, :])).astype(jnp.bfloat16)
+    send_logits(with_positives, [held_ref[8 * k : 8 * (k + 1), :] for k in range(3)], out_ref)
+
+
+def send_logits(logits, others, out_ref):
+    count = logits.shape[0]
+    logits16 = logits.astype(jnp.bfloat16)
+    others16 = [jnp.concatenate(halves(other), axis=0).astype(jnp.bfloat16) for other in others]
     for t in range(out_ref.shape[0]):
-        out_ref[t, :count, :] = sent
-        out_ref[t, count : count + 16, :] = listed16
-        out_ref[t, count + 16 : count + 32, :] = squares16
-
-
-def softmax_kernel(arrived_ref, positive_hot_ref, out_ref, inverse_ref):
-    count = positive_hot_ref.shape[0]
+        out_ref[t, :count, :] = logits16
+        for k, other16 in enumerate(others16):
+            out_ref[t, count + 16 * k : count + 16 * (k + 1), :] = other16
+
+
+def summed_logits(arrived_ref):
     summed = arrived_ref[0].astype(jnp.float32)
     for t in range(1, arrived_ref.shape[0]):
         summed = summed + arrived_ref[t].astype(jnp.float32)
-    query_at, half = query_block()
-    first_query = query_at * LANES + half * HALF
-    start = count // 2
-    with_positives = jnp.concatenate(unfold_half(summed[:start]), axis=0)
-    high, low = unfold_half(summed[start : start + 16])
-    hard, listed_squares = high[:8] + low[:8], high[8:] + low[8:]
-    squares = summed[start + 16 : start + 24] + summed[start + 24 : start + 32]
-
-    def valid(value, other):
-        return jnp.where(in_first_half(value.shape), value, other)
-
-    inverse_listed = lax.rsqrt(valid(listed_squares, 1.0) + EPSILON * EPSILON)
+    count = summed.shape[0] - 48
+    blocks = [summed[count + 16 * k : count + 16 * (k + 1)] for k in range(3)]
+    return summed[:count], [block[:8] + block[8:] for block in blocks]
+
+
+def pass_logits_kernel(arrived_ref, out_ref):
+    logits, others = summed_logits(arrived_ref)
+    send_logits(logits, others, out_ref)
+
+
+def softmax_kernel(arrived_ref, positive_hot_ref, out_ref, inverse_ref):
+    count = positive_hot_ref.shape[0]
+    with_positives, (hard, listed_squares, squares) = summed_logits(arrived_ref)
+    first_query = lax.axis_index("core") * LANES
+    inverse_listed = lax.rsqrt(listed_squares + EPSILON * EPSILON)
     inverse = lax.rsqrt(squares + EPSILON * EPSILON)
     inverse_ref[...] = inverse
     inverse_query = inverse_listed[7:8, :]
@@ -155,12 +136,11 @@
         hot = positive_hot_ref[:, LANES * k : LANES * (k + 1)].astype(jnp.float32)
         picked = picked + hot * inverse[k : k + 1, :]
     inverse_positive = jnp.sum(picked, axis=1, keepdims=True)
-    logits = valid(with_positives, 0.0) * inverse_positive * inverse_query / SOFTMAX_TEMPER
-    hard = valid(hard, 0.0) * inverse_listed * inverse_query / SOFTMAX_TEMPER
+    logits = with_positives * inverse_positive * inverse_query / SOFTMAX_TEMPER
+    hard = hard * inverse_listed * inverse_query / SOFTMAX_TEMPER
     is_hard = iota(hard.shape, 0) < 7
     is_own = iota(logits.shape, 0) == iota(logits.shape, 1) + first_query
-    is_own = is_own & in_first_half(logits.shape)
-    weights = valid(jnp.exp(logits - 1.0 / SOFTMAX_TEMPER), 1.0)
+    weights = jnp.exp(logits - 1.0 / SOFTMAX_TEMPER)
     hard_weights = jnp.where(is_hard, jnp.exp(hard - 1.0 / SOFTMAX_TEMPER), 0.0)
     totals = jnp.sum(weights, axis=0, keepdims=True) + jnp.sum(hard_weights, axis=0, keepdims=True)
     target = jnp.sum(jnp.where(is_own, logits, 0.0), axis=0, keepdims=True)
@@ -172,22 +152,16 @@
 
     coef = rounded(scaling_factor * (weights / totals - is_own.astype(jnp.float32)))
     hard_coef = rounded(scaling_factor * (hard_weights / totals))
-    weighted = valid(coef * logits * SOFTMAX_TEMPER, 0.0)
+    weighted = coef * logits * SOFTMAX_TEMPER
     hard_weighted = jnp.where(is_hard, hard_coef * hard * SOFTMAX_TEMPER, 0.0)
     along_query = jnp.sum(weighted, axis=0, keepdims=True) + jnp.sum(
         hard_weighted, axis=0, keepdims=True
     )
-    folded_coef = fold_half(coef[:start], coef[start:], 0)
-    folded_hard = fold_half(
-        jnp.where(is_hard, hard_coef, along_query), jnp.where(is_hard, hard_weighted, losses), 0
-    )
-    for k in range(out_ref.shape[0]):
-        out_ref[k, :start, :] = folded_coef
-        out_ref[k, start : start + 8, :] = folded_hard
-        out_ref[k, start + 8 :, :] = jnp.zeros_like(out_ref[k, start + 8 :, :])
-        columns_to_lanes(
-            jnp.sum(weighted, axis=1, keepdims=True), out_ref.at[k, start + 8 : start + 16]
-        )
+    out_ref[:count, :] = coef
+    out_ref[count : count + 8, :] = jnp.where(is_hard, hard_coef, along_query)
+    out_ref[count + 8 : count + 16, :] = jnp.where(is_hard, hard_weighted, losses)
+    out_ref[count + 16 :, :] = jnp.zeros_like(out_ref[count + 16 :, :])
+    columns_to_lanes(jnp.sum(weighted, axis=1, keepdims=True), out_ref.at[count + 16 :])
 
 
 def resid_grad_kernel(
@@ -211,19 +185,12 @@
     across = (((1,), (1,)), ((), ()))
 
     def joined(start, stop):
-        firsts, seconds = [], []
-        for k in (0, 2):
-            first, second = both_ref[k, start:stop, :], both_ref[k + 1, start:stop, :]
-            firsts.append(fold_half(first, second, 0))
-            seconds.append(fold_half(pltpu.roll(first, HALF, 1), pltpu.roll(second, HALF, 1), 0))
-        return jnp.concatenate(firsts, axis=1), jnp.concatenate(seconds, axis=1)
-
-    start = count // 2
-    coef16 = jnp.concatenate(joined(0, start), axis=0).astype(jnp.bfloat16)
-    hard, hard_weighted = joined(start, start + 8)
-    along_passage = both_ref[0, start + 8 : start + 16, :]
-    for k in range(1, both_ref.shape[0]):
-        along_passage = along_passage + both_ref[k, start + 8 : start + 16, :]
+        return jnp.concatenate([both_ref[0, start:stop, :], both_ref[1, start:stop, :]], axis=1)
+
+    coef16 = joined(0, count).astype(jnp.bfloat16)
+    hard = joined(count, count + 8)
+    hard_weighted = joined(count + 8, count + 16)
+    along_passage = both_ref[0, count + 16 :, :] + both_ref[1, count + 16 :, :]
     along_passage = jnp.concatenate([along_passage[0:1], along_passage[1:2]], axis=1)
     inverse = jnp.concatenate([inverse_ref[k : k + 1, :] for k in range(8)], axis=1)
 
@@ -350,34 +317,31 @@
         out_ref[rows:, :] = query_ref[features, :].T
 
 
-def stack_kernel(first_ref, second_ref, out_ref, token_ref):
-    rows = first_ref.shape[0]
-    out_ref[:rows, :] = first_ref[...]
-    out_ref[rows:, :] = second_ref[...]
-    token_ref[0] = jnp.float32(0.0)
-
-
 def contrast(everyone, resid, gains, tables, after, after_logits):
     tensor_count = lax.axis_size("tensor")
     sequences, width = resid.shape
     listed, query_hot, positive_hot = tables
     count, total_rows = positive_hot.shape
     rows = everyone.reshape(total_rows, width)
+    lines = [[line * 4 + k for k in range(4)] for line in range(4)]
+    across = [[k * 4 + line for k in range(4)] for line in range(4)]
+    copies = ((4, count + 48, LANES), jnp.bfloat16)
     (sent,) = kernel_call(
         partial_logits_kernel,
-        [((tensor_count, count // 2 + 32, LANES), jnp.bfloat16)],
+        [copies],
         [rows, query_hot, positive_hot, listed, gains],
         after=after,
         scratch=[pltpu.VMEM((24, LANES), jnp.float32)],
     )
-    arrived = exchange(sent, "tensor")
+    (sent,) = kernel_call(pass_logits_kernel, [copies], [exchange(sent, "tensor", lines)])
+    arrived = exchange(sent, "tensor", across)
     coefs, inverse = kernel_call(
         softmax_kernel,
-        [((4, count // 2 + 16, LANES), jnp.float32), ((8, LANES), jnp.float32)],
+        [((count + 24, LANES), jnp.float32), ((8, LANES), jnp.float32)],
         [arrived, positive_hot],
         after=after_logits,
     )
-    both = exchange(coefs, ("z_pair", "core"))
+    both = lax.all_gather(coefs, "core", axis=0)
     d_resid16, loss = kernel_call(
         resid_grad_kernel,
         [((tensor_count, sequences, width), jnp.bfloat16), ((1,), jnp.float32)],
@@ -573,9 +537,9 @@
     token_ref[0] = jnp.float32(0.0)
 
 
-def product_kernel(own_ref, other_ref, layout_ref, weights_ref, out_ref):
+def product_kernel(own_ref, other_ref, layout_ref, kept_ref, fetched_ref, out_ref):
     tensor_count, tall, _ = out_ref.shape
-    height = tall * LANES // weights_ref.shape[1]
+    height = tall * LANES // kept_ref.shape[1]
     tokens_count = height * tensor_count
     sequences = own_ref.shape[0] - 2 * tokens_count
     at, _ = layout_rows(tokens_count, sequences, height)
@@ -593,20 +557,20 @@
     d_key = own[:tokens_count] + other[:tokens_count]
     d_value = own[tokens_count : 2 * tokens_count] + other[tokens_count : 2 * tokens_count]
     is_even = is_even_tensor()
-    gradients = jnp.concatenate(
-        [
-            jnp.where(is_even, d_key, d_value),
-            spread(own[2 * tokens_count :]),
-            jnp.where(is_even, d_value, d_key),
-            spread(other[2 * tokens_count :]),
-        ],
-        axis=1,
+    own16 = jnp.concatenate(
+        [jnp.where(is_even, d_key, d_value), spread(own[2 * tokens_count :])], axis=1
+    ).astype(jnp.bfloat16)
+    other16 = jnp.concatenate(
+        [jnp.where(is_even, d_value, d_key), spread(other[2 * tokens_count :])], axis=1
     ).astype(jnp.bfloat16)
     wide = 2 * LANES
-    for k in range(weights_ref.shape[1] // wide):
-        term = jnp.dot(
-            gradients, weights_ref[:, wide * k : wide * (k + 1)], preferred_element_type=jnp.float32
-        ).astype(jnp.bfloat16)
+    for k in range(kept_ref.shape[1] // wide):
+        columns = slice(wide * k, wide * (k + 1))
+        term = jnp.dot(own16, kept_ref[:, columns], preferred_element_type=jnp.float32)
+        term = term + jnp.dot(
+            other16, fetched_ref[:, columns], preferred_element_type=jnp.float32
+        )
+        term = term.astype(jnp.bfloat16)
         for c in (2 * k, 2 * k + 1):
             block = term[:, LANES * (c - 2 * k) : LANES * (c - 2 * k + 1)]
             out_ref[:, height * c : height * (c + 1), :] = block.reshape(-1, height, LANES)
@@ -774,11 +738,6 @@
     wo_t, transposed = kernel_call(
         transpose_kernel, [((features, head_width), bf16), ((1,), f32)], [wo], after=[resid]
     )
-    pair_weights, fetched = kernel_call(
-        stack_kernel,
-        [((4 * head_width, features // 2), bf16), ((1,), f32)],
-        [kept_weights, other_weights],
-    )
     layout_again, placed = sequence_layout(resid)
     tables = kernel_call(
         candidate_kernel,
@@ -792,7 +751,7 @@
     )
     everyone = lax.all_gather(exchange(scaled, ("z_far", "z_pair")), "core", axis=1)
     loss, d_resid16 = contrast(
-        everyone, resid, output_gain, tables, [transposed, placed], [fetched]
+        everyone, resid, output_gain, tables, [transposed, placed], [other_weights]
     )
     gradient_shape = (2 * tokens_count + sequences, head_width)
     own_gradients, sent_gradients = kernel_call(
@@ -808,7 +767,7 @@
     (product,) = kernel_call(
         product_kernel,
         [((tensor_count, own_rows * features // LANES // 2, LANES), bf16)],
-        [own_gradients, other_gradients, layout_again, pair_weights],
+        [own_gradients, other_gradients, layout_again, kept_weights, other_weights],
         after=[summed],
     )
     terms = exchange(product, "tensor")

time: 165 us -> 163 us (0.988)
  the two profiles are of different devices: /device:TPU:2 before, /device:TPU:32 now
where the time goes in v10:
time: 163 us; the launch traced here: 162 us
  blocking collectives  92.9 us (57%)
  starting transfers between devices  26.2 us (16%)
  waiting for transfers between devices  17.7 us (11%)
  Pallas kernels  15.4 us (9%)
  local copies, waits for them, and re-layouts  8.84 us (5%)
    all_to_all x5, blocking collectives, exchange(): lax.all_to_all(blocks, axis, 0, 0, axis_index_groups=groups, tiled=True)  88.4 us
    all_to_all x2, starting transfers between devices, exchange(): lax.all_to_all(blocks, axis, 0, 0, axis_index_groups=groups, tiled=True)  18.7 us
    pallas_call x17, Pallas kernels, kernel_call(): pl.pallas_call(kernel, out_shape=[jax.ShapeDtypeStruct(shape, dtype) for...  15.4 us
    all_to_all x2, waiting for transfers between devices, exchange(): lax.all_to_all(blocks, axis, 0, 0, axis_index_groups=groups, tiled=True)  10.8 us
    unnamed x62, local copies, waits for them, and re-layouts  8.84 us
    ppermute x3, starting transfers between devices, swapped(): return lax.ppermute(value, axis, pairs)  7.54 us
    ppermute x3, waiting for transfers between devices, swapped(): return lax.ppermute(value, axis, pairs)  6.86 us
  transfers between devices with their start and end apart: 5, of which 4 were waited for; matrix products, arithmetic and copies ran while one was open for 0% of the time, Pallas kernels for 4%

profile of v10, /device:TPU:32, one launch (start us, length us, event | category | flops | bytes accessed | tf_op | source)
XLA Modules:
  0.0 161.9 jit_solution(878105429960802861)
XLA Ops:
  0.6 0.0 copy-start.4
  0.6 0.9 copy-done.4
  1.5 0.7 copy-done.21
  2.3 0.3 shard_map.122
  2.6 0.0 copy-start.1
  2.6 0.0 copy-start.2
  2.6 35.4 %all_to_all.35.refs_0_ = bf16[16,512,128]{2,1,0:T(8,128)(2,1)S(1)} all-to-all(bf16[16,512,128]{2,1,0:T(8,128)(2,1)S(1)} %shard_map.122), channel_id=1, replica_groups=mesh['z_far'=8,'z_pair'=2,'core'=2,'tensor'=16] {'tensor'}, dimensions={0} | all-to-all | bytes 4194304 | tf_op jit(solution)/shard_map/all_to_all | solution.py:38
  38.0 0.0 copy-done.1
  38.0 0.0 copy-done.2
  38.0 0.0 copy-start.5
  38.0 0.0 copy-start.26
  38.0 0.0 copy-start.28
  38.0 1.2 shard_map.123
  39.3 0.0 copy-start.7
  39.3 0.0 copy-start.20
  39.3 2.6 %collective-permute-start = (bf16[256,128]{1,0:T(8,128)(2,1)S(1)}, bf16[256,128]{1,0:T(8,128)(2,1)S(1)}, u32[]{:S(2)}, u32[]{:S(2)}) collective-permute-start(bf16[256,128]{1,0:T(8,128)(2,1)S(1)} %get-tuple-element.28), channel_id=1, source_target_pairs={{0,1},{1,0},{2,3},{3,2},{4,5},{5,4},{6,7},{7,6},{8,9},{9,8},{10,11... | collective-permute-start | bytes 196616 | tf_op jit(solution)/shard_map/ppermute | solution.py:25
  41.9 0.0 copy-done.24
  41.9 0.7 shard_map.124
  42.6 3.0 %collective-permute-done.refs_1_ = bf16[256,128]{1,0:T(8,128)(2,1)S(1)} collective-permute-done((bf16[256,128]{1,0:T(8,128)(2,1)S(1)}, bf16[256,128]{1,0:T(8,128)(2,1)S(1)}, u32[]{:S(2)}, u32[]{:S(2)}) %collective-permute-start) | collective-permute-done | bytes 65568 | tf_op jit(solution)/shard_map/ppermute | solution.py:25
  45.6 0.0 copy-done
  45.6 0.0 copy-done.5
  45.6 0.0 copy-done.26
  45.6 0.0 copy-done.28
  45.6 1.0 shard_map.125
  46.7 11.6 %all_to_all.36.refs_0_ = bf16[16,32,256]{2,1,0:T(8,128)(2,1)S(1)} all-to-all(bf16[16,32,256]{2,1,0:T(8,128)(2,1)S(1)} %get-tuple-element.31), channel_id=1, replica_groups=mesh['z_far'=8,'z_pair'=2,'core'=2,'tensor'=16] {'tensor'}, dimensions={0} | all-to-all | bytes 524288 | tf_op jit(solution)/shard_map/all_to_all | solution.py:38
  58.3 0.1 shard_map.126
  58.4 0.7 copy-done.19
  59.1 15.2 %all-to-all-start.2 = ((bf16[16,32,256]{2,1,0:T(8,128)(2,1)}), bf16[16,32,256]{2,1,0:T(8,128)(2,1)}, u32[]{:S(2)}, u32[]{:S(2)}) async-start(bf16[16,32,256]{2,1,0:T(8,128)(2,1)} %copy-done.19), calls=%async_computation.2 | async-start | bytes 524288 | tf_op jit(solution)/shard_map/all_to_all | solution.py:38
  74.3 0.9 copy-done.8
  75.2 1.6 shard_map.132
  76.8 1.0 copy-done.11
  77.8 2.5 %collective-permute-start.1 = (bf16[256,2048]{1,0:T(8,128)(2,1)}, bf16[256,2048]{1,0:T(8,128)(2,1)S(1)}, u32[]{:S(2)}, u32[]{:S(2)}) collective-permute-start(bf16[256,2048]{1,0:T(8,128)(2,1)} %get-tuple-element.39), channel_id=1, source_target_pairs={{0,1},{1,0},{2,3},{3,2},{4,5},{5,4},{6,7},{7,6},{8,9},{9,8},{10,11... | collective-permute-start | bytes 3145736 | tf_op jit(solution)/shard_map/ppermute | solution.py:25
  80.3 0.7 copy-done.14
  81.0 0.7 copy-done.25
  81.7 0.7 shard_map.129
  82.4 0.7 copy-done.15
  83.1 0.5 shard_map.128
  83.7 1.0 copy-done.9
  84.7 0.0 copy-done.23
  84.7 0.7 copy-done.30
  85.3 0.2 shard_map.127
  85.6 3.9 %all-to-all-done.2 = bf16[16,32,256]{2,1,0:T(8,128)(2,1)} async-done(((bf16[16,32,256]{2,1,0:T(8,128)(2,1)}), bf16[16,32,256]{2,1,0:T(8,128)(2,1)}, u32[]{:S(2)}, u32[]{:S(2)}) %all-to-all-start.2) | async-done | bytes 262176 | tf_op jit(solution)/shard_map/all_to_all | solution.py:38
  89.5 2.4 %all-gather = bf16[16,64,256]{2,1,0:T(8,128)(2,1)S(1)} all-gather(bf16[16,32,256]{2,1,0:T(8,128)(2,1)} %all-to-all-done.2), channel_id=2, replica_groups=mesh['z_far'=8,'z_pair'=2,'core'=2,'tensor'=16] {'core'}, dimensions={1}, use_global_device_ids=true | all-gather | bytes 786432 | tf_op jit(solution)/shard_map/all_gather | solution.py:752
  91.9 2.7 %shard_map.130 = bf16[4,304,128]{2,1,0:T(8,128)(2,1)S(1)} custom-call(bf16[1024,256]{1,0:T(8,128)(2,1)S(1)} %bitcast.9, bf16[256,1024]{1,0:T(8,128)(2,1)S(1)} %get-tuple-element.34.refs_1_.refs_4_, bf16[256,1024]{1,0:T(8,128)(2,1)S(1)} %get-tuple-element.35.refs_2_.refs_1_.refs_3_, s32[16,256]{1,0:T(8,128)S(1)} %get-tuple-element.36.refs_3_.refs_5_, ...), custom_call_target="tpu_custom_call" | custom-call | tf_op jit(solution)/shard_map/pallas_call | solution.py:262
  94.6 0.0 copy-start.16
  94.6 10.1 %all_to_all.37.refs_0_ = bf16[4,304,128]{2,1,0:T(8,128)(2,1)S(1)} all-to-all(bf16[4,304,128]{2,1,0:T(8,128)(2,1)S(1)} %shard_map.130), channel_id=1, replica_groups={{0,1,2,3},{4,5,6,7},{8,9,10,11},{12,13,14,15},{16,17,18,19},{20,21,22,2..., dimensions={0} | all-to-all | bytes 622592 | tf_op jit(solution)/shard_map/all_to_all | solution.py:38
  104.8 0.7 copy-done.3
  105.5 3.5 %all-to-all-start.4 = ((bf16[4,304,128]{2,1,0:T(8,128)(2,1)}), bf16[4,304,128]{2,1,0:T(8,128)(2,1)S(1)}, u32[]{:S(2)}, u32[]{:S(2)}) async-start(bf16[4,304,128]{2,1,0:T(8,128)(2,1)} %copy-done.3), calls=%async_computation.4 | async-start | bytes 622592 | tf_op jit(solution)/shard_map/all_to_all | solution.py:38
  108.9 0.0 copy-start.27
  108.9 0.0 copy-start.29
  109.0 0.0 collective-permute-done.1.refs_2_.refs_4_
  109.0 6.9 %all-to-all-done.4.refs_0_ = bf16[4,304,128]{2,1,0:T(8,128)(2,1)S(1)} async-done(((bf16[4,304,128]{2,1,0:T(8,128)(2,1)}), bf16[4,304,128]{2,1,0:T(8,128)(2,1)S(1)}, u32[]{:S(2)}, u32[]{:S(2)}) %all-to-all-start.4) | async-done | bytes 311328 | tf_op jit(solution)/shard_map/all_to_all | solution.py:38
  115.8 0.3 shard_map.133
  116.2 2.1 %all-gather.1 = f32[560,128]{1,0:T(8,128)S(1)} all-gather(f32[280,128]{1,0:T(8,128)S(1)} %get-tuple-element.40), channel_id=3, replica_groups=mesh['z_far'=8,'z_pair'=2,'core'=2,'tensor'=16] {'core'}, dimensions={0}, use_global_device_ids=true | all-gather | bytes 430080 | tf_op jit(solution)/shard_map/all_gather | solution.py:344
  118.3 1.3 shard_map.134
  119.6 13.0 %all_to_all.38.refs_0_ = bf16[16,32,256]{2,1,0:T(8,128)(2,1)S(1)} all-to-all(bf16[16,32,256]{2,1,0:T(8,128)(2,1)S(1)} %get-tuple-element.42), channel_id=1, replica_groups=mesh['z_far'=8,'z_pair'=2,'core'=2,'tensor'=16] {'tensor'}, dimensions={0} | all-to-all | bytes 524288 | tf_op jit(solution)/shard_map/all_to_all | solution.py:38
  132.6 0.0 copy-done.18
  132.6 1.5 shard_map.135
  134.2 2.5 %collective-permute-start.2 = (bf16[544,128]{1,0:T(8,128)(2,1)S(1)}, bf16[544,128]{1,0:T(8,128)(2,1)S(1)}, u32[]{:S(2)}, u32[]{:S(2)}) collective-permute-start(bf16[544,128]{1,0:T(8,128)(2,1)S(1)} %get-tuple-element.48), channel_id=1, source_target_pairs={{0,1},{1,0},{2,3},{3,2},{4,5},{5,4},{6,7},{7,6},{8,9},{9,8},{10,11... | collective-permute-start | bytes 417800 | tf_op jit(solution)/shard_map/ppermute | solution.py:25
  136.6 0.6 shard_map.136
  137.2 3.9 %collective-permute-done.2.refs_1_ = bf16[544,128]{1,0:T(8,128)(2,1)S(1)} collective-permute-done((bf16[544,128]{1,0:T(8,128)(2,1)S(1)}, bf16[544,128]{1,0:T(8,128)(2,1)S(1)}, u32[]{:S(2)}, u32[]{:S(2)}) %collective-permute-start.2) | collective-permute-done | bytes 139296 | tf_op jit(solution)/shard_map/ppermute | solution.py:25
  141.1 1.6 shard_map.137
  142.7 18.2 %all_to_all.39.refs_0_ = bf16[16,256,128]{2,1,0:T(8,128)(2,1)S(1)} all-to-all(bf16[16,256,128]{2,1,0:T(8,128)(2,1)S(1)} %shard_map.137), channel_id=1, replica_groups=mesh['z_far'=8,'z_pair'=2,'core'=2,'tensor'=16] {'tensor'}, dimensions={0} | all-to-all | bytes 2097152 | tf_op jit(solution)/shard_map/all_to_all | solution.py:38
  160.9 1.0 shard_map.138
  (32 shorter events, 0.1 us)
Async XLA Ops:
  0.6 0.9 copy-start.4
  1.5 0.7 copy-start.21
  2.6 35.4 %copy-start.1 = (bf16[4096,128]{1,0:T(8,128)(2,1)S(1)}, bf16[4096,128]{1,0:T(8,128)(2,1)}, u32[]{:S(2)}) copy-start(bf16[4096,128]{1,0:T(8,128)(2,1)} %refs_0_.9) | copy-start | bytes 3145732
  2.6 35.4 %copy-start.2 = (bf16[4096,128]{1,0:T(8,128)(2,1)S(1)}, bf16[4096,128]{1,0:T(8,128)(2,1)}, u32[]{:S(2)}) copy-start(bf16[4096,128]{1,0:T(8,128)(2,1)} %refs_1_.4) | copy-start | bytes 3145732
  38.0 3.9 %copy-start.24 = (s32[1,32]{1,0:T(1,128)S(1)}, s32[1,32]{1,0:T(1,128)}, u32[]{:S(2)}) copy-start(s32[1,32]{1,0:T(1,128)} %refs_0_.8) | copy-start | bytes 388
  38.0 7.6 %copy-start = (bf16[128,4096]{1,0:T(8,128)(2,1)S(1)}, bf16[128,4096]{1,0:T(8,128)(2,1)}, u32[]{:S(2)}) copy-start(bf16[128,4096]{1,0:T(8,128)(2,1)} %refs_0_.7) | copy-start | bytes 3145732
  38.0 7.6 %copy-start.5 = (bf16[16,4096]{1,0:T(8,128)(2,1)S(1)}, bf16[16,4096]{1,0:T(8,128)(2,1)}, u32[]{:S(2)}) copy-start(bf16[16,4096]{1,0:T(8,128)(2,1)} %refs_1_.5) | copy-start | bytes 393220
  38.0 7.6 %copy-start.26 = (f32[128]{0:T(128)S(1)}, f32[128]{0:T(128)}, u32[]{:S(2)}) copy-start(f32[128]{0:T(128)} %param.18) | copy-start | bytes 1540
  38.0 7.6 %copy-start.28 = (f32[128]{0:T(128)S(1)}, f32[128]{0:T(128)}, u32[]{:S(2)}) copy-start(f32[128]{0:T(128)} %param.19) | copy-start | bytes 1540
  39.3 7.4 %copy-start.7 = (f32[256,128]{1,0:T(8,128)}, f32[256,128]{1,0:T(8,128)S(1)}, u32[]{:S(2)}) copy-start(f32[256,128]{1,0:T(8,128)S(1)} %get-tuple-element.29.refs_1_.refs_2_) | copy-start | bytes 393220
  39.3 19.0 %copy-start.20 = (f32[4096]{0:T(1024)S(1)}, f32[4096]{0:T(1024)}, u32[]{:S(2)}) copy-start(f32[4096]{0:T(1024)} %param.21) | copy-start | bytes 49156
  39.3 6.3 %collective-permute-start = (bf16[256,128]{1,0:T(8,128)(2,1)S(1)}, bf16[256,128]{1,0:T(8,128)(2,1)S(1)}, u32[]{:S(2)}, u32[]{:S(2)}) collective-permute-start(bf16[256,128]{1,0:T(8,128)(2,1)S(1)} %get-tuple-element.28), channel_id=1, source_target_pairs={{0,1},{1,0},{2,3},{3,2},{4,5},{5,4},{6,7},{7,6},{8,9},{9,8},{10,11... | collective-permute-start | bytes 196616 | tf_op jit(solution)/shard_map/ppermute | solution.py:25
  46.7 11.7 %copy-start.17 = (f32[896,128]{1,0:T(8,128)}, f32[896,128]{1,0:T(8,128)S(1)}, u32[]{:S(2)}) copy-start(f32[896,128]{1,0:T(8,128)S(1)} %get-tuple-element.44.refs_2_) | copy-start | bytes 1376260
  58.3 26.3 %copy-start.23 = (s32[256,7]{0,1:T(8,128)S(1)}, s32[256,7]{0,1:T(8,128)}, u32[]{:S(2)}) copy-start(s32[256,7]{0,1:T(8,128)} %param.14) | copy-start | bytes 21508
  58.4 0.7 copy-start.19
  59.1 21.2 %copy-start.13 = (f32[32,256]{1,0:T(8,128)}, f32[32,256]{1,0:T(8,128)S(1)}, u32[]{:S(2)}) copy-start(f32[32,256]{1,0:T(8,128)S(1)} %get-tuple-element.33.refs_2_.refs_1_.refs_6_) | copy-start | bytes 98308
  59.1 30.4 %all-to-all-start.2 = ((bf16[16,32,256]{2,1,0:T(8,128)(2,1)}), bf16[16,32,256]{2,1,0:T(8,128)(2,1)}, u32[]{:S(2)}, u32[]{:S(2)}) async-start(bf16[16,32,256]{2,1,0:T(8,128)(2,1)} %copy-done.19), calls=%async_computation.2 | async-start | bytes 524288 | tf_op jit(solution)/shard_map/all_to_all | solution.py:38
  74.3 0.9 copy-start.8
  76.8 1.0 copy-start.11
  77.8 31.2 %collective-permute-start.1 = (bf16[256,2048]{1,0:T(8,128)(2,1)}, bf16[256,2048]{1,0:T(8,128)(2,1)S(1)}, u32[]{:S(2)}, u32[]{:S(2)}) collective-permute-start(bf16[256,2048]{1,0:T(8,128)(2,1)} %get-tuple-element.39), channel_id=1, source_target_pairs={{0,1},{1,0},{2,3},{3,2},{4,5},{5,4},{6,7},{7,6},{8,9},{9,8},{10,11... | collective-permute-start | bytes 3145736 | tf_op jit(solution)/shard_map/ppermute | solution.py:25
  80.2 0.8 copy-start.14
  81.0 0.7 copy-start.25
  82.4 0.8 copy-start.15
  83.7 1.0 copy-start.9
  84.7 0.7 copy-start.30
  94.6 23.8 %copy-start.16 = (f32[32,256]{1,0:T(8,128)S(1)}, f32[32,256]{1,0:T(8,128)}, u32[]{:S(2)}) copy-start(f32[32,256]{1,0:T(8,128)} %copy-done.13) | copy-start | bytes 98308
  104.8 0.7 copy-start.3
  105.5 10.4 %all-to-all-start.4 = ((bf16[4,304,128]{2,1,0:T(8,128)(2,1)}), bf16[4,304,128]{2,1,0:T(8,128)(2,1)S(1)}, u32[]{:S(2)}, u32[]{:S(2)}) async-start(bf16[4,304,128]{2,1,0:T(8,128)(2,1)} %copy-done.3), calls=%async_computation.4 | async-start | bytes 622592 | tf_op jit(solution)/shard_map/all_to_all | solution.py:38
  108.9 23.7 %copy-start.27 = (f32[128]{0:T(128)S(1)}, f32[128]{0:T(128)}, u32[]{:S(2)}) copy-start(f32[128]{0:T(128)} %param.18) | copy-start | bytes 1540
  108.9 23.7 %copy-start.29 = (f32[128]{0:T(128)S(1)}, f32[128]{0:T(128)}, u32[]{:S(2)}) copy-start(f32[128]{0:T(128)} %param.19) | copy-start | bytes 1540
  115.8 16.8 %copy-start.10 = (bf16[4096,128]{1,0:T(8,128)(2,1)S(1)}, bf16[4096,128]{1,0:T(8,128)(2,1)}, u32[]{:S(2)}) copy-start(bf16[4096,128]{1,0:T(8,128)(2,1)} %copy-done.9) | copy-start | bytes 3145732
  115.8 16.8 %copy-start.18 = (f32[896,128]{1,0:T(8,128)S(1)}, f32[896,128]{1,0:T(8,128)}, u32[]{:S(2)}) copy-start(f32[896,128]{1,0:T(8,128)} %copy-done.17) | copy-start | bytes 1376260
  119.6 21.5 %copy-start.12 = (bf16[256,2048]{1,0:T(8,128)(2,1)S(1)}, bf16[256,2048]{1,0:T(8,128)(2,1)}, u32[]{:S(2)}) copy-start(bf16[256,2048]{1,0:T(8,128)(2,1)} %copy-done.11) | copy-start | bytes 3145732
  134.2 6.9 %collective-permute-start.2 = (bf16[544,128]{1,0:T(8,128)(2,1)S(1)}, bf16[544,128]{1,0:T(8,128)(2,1)S(1)}, u32[]{:S(2)}, u32[]{:S(2)}) collective-permute-start(bf16[544,128]{1,0:T(8,128)(2,1)S(1)} %get-tuple-element.48), channel_id=1, source_target_pairs={{0,1},{1,0},{2,3},{3,2},{4,5},{5,4},{6,7},{7,6},{8,9},{9,8},{10,11... | collective-permute-start | bytes 417800 | tf_op jit(solution)/shard_map/ppermute | solution.py:25
  141.1 19.8 %copy-start.6 = (bf16[16,4096]{1,0:T(8,128)(2,1)S(1)}, bf16[16,4096]{1,0:T(8,128)(2,1)}, u32[]{:S(2)}) copy-start(bf16[16,4096]{1,0:T(8,128)(2,1)} %refs_1_.5) | copy-start | bytes 393220
  141.1 19.8 %copy-start.22 = (f32[4096]{0:T(1024)S(1)}, f32[4096]{0:T(1024)}, u32[]{:S(2)}) copy-start(f32[4096]{0:T(1024)} %param.15) | copy-start | bytes 49156

commit v11 on v10

--- a/solution.py
+++ b/solution.py
@@ -323,8 +323,18 @@
     listed, query_hot, positive_hot = tables
     count, total_rows = positive_hot.shape
     rows = everyone.reshape(total_rows, width)
+    axes = ("z_far", "z_pair", "core", "tensor")
     lines = [[line * 4 + k for k in range(4)] for line in range(4)]
     across = [[k * 4 + line for k in range(4)] for line in range(4)]
+
+    def everywhere(of_cores):
+        planes = lax.axis_size("z_far") * lax.axis_size("z_pair") * lax.axis_size("core")
+        return [
+            [plane * tensor_count + t for t in line]
+            for plane in range(planes)
+            for line in of_cores[plane % 2]
+        ]
+
     copies = ((4, count + 48, LANES), jnp.bfloat16)
     (sent,) = kernel_call(
         partial_logits_kernel,
@@ -333,8 +343,8 @@
         after=after,
         scratch=[pltpu.VMEM((24, LANES), jnp.float32)],
     )
-    (sent,) = kernel_call(pass_logits_kernel, [copies], [exchange(sent, "tensor", lines)])
-    arrived = exchange(sent, "tensor", across)
+    (sent,) = kernel_call(pass_logits_kernel, [copies], [exchange(sent, axes, everywhere([lines, across]))])
+    arrived = exchange(sent, axes, everywhere([across, lines]))
     coefs, inverse = kernel_call(
         softmax_kernel,
         [((count + 24, LANES), jnp.float32), ((8, LANES), jnp.float32)],

time: 163 us -> 161 us (0.988)
  blocking collectives: 92.9 us -> 91.2 us
    all_to_all x5, blocking collectives: 88.4 us -> 86.7 us  [exchange(): lax.all_to_all(blocks, axis, 0, 0, axis_index_groups=groups, tiled=True)]
where the time goes in v11:
time: 161 us; the launch traced here: 160 us
  blocking collectives  91.2 us (57%)
  starting transfers between devices  26.2 us (16%)
  waiting for transfers between devices  17.7 us (11%)
  Pallas kernels  15.4 us (10%)
  local copies, waits for them, and re-layouts  8.84 us (5%)
    all_to_all x5, blocking collectives, exchange(): lax.all_to_all(blocks, axis, 0, 0, axis_index_groups=groups, tiled=True)  86.7 us
    all_to_all x2, starting transfers between devices, exchange(): lax.all_to_all(blocks, axis, 0, 0, axis_index_groups=groups, tiled=True)  18.7 us
    pallas_call x17, Pallas kernels, kernel_call(): pl.pallas_call(kernel, out_shape=[jax.ShapeDtypeStruct(shape, dtype) for...  15.4 us
    all_to_all x2, waiting for transfers between devices, exchange(): lax.all_to_all(blocks, axis, 0, 0, axis_index_groups=groups, tiled=True)  10.8 us
    unnamed x62, local copies, waits for them, and re-layouts  8.84 us
    ppermute x3, starting transfers between devices, swapped(): return lax.ppermute(value, axis, pairs)  7.54 us
    ppermute x3, waiting for transfers between devices, swapped(): return lax.ppermute(value, axis, pairs)  6.86 us
  transfers between devices with their start and end apart: 5, of which 4 were waited for; matrix products, arithmetic and copies ran while one was open for 0% of the time, Pallas kernels for 4%

profile of v11, /device:TPU:32, one launch (start us, length us, event | category | flops | bytes accessed | tf_op | source)
XLA Modules:
  0.0 160.3 jit_solution(15906044799945010307)
XLA Ops:
  0.6 0.0 copy-start.4
  0.6 0.9 copy-done.4
  1.5 0.7 copy-done.21
  2.3 0.3 shard_map.122
  2.6 0.0 copy-start.1
  2.6 0.0 copy-start.2
  2.6 35.4 %all_to_all.35.refs_0_ = bf16[16,512,128]{2,1,0:T(8,128)(2,1)S(1)} all-to-all(bf16[16,512,128]{2,1,0:T(8,128)(2,1)S(1)} %shard_map.122), channel_id=1, replica_groups=mesh['z_far'=8,'z_pair'=2,'core'=2,'tensor'=16] {'tensor'}, dimensions={0} | all-to-all | bytes 4194304 | tf_op jit(solution)/shard_map/all_to_all | solution.py:38
  38.0 0.0 copy-done.1
  38.0 0.0 copy-done.2
  38.0 0.0 copy-start.5
  38.0 0.0 copy-start.26
  38.0 0.0 copy-start.28
  38.0 1.2 shard_map.123
  39.3 0.0 copy-start.7
  39.3 0.0 copy-start.20
  39.3 2.6 %collective-permute-start = (bf16[256,128]{1,0:T(8,128)(2,1)S(1)}, bf16[256,128]{1,0:T(8,128)(2,1)S(1)}, u32[]{:S(2)}, u32[]{:S(2)}) collective-permute-start(bf16[256,128]{1,0:T(8,128)(2,1)S(1)} %get-tuple-element.28), channel_id=1, source_target_pairs={{0,1},{1,0},{2,3},{3,2},{4,5},{5,4},{6,7},{7,6},{8,9},{9,8},{10,11... | collective-permute-start | bytes 196616 | tf_op jit(solution)/shard_map/ppermute | solution.py:25
  41.9 0.0 copy-done.24
  41.9 0.7 shard_map.124
  42.6 3.0 %collective-permute-done.refs_1_ = bf16[256,128]{1,0:T(8,128)(2,1)S(1)} collective-permute-done((bf16[256,128]{1,0:T(8,128)(2,1)S(1)}, bf16[256,128]{1,0:T(8,128)(2,1)S(1)}, u32[]{:S(2)}, u32[]{:S(2)}) %collective-permute-start) | collective-permute-done | bytes 65568 | tf_op jit(solution)/shard_map/ppermute | solution.py:25
  45.6 0.0 copy-done
  45.6 0.0 copy-done.5
  45.6 0.0 copy-done.26
  45.6 1.0 shard_map.125
  46.7 11.6 %all_to_all.36.refs_0_ = bf16[16,32,256]{2,1,0:T(8,128)(2,1)S(1)} all-to-all(bf16[16,32,256]{2,1,0:T(8,128)(2,1)S(1)} %get-tuple-element.31), channel_id=1, replica_groups=mesh['z_far'=8,'z_pair'=2,'core'=2,'tensor'=16] {'tensor'}, dimensions={0} | all-to-all | bytes 524288 | tf_op jit(solution)/shard_map/all_to_all | solution.py:38
  58.3 0.1 shard_map.126
  58.4 0.7 copy-done.19
  59.1 15.2 %all-to-all-start.2 = ((bf16[16,32,256]{2,1,0:T(8,128)(2,1)}), bf16[16,32,256]{2,1,0:T(8,128)(2,1)}, u32[]{:S(2)}, u32[]{:S(2)}) async-start(bf16[16,32,256]{2,1,0:T(8,128)(2,1)} %copy-done.19), calls=%async_computation.2 | async-start | bytes 524288 | tf_op jit(solution)/shard_map/all_to_all | solution.py:38
  74.3 0.9 copy-done.8
  75.2 1.6 shard_map.132
  76.8 1.0 copy-done.11
  77.8 2.5 %collective-permute-start.1 = (bf16[256,2048]{1,0:T(8,128)(2,1)}, bf16[256,2048]{1,0:T(8,128)(2,1)S(1)}, u32[]{:S(2)}, u32[]{:S(2)}) collective-permute-start(bf16[256,2048]{1,0:T(8,128)(2,1)} %get-tuple-element.39), channel_id=1, source_target_pairs={{0,1},{1,0},{2,3},{3,2},{4,5},{5,4},{6,7},{7,6},{8,9},{9,8},{10,11... | collective-permute-start | bytes 3145736 | tf_op jit(solution)/shard_map/ppermute | solution.py:25
  80.3 0.7 copy-done.14
  81.0 0.7 copy-done.25
  81.7 0.7 shard_map.129
  82.4 0.7 copy-done.15
  83.1 0.5 shard_map.128
  83.7 1.0 copy-done.9
  84.7 0.0 copy-done.23
  84.7 0.7 copy-done.30
  85.3 0.2 shard_map.127
  85.6 3.9 %all-to-all-done.2 = bf16[16,32,256]{2,1,0:T(8,128)(2,1)} async-done(((bf16[16,32,256]{2,1,0:T(8,128)(2,1)}), bf16[16,32,256]{2,1,0:T(8,128)(2,1)}, u32[]{:S(2)}, u32[]{:S(2)}) %all-to-all-start.2) | async-done | bytes 262176 | tf_op jit(solution)/shard_map/all_to_all | solution.py:38
  89.5 2.4 %all-gather = bf16[16,64,256]{2,1,0:T(8,128)(2,1)S(1)} all-gather(bf16[16,32,256]{2,1,0:T(8,128)(2,1)} %all-to-all-done.2), channel_id=2, replica_groups=mesh['z_far'=8,'z_pair'=2,'core'=2,'tensor'=16] {'core'}, dimensions={1}, use_global_device_ids=true | all-gather | bytes 786432 | tf_op jit(solution)/shard_map/all_gather | solution.py:762
  91.9 2.7 %shard_map.130 = bf16[4,304,128]{2,1,0:T(8,128)(2,1)S(1)} custom-call(bf16[1024,256]{1,0:T(8,128)(2,1)S(1)} %bitcast.9, bf16[256,1024]{1,0:T(8,128)(2,1)S(1)} %get-tuple-element.34.refs_1_.refs_4_, bf16[256,1024]{1,0:T(8,128)(2,1)S(1)} %get-tuple-element.35.refs_2_.refs_1_.refs_3_, s32[16,256]{1,0:T(8,128)S(1)} %get-tuple-element.36.refs_3_.refs_5_, ...), custom_call_target="tpu_custom_call" | custom-call | tf_op jit(solution)/shard_map/pallas_call | solution.py:262
  94.6 0.0 copy-start.16
  94.6 9.3 %all_to_all.37.refs_0_ = bf16[4,304,128]{2,1,0:T(8,128)(2,1)S(1)} all-to-all(bf16[4,304,128]{2,1,0:T(8,128)(2,1)S(1)} %shard_map.130), channel_id=1, replica_groups={{0,1,2,3},{4,5,6,7},{8,9,10,11},{12,13,14,15},{16,20,24,28},{17,21,25,2..., dimensions={0} | all-to-all | bytes 622592 | tf_op jit(solution)/shard_map/all_to_all | solution.py:38
  103.9 0.7 copy-done.3
  104.6 3.5 %all-to-all-start.4 = ((bf16[4,304,128]{2,1,0:T(8,128)(2,1)}), bf16[4,304,128]{2,1,0:T(8,128)(2,1)S(1)}, u32[]{:S(2)}, u32[]{:S(2)}) async-start(bf16[4,304,128]{2,1,0:T(8,128)(2,1)} %copy-done.3), calls=%async_computation.4 | async-start | bytes 622592 | tf_op jit(solution)/shard_map/all_to_all | solution.py:38
  108.1 0.0 copy-start.27
  108.1 0.0 copy-start.29
  108.1 0.0 collective-permute-done.1.refs_2_.refs_4_
  108.1 6.9 %all-to-all-done.4.refs_0_ = bf16[4,304,128]{2,1,0:T(8,128)(2,1)S(1)} async-done(((bf16[4,304,128]{2,1,0:T(8,128)(2,1)}), bf16[4,304,128]{2,1,0:T(8,128)(2,1)S(1)}, u32[]{:S(2)}, u32[]{:S(2)}) %all-to-all-start.4) | async-done | bytes 311328 | tf_op jit(solution)/shard_map/all_to_all | solution.py:38
  115.0 0.3 shard_map.133
  115.4 2.1 %all-gather.1 = f32[560,128]{1,0:T(8,128)S(1)} all-gather(f32[280,128]{1,0:T(8,128)S(1)} %get-tuple-element.40), channel_id=3, replica_groups=mesh['z_far'=8,'z_pair'=2,'core'=2,'tensor'=16] {'core'}, dimensions={0}, use_global_device_ids=true | all-gather | bytes 430080 | tf_op jit(solution)/shard_map/all_gather | solution.py:354
  117.5 0.0 copy-done.16
  117.5 1.3 shard_map.134
  118.8 12.2 %all_to_all.38.refs_0_ = bf16[16,32,256]{2,1,0:T(8,128)(2,1)S(1)} all-to-all(bf16[16,32,256]{2,1,0:T(8,128)(2,1)S(1)} %get-tuple-element.42), channel_id=1, replica_groups=mesh['z_far'=8,'z_pair'=2,'core'=2,'tensor'=16] {'tensor'}, dimensions={0} | all-to-all | bytes 524288 | tf_op jit(solution)/shard_map/all_to_all | solution.py:38
  131.0 1.5 shard_map.135
  132.5 2.5 %collective-permute-start.2 = (bf16[544,128]{1,0:T(8,128)(2,1)S(1)}, bf16[544,128]{1,0:T(8,128)(2,1)S(1)}, u32[]{:S(2)}, u32[]{:S(2)}) collective-permute-start(bf16[544,128]{1,0:T(8,128)(2,1)S(1)} %get-tuple-element.48), channel_id=1, source_target_pairs={{0,1},{1,0},{2,3},{3,2},{4,5},{5,4},{6,7},{7,6},{8,9},{9,8},{10,11... | collective-permute-start | bytes 417800 | tf_op jit(solution)/shard_map/ppermute | solution.py:25
  135.0 0.6 shard_map.136
  135.5 3.9 %collective-permute-done.2.refs_1_ = bf16[544,128]{1,0:T(8,128)(2,1)S(1)} collective-permute-done((bf16[544,128]{1,0:T(8,128)(2,1)S(1)}, bf16[544,128]{1,0:T(8,128)(2,1)S(1)}, u32[]{:S(2)}, u32[]{:S(2)}) %collective-permute-start.2) | collective-permute-done | bytes 139296 | tf_op jit(solution)/shard_map/ppermute | solution.py:25
  139.4 0.0 copy-done.12
  139.5 1.6 shard_map.137
  141.0 18.2 %all_to_all.39.refs_0_ = bf16[16,256,128]{2,1,0:T(8,128)(2,1)S(1)} all-to-all(bf16[16,256,128]{2,1,0:T(8,128)(2,1)S(1)} %shard_map.137), channel_id=1, replica_groups=mesh['z_far'=8,'z_pair'=2,'core'=2,'tensor'=16] {'tensor'}, dimensions={0} | all-to-all | bytes 2097152 | tf_op jit(solution)/shard_map/all_to_all | solution.py:38
  159.3 1.0 shard_map.138
  (32 shorter events, 0.1 us)
Async XLA Ops:
  0.6 0.9 copy-start.4
  1.5 0.7 copy-start.21
  2.6 35.4 %copy-start.1 = (bf16[4096,128]{1,0:T(8,128)(2,1)S(1)}, bf16[4096,128]{1,0:T(8,128)(2,1)}, u32[]{:S(2)}) copy-start(bf16[4096,128]{1,0:T(8,128)(2,1)} %refs_0_.9) | copy-start | bytes 3145732
  2.6 35.4 %copy-start.2 = (bf16[4096,128]{1,0:T(8,128)(2,1)S(1)}, bf16[4096,128]{1,0:T(8,128)(2,1)}, u32[]{:S(2)}) copy-start(bf16[4096,128]{1,0:T(8,128)(2,1)} %refs_1_.4) | copy-start | bytes 3145732
  38.0 3.9 %copy-start.24 = (s32[1,32]{1,0:T(1,128)S(1)}, s32[1,32]{1,0:T(1,128)}, u32[]{:S(2)}) copy-start(s32[1,32]{1,0:T(1,128)} %refs_0_.8) | copy-start | bytes 388
  38.0 7.6 %copy-start = (bf16[128,4096]{1,0:T(8,128)(2,1)S(1)}, bf16[128,4096]{1,0:T(8,128)(2,1)}, u32[]{:S(2)}) copy-start(bf16[128,4096]{1,0:T(8,128)(2,1)} %refs_0_.7) | copy-start | bytes 3145732
  38.0 7.6 %copy-start.5 = (bf16[16,4096]{1,0:T(8,128)(2,1)S(1)}, bf16[16,4096]{1,0:T(8,128)(2,1)}, u32[]{:S(2)}) copy-start(bf16[16,4096]{1,0:T(8,128)(2,1)} %refs_1_.5) | copy-start | bytes 393220
  38.0 7.6 %copy-start.26 = (f32[128]{0:T(128)S(1)}, f32[128]{0:T(128)}, u32[]{:S(2)}) copy-start(f32[128]{0:T(128)} %param.18) | copy-start | bytes 1540
  38.0 7.6 %copy-start.28 = (f32[128]{0:T(128)S(1)}, f32[128]{0:T(128)}, u32[]{:S(2)}) copy-start(f32[128]{0:T(128)} %param.19) | copy-start | bytes 1540
  39.3 7.4 %copy-start.7 = (f32[256,128]{1,0:T(8,128)}, f32[256,128]{1,0:T(8,128)S(1)}, u32[]{:S(2)}) copy-start(f32[256,128]{1,0:T(8,128)S(1)} %get-tuple-element.29.refs_1_.refs_2_) | copy-start | bytes 393220
  39.3 19.0 %copy-start.20 = (f32[4096]{0:T(1024)S(1)}, f32[4096]{0:T(1024)}, u32[]{:S(2)}) copy-start(f32[4096]{0:T(1024)} %param.21) | copy-start | bytes 49156
  39.3 6.3 %collective-permute-start = (bf16[256,128]{1,0:T(8,128)(2,1)S(1)}, bf16[256,128]{1,0:T(8,128)(2,1)S(1)}, u32[]{:S(2)}, u32[]{:S(2)}) collective-permute-start(bf16[256,128]{1,0:T(8,128)(2,1)S(1)} %get-tuple-element.28), channel_id=1, source_target_pairs={{0,1},{1,0},{2,3},{3,2},{4,5},{5,4},{6,7},{7,6},{8,9},{9,8},{10,11... | collective-permute-start | bytes 196616 | tf_op jit(solution)/shard_map/ppermute | solution.py:25
  46.7 11.7 %copy-start.17 = (f32[896,128]{1,0:T(8,128)}, f32[896,128]{1,0:T(8,128)S(1)}, u32[]{:S(2)}) copy-start(f32[896,128]{1,0:T(8,128)S(1)} %get-tuple-element.44.refs_2_) | copy-start | bytes 1376260
  58.3 26.3 %copy-start.23 = (s32[256,7]{0,1:T(8,128)S(1)}, s32[256,7]{0,1:T(8,128)}, u32[]{:S(2)}) copy-start(s32[256,7]{0,1:T(8,128)} %param.14) | copy-start | bytes 21508
  58.4 0.7 copy-start.19
  59.1 21.2 %copy-start.13 = (f32[32,256]{1,0:T(8,128)}, f32[32,256]{1,0:T(8,128)S(1)}, u32[]{:S(2)}) copy-start(f32[32,256]{1,0:T(8,128)S(1)} %get-tuple-element.33.refs_2_.refs_1_.refs_6_) | copy-start | bytes 98308
  59.1 30.4 %all-to-all-start.2 = ((bf16[16,32,256]{2,1,0:T(8,128)(2,1)}), bf16[16,32,256]{2,1,0:T(8,128)(2,1)}, u32[]{:S(2)}, u32[]{:S(2)}) async-start(bf16[16,32,256]{2,1,0:T(8,128)(2,1)} %copy-done.19), calls=%async_computation.2 | async-start | bytes 524288 | tf_op jit(solution)/shard_map/all_to_all | solution.py:38
  74.3 0.9 copy-start.8
  76.8 1.0 copy-start.11
  77.8 30.4 %collective-permute-start.1 = (bf16[256,2048]{1,0:T(8,128)(2,1)}, bf16[256,2048]{1,0:T(8,128)(2,1)S(1)}, u32[]{:S(2)}, u32[]{:S(2)}) collective-permute-start(bf16[256,2048]{1,0:T(8,128)(2,1)} %get-tuple-element.39), channel_id=1, source_target_pairs={{0,1},{1,0},{2,3},{3,2},{4,5},{5,4},{6,7},{7,6},{8,9},{9,8},{10,11... | collective-permute-start | bytes 3145736 | tf_op jit(solution)/shard_map/ppermute | solution.py:25
  80.2 0.8 copy-start.14
  81.0 0.7 copy-start.25
  82.4 0.8 copy-start.15
  83.7 1.0 copy-start.9
  84.7 0.7 copy-start.30
  94.6 22.9 %copy-start.16 = (f32[32,256]{1,0:T(8,128)S(1)}, f32[32,256]{1,0:T(8,128)}, u32[]{:S(2)}) copy-start(f32[32,256]{1,0:T(8,128)} %copy-done.13) | copy-start | bytes 98308
  103.9 0.7 copy-start.3
  104.6 10.4 %all-to-all-start.4 = ((bf16[4,304,128]{2,1,0:T(8,128)(2,1)}), bf16[4,304,128]{2,1,0:T(8,128)(2,1)S(1)}, u32[]{:S(2)}, u32[]{:S(2)}) async-start(bf16[4,304,128]{2,1,0:T(8,128)(2,1)} %copy-done.3), calls=%async_computation.4 | async-start | bytes 622592 | tf_op jit(solution)/shard_map/all_to_all | solution.py:38
  108.1 22.9 %copy-start.27 = (f32[128]{0:T(128)S(1)}, f32[128]{0:T(128)}, u32[]{:S(2)}) copy-start(f32[128]{0:T(128)} %param.18) | copy-start | bytes 1540
  108.1 22.8 %copy-start.29 = (f32[128]{0:T(128)S(1)}, f32[128]{0:T(128)}, u32[]{:S(2)}) copy-start(f32[128]{0:T(128)} %param.19) | copy-start | bytes 1540
  115.0 16.0 %copy-start.10 = (bf16[4096,128]{1,0:T(8,128)(2,1)S(1)}, bf16[4096,128]{1,0:T(8,128)(2,1)}, u32[]{:S(2)}) copy-start(bf16[4096,128]{1,0:T(8,128)(2,1)} %copy-done.9) | copy-start | bytes 3145732
  115.0 16.0 %copy-start.18 = (f32[896,128]{1,0:T(8,128)S(1)}, f32[896,128]{1,0:T(8,128)}, u32[]{:S(2)}) copy-start(f32[896,128]{1,0:T(8,128)} %copy-done.17) | copy-start | bytes 1376260
  118.8 20.7 %copy-start.12 = (bf16[256,2048]{1,0:T(8,128)(2,1)S(1)}, bf16[256,2048]{1,0:T(8,128)(2,1)}, u32[]{:S(2)}) copy-start(bf16[256,2048]{1,0:T(8,128)(2,1)} %copy-done.11) | copy-start | bytes 3145732
  132.5 6.9 %collective-permute-start.2 = (bf16[544,128]{1,0:T(8,128)(2,1)S(1)}, bf16[544,128]{1,0:T(8,128)(2,1)S(1)}, u32[]{:S(2)}, u32[]{:S(2)}) collective-permute-start(bf16[544,128]{1,0:T(8,128)(2,1)S(1)} %get-tuple-element.48), channel_id=1, source_target_pairs={{0,1},{1,0},{2,3},{3,2},{4,5},{5,4},{6,7},{7,6},{8,9},{9,8},{10,11... | collective-permute-start | bytes 417800 | tf_op jit(solution)/shard_map/ppermute | solution.py:25
  139.4 19.8 %copy-start.6 = (bf16[16,4096]{1,0:T(8,128)(2,1)S(1)}, bf16[16,4096]{1,0:T(8,128)(2,1)}, u32[]{:S(2)}) copy-start(bf16[16,4096]{1,0:T(8,128)(2,1)} %refs_1_.5) | copy-start | bytes 393220
  139.4 19.8 %copy-start.22 = (f32[4096]{0:T(1024)S(1)}, f32[4096]{0:T(1024)}, u32[]{:S(2)}) copy-start(f32[4096]{0:T(1024)} %param.15) | copy-start | bytes 49156

commit v12 on v11

--- a/solution.py
+++ b/solution.py
@@ -343,13 +343,12 @@
         after=after,
         scratch=[pltpu.VMEM((24, LANES), jnp.float32)],
     )
-    (sent,) = kernel_call(pass_logits_kernel, [copies], [exchange(sent, axes, everywhere([lines, across]))])
+    (sent,) = kernel_call(pass_logits_kernel, [copies], [exchange(sent, axes, everywhere([lines, across]))], after=after_logits)
     arrived = exchange(sent, axes, everywhere([across, lines]))
     coefs, inverse = kernel_call(
         softmax_kernel,
         [((count + 24, LANES), jnp.float32), ((8, LANES), jnp.float32)],
         [arrived, positive_hot],
-        after=after_logits,
     )
     both = lax.all_gather(coefs, "core", axis=0)
     d_resid16, loss = kernel_call(

time: 161 us -> 161 us (level)
    ppermute x3, waiting for transfers between devices: 6.86 us -> 8.77 us  [swapped(): return lax.ppermute(value, axis, pairs)]
    all_to_all x2, waiting for transfers between devices: 10.8 us -> 8.91 us  [exchange(): lax.all_to_all(blocks, axis, 0, 0, axis_index_groups=groups, tiled=True)]
  transfers between devices with their start and end apart: 5 -> 5, of which waited for: 4 -> 5; matrix products, arithmetic and copies ran while one was open for 0% -> 0% of each run, Pallas kernels for 4% -> 4%
where the time goes in v12:
time: 161 us; the launch traced here: 160 us
  blocking collectives  91.1 us (57%)
  starting transfers between devices  26.3 us (16%)
  waiting for transfers between devices  17.7 us (11%)
  Pallas kernels  15.4 us (10%)
  local copies, waits for them, and re-layouts  8.84 us (5%)
    all_to_all x5, blocking collectives, exchange(): lax.all_to_all(blocks, axis, 0, 0, axis_index_groups=groups, tiled=True)  86.8 us
    all_to_all x2, starting transfers between devices, exchange(): lax.all_to_all(blocks, axis, 0, 0, axis_index_groups=groups, tiled=True)  18.8 us
    pallas_call x17, Pallas kernels, kernel_call(): pl.pallas_call(kernel, out_shape=[jax.ShapeDtypeStruct(shape, dtype) for...  15.4 us
    all_to_all x2, waiting for transfers between devices, exchange(): lax.all_to_all(blocks, axis, 0, 0, axis_index_groups=groups, tiled=True)  8.91 us
    unnamed x62, local copies, waits for them, and re-layouts  8.84 us
    ppermute x3, waiting for transfers between devices, swapped(): return lax.ppermute(value, axis, pairs)  8.77 us
    ppermute x3, starting transfers between devices, swapped(): return lax.ppermute(value, axis, pairs)  7.54 us
  transfers between devices with their start and end apart: 5, of which 5 were waited for; matrix products, arithmetic and copies ran while one was open for 0% of the time, Pallas kernels for 4%

profile of v12, /device:TPU:32, one launch (start us, length us, event | category | flops | bytes accessed | tf_op | source)
XLA Modules:
  0.0 160.3 jit_solution(16022073019545727412)
XLA Ops:
  0.6 0.0 copy-start.4
  0.6 0.9 copy-done.4
  1.5 0.7 copy-done.21
  2.3 0.3 shard_map.122
  2.6 0.0 copy-start.1
  2.6 0.0 copy-start.2
  2.6 35.4 %all_to_all.35.refs_0_ = bf16[16,512,128]{2,1,0:T(8,128)(2,1)S(1)} all-to-all(bf16[16,512,128]{2,1,0:T(8,128)(2,1)S(1)} %shard_map.122), channel_id=1, replica_groups=mesh['z_far'=8,'z_pair'=2,'core'=2,'tensor'=16] {'tensor'}, dimensions={0} | all-to-all | bytes 4194304 | tf_op jit(solution)/shard_map/all_to_all | solution.py:38
  38.0 0.0 copy-done.1
  38.0 0.0 copy-done.2
  38.0 0.0 copy-start.5
  38.0 0.0 copy-start.26
  38.0 0.0 copy-start.28
  38.0 1.2 shard_map.123
  39.3 0.0 copy-start.7
  39.3 0.0 copy-start.20
  39.3 2.6 %collective-permute-start = (bf16[256,128]{1,0:T(8,128)(2,1)S(1)}, bf16[256,128]{1,0:T(8,128)(2,1)S(1)}, u32[]{:S(2)}, u32[]{:S(2)}) collective-permute-start(bf16[256,128]{1,0:T(8,128)(2,1)S(1)} %get-tuple-element.28), channel_id=1, source_target_pairs={{0,1},{1,0},{2,3},{3,2},{4,5},{5,4},{6,7},{7,6},{8,9},{9,8},{10,11... | collective-permute-start | bytes 196616 | tf_op jit(solution)/shard_map/ppermute | solution.py:25
  41.9 0.0 copy-done.24
  41.9 0.7 shard_map.124
  42.6 3.0 %collective-permute-done.refs_1_ = bf16[256,128]{1,0:T(8,128)(2,1)S(1)} collective-permute-done((bf16[256,128]{1,0:T(8,128)(2,1)S(1)}, bf16[256,128]{1,0:T(8,128)(2,1)S(1)}, u32[]{:S(2)}, u32[]{:S(2)}) %collective-permute-start) | collective-permute-done | bytes 65568 | tf_op jit(solution)/shard_map/ppermute | solution.py:25
  45.6 0.0 copy-done
  45.6 0.0 copy-done.26
  45.6 1.0 shard_map.125
  46.7 11.6 %all_to_all.36.refs_0_ = bf16[16,32,256]{2,1,0:T(8,128)(2,1)S(1)} all-to-all(bf16[16,32,256]{2,1,0:T(8,128)(2,1)S(1)} %get-tuple-element.31), channel_id=1, replica_groups=mesh['z_far'=8,'z_pair'=2,'core'=2,'tensor'=16] {'tensor'}, dimensions={0} | all-to-all | bytes 524288 | tf_op jit(solution)/shard_map/all_to_all | solution.py:38
  58.3 0.1 shard_map.126
  58.4 0.7 copy-done.19
  59.1 15.2 %all-to-all-start.2 = ((bf16[16,32,256]{2,1,0:T(8,128)(2,1)}), bf16[16,32,256]{2,1,0:T(8,128)(2,1)}, u32[]{:S(2)}, u32[]{:S(2)}) async-start(bf16[16,32,256]{2,1,0:T(8,128)(2,1)} %copy-done.19), calls=%async_computation.2 | async-start | bytes 524288 | tf_op jit(solution)/shard_map/all_to_all | solution.py:38
  74.3 0.9 copy-done.8
  75.2 1.6 shard_map.131
  76.8 1.0 copy-done.11
  77.8 2.5 %collective-permute-start.1 = (bf16[256,2048]{1,0:T(8,128)(2,1)}, bf16[256,2048]{1,0:T(8,128)(2,1)S(1)}, u32[]{:S(2)}, u32[]{:S(2)}) collective-permute-start(bf16[256,2048]{1,0:T(8,128)(2,1)} %get-tuple-element.39), channel_id=1, source_target_pairs={{0,1},{1,0},{2,3},{3,2},{4,5},{5,4},{6,7},{7,6},{8,9},{9,8},{10,11... | collective-permute-start | bytes 3145736 | tf_op jit(solution)/shard_map/ppermute | solution.py:25
  80.3 0.7 copy-done.14
  81.0 0.7 copy-done.25
  81.7 0.7 shard_map.129
  82.4 0.7 copy-done.15
  83.1 0.5 shard_map.128
  83.7 1.0 copy-done.9
  84.7 0.0 copy-done.23
  84.7 0.7 copy-done.30
  85.3 0.2 shard_map.127
  85.6 3.9 %all-to-all-done.2 = bf16[16,32,256]{2,1,0:T(8,128)(2,1)} async-done(((bf16[16,32,256]{2,1,0:T(8,128)(2,1)}), bf16[16,32,256]{2,1,0:T(8,128)(2,1)}, u32[]{:S(2)}, u32[]{:S(2)}) %all-to-all-start.2) | async-done | bytes 262176 | tf_op jit(solution)/shard_map/all_to_all | solution.py:38
  89.5 2.4 %all-gather = bf16[16,64,256]{2,1,0:T(8,128)(2,1)S(1)} all-gather(bf16[16,32,256]{2,1,0:T(8,128)(2,1)} %all-to-all-done.2), channel_id=2, replica_groups=mesh['z_far'=8,'z_pair'=2,'core'=2,'tensor'=16] {'core'}, dimensions={1}, use_global_device_ids=true | all-gather | bytes 786432 | tf_op jit(solution)/shard_map/all_gather | solution.py:761
  91.9 2.7 %shard_map.130 = bf16[4,304,128]{2,1,0:T(8,128)(2,1)S(1)} custom-call(bf16[1024,256]{1,0:T(8,128)(2,1)S(1)} %bitcast.9, bf16[256,1024]{1,0:T(8,128)(2,1)S(1)} %get-tuple-element.34.refs_1_.refs_4_, bf16[256,1024]{1,0:T(8,128)(2,1)S(1)} %get-tuple-element.35.refs_2_.refs_1_.refs_3_, s32[16,256]{1,0:T(8,128)S(1)} %get-tuple-element.36.refs_3_.refs_5_, ...), custom_call_target="tpu_custom_call" | custom-call | tf_op jit(solution)/shard_map/pallas_call | solution.py:262
  94.6 0.7 copy-done.3
  95.3 3.6 %all-to-all-start.3 = ((bf16[4,304,128]{2,1,0:T(8,128)(2,1)}), bf16[4,304,128]{2,1,0:T(8,128)(2,1)S(1)}, u32[]{:S(2)}, u32[]{:S(2)}) async-start(bf16[4,304,128]{2,1,0:T(8,128)(2,1)} %copy-done.3), calls=%async_computation.3 | async-start | bytes 622592 | tf_op jit(solution)/shard_map/all_to_all | solution.py:38
  98.9 1.9 %collective-permute-done.1.refs_1_.refs_4_ = bf16[256,2048]{1,0:T(8,128)(2,1)S(1)} collective-permute-done((bf16[256,2048]{1,0:T(8,128)(2,1)}, bf16[256,2048]{1,0:T(8,128)(2,1)S(1)}, u32[]{:S(2)}, u32[]{:S(2)}) %collective-permute-start.1) | collective-permute-done | bytes 1048608 | tf_op jit(solution)/shard_map/ppermute | solution.py:25
  100.8 5.0 %all-to-all-done.3.refs_0_ = bf16[4,304,128]{2,1,0:T(8,128)(2,1)S(1)} async-done(((bf16[4,304,128]{2,1,0:T(8,128)(2,1)}), bf16[4,304,128]{2,1,0:T(8,128)(2,1)S(1)}, u32[]{:S(2)}, u32[]{:S(2)}) %all-to-all-start.3) | async-done | bytes 311328 | tf_op jit(solution)/shard_map/all_to_all | solution.py:38
  105.8 0.0 copy-start.10
  105.8 0.0 copy-start.18
  105.8 0.0 copy-start.27
  105.9 0.0 copy-start.29
  105.9 9.4 %all_to_all.37.refs_0_ = bf16[4,304,128]{2,1,0:T(8,128)(2,1)S(1)} all-to-all(bf16[4,304,128]{2,1,0:T(8,128)(2,1)S(1)} %shard_map.132), channel_id=1, replica_groups={{0,4,8,12},{1,5,9,13},{2,6,10,14},{3,7,11,15},{16,17,18,19},{20,21,22,2..., dimensions={0} | all-to-all | bytes 622592 | tf_op jit(solution)/shard_map/all_to_all | solution.py:38
  115.3 0.3 shard_map.133
  115.6 2.0 %all-gather.1 = f32[560,128]{1,0:T(8,128)S(1)} all-gather(f32[280,128]{1,0:T(8,128)S(1)} %get-tuple-element.40), channel_id=3, replica_groups=mesh['z_far'=8,'z_pair'=2,'core'=2,'tensor'=16] {'core'}, dimensions={0}, use_global_device_ids=true | all-gather | bytes 430080 | tf_op jit(solution)/shard_map/all_gather | solution.py:353
  117.7 1.3 shard_map.134
  119.0 12.1 %all_to_all.38.refs_0_ = bf16[16,32,256]{2,1,0:T(8,128)(2,1)S(1)} all-to-all(bf16[16,32,256]{2,1,0:T(8,128)(2,1)S(1)} %get-tuple-element.42), channel_id=1, replica_groups=mesh['z_far'=8,'z_pair'=2,'core'=2,'tensor'=16] {'tensor'}, dimensions={0} | all-to-all | bytes 524288 | tf_op jit(solution)/shard_map/all_to_all | solution.py:38
  131.0 0.0 copy-done.29
  131.1 1.5 shard_map.135
  132.6 2.5 %collective-permute-start.2 = (bf16[544,128]{1,0:T(8,128)(2,1)S(1)}, bf16[544,128]{1,0:T(8,128)(2,1)S(1)}, u32[]{:S(2)}, u32[]{:S(2)}) collective-permute-start(bf16[544,128]{1,0:T(8,128)(2,1)S(1)} %get-tuple-element.48), channel_id=1, source_target_pairs={{0,1},{1,0},{2,3},{3,2},{4,5},{5,4},{6,7},{7,6},{8,9},{9,8},{10,11... | collective-permute-start | bytes 417800 | tf_op jit(solution)/shard_map/ppermute | solution.py:25
  135.1 0.6 shard_map.136
  135.6 3.9 %collective-permute-done.2.refs_1_ = bf16[544,128]{1,0:T(8,128)(2,1)S(1)} collective-permute-done((bf16[544,128]{1,0:T(8,128)(2,1)S(1)}, bf16[544,128]{1,0:T(8,128)(2,1)S(1)}, u32[]{:S(2)}, u32[]{:S(2)}) %collective-permute-start.2) | collective-permute-done | bytes 139296 | tf_op jit(solution)/shard_map/ppermute | solution.py:25
  139.5 0.0 copy-done.12
  139.5 1.6 shard_map.137
  141.1 18.2 %all_to_all.39.refs_0_ = bf16[16,256,128]{2,1,0:T(8,128)(2,1)S(1)} all-to-all(bf16[16,256,128]{2,1,0:T(8,128)(2,1)S(1)} %shard_map.137), channel_id=1, replica_groups=mesh['z_far'=8,'z_pair'=2,'core'=2,'tensor'=16] {'tensor'}, dimensions={0} | all-to-all | bytes 2097152 | tf_op jit(solution)/shard_map/all_to_all | solution.py:38
  159.3 1.0 shard_map.138
  (32 shorter events, 0.1 us)
Async XLA Ops:
  0.6 0.9 copy-start.4
  1.5 0.7 copy-start.21
  2.6 35.4 %copy-start.1 = (bf16[4096,128]{1,0:T(8,128)(2,1)S(1)}, bf16[4096,128]{1,0:T(8,128)(2,1)}, u32[]{:S(2)}) copy-start(bf16[4096,128]{1,0:T(8,128)(2,1)} %refs_0_.9) | copy-start | bytes 3145732
  2.6 35.4 %copy-start.2 = (bf16[4096,128]{1,0:T(8,128)(2,1)S(1)}, bf16[4096,128]{1,0:T(8,128)(2,1)}, u32[]{:S(2)}) copy-start(bf16[4096,128]{1,0:T(8,128)(2,1)} %refs_1_.4) | copy-start | bytes 3145732
  38.0 3.9 %copy-start.24 = (s32[1,32]{1,0:T(1,128)S(1)}, s32[1,32]{1,0:T(1,128)}, u32[]{:S(2)}) copy-start(s32[1,32]{1,0:T(1,128)} %refs_0_.8) | copy-start | bytes 388
  38.0 7.6 %copy-start = (bf16[128,4096]{1,0:T(8,128)(2,1)S(1)}, bf16[128,4096]{1,0:T(8,128)(2,1)}, u32[]{:S(2)}) copy-start(bf16[128,4096]{1,0:T(8,128)(2,1)} %refs_0_.7) | copy-start | bytes 3145732
  38.0 7.6 %copy-start.5 = (bf16[16,4096]{1,0:T(8,128)(2,1)S(1)}, bf16[16,4096]{1,0:T(8,128)(2,1)}, u32[]{:S(2)}) copy-start(bf16[16,4096]{1,0:T(8,128)(2,1)} %refs_1_.5) | copy-start | bytes 393220
  38.0 7.6 %copy-start.26 = (f32[128]{0:T(128)S(1)}, f32[128]{0:T(128)}, u32[]{:S(2)}) copy-start(f32[128]{0:T(128)} %param.18) | copy-start | bytes 1540
  38.0 7.6 %copy-start.28 = (f32[128]{0:T(128)S(1)}, f32[128]{0:T(128)}, u32[]{:S(2)}) copy-start(f32[128]{0:T(128)} %param.19) | copy-start | bytes 1540
  39.3 7.4 %copy-start.7 = (f32[256,128]{1,0:T(8,128)}, f32[256,128]{1,0:T(8,128)S(1)}, u32[]{:S(2)}) copy-start(f32[256,128]{1,0:T(8,128)S(1)} %get-tuple-element.29.refs_1_.refs_2_) | copy-start | bytes 393220
  39.3 19.0 %copy-start.20 = (f32[4096]{0:T(1024)S(1)}, f32[4096]{0:T(1024)}, u32[]{:S(2)}) copy-start(f32[4096]{0:T(1024)} %param.21) | copy-start | bytes 49156
  39.3 6.3 %collective-permute-start = (bf16[256,128]{1,0:T(8,128)(2,1)S(1)}, bf16[256,128]{1,0:T(8,128)(2,1)S(1)}, u32[]{:S(2)}, u32[]{:S(2)}) collective-permute-start(bf16[256,128]{1,0:T(8,128)(2,1)S(1)} %get-tuple-element.28), channel_id=1, source_target_pairs={{0,1},{1,0},{2,3},{3,2},{4,5},{5,4},{6,7},{7,6},{8,9},{9,8},{10,11... | collective-permute-start | bytes 196616 | tf_op jit(solution)/shard_map/ppermute | solution.py:25
  46.7 11.7 %copy-start.17 = (f32[896,128]{1,0:T(8,128)}, f32[896,128]{1,0:T(8,128)S(1)}, u32[]{:S(2)}) copy-start(f32[896,128]{1,0:T(8,128)S(1)} %get-tuple-element.44.refs_2_) | copy-start | bytes 1376260
  58.3 26.3 %copy-start.23 = (s32[256,7]{0,1:T(8,128)S(1)}, s32[256,7]{0,1:T(8,128)}, u32[]{:S(2)}) copy-start(s32[256,7]{0,1:T(8,128)} %param.14) | copy-start | bytes 21508
  58.4 0.7 copy-start.19
  59.1 21.2 %copy-start.13 = (f32[32,256]{1,0:T(8,128)}, f32[32,256]{1,0:T(8,128)S(1)}, u32[]{:S(2)}) copy-start(f32[32,256]{1,0:T(8,128)S(1)} %get-tuple-element.33.refs_2_.refs_1_.refs_6_) | copy-start | bytes 98308
  59.1 30.4 %all-to-all-start.2 = ((bf16[16,32,256]{2,1,0:T(8,128)(2,1)}), bf16[16,32,256]{2,1,0:T(8,128)(2,1)}, u32[]{:S(2)}, u32[]{:S(2)}) async-start(bf16[16,32,256]{2,1,0:T(8,128)(2,1)} %copy-done.19), calls=%async_computation.2 | async-start | bytes 524288 | tf_op jit(solution)/shard_map/all_to_all | solution.py:38
  74.3 0.9 copy-start.8
  76.8 1.0 copy-start.11
  77.8 23.0 %collective-permute-start.1 = (bf16[256,2048]{1,0:T(8,128)(2,1)}, bf16[256,2048]{1,0:T(8,128)(2,1)S(1)}, u32[]{:S(2)}, u32[]{:S(2)}) collective-permute-start(bf16[256,2048]{1,0:T(8,128)(2,1)} %get-tuple-element.39), channel_id=1, source_target_pairs={{0,1},{1,0},{2,3},{3,2},{4,5},{5,4},{6,7},{7,6},{8,9},{9,8},{10,11... | collective-permute-start | bytes 3145736 | tf_op jit(solution)/shard_map/ppermute | solution.py:25
  80.2 0.8 copy-start.14
  81.0 0.7 copy-start.25
  82.4 0.8 copy-start.15
  83.7 1.0 copy-start.9
  84.7 0.7 copy-start.30
  94.6 0.7 copy-start.3
  95.3 22.4 %copy-start.16 = (f32[32,256]{1,0:T(8,128)S(1)}, f32[32,256]{1,0:T(8,128)}, u32[]{:S(2)}) copy-start(f32[32,256]{1,0:T(8,128)} %copy-done.13) | copy-start | bytes 98308
  95.3 10.5 %all-to-all-start.3 = ((bf16[4,304,128]{2,1,0:T(8,128)(2,1)}), bf16[4,304,128]{2,1,0:T(8,128)(2,1)S(1)}, u32[]{:S(2)}, u32[]{:S(2)}) async-start(bf16[4,304,128]{2,1,0:T(8,128)(2,1)} %copy-done.3), calls=%async_computation.3 | async-start | bytes 622592 | tf_op jit(solution)/shard_map/all_to_all | solution.py:38
  105.8 25.2 %copy-start.10 = (bf16[4096,128]{1,0:T(8,128)(2,1)S(1)}, bf16[4096,128]{1,0:T(8,128)(2,1)}, u32[]{:S(2)}) copy-start(bf16[4096,128]{1,0:T(8,128)(2,1)} %copy-done.9) | copy-start | bytes 3145732
  105.8 25.2 %copy-start.18 = (f32[896,128]{1,0:T(8,128)S(1)}, f32[896,128]{1,0:T(8,128)}, u32[]{:S(2)}) copy-start(f32[896,128]{1,0:T(8,128)} %copy-done.17) | copy-start | bytes 1376260
  105.8 25.2 %copy-start.27 = (f32[128]{0:T(128)S(1)}, f32[128]{0:T(128)}, u32[]{:S(2)}) copy-start(f32[128]{0:T(128)} %param.18) | copy-start | bytes 1540
  105.9 25.2 %copy-start.29 = (f32[128]{0:T(128)S(1)}, f32[128]{0:T(128)}, u32[]{:S(2)}) copy-start(f32[128]{0:T(128)} %param.19) | copy-start | bytes 1540
  119.0 20.6 %copy-start.12 = (bf16[256,2048]{1,0:T(8,128)(2,1)S(1)}, bf16[256,2048]{1,0:T(8,128)(2,1)}, u32[]{:S(2)}) copy-start(bf16[256,2048]{1,0:T(8,128)(2,1)} %copy-done.11) | copy-start | bytes 3145732
  132.6 6.9 %collective-permute-start.2 = (bf16[544,128]{1,0:T(8,128)(2,1)S(1)}, bf16[544,128]{1,0:T(8,128)(2,1)S(1)}, u32[]{:S(2)}, u32[]{:S(2)}) collective-permute-start(bf16[544,128]{1,0:T(8,128)(2,1)S(1)} %get-tuple-element.48), channel_id=1, source_target_pairs={{0,1},{1,0},{2,3},{3,2},{4,5},{5,4},{6,7},{7,6},{8,9},{9,8},{10,11... | collective-permute-start | bytes 417800 | tf_op jit(solution)/shard_map/ppermute | solution.py:25
  139.5 19.8 %copy-start.6 = (bf16[16,4096]{1,0:T(8,128)(2,1)S(1)}, bf16[16,4096]{1,0:T(8,128)(2,1)}, u32[]{:S(2)}) copy-start(bf16[16,4096]{1,0:T(8,128)(2,1)} %refs_1_.5) | copy-start | bytes 393220
  139.5 19.8 %copy-start.22 = (f32[4096]{0:T(1024)S(1)}, f32[4096]{0:T(1024)}, u32[]{:S(2)}) copy-start(f32[4096]{0:T(1024)} %param.15) | copy-start | bytes 49156

commit v13 on v11

--- a/solution.py
+++ b/solution.py
@@ -360,9 +360,13 @@
     return loss, exchange(d_resid16, "tensor")
 
 
-def copied_norm_kernel(hidden_ref, gain_ref, out_ref):
+def unit_rows_kernel(hidden_ref, out_ref):
     hidden32 = hidden_ref[...].astype(jnp.float32)
-    normed = (hidden32 * rms_scale(hidden32) * gain_ref[...]).astype(jnp.bfloat16)
+    out_ref[...] = hidden32 * rms_scale(hidden32)
+
+
+def copied_norm_kernel(unit_ref, gain_ref, out_ref):
+    normed = (unit_ref[...] * gain_ref[...]).astype(jnp.bfloat16)
     height = normed.shape[0]
     for c in range(normed.shape[1] // LANES):
         block = normed[:, LANES * c : LANES * (c + 1)]
@@ -709,8 +713,9 @@
     flat = (tensor_count, own_rows * features // LANES, LANES)
     gain_rows = [q_gain[None, :], k_gain[None, :]]
 
+    (unit_rows,) = kernel_call(unit_rows_kernel, [((own_rows, features), f32)], [hidden])
     (copies,) = kernel_call(
-        copied_norm_kernel, [(flat, bf16)], [hidden, in_gain[None, :]]
+        copied_norm_kernel, [(flat, bf16)], [unit_rows, in_gain[None, :]]
     )
     piece = exchange(copies, "tensor")
     kv_own, kv_own16, query_all = kernel_call(

time: 161 us -> 161 us (level)
    pallas_call x17 -> x18, Pallas kernels: 15.4 us -> 15.4 us  [kernel_call(): pl.pallas_call(kernel, out_shape=[jax.ShapeDtypeStruct(shape, dtype) for...]
where the time goes in v13:
time: 161 us; the launch traced here: 160 us
  blocking collectives  91.2 us (57%)
  starting transfers between devices  26.2 us (16%)
  waiting for transfers between devices  17.7 us (11%)
  Pallas kernels  15.4 us (10%)
  local copies, waits for them, and re-layouts  8.84 us (5%)
    all_to_all x5, blocking collectives, exchange(): lax.all_to_all(blocks, axis, 0, 0, axis_index_groups=groups, tiled=True)  86.7 us
    all_to_all x2, starting transfers between devices, exchange(): lax.all_to_all(blocks, axis, 0, 0, axis_index_groups=groups, tiled=True)  18.7 us
    pallas_call x18, Pallas kernels, kernel_call(): pl.pallas_call(kernel, out_shape=[jax.ShapeDtypeStruct(shape, dtype) for...  15.4 us
    all_to_all x2, waiting for transfers between devices, exchange(): lax.all_to_all(blocks, axis, 0, 0, axis_index_groups=groups, tiled=True)  10.8 us
    unnamed x62, local copies, waits for them, and re-layouts  8.84 us
    ppermute x3, starting transfers between devices, swapped(): return lax.ppermute(value, axis, pairs)  7.54 us
    ppermute x3, waiting for transfers between devices, swapped(): return lax.ppermute(value, axis, pairs)  6.87 us
  transfers between devices with their start and end apart: 5, of which 4 were waited for; matrix products, arithmetic and copies ran while one was open for 0% of the time, Pallas kernels for 4%

profile of v13, /device:TPU:32, one launch (start us, length us, event | category | flops | bytes accessed | tf_op | source)
XLA Modules:
  0.0 160.3 jit_solution(9174557472182660561)
XLA Ops:
  0.6 0.0 copy-start.4
  0.6 0.9 copy-done.4
  1.5 0.1 shard_map.122.refs_0_
  1.7 0.0 copy-start.21
  1.7 0.7 copy-done.21
  2.4 0.2 shard_map.123
  2.6 0.0 copy-start.1
  2.6 0.0 copy-start.2
  2.6 35.4 %all_to_all.35.refs_0_ = bf16[16,512,128]{2,1,0:T(8,128)(2,1)S(1)} all-to-all(bf16[16,512,128]{2,1,0:T(8,128)(2,1)S(1)} %shard_map.123), channel_id=1, replica_groups=mesh['z_far'=8,'z_pair'=2,'core'=2,'tensor'=16] {'tensor'}, dimensions={0} | all-to-all | bytes 4194304 | tf_op jit(solution)/shard_map/all_to_all | solution.py:38
  38.0 0.0 copy-done.1
  38.0 0.0 copy-start.5
  38.0 0.0 copy-start.26
  38.0 0.0 copy-start.28
  38.0 1.2 shard_map.124
  39.3 0.0 copy-start.7
  39.3 0.0 copy-start.20
  39.3 2.6 %collective-permute-start = (bf16[256,128]{1,0:T(8,128)(2,1)S(1)}, bf16[256,128]{1,0:T(8,128)(2,1)S(1)}, u32[]{:S(2)}, u32[]{:S(2)}) collective-permute-start(bf16[256,128]{1,0:T(8,128)(2,1)S(1)} %get-tuple-element.28), channel_id=1, source_target_pairs={{0,1},{1,0},{2,3},{3,2},{4,5},{5,4},{6,7},{7,6},{8,9},{9,8},{10,11... | collective-permute-start | bytes 196616 | tf_op jit(solution)/shard_map/ppermute | solution.py:25
  41.9 0.0 copy-done.24
  41.9 0.7 shard_map.125
  42.6 3.0 %collective-permute-done.refs_1_ = bf16[256,128]{1,0:T(8,128)(2,1)S(1)} collective-permute-done((bf16[256,128]{1,0:T(8,128)(2,1)S(1)}, bf16[256,128]{1,0:T(8,128)(2,1)S(1)}, u32[]{:S(2)}, u32[]{:S(2)}) %collective-permute-start) | collective-permute-done | bytes 65568 | tf_op jit(solution)/shard_map/ppermute | solution.py:25
  45.6 0.0 copy-done.5
  45.6 1.0 shard_map.126
  46.7 0.0 copy-done.7
  46.7 0.0 copy-start.17
  46.7 11.6 %all_to_all.36.refs_0_ = bf16[16,32,256]{2,1,0:T(8,128)(2,1)S(1)} all-to-all(bf16[16,32,256]{2,1,0:T(8,128)(2,1)S(1)} %get-tuple-element.31), channel_id=1, replica_groups=mesh['z_far'=8,'z_pair'=2,'core'=2,'tensor'=16] {'tensor'}, dimensions={0} | all-to-all | bytes 524288 | tf_op jit(solution)/shard_map/all_to_all | solution.py:38
  58.3 0.1 shard_map.127
  58.4 0.7 copy-done.19
  59.1 15.2 %all-to-all-start.2 = ((bf16[16,32,256]{2,1,0:T(8,128)(2,1)}), bf16[16,32,256]{2,1,0:T(8,128)(2,1)}, u32[]{:S(2)}, u32[]{:S(2)}) async-start(bf16[16,32,256]{2,1,0:T(8,128)(2,1)} %copy-done.19), calls=%async_computation.2 | async-start | bytes 524288 | tf_op jit(solution)/shard_map/all_to_all | solution.py:38
  74.3 0.9 copy-done.8
  75.2 1.6 shard_map.133
  76.8 1.0 copy-done.11
  77.8 2.5 %collective-permute-start.1 = (bf16[256,2048]{1,0:T(8,128)(2,1)}, bf16[256,2048]{1,0:T(8,128)(2,1)S(1)}, u32[]{:S(2)}, u32[]{:S(2)}) collective-permute-start(bf16[256,2048]{1,0:T(8,128)(2,1)} %get-tuple-element.39), channel_id=1, source_target_pairs={{0,1},{1,0},{2,3},{3,2},{4,5},{5,4},{6,7},{7,6},{8,9},{9,8},{10,11... | collective-permute-start | bytes 3145736 | tf_op jit(solution)/shard_map/ppermute | solution.py:25
  80.3 0.7 copy-done.14
  81.0 0.7 copy-done.25
  81.7 0.7 shard_map.130
  82.4 0.7 copy-done.15
  83.1 0.5 shard_map.129
  83.7 1.0 copy-done.9
  84.7 0.0 copy-done.23
  84.7 0.7 copy-done.30
  85.3 0.2 shard_map.128
  85.6 3.9 %all-to-all-done.2 = bf16[16,32,256]{2,1,0:T(8,128)(2,1)} async-done(((bf16[16,32,256]{2,1,0:T(8,128)(2,1)}), bf16[16,32,256]{2,1,0:T(8,128)(2,1)}, u32[]{:S(2)}, u32[]{:S(2)}) %all-to-all-start.2) | async-done | bytes 262176 | tf_op jit(solution)/shard_map/all_to_all | solution.py:38
  89.5 2.4 %all-gather = bf16[16,64,256]{2,1,0:T(8,128)(2,1)S(1)} all-gather(bf16[16,32,256]{2,1,0:T(8,128)(2,1)} %all-to-all-done.2), channel_id=2, replica_groups=mesh['z_far'=8,'z_pair'=2,'core'=2,'tensor'=16] {'core'}, dimensions={1}, use_global_device_ids=true | all-gather | bytes 786432 | tf_op jit(solution)/shard_map/all_gather | solution.py:767
  91.9 2.7 %shard_map.131 = bf16[4,304,128]{2,1,0:T(8,128)(2,1)S(1)} custom-call(bf16[1024,256]{1,0:T(8,128)(2,1)S(1)} %bitcast.9, bf16[256,1024]{1,0:T(8,128)(2,1)S(1)} %get-tuple-element.34.refs_1_.refs_4_, bf16[256,1024]{1,0:T(8,128)(2,1)S(1)} %get-tuple-element.35.refs_2_.refs_1_.refs_3_, s32[16,256]{1,0:T(8,128)S(1)} %get-tuple-element.36.refs_3_.refs_5_, ...), custom_call_target="tpu_custom_call" | custom-call | tf_op jit(solution)/shard_map/pallas_call | solution.py:262
  94.6 9.3 %all_to_all.37.refs_0_ = bf16[4,304,128]{2,1,0:T(8,128)(2,1)S(1)} all-to-all(bf16[4,304,128]{2,1,0:T(8,128)(2,1)S(1)} %shard_map.131), channel_id=1, replica_groups={{0,1,2,3},{4,5,6,7},{8,9,10,11},{12,13,14,15},{16,20,24,28},{17,21,25,2..., dimensions={0} | all-to-all | bytes 622592 | tf_op jit(solution)/shard_map/all_to_all | solution.py:38
  103.9 0.0 copy-start.3
  103.9 0.7 copy-done.3
  104.6 3.5 %all-to-all-start.4 = ((bf16[4,304,128]{2,1,0:T(8,128)(2,1)}), bf16[4,304,128]{2,1,0:T(8,128)(2,1)S(1)}, u32[]{:S(2)}, u32[]{:S(2)}) async-start(bf16[4,304,128]{2,1,0:T(8,128)(2,1)} %copy-done.3), calls=%async_computation.4 | async-start | bytes 622592 | tf_op jit(solution)/shard_map/all_to_all | solution.py:38
  108.1 0.0 copy-start.27
  108.1 0.0 copy-start.29
  108.1 0.0 collective-permute-done.1.refs_2_.refs_4_
  108.1 6.9 %all-to-all-done.4.refs_0_ = bf16[4,304,128]{2,1,0:T(8,128)(2,1)S(1)} async-done(((bf16[4,304,128]{2,1,0:T(8,128)(2,1)}), bf16[4,304,128]{2,1,0:T(8,128)(2,1)S(1)}, u32[]{:S(2)}, u32[]{:S(2)}) %all-to-all-start.4) | async-done | bytes 311328 | tf_op jit(solution)/shard_map/all_to_all | solution.py:38
  115.0 0.3 shard_map.134
  115.4 2.1 %all-gather.1 = f32[560,128]{1,0:T(8,128)S(1)} all-gather(f32[280,128]{1,0:T(8,128)S(1)} %get-tuple-element.40), channel_id=3, replica_groups=mesh['z_far'=8,'z_pair'=2,'core'=2,'tensor'=16] {'core'}, dimensions={0}, use_global_device_ids=true | all-gather | bytes 430080 | tf_op jit(solution)/shard_map/all_gather | solution.py:354
  117.5 1.3 shard_map.135
  118.8 0.0 copy-start.12
  118.8 12.2 %all_to_all.38.refs_0_ = bf16[16,32,256]{2,1,0:T(8,128)(2,1)S(1)} all-to-all(bf16[16,32,256]{2,1,0:T(8,128)(2,1)S(1)} %get-tuple-element.42), channel_id=1, replica_groups=mesh['z_far'=8,'z_pair'=2,'core'=2,'tensor'=16] {'tensor'}, dimensions={0} | all-to-all | bytes 524288 | tf_op jit(solution)/shard_map/all_to_all | solution.py:38
  131.0 1.5 shard_map.136
  132.5 2.5 %collective-permute-start.2 = (bf16[544,128]{1,0:T(8,128)(2,1)S(1)}, bf16[544,128]{1,0:T(8,128)(2,1)S(1)}, u32[]{:S(2)}, u32[]{:S(2)}) collective-permute-start(bf16[544,128]{1,0:T(8,128)(2,1)S(1)} %get-tuple-element.48), channel_id=1, source_target_pairs={{0,1},{1,0},{2,3},{3,2},{4,5},{5,4},{6,7},{7,6},{8,9},{9,8},{10,11... | collective-permute-start | bytes 417800 | tf_op jit(solution)/shard_map/ppermute | solution.py:25
  135.0 0.6 shard_map.137
  135.5 3.9 %collective-permute-done.2.refs_1_ = bf16[544,128]{1,0:T(8,128)(2,1)S(1)} collective-permute-done((bf16[544,128]{1,0:T(8,128)(2,1)S(1)}, bf16[544,128]{1,0:T(8,128)(2,1)S(1)}, u32[]{:S(2)}, u32[]{:S(2)}) %collective-permute-start.2) | collective-permute-done | bytes 139296 | tf_op jit(solution)/shard_map/ppermute | solution.py:25
  139.5 1.6 shard_map.138
  141.0 18.2 %all_to_all.39.refs_0_ = bf16[16,256,128]{2,1,0:T(8,128)(2,1)S(1)} all-to-all(bf16[16,256,128]{2,1,0:T(8,128)(2,1)S(1)} %shard_map.138), channel_id=1, replica_groups=mesh['z_far'=8,'z_pair'=2,'core'=2,'tensor'=16] {'tensor'}, dimensions={0} | all-to-all | bytes 2097152 | tf_op jit(solution)/shard_map/all_to_all | solution.py:38
  159.3 1.0 shard_map.139
  (33 shorter events, 0.1 us)
Async XLA Ops:
  0.6 0.9 copy-start.4
  1.7 0.7 copy-start.21
  2.6 35.4 %copy-start.1 = (bf16[4096,128]{1,0:T(8,128)(2,1)S(1)}, bf16[4096,128]{1,0:T(8,128)(2,1)}, u32[]{:S(2)}) copy-start(bf16[4096,128]{1,0:T(8,128)(2,1)} %refs_0_.9) | copy-start | bytes 3145732
  2.6 35.4 %copy-start.2 = (bf16[4096,128]{1,0:T(8,128)(2,1)S(1)}, bf16[4096,128]{1,0:T(8,128)(2,1)}, u32[]{:S(2)}) copy-start(bf16[4096,128]{1,0:T(8,128)(2,1)} %refs_1_.4) | copy-start | bytes 3145732
  38.0 3.9 %copy-start.24 = (s32[1,32]{1,0:T(1,128)S(1)}, s32[1,32]{1,0:T(1,128)}, u32[]{:S(2)}) copy-start(s32[1,32]{1,0:T(1,128)} %refs_0_.8) | copy-start | bytes 388
  38.0 7.6 %copy-start = (bf16[128,4096]{1,0:T(8,128)(2,1)S(1)}, bf16[128,4096]{1,0:T(8,128)(2,1)}, u32[]{:S(2)}) copy-start(bf16[128,4096]{1,0:T(8,128)(2,1)} %refs_0_.7) | copy-start | bytes 3145732
  38.0 7.6 %copy-start.5 = (bf16[16,4096]{1,0:T(8,128)(2,1)S(1)}, bf16[16,4096]{1,0:T(8,128)(2,1)}, u32[]{:S(2)}) copy-start(bf16[16,4096]{1,0:T(8,128)(2,1)} %refs_1_.5) | copy-start | bytes 393220
  38.0 7.6 %copy-start.26 = (f32[128]{0:T(128)S(1)}, f32[128]{0:T(128)}, u32[]{:S(2)}) copy-start(f32[128]{0:T(128)} %param.18) | copy-start | bytes 1540
  38.0 7.6 %copy-start.28 = (f32[128]{0:T(128)S(1)}, f32[128]{0:T(128)}, u32[]{:S(2)}) copy-start(f32[128]{0:T(128)} %param.19) | copy-start | bytes 1540
  39.3 7.4 %copy-start.7 = (f32[256,128]{1,0:T(8,128)}, f32[256,128]{1,0:T(8,128)S(1)}, u32[]{:S(2)}) copy-start(f32[256,128]{1,0:T(8,128)S(1)} %get-tuple-element.29.refs_1_.refs_2_) | copy-start | bytes 393220
  39.3 19.0 %copy-start.20 = (f32[4096]{0:T(1024)S(1)}, f32[4096]{0:T(1024)}, u32[]{:S(2)}) copy-start(f32[4096]{0:T(1024)} %param.21) | copy-start | bytes 49156
  39.3 6.3 %collective-permute-start = (bf16[256,128]{1,0:T(8,128)(2,1)S(1)}, bf16[256,128]{1,0:T(8,128)(2,1)S(1)}, u32[]{:S(2)}, u32[]{:S(2)}) collective-permute-start(bf16[256,128]{1,0:T(8,128)(2,1)S(1)} %get-tuple-element.28), channel_id=1, source_target_pairs={{0,1},{1,0},{2,3},{3,2},{4,5},{5,4},{6,7},{7,6},{8,9},{9,8},{10,11... | collective-permute-start | bytes 196616 | tf_op jit(solution)/shard_map/ppermute | solution.py:25
  46.7 11.6 %copy-start.17 = (f32[896,128]{1,0:T(8,128)}, f32[896,128]{1,0:T(8,128)S(1)}, u32[]{:S(2)}) copy-start(f32[896,128]{1,0:T(8,128)S(1)} %get-tuple-element.44.refs_2_) | copy-start | bytes 1376260
  58.3 26.3 %copy-start.23 = (s32[256,7]{0,1:T(8,128)S(1)}, s32[256,7]{0,1:T(8,128)}, u32[]{:S(2)}) copy-start(s32[256,7]{0,1:T(8,128)} %param.14) | copy-start | bytes 21508
  58.4 0.7 copy-start.19
  59.1 21.2 %copy-start.13 = (f32[32,256]{1,0:T(8,128)}, f32[32,256]{1,0:T(8,128)S(1)}, u32[]{:S(2)}) copy-start(f32[32,256]{1,0:T(8,128)S(1)} %get-tuple-element.33.refs_2_.refs_1_.refs_6_) | copy-start | bytes 98308
  59.1 30.4 %all-to-all-start.2 = ((bf16[16,32,256]{2,1,0:T(8,128)(2,1)}), bf16[16,32,256]{2,1,0:T(8,128)(2,1)}, u32[]{:S(2)}, u32[]{:S(2)}) async-start(bf16[16,32,256]{2,1,0:T(8,128)(2,1)} %copy-done.19), calls=%async_computation.2 | async-start | bytes 524288 | tf_op jit(solution)/shard_map/all_to_all | solution.py:38
  74.3 0.9 copy-start.8
  76.8 1.0 copy-start.11
  77.8 30.4 %collective-permute-start.1 = (bf16[256,2048]{1,0:T(8,128)(2,1)}, bf16[256,2048]{1,0:T(8,128)(2,1)S(1)}, u32[]{:S(2)}, u32[]{:S(2)}) collective-permute-start(bf16[256,2048]{1,0:T(8,128)(2,1)} %get-tuple-element.39), channel_id=1, source_target_pairs={{0,1},{1,0},{2,3},{3,2},{4,5},{5,4},{6,7},{7,6},{8,9},{9,8},{10,11... | collective-permute-start | bytes 3145736 | tf_op jit(solution)/shard_map/ppermute | solution.py:25
  80.2 0.8 copy-start.14
  81.0 0.7 copy-start.25
  82.4 0.8 copy-start.15
  83.7 1.0 copy-start.9
  84.7 0.7 copy-start.30
  94.6 22.9 %copy-start.16 = (f32[32,256]{1,0:T(8,128)S(1)}, f32[32,256]{1,0:T(8,128)}, u32[]{:S(2)}) copy-start(f32[32,256]{1,0:T(8,128)} %copy-done.13) | copy-start | bytes 98308
  103.9 0.7 copy-start.3
  104.6 10.4 %all-to-all-start.4 = ((bf16[4,304,128]{2,1,0:T(8,128)(2,1)}), bf16[4,304,128]{2,1,0:T(8,128)(2,1)S(1)}, u32[]{:S(2)}, u32[]{:S(2)}) async-start(bf16[4,304,128]{2,1,0:T(8,128)(2,1)} %copy-done.3), calls=%async_computation.4 | async-start | bytes 622592 | tf_op jit(solution)/shard_map/all_to_all | solution.py:38
  108.1 22.9 %copy-start.27 = (f32[128]{0:T(128)S(1)}, f32[128]{0:T(128)}, u32[]{:S(2)}) copy-start(f32[128]{0:T(128)} %param.18) | copy-start | bytes 1540
  108.1 22.8 %copy-start.29 = (f32[128]{0:T(128)S(1)}, f32[128]{0:T(128)}, u32[]{:S(2)}) copy-start(f32[128]{0:T(128)} %param.19) | copy-start | bytes 1540
  115.0 16.0 %copy-start.10 = (bf16[4096,128]{1,0:T(8,128)(2,1)S(1)}, bf16[4096,128]{1,0:T(8,128)(2,1)}, u32[]{:S(2)}) copy-start(bf16[4096,128]{1,0:T(8,128)(2,1)} %copy-done.9) | copy-start | bytes 3145732
  115.0 16.0 %copy-start.18 = (f32[896,128]{1,0:T(8,128)S(1)}, f32[896,128]{1,0:T(8,128)}, u32[]{:S(2)}) copy-start(f32[896,128]{1,0:T(8,128)} %copy-done.17) | copy-start | bytes 1376260
  118.8 20.7 %copy-start.12 = (bf16[256,2048]{1,0:T(8,128)(2,1)S(1)}, bf16[256,2048]{1,0:T(8,128)(2,1)}, u32[]{:S(2)}) copy-start(bf16[256,2048]{1,0:T(8,128)(2,1)} %copy-done.11) | copy-start | bytes 3145732
  132.5 6.9 %collective-permute-start.2 = (bf16[544,128]{1,0:T(8,128)(2,1)S(1)}, bf16[544,128]{1,0:T(8,128)(2,1)S(1)}, u32[]{:S(2)}, u32[]{:S(2)}) collective-permute-start(bf16[544,128]{1,0:T(8,128)(2,1)S(1)} %get-tuple-element.48), channel_id=1, source_target_pairs={{0,1},{1,0},{2,3},{3,2},{4,5},{5,4},{6,7},{7,6},{8,9},{9,8},{10,11... | collective-permute-start | bytes 417800 | tf_op jit(solution)/shard_map/ppermute | solution.py:25
  139.5 19.8 %copy-start.6 = (bf16[16,4096]{1,0:T(8,128)(2,1)S(1)}, bf16[16,4096]{1,0:T(8,128)(2,1)}, u32[]{:S(2)}) copy-start(bf16[16,4096]{1,0:T(8,128)(2,1)} %refs_1_.5) | copy-start | bytes 393220
  139.5 19.8 %copy-start.22 = (f32[4096]{0:T(1024)S(1)}, f32[4096]{0:T(1024)}, u32[]{:S(2)}) copy-start(f32[4096]{0:T(1024)} %param.15) | copy-start | bytes 49156
